TPU v7x, 128 devices: a whole 4x4x4 slice. The times are simulated.
128 devices in a mesh: coarse: 8 (over x, core), fine: 16 (over y, z).
Axes of the slice: x: 4, y: 4, z: 4, core: 2. Of those that a mesh axis runs over, the one named last changes fastest.
Arguments:
- c_old: float32 [32, 128, 256], P('coarse', 'fine'), may hold values from -6 to 6
- s_old: float32 [16, 32, 128, 256], P(None, 'coarse', 'fine'), may hold values from -6 to 6
- rate_time: float32 [16, 32, 128, 256], P(None, 'coarse', 'fine'), may hold values from 0.01 to 100
- capacity: float32 [16], replicated, may hold values from 0.05 to 0.5
- agg_count: int32 [128], P(('coarse', 'fine')), may hold values from 1 to 256, 16384 in all
- coarse_order: int32 [16384], replicated, may hold values from 0 to 16383, as said below
- coarse_cols: int32 [8, 16384], P(None, 'coarse'), may hold values from 0 to 16383
- coarse_off: float32 [8, 16384], P(None, 'coarse'), may hold values from -16 to 16
- coarse_diag: float32 [16384], P('coarse'), may hold values from 160 to 256
Outputs:
- mobile: float32 [32, 128, 256], P('coarse', 'fine')
- immobile: float32 [16, 32, 128, 256], P(None, 'coarse', 'fine')
Inputs may be any that keep to these rules, and one draw needn't show every extreme that they name: agg_count sums to 16384, and some subdomain has exactly 256 aggregates. coarse_order names each coarse unknown once; aggregates g and h name unknowns of the same block of 128 consecutive unknowns only if g - h is a multiple of 128, so one subdomain names at most 2 unknowns of one block, and the subdomain with 256 aggregates names exactly 2 of some block.
All inputs are finite; a program needn't handle non-finite values. No bound on the sum of `agg_count` on one device may be relied on, other than what follows from the above.
Results may differ from a plain program's by a relative error of at most 0.0003.
Values sent between devices are 32-bit elements; how exact they have to be, the bound alone decides.
No kernel may reach another device: no remote copies, remote signals or barrier semaphores. Data moves between devices by JAX's collectives and lax.ppermute only.
A program may use at most 64 MiB of HBM per device.

v0:
```python
import jax
import jax.numpy as jnp
from jax import lax
from jax.sharding import PartitionSpec as P

AGG_CELLS = 64
KJ = 3
ITERS = 2


diffusion_number = 8.0
upwind_number = 2.0
smooth_weight = 0.8
coarse_weight = 0.8


def padded_2(cells, sides, width):
    for axis, dim in sides:
        count = lax.axis_size(axis)
        ends = count - 1
        head = lax.slice_in_dim(cells, 0, width, axis=dim)
        tail = lax.slice_in_dim(cells, cells.shape[dim] - width, cells.shape[dim], axis=dim)
        cells = jnp.concatenate(
            [
                lax.ppermute(tail, axis, [(i, (i + 1) % count) for i in range(ends)]),
                cells,
                lax.ppermute(head, axis, [((i + 1) % count, i) for i in range(ends)]),
            ],
            axis=dim,
        )
    return cells


def entering(shard, axis, combine, identity):
    length, place = (lax.axis_size(axis), lax.axis_index(axis))
    everything = lax.all_gather(shard, axis)
    start = jnp.broadcast_to(jnp.asarray(identity, shard.dtype), shard.shape)

    def hop(k, before):
        reached = k < place
        new = combine(before, everything[k])
        return jnp.where(reached, new, before)

    return lax.fori_loop(0, length, hop, start)


def apply_fine(field, mass):
    padded = padded_2(field, (("coarse", 0), ("fine", 1)), 1)
    beside_all = padded[2:, 1:-1] + padded[:-2, 1:-1]
    beside_all = beside_all + padded[1:-1, 2:] + padded[1:-1, :-2]
    zero_plane = jnp.zeros_like(field[:, :, :1])
    behind = jnp.concatenate([zero_plane, field[:, :, :-1]], 2)
    ahead = jnp.concatenate([field[:, :, 1:], zero_plane], 2)
    centre = mass + 6.0 * diffusion_number + upwind_number
    return (
        centre * field - diffusion_number * (beside_all + behind + ahead) - upwind_number * behind
    )


def solve_small(gram, right):
    count = right.shape[0]
    matrix = [[gram[row, column] for column in range(count)] for row in range(count)]
    vector = [right[row] for row in range(count)]
    for pivot in range(count):
        for row in range(pivot + 1, count):
            factor = matrix[row][pivot] / matrix[pivot][pivot]
            for column in range(pivot, count):
                matrix[row][column] = matrix[row][column] - factor * matrix[pivot][column]
            vector[row] = vector[row] - factor * vector[pivot]
    result = [None] * count
    for row in reversed(range(count)):
        partial_sum = vector[row]
        for column in range(row + 1, count):
            partial_sum = partial_sum - matrix[row][column] * result[column]
        result[row] = partial_sum / matrix[row][row]
    return result


def least_squares(columns, beta):
    hessen = jnp.stack(columns, axis=1)
    gram = jnp.dot(hessen.T, hessen, precision=lax.Precision.HIGHEST)
    return solve_small(gram, beta * hessen[0])


def add_counts(earlier, later):
    return earlier + later


def spread(values):
    return lax.all_gather(values, "coarse", axis=0, tiled=True)


def local(
    c_old, s_old, rate_time, capacity, agg_count, coarse_order, coarse_cols, coarse_off, coarse_diag
):
    share = rate_time / (1.0 + rate_time)
    weighted = capacity[:, None, None, None] * share
    mass = 1.0 + jnp.sum(weighted, 0)
    source = c_old + jnp.sum(weighted * s_old, 0)
    cells = c_old.size
    slot_count = 2 * cells // AGG_CELLS
    total_rows = coarse_order.shape[0]
    before = entering(agg_count, ("coarse", "fine"), add_counts, jnp.zeros((1,), jnp.int32))[0]
    own_count = agg_count[0]
    row_count = cells // 128
    span = 128 * slot_count // cells + 2
    cell_slots = jnp.arange(cells, dtype=jnp.int32) * own_count // cells
    row_first = jnp.arange(row_count, dtype=jnp.int32) * 128 * own_count // cells
    offset_in_row = cell_slots.reshape(row_count, 128) - row_first[:, None]
    member = (offset_in_row[None, :, :] == jnp.arange(span, dtype=jnp.int32)[:, None, None]).astype(
        jnp.float32
    )
    target_slot = jnp.minimum(
        row_first[None, :] + jnp.arange(span, dtype=jnp.int32)[:, None], slot_count - 1
    )
    padded_order = jnp.concatenate([coarse_order, jnp.zeros((slot_count,), jnp.int32)])
    slot_rows = lax.dynamic_slice_in_dim(padded_order, before.astype(jnp.int32), slot_count)
    centre = mass + 6.0 * diffusion_number + upwind_number
    beta = jnp.sqrt(lax.psum(jnp.sum(source * source), ("coarse", "fine")))
    basis = [source / beta]
    directions = []
    columns = []
    for step in range(ITERS):
        precondition_vector = basis[step]
        parts = jnp.sum(member * precondition_vector.reshape(row_count, 128)[None], 2)
        slot_sums = jnp.zeros((slot_count,), jnp.float32).at[target_slot].add(parts)
        dense = jnp.zeros((total_rows,), jnp.float32).at[slot_rows].add(slot_sums)
        summed = lax.psum(dense, "fine")
        coarse_rhs = lax.psum_scatter(summed, "coarse", scatter_dimension=0, tiled=True)
        smooth = smooth_weight * precondition_vector / centre
        smooth = smooth + smooth_weight * (precondition_vector - apply_fine(smooth, mass)) / centre
        correction = coarse_weight * coarse_rhs / coarse_diag
        for sweep in range(KJ - 1):
            whole = spread(correction)
            applied = coarse_diag * correction + jnp.sum(coarse_off * whole[coarse_cols], 0)
            correction = correction + coarse_weight * (coarse_rhs - applied) / coarse_diag
        whole = spread(correction)
        picked = whole[slot_rows][target_slot]
        direction = smooth + jnp.sum(member * picked[:, :, None], 0).reshape(
            precondition_vector.shape
        )
        directions.append(direction)
        image = apply_fine(direction, mass)
        products = lax.psum(
            jnp.stack([jnp.sum(earlier * image) for earlier in basis]), ("coarse", "fine")
        )
        for index in range(len(basis)):
            image = image - products[index] * basis[index]
        leftover = jnp.sqrt(lax.psum(jnp.sum(image * image), ("coarse", "fine")))
        columns.append(
            jnp.concatenate([products, leftover[None], jnp.zeros((ITERS - step - 1,), jnp.float32)])
        )
        if step + 1 < ITERS:
            basis.append(image / leftover)
    weights = least_squares(columns, beta)
    mobile = weights[0] * directions[0]
    index = 1
    mobile = mobile + weights[index] * directions[index]
    immobile = (s_old + rate_time * mobile[None]) / (1.0 + rate_time)
    return (mobile, immobile)


def solution(mesh):
    return jax.shard_map(
        local,
        mesh=mesh,
        in_specs=(
            P("coarse", "fine", None),
            P(None, "coarse", "fine", None),
            P(None, "coarse", "fine", None),
            P(),
            P(("coarse", "fine")),
            P(),
            P(None, "coarse"),
            P(None, "coarse"),
            P("coarse"),
        ),
        out_specs=(P("coarse", "fine", None), P(None, "coarse", "fine", None)),
        check_vma=False,
    )
```

profile of v0, /device:TPU:1, one launch (start us, length us, event | category | flops | bytes accessed | tf_op | source)
XLA Modules:
  0.0 1284.1 jit_solution(10812599081475873261)
XLA Ops:
  7.2 1.4 fusion.52
  9.2 68.7 %psum.49 = f32[]{:T(128)} all-reduce(f32[]{:T(128)} %get-tuple-element.101), channel_id=1, replica_groups=mesh['coarse'=8,'fine'=16] {'coarse','fine'}, use_global_device_ids=true, to_apply=%region_2.3 | all-reduce | flops 1 | bytes 8 | tf_op jit(solution)/shard_map/psum | solution.py:119
  78.6 2.6 collective-permute-start.1
  81.2 1.9 collective-permute-start
  83.9 63.3 %all-reduce.9 = s32[128]{0:T(128)S(1)} all-reduce(s32[128]{0:T(128)S(1)} %dynamic-update-slice), channel_id=2, replica_groups=mesh['coarse'=8,'fine'=16] {'coarse','fine'}, use_global_device_ids=true, to_apply=%add.9 | all-reduce | flops 128 | bytes 1024
  147.3 168.3 %while.13 = (s32[]{:T(128)}, s32[1]{0:T(128)}, s32[]{:T(128)}, s32[128,1]{0,1:T(1,128)S(1)}, s32[]{:T(128)}) while((s32[]{:T(128)}, s32[1]{0:T(128)}, s32[]{:T(128)}, s32[128,1]{0,1:T(1,128)S(1)}, s32[]{:T(128)}) %tuple.63), condition=%wide.region_5.6_spmd, body=%wide.region_4.5_spmd.sunk | while | flops 5 | bytes 115 | solution.py:44
  316.6 3.9 scatter_custom_fusion
  320.5 2.5 scatter_custom_fusion.1
  326.0 1.3 collective-permute-start.2
  327.3 4.0 collective-permute-start.3
  331.3 45.6 %all-reduce.15.cloned.1.call-done = f32[16384]{0:T(1024)} async-done(((f32[16384]{0:T(1024)}), f32[16384]{0:T(1024)}) %all-reduce.15.cloned.1.call-update) | async-done | bytes 65552
  377.6 34.0 %psum.56 = f32[2048]{0:T(1024)S(1)} all-reduce(f32[2048]{0:T(1024)S(1)} %dynamic-slice-done.1), channel_id=1, replica_groups=mesh['coarse'=8,'fine'=16] {'fine'}, use_global_device_ids=true, to_apply=%region_9.10 | all-reduce | flops 2048 | bytes 16384 | tf_op jit(solution)/shard_map/psum | solution.py:128
  411.6 22.4 %all_gather.26 = f32[16384]{0:T(1024)S(1)} all-gather(f32[2048]{0:T(1024)S(1)} %multiply_divide_fusion.3), channel_id=1, replica_groups=mesh['coarse'=8,'fine'=16] {'coarse'}, dimensions={0}, use_global_device_ids=true | all-gather | bytes 73728 | tf_op jit(solution)/shard_map/all_gather | solution.py:90
  434.1 90.5 %gather_fusion = f32[16384]{0:T(1024)S(1)} fusion(f32[16384]{0:T(1024)S(1)} %all_gather.26, s32[16384]{0:T(1024)S(1)} %broadcast_clamp_fusion), kind=kCustom, calls=%fused_computation | custom fusion | bytes 196608 | tf_op jit(solution)/shard_map/gather | solution.py:135
  525.5 12.8 all_gather.27
  538.2 90.5 %gather_fusion.1 = f32[16384]{0:T(1024)S(1)} fusion(f32[16384]{0:T(1024)S(1)} %all_gather.27, s32[16384]{0:T(1024)S(1)} %broadcast_clamp_fusion), kind=kCustom, calls=%fused_computation.1 | custom fusion | bytes 196608 | tf_op jit(solution)/shard_map/gather | solution.py:135
  628.9 12.8 all_gather.28
  641.6 1.7 gather_fusion.2
  643.3 2.8 gather_fusion.3
  646.5 1.9 collective-permute-start.5
  648.4 2.4 collective-permute-start.4
  650.9 2.5 collective-permute-done.4
  653.4 1.3 collective-permute-start.6
  654.7 4.0 collective-permute-start.7
  660.1 63.2 %psum.51 = f32[1]{0:T(128)} all-reduce(f32[1]{0:T(128)} %bitcast.5), channel_id=1, replica_groups=mesh['coarse'=8,'fine'=16] {'coarse','fine'}, use_global_device_ids=true, to_apply=%region_15.16 | all-reduce | flops 1 | bytes 8 | tf_op jit(solution)/shard_map/psum | solution.py:144
  724.5 63.4 %psum.52 = f32[]{:T(128)} all-reduce(f32[]{:T(128)} %multiply_reduce_fusion.8), channel_id=1, replica_groups=mesh['coarse'=8,'fine'=16] {'coarse','fine'}, use_global_device_ids=true, to_apply=%region_17.18 | all-reduce | flops 1 | bytes 8 | tf_op jit(solution)/shard_map/psum | solution.py:149
  789.3 2.5 collective-permute-start.9
  791.8 1.9 collective-permute-start.8
  794.0 3.9 scatter_custom_fusion.2
  797.9 2.5 scatter_custom_fusion.3
  801.7 4.0 collective-permute-start.11
  805.7 49.1 %all-reduce.17.cloned.1.call-done = f32[16384]{0:T(1024)} async-done(((f32[16384]{0:T(1024)}), f32[16384]{0:T(1024)}) %all-reduce.17.cloned.1.call-update) | async-done | bytes 65552
  855.5 34.0 %psum.57 = f32[2048]{0:T(1024)S(1)} all-reduce(f32[2048]{0:T(1024)S(1)} %dynamic-slice-done), channel_id=1, replica_groups=mesh['coarse'=8,'fine'=16] {'fine'}, use_global_device_ids=true, to_apply=%region_21.22 | all-reduce | flops 2048 | bytes 16384 | tf_op jit(solution)/shard_map/psum | solution.py:128
  889.5 22.4 %all_gather.29 = f32[16384]{0:T(1024)S(1)} all-gather(f32[2048]{0:T(1024)S(1)} %multiply_divide_fusion.2), channel_id=1, replica_groups=mesh['coarse'=8,'fine'=16] {'coarse'}, dimensions={0}, use_global_device_ids=true | all-gather | bytes 73728 | tf_op jit(solution)/shard_map/all_gather | solution.py:90
  911.9 90.5 %gather_fusion.4 = f32[16384]{0:T(1024)S(1)} fusion(f32[16384]{0:T(1024)S(1)} %all_gather.29, s32[16384]{0:T(1024)S(1)} %broadcast_clamp_fusion), kind=kCustom, calls=%fused_computation.4 | custom fusion | bytes 196608 | tf_op jit(solution)/shard_map/gather | solution.py:135
  1002.5 12.8 all_gather.30
  1015.3 90.5 %gather_fusion.5 = f32[16384]{0:T(1024)S(1)} fusion(f32[16384]{0:T(1024)S(1)} %all_gather.30, s32[16384]{0:T(1024)S(1)} %broadcast_clamp_fusion), kind=kCustom, calls=%fused_computation.5 | custom fusion | bytes 196608 | tf_op jit(solution)/shard_map/gather | solution.py:135
  1105.9 12.8 all_gather.31
  1118.7 1.7 gather_fusion.6
  1120.4 2.8 gather_fusion.7
  1123.6 2.1 collective-permute-start.13
  1125.6 2.4 collective-permute-start.12
  1128.1 2.5 collective-permute-done.12
  1131.9 4.0 collective-permute-start.15
  1137.4 1.4 pad_maximum_fusion.45
  1138.7 63.1 %psum.54 = f32[2]{0:T(128)S(1)} all-reduce(f32[2]{0:T(128)S(1)} %pad_maximum_fusion.45), channel_id=1, replica_groups=mesh['coarse'=8,'fine'=16] {'coarse','fine'}, use_global_device_ids=true, to_apply=%region_28.29 | all-reduce | flops 2 | bytes 16 | tf_op jit(solution)/shard_map/psum | solution.py:144
  1202.4 2.0 multiply_reduce_fusion.5
  1205.1 63.2 %psum.55 = f32[]{:T(128)} all-reduce(f32[]{:T(128)} %multiply_reduce_fusion.5), channel_id=1, replica_groups=mesh['coarse'=8,'fine'=16] {'coarse','fine'}, use_global_device_ids=true, to_apply=%region_30.31 | all-reduce | flops 1 | bytes 8 | tf_op jit(solution)/shard_map/psum | solution.py:149
  (239 shorter events, 101.4 us)
Async XLA Ops:
  7.2 1.4 copy-start.7
  7.2 369.8 %all-reduce.15.cloned.1.call-start = ((), (), s32[]{:S(2)}) async-start(), calls=%async_computation | async-start | bytes 131072
  78.6 247.3 %collective-permute-start.1 = (f32[1,8,256]{2,1,0:T(8,128)S(1)}, f32[1,8,256]{2,1,0:T(8,128)S(1)}, u32[]{:S(2)}, u32[]{:S(2)}) collective-permute-start(f32[1,8,256]{2,1,0:T(8,128)S(1)} %get-tuple-element.125), channel_id=1, source_target_pairs={{0,16},{16,32},{32,48},{48,64},{64,80},{80,96},{96,112},{1,17},{17... | collective-permute-start | bytes 24584 | tf_op jit(solution)/shard_map/ppermute | solution.py:25
  81.2 244.7 %collective-permute-start = (f32[1,8,256]{2,1,0:T(8,128)S(1)}, f32[1,8,256]{2,1,0:T(8,128)S(1)}, u32[]{:S(2)}, u32[]{:S(2)}) collective-permute-start(f32[1,8,256]{2,1,0:T(8,128)S(1)} %get-tuple-element.126), channel_id=1, source_target_pairs={{16,0},{32,16},{48,32},{64,48},{80,64},{96,80},{112,96},{17,1},{33... | collective-permute-start | bytes 24584 | tf_op jit(solution)/shard_map/ppermute | solution.py:27
  315.7 0.8 copy-start.5
  323.1 531.7 %all-reduce.17.cloned.1.call-start = ((), (), s32[]{:S(2)}) async-start(), calls=%async_computation.1 | async-start | bytes 131072
  323.1 0.8 copy-start.6
  324.1 0.7 copy-start.8
  326.0 320.4 %collective-permute-start.2 = (f32[6,1,256]{2,1,0:T(1,128)S(1)}, f32[6,1,256]{2,1,0:T(1,128)S(1)}, u32[]{:S(2)}, u32[]{:S(2)}) collective-permute-start(f32[6,1,256]{2,1,0:T(1,128)S(1)} %get-tuple-element.109), channel_id=1, source_target_pairs={{1,0},{2,1},{3,2},{4,3},{5,4},{6,5},{7,6},{8,7},{9,8},{10,9},{11,1... | collective-permute-start | bytes 18440 | tf_op jit(solution)/shard_map/ppermute | solution.py:27
  327.3 319.1 %collective-permute-start.3 = (f32[6,1,256]{2,1,0:T(1,128)S(1)}, f32[6,1,256]{2,1,0:T(1,128)S(1)}, u32[]{:S(2)}, u32[]{:S(2)}) collective-permute-start(f32[6,1,256]{2,1,0:T(1,128)S(1)} %get-tuple-element.110), channel_id=1, source_target_pairs={{0,1},{1,2},{2,3},{3,4},{4,5},{5,6},{6,7},{7,8},{8,9},{9,10},{10,1... | collective-permute-start | bytes 18440 | tf_op jit(solution)/shard_map/ppermute | solution.py:25
  376.9 0.7 dynamic-slice-start.1
  377.6 34.0 %copy-start.3 = (f32[2048]{0:T(1024)S(1)}, f32[2048]{0:T(1024)}, u32[]{:S(2)}) copy-start(f32[2048]{0:T(1024)} %param.19) | copy-start | bytes 24580
  524.6 0.8 copy-start.2
  646.5 4.3 collective-permute-start.5
  648.4 5.0 collective-permute-start.4
  653.4 5.4 collective-permute-start.6
  654.7 4.8 collective-permute-start.7
  789.3 11.1 collective-permute-start.9
  791.8 8.6 collective-permute-start.8
  800.4 323.0 %collective-permute-start.10 = (f32[6,1,256]{2,1,0:T(1,128)S(1)}, f32[6,1,256]{2,1,0:T(1,128)S(1)}, u32[]{:S(2)}, u32[]{:S(2)}) collective-permute-start(f32[6,1,256]{2,1,0:T(1,128)S(1)} %get-tuple-element.105), channel_id=1, source_target_pairs={{1,0},{2,1},{3,2},{4,3},{5,4},{6,5},{7,6},{8,7},{9,8},{10,9},{11,1... | collective-permute-start | bytes 18440 | tf_op jit(solution)/shard_map/ppermute | solution.py:27
  801.7 321.7 %collective-permute-start.11 = (f32[6,1,256]{2,1,0:T(1,128)S(1)}, f32[6,1,256]{2,1,0:T(1,128)S(1)}, u32[]{:S(2)}, u32[]{:S(2)}) collective-permute-start(f32[6,1,256]{2,1,0:T(1,128)S(1)} %get-tuple-element.106), channel_id=1, source_target_pairs={{0,1},{1,2},{2,3},{3,4},{4,5},{5,6},{6,7},{7,8},{8,9},{9,10},{10,1... | collective-permute-start | bytes 18440 | tf_op jit(solution)/shard_map/ppermute | solution.py:25
  854.8 0.7 dynamic-slice-start
  1123.4 152.9 %copy-start.1 = (f32[16,4,8,256]{3,2,1,0:T(8,128)S(1)}, f32[16,4,8,256]{3,2,1,0:T(8,128)}, u32[]{:S(2)}) copy-start(f32[16,4,8,256]{3,2,1,0:T(8,128)} %param.12) | copy-start | bytes 1572868
  1123.4 152.9 %copy-start = (f32[16,4,8,256]{3,2,1,0:T(8,128)S(1)}, f32[16,4,8,256]{3,2,1,0:T(8,128)}, u32[]{:S(2)}) copy-start(f32[16,4,8,256]{3,2,1,0:T(8,128)} %param.13) | copy-start | bytes 1572868
  1123.6 4.5 collective-permute-start.13
  1125.6 5.0 collective-permute-start.12
  1130.6 5.4 collective-permute-start.14
  1131.9 4.8 collective-permute-start.15
  1276.3 0.9 copy-start.4
Sparse Core Ops, SparseCore 0:
  323.2 53.6 all-reduce.14
  800.5 54.2 all-reduce.16
where the time goes:
time: 1290 us; the launch traced here: 1280 us
  blocking collectives  549 us (43%)
  local copies, waits for them, and re-layouts  462 us (36%)
  waiting for transfers between devices  101 us (8%)
  loops' own time  85.3 us (7%)
  starting transfers between devices  38.9 us (3%)
  other arithmetic  24.1 us (2%)
  between operations  24.1 us (2%)
    gather x8, local copies, waits for them, and re-layouts, local(): whole[coarse_cols]  362 us
    psum x2, blocking collectives, local(): leftover = jnp.sqrt(lax.psum(jnp.sum(image * image), ('coarse', 'fine')))  127 us
    psum x2, blocking collectives, local(): lax.psum(jnp.stack([jnp.sum(earlier * image) for earlier in basis]), ('co...  126 us
    all_gather x6, blocking collectives, spread(): return lax.all_gather(values, 'coarse', axis=0, tiled=True)  95.8 us
    unnamed x4, waiting for transfers between devices  94.7 us
    another operation x1, loops' own time, entering(): return lax.fori_loop(0, length, hop, start)  85.3 us
    dynamic_slice x128, local copies, waits for them, and re-layouts, hop(): new = combine(before, everything[k])  83 us
    psum x1, blocking collectives, local(): beta = jnp.sqrt(lax.psum(jnp.sum(source * source), ('coarse', 'fine')))  68.7 us
  transfers between devices with their start and end apart: 18, of which 6 were waited for; matrix products, arithmetic and copies ran while one was open for 37% of the time, Pallas kernels for 0%

commit v1 on v0

v1 whole, which is shorter than its diff:
```python
import jax
import jax.numpy as jnp
from jax import lax
from jax.experimental import pallas as pl
from jax.experimental.pallas import tpu as pltpu
from jax.sharding import PartitionSpec as P

BOTH = ("coarse", "fine")
CX, CY, CZ = 4, 8, 256
RATES = 16
KC = 8
DEVICES = 128
LANES = 128
SLOTS = 256
SHARDS = 8
SHARD_ROWS = 2048
FLOW = 50.0
F32, BF16, I32 = jnp.float32, jnp.bfloat16, jnp.int32
VM = pl.BlockSpec(memory_space=pltpu.VMEM)
SM = pl.BlockSpec(memory_space=pltpu.SMEM)


def iota(shape, dim):
    return lax.broadcasted_iota(I32, shape, dim)


def lane_take(table, index):
    return jnp.take_along_axis(table, index, axis=1, mode="promise_in_bounds")


def nt(left, right):
    return lax.dot_general(left, right, (((1,), (1,)), ((), ())), preferred_element_type=F32)


def nn(left, right):
    return jnp.dot(left, right, preferred_element_type=F32)


def split2(values):
    high = values.astype(BF16)
    return high, (values - high.astype(F32)).astype(BF16)


def split3(values):
    high = values.astype(BF16)
    rest = values - high.astype(F32)
    mid = rest.astype(BF16)
    return high, mid, (rest - mid.astype(F32)).astype(BF16)


def slots_of(plane, half, count):
    row = (plane * CY + iota((CY, LANES), 0)) * 2 + half
    return ((row * LANES + iota((CY, LANES), 1)) * count) >> 13


def restrict(cells, count):
    slot = iota((CY, SLOTS), 1)
    total = jnp.zeros((CY, SLOTS), F32)
    for plane in range(CX):
        for half in range(2):
            values = cells[plane][:, half * LANES : (half + 1) * LANES]
            row = (plane * CY + iota((CY, 1), 0)) * 2 + half
            first = (row * count) >> 6
            member = slots_of(plane, half, count) - first
            relative = slot - first
            for k in range(5):
                part = jnp.sum(jnp.where(member == k, values, 0.0), axis=1, keepdims=True)
                total = total + jnp.where(relative == k, part, 0.0)
    return jnp.sum(total, axis=0, keepdims=True)


def prolong(entries, count):
    low = jnp.broadcast_to(entries[:, :LANES], (CY, LANES))
    high = jnp.broadcast_to(entries[:, LANES:], (CY, LANES))
    planes = []
    for plane in range(CX):
        halves = []
        for half in range(2):
            slot = slots_of(plane, half, count)
            place = slot & 127
            halves.append(jnp.where(slot < LANES, lane_take(low, place), lane_take(high, place)))
        planes.append(jnp.concatenate(halves, axis=1))
    return planes


def couple(left, mid, right, up, down):
    length = mid.shape[1]
    lane = iota(mid.shape, 1)
    behind = jnp.where(lane == 0, 0.0, pltpu.roll(mid, 1, 1))
    ahead = jnp.where(lane == length - 1, 0.0, pltpu.roll(mid, length - 1, 1))
    return 8.0 * (left + right + up + down + ahead) + 10.0 * behind


def source_kernel(cap, count, place, c_old, s_old, rate, diag, c_out, ic_out, s_out, zs_out, pay):
    n = count[0]
    planes = []
    for x in range(CX):
        mass = jnp.zeros((CY, CZ), F32)
        extra = jnp.zeros((CY, CZ), F32)
        for k in range(RATES):
            r = rate[k, x]
            weighted = cap[k] * (r / (1.0 + r))
            mass = mass + weighted
            extra = extra + weighted * s_old[k, x]
        centre = (1.0 + mass) + FLOW
        source = c_old[x] + extra
        inverse = 1.0 / centre
        c_out[x] = centre
        ic_out[x] = inverse
        s_out[x] = source
        zs_out[x] = 0.8 * source * inverse
        planes.append(source)
    sums = restrict(planes, n)
    kind = iota((8, LANES), 0) & 3
    rows = [
        sums[:, :LANES],
        sums[:, LANES:],
        diag[pl.ds(place[1], 1), :],
        jnp.full((1, LANES), n, I32).astype(F32),
    ]
    tile = jnp.broadcast_to(rows[3], (8, LANES))
    for k in range(3):
        tile = jnp.where(kind == k, rows[k], tile)
    for i in range(DEVICES // 2):
        pay[pl.ds(8 * i, 8), :] = tile


def order_kernel(order, inverse_out, blocks_out):
    numbers = order[...]
    blocks = (iota((LANES, LANES), 0) == (numbers[0:1, :] >> 7)).astype(F32).astype(BF16)
    blocks_out[...] = blocks
    lows = nt(blocks, (numbers & 127).astype(F32).astype(BF16)).astype(I32)
    lane = iota((LANES, LANES), 1)
    found = jnp.zeros((LANES, LANES), I32)
    for q in range(LANES):
        found = jnp.where(lows[:, q : q + 1] == lane, q, found)
    inverse_out[...] = found


def offsets_of(counts):
    strict = (iota((LANES, LANES), 1) < iota((LANES, LANES), 0)).astype(F32).astype(BF16)
    by_row = nn(strict, counts.astype(BF16)).astype(I32)
    later = iota((LANES, LANES), 0) < iota((LANES, LANES), 1)
    by_lane = jnp.sum(jnp.where(later, counts, 0.0), axis=0, keepdims=True).astype(I32)
    return by_row, by_lane


def assemble(low, high, offsets, inverse, blocks):
    by_row, by_lane = offsets
    lane = iota((LANES, LANES), 1)
    shift = by_row & 127
    place = (lane - shift) & 127
    low = lane_take(low, place)
    high = lane_take(high, place)
    kept = lane >= shift
    rows = (jnp.where(kept, low, 0.0), jnp.where(kept, high, low), jnp.where(kept, 0.0, high))
    start = by_lane >> 7
    table = jnp.zeros((LANES, LANES), F32)
    for j in range(3):
        spot = (iota((LANES, LANES), 0) == start + j).astype(F32).astype(BF16)
        for part in split3(rows[j]):
            table = table + nn(spot, part)
    by_block = jnp.zeros((LANES, LANES), F32)
    for part in split3(table):
        by_block = by_block + nt(blocks, part)
    return lane_take(by_block, inverse)


def fetch(table, unknown):
    inner = unknown & (SHARD_ROWS - 1)
    shard = unknown >> 11
    found = jnp.zeros((SHARDS * 32, SLOTS), F32)
    for chunk in range(SHARD_ROWS // 256):
        spot = (iota((256, SLOTS), 0) + chunk * 256 == inner).astype(F32).astype(BF16)
        found = found + nn(table[:, chunk * 256 : (chunk + 1) * 256], spot)
    found = found.reshape(SHARDS, 32, SLOTS)
    picked = jnp.zeros((32, SLOTS), F32)
    for g in range(SHARDS):
        picked = picked + jnp.where(shard == g, found[g], 0.0)
    return picked[0:8], picked[8:16], picked[16:24] + picked[24:32]


def coarse_solve(values, plan, own):
    high, low = split2(values.T)
    table = jnp.concatenate([high, low], axis=1)
    row = iota((LANES, SLOTS), 0).astype(F32)

    def gather(block, inner):
        spot = (row == block).astype(F32).astype(BF16)
        found = nn(table, jnp.concatenate([spot, spot], axis=0))
        return jnp.sum(jnp.where(row == inner, found, 0.0).reshape(16, 8, SLOTS), axis=0)

    def entry(k, total):
        part = -1.4 * gather(plan[KC, pl.ds(k, 1), :], plan[KC, pl.ds(8 + k, 1), :])
        for j in range(KC):
            weight = plan[k, 16 + j : 17 + j, :]
            part = part + weight * gather(plan[k, j : j + 1, :], plan[k, 8 + j : 9 + j, :])
        return total + plan[KC, pl.ds(16 + k, 1), :] * part

    total = 1.24 * gather(own[0:1, :], own[1:2, :])
    total = lax.fori_loop(0, KC, entry, total)
    return jnp.sum(total, axis=0, keepdims=True)


def plan_rows(ref, k, parts):
    ref[k, 0:8, :] = parts[0]
    ref[k, 8:16, :] = parts[1]
    ref[k, 16:24, :] = parts[2]


def first_kernel(
    count, place, gathered, order, inverse, blocks, tabs, zs, ic,
    pe_out, plan, own, xa, xb, table,
):
    n = count[0]
    me = place[0] * 16 + place[1]
    counts = gathered[pl.ds(3, DEVICES, stride=4), :]
    offsets = offsets_of(counts)
    sums = assemble(
        gathered[pl.ds(0, DEVICES, stride=4), :],
        gathered[pl.ds(1, DEVICES, stride=4), :],
        offsets, inverse[...], blocks[...],
    )
    values = 0.8 * sums / gathered[pl.ds(2, DEVICES, stride=4), :]

    for g in range(SHARDS):
        cols = tabs[16 * g : 16 * g + 8, :]
        high = jnp.floor(cols * (1.0 / 128.0))
        pair = jnp.concatenate([high, cols - 128.0 * high], axis=0)
        table[32 * g : 32 * g + 16, :] = pair.astype(BF16)
        off = tabs[16 * g + 8 : 16 * g + 16, :]
        big = off.astype(BF16).astype(F32)
        table[32 * g + 16 : 32 * g + 32, :] = jnp.concatenate([big, off - big], axis=0).astype(BF16)

    row = iota((LANES, LANES), 0)
    mine = jnp.sum(jnp.where(row == me, offsets[0].astype(F32), 0.0), axis=0, keepdims=True).astype(I32)
    numbers = order[...].astype(F32)
    start = mine >> 7
    lines = []
    spread = (iota((8, LANES), 1) + mine) & 127
    for j in range(3):
        line = jnp.sum(jnp.where(row == start + j, numbers, 0.0), axis=0, keepdims=True)
        lines.append(lane_take(jnp.broadcast_to(line, (8, LANES)), spread))
    inside = iota((8, LANES), 1) + (mine & 127) < LANES
    unknown = jnp.concatenate(
        [jnp.where(inside, lines[0], lines[1]), jnp.where(inside, lines[1], lines[2])], axis=1
    )[0:1].astype(I32)
    own[0:1, :] = (unknown >> 7).astype(F32)
    own[1:2, :] = (unknown & 127).astype(F32)

    plan_rows(plan, KC, fetch(table, unknown))

    def level(k, carry):
        col = 128.0 * plan[KC, pl.ds(k, 1), :] + plan[KC, pl.ds(8 + k, 1), :]
        plan_rows(plan, k, fetch(table, col.astype(I32)))
        return carry

    lax.fori_loop(0, KC, level, 0)

    pe = prolong(coarse_solve(values, plan, own), n)
    for x in range(CX):
        pe_out[x] = pe[x]

    def message(out, upper):
        for k in range(3):
            out[k] = zs[CX - 3 + k] if upper else zs[k]
        for k in range(2):
            out[3 + k] = ic[CX - 2 + k] if upper else ic[k]
            out[5 + k] = pe[CX - 2 + k] if upper else pe[k]

    even = (place[0] & 1) == 0

    @pl.when(even)
    def _():
        message(xa, True)
        message(xb, False)

    @pl.when(jnp.logical_not(even))
    def _():
        message(xa, False)
        message(xb, True)


def below_above(parity, a, b):
    even = parity == 0
    return (lambda *i: jnp.where(even, b[i], a[i])), (lambda *i: jnp.where(even, a[i], b[i]))


def widen_kernel(place, zs, ic, pe, xa, xb, ya, yb):
    below, above = below_above(place[0] & 1, xa, xb)
    own = (zs, ic, pe)
    depth = (3, 2, 2)
    base = (0, 3, 5)

    def plane(field, x):
        if x < 0:
            return below(base[field] + depth[field] + x)
        if x >= CX:
            return above(base[field] + x - CX)
        return own[field][x]

    even = (place[1] & 1) == 0
    for x in range(-2, CX + 2):
        fields = [plane(f, x) for f in range(3)]
        upper = jnp.concatenate([fields[f][CY - depth[f] :] for f in range(3)] + [fields[0][0:1]], axis=0)
        lower = jnp.concatenate([fields[f][: depth[f]] for f in range(3)] + [fields[0][0:1]], axis=0)
        ya[x + 2] = jnp.where(even, upper, lower)
        yb[x + 2] = jnp.where(even, lower, upper)


def second_kernel(count, place, zs, ic, pe, c, xa, xb, ya, yb, z1_out, w1_out, sw_out, pay):
    below, above = below_above(place[0] & 1, xa, xb)
    near, far = below_above(place[1] & 1, ya, yb)
    own = (zs, ic, pe)
    depth = (3, 2, 2)
    base = (0, 3, 5)

    def plane(field, x):
        if x < 0:
            middle = below(base[field] + depth[field] + x)
        elif x >= CX:
            middle = above(base[field] + x - CX)
        else:
            middle = own[field][x]
        d = depth[field]
        if -2 <= x < CX + 2:
            low = near(x + 2)[base[field] : base[field] + d]
            high = far(x + 2)[base[field] : base[field] + d]
        else:
            low = jnp.zeros((d, CZ), F32)
            high = low
        blank = jnp.zeros((8 - d, CZ), F32)
        return jnp.concatenate([blank, low, middle, high, blank], axis=0)

    def neighbours(get, x):
        mid = get(x)
        rows = mid.shape[0]
        return couple(get(x - 1), mid, get(x + 1), pltpu.roll(mid, 1, 0), pltpu.roll(mid, rows - 1, 0))

    z = {x: plane(0, x) for x in range(-3, CX + 3)}
    inv = {x: plane(1, x) for x in range(-2, CX + 2)}
    first = {}
    for x in range(-2, CX + 2):
        first[x] = 1.2 * z[x] + 0.8 * inv[x] * neighbours(z.get, x) + plane(2, x)
    zw = {}
    image = []
    for x in range(-1, CX + 1):
        beside = neighbours(first.get, x)
        zw[x] = 0.8 * (first[x] - inv[x] * beside)
        if 0 <= x < CX:
            here = c[x] * first[x][8:16] - beside[8:16]
            image.append(here)
            z1_out[x] = first[x][8:16]
            w1_out[x] = here
    for x in range(CX):
        smooth = 1.2 * zw[x] + 0.8 * inv[x] * neighbours(zw.get, x)
        sw_out[x] = smooth[8:16]
    sums = restrict(image, count[0])
    kind = iota((8, LANES), 0) & 1
    tile = jnp.where(kind == 0, sums[:, :LANES], sums[:, LANES:])
    for i in range(DEVICES // 4):
        pay[pl.ds(8 * i, 8), :] = tile


def third_kernel(
    count, place, sums, gathered, inverse, blocks, plan, own, sw,
    p_out, xa, xb, ya, yb,
):
    offsets = offsets_of(gathered[pl.ds(3, DEVICES, stride=4), :])
    values = assemble(
        sums[pl.ds(0, DEVICES, stride=2), :],
        sums[pl.ds(1, DEVICES, stride=2), :],
        offsets, inverse[...], blocks[...],
    )
    values = 0.8 * values / gathered[pl.ds(2, DEVICES, stride=4), :]
    pe = prolong(coarse_solve(values, plan, own), count[0])
    p = [sw[x] + pe[x] for x in range(CX)]
    for x in range(CX):
        p_out[x] = p[x]
    even = (place[0] & 1) == 0
    xa[...] = jnp.where(even, p[CX - 1], p[0])
    xb[...] = jnp.where(even, p[0], p[CX - 1])
    even = (place[1] & 1) == 0
    upper = jnp.concatenate([p[x][CY - 1 : CY] for x in range(CX)] * 2, axis=0)
    lower = jnp.concatenate([p[x][0:1] for x in range(CX)] * 2, axis=0)
    ya[...] = jnp.where(even, upper, lower)
    yb[...] = jnp.where(even, lower, upper)


def products_kernel(place, s, w1, p, c, xa, xb, ya, yb, pay):
    even = (place[0] & 1) == 0
    below, above = jnp.where(even, xb[...], xa[...]), jnp.where(even, xa[...], xb[...])
    even = (place[1] & 1) == 0
    near, far = jnp.where(even, yb[...], ya[...]), jnp.where(even, ya[...], yb[...])
    sums = [jnp.zeros((CY, CZ), F32) for _ in range(6)]
    row = iota((CY, CZ), 0)
    for x in range(CX):
        mid = p[x]
        left = p[x - 1] if x else below
        right = p[x + 1] if x + 1 < CX else above
        up = jnp.where(row == 0, near[x : x + 1], pltpu.roll(mid, 1, 0))
        down = jnp.where(row == CY - 1, far[x : x + 1], pltpu.roll(mid, CY - 1, 0))
        q = c[x] * mid - couple(left, mid, right, up, down)
        a, b = s[x], w1[x]
        for k, term in enumerate((a * a, a * b, a * q, b * b, b * q, q * q)):
            sums[k] = sums[k] + term
    lane = iota((8, LANES), 1)
    tile = jnp.zeros((8, LANES), F32)
    for k in range(6):
        tile = tile + jnp.where(lane == k, jnp.sum(sums[k], keepdims=True), 0.0)
    for i in range(DEVICES // 8):
        pay[pl.ds(8 * i, 8), :] = tile


def update_kernel(parts, z1, p, s_old, rate, mobile, immobile):
    total = jnp.sum(parts[...], axis=0, keepdims=True)
    ss, sw, sq, ww, wq, qq = [total[:, k : k + 1] for k in range(6)]
    factor = wq / ww
    y2 = (sq - factor * sw) / (qq - factor * wq)
    y1 = (sw - wq * y2) / ww
    for x in range(CX):
        new = y1 * z1[x] + y2 * p[x]
        mobile[x] = new
        for k in range(RATES):
            r = rate[k, x]
            immobile[k, x] = (s_old[k, x] + r * new) / (1.0 + r)


def call(kernel, ins, outs, scratch=(), flops=10_000, vmem=48 << 20):
    shapes = [jax.ShapeDtypeStruct(shape, dtype) for shape, dtype in outs]
    return pl.pallas_call(
        kernel,
        out_shape=shapes,
        in_specs=ins,
        out_specs=[VM] * len(shapes),
        scratch_shapes=list(scratch),
        cost_estimate=pl.CostEstimate(flops=flops, bytes_accessed=100_000, transcendentals=0),
        compiler_params=pltpu.CompilerParams(vmem_limit_bytes=vmem),
    )


FIELD = ((CX, CY, CZ), F32)


def swaps(count):
    first = [(i, i ^ 1) for i in range(count)]
    second = [(i, ((i - 1) ^ 1) + 1) for i in range(1, count - 1)]
    return first, second


def trade(a, b, axis):
    first, second = swaps(lax.axis_size(axis))
    return lax.ppermute(a, axis, first), lax.ppermute(b, axis, second)


def everyone(pay, rows):
    moved = lax.all_to_all(pay.reshape(DEVICES, rows, LANES), BOTH, 0, 0)
    return moved.reshape(DEVICES * rows, LANES)


def local(
    c_old, s_old, rate_time, capacity, agg_count, coarse_order, coarse_cols, coarse_off, coarse_diag
):
    place = jnp.stack([lax.axis_index("coarse"), lax.axis_index("fine")]).astype(I32)
    scaled = 0.8 * coarse_off / coarse_diag[None, :]
    tab = jnp.concatenate([coarse_cols.astype(F32), scaled], axis=0)
    tabs = lax.all_gather(tab, "coarse", axis=0, tiled=True)
    order = coarse_order.reshape(LANES, LANES)

    c, ic, s, zs, pay = call(
        source_kernel, [SM, SM, SM, VM, VM, VM, VM],
        [FIELD, FIELD, FIELD, FIELD, ((4 * DEVICES, LANES), F32)],
    )(capacity, agg_count, place, c_old, s_old, rate_time, coarse_diag.reshape(16, LANES))
    gathered = everyone(pay, 4)
    inverse, blocks = call(
        order_kernel, [VM], [((LANES, LANES), I32), ((LANES, LANES), BF16)], flops=10_000_000
    )(order)

    pe, plan, own, xa, xb = call(
        first_kernel, [SM, SM] + [VM] * 7,
        [FIELD, ((KC + 1, 24, SLOTS), F32), ((8, SLOTS), F32), ((7, CY, CZ), F32), ((7, CY, CZ), F32)],
        scratch=[pltpu.VMEM((SHARDS * 32, SHARD_ROWS), BF16)],
    )(agg_count, place, gathered, order, inverse, blocks, tabs, zs, ic)
    xa, xb = trade(xa, xb, "coarse")
    ya, yb = call(
        widen_kernel, [SM] + [VM] * 5, [((CX + 4, CY, CZ), F32)] * 2
    )(place, zs, ic, pe, xa, xb)
    ya, yb = trade(ya, yb, "fine")
    z1, w1, sw, pay = call(
        second_kernel, [SM, SM] + [VM] * 8, [FIELD, FIELD, FIELD, ((2 * DEVICES, LANES), F32)]
    )(agg_count, place, zs, ic, pe, c, xa, xb, ya, yb)
    sums = everyone(pay, 2)

    p, xa, xb, ya, yb = call(
        third_kernel, [SM, SM] + [VM] * 7, [FIELD] + [((CY, CZ), F32)] * 4
    )(agg_count, place, sums, gathered, inverse, blocks, plan, own, sw)
    xa, xb = trade(xa, xb, "coarse")
    ya, yb = trade(ya, yb, "fine")
    (pay,) = call(
        products_kernel, [SM] + [VM] * 8, [((DEVICES, LANES), F32)]
    )(place, s, w1, p, c, xa, xb, ya, yb)
    parts = everyone(pay, 1)
    mobile, immobile = call(
        update_kernel, [VM] * 5, [FIELD, ((RATES, CX, CY, CZ), F32)]
    )(parts, z1, p, s_old, rate_time)
    return mobile, immobile


def solution(mesh):
    return jax.shard_map(
        local,
        mesh=mesh,
        in_specs=(
            P("coarse", "fine", None),
            P(None, "coarse", "fine", None),
            P(None, "coarse", "fine", None),
            P(),
            P(("coarse", "fine")),
            P(),
            P(None, "coarse"),
            P(None, "coarse"),
            P("coarse"),
        ),
        out_specs=(P("coarse", "fine", None), P(None, "coarse", "fine", None)),
        check_vma=False,
    )
```

time: 1290 us -> 120 us (0.09)
  blocking collectives: 549 us -> 41.9 us
  local copies, waits for them, and re-layouts: 462 us -> 2.94 us
  loops' own time: 85.3 us -> 0 us
  waiting for transfers between devices: 101 us -> 17.6 us
  other arithmetic: 24.1 us -> 1.66 us
  Pallas kernels: 0 us -> 20.7 us
  starting transfers between devices: 38.9 us -> 19.6 us
    psum x7 -> x0, blocking collectives: 389 us -> none  [the longest x2 127 us: local(): leftover = jnp.sqrt(lax.psum(jnp.sum(image * image), ('coarse', 'fine')))]
    gather x14 -> x0, local copies, waits for them, and re-layouts: 371 us -> none  [the longest x8 362 us: local(): whole[coarse_cols]]
    all_gather x6 -> x0, blocking collectives: 95.8 us -> none  [spread(): return lax.all_gather(values, 'coarse', axis=0, tiled=True)]
    unnamed x4 -> x1, waiting for transfers between devices: 94.7 us -> 0.02 us
    another operation x1 -> x0, loops' own time: 85.3 us -> none  [entering(): return lax.fori_loop(0, length, hop, start)]
    dynamic_slice x128 -> x0, local copies, waits for them, and re-layouts: 83 us -> none  [hop(): new = combine(before, everything[k])]
    unnamed x1 -> x0, blocking collectives: 63.3 us -> none
    all_to_all x0 -> x2, blocking collectives: none -> 41.9 us  [everyone(): moved = lax.all_to_all(pay.reshape(DEVICES, rows, LANES), BOTH, 0, 0)]
  transfers between devices with their start and end apart: 18 -> 10, of which waited for: 6 -> 5; matrix products, arithmetic and copies ran while one was open for 37% -> 0% of each run, Pallas kernels for 0% -> 4%
where the time goes in v1:
time: 120 us; the launch traced here: 119 us
  blocking collectives  41.9 us (35%)
  Pallas kernels  20.7 us (17%)
  starting transfers between devices  19.6 us (16%)
  waiting for transfers between devices  17.6 us (15%)
  between operations  14.8 us (12%)
  local copies, waits for them, and re-layouts  2.94 us (2%)
  other arithmetic  1.66 us (1%)
    all_to_all x2, blocking collectives, everyone(): moved = lax.all_to_all(pay.reshape(DEVICES, rows, LANES), BOTH, 0, 0)  41.9 us
    all_to_all x1, starting transfers between devices, everyone(): moved = lax.all_to_all(pay.reshape(DEVICES, rows, LANES), BOTH, 0, 0)  11.5 us
    all_to_all x1, waiting for transfers between devices, everyone(): moved = lax.all_to_all(pay.reshape(DEVICES, rows, LANES), BOTH, 0, 0)  10.2 us
    pallas_call x1, Pallas kernels, local(): call(first_kernel, [SM, SM] + [VM] * 7, [FIELD, ((KC + 1, 24, SLOTS), F32...  8.38 us
    ppermute x8, starting transfers between devices, trade(): return (lax.ppermute(a, axis, first), lax.ppermute(b, axis, second))  8.05 us
    ppermute x8, waiting for transfers between devices, trade(): return (lax.ppermute(a, axis, first), lax.ppermute(b, axis, second))  7.04 us
    pallas_call x1, Pallas kernels, local(): call(third_kernel, [SM, SM] + [VM] * 7, [FIELD] + [((CY, CZ), F32)] * 4)  4.44 us
    unnamed x18, local copies, waits for them, and re-layouts  2.94 us
  transfers between devices with their start and end apart: 10, of which 5 were waited for; matrix products, arithmetic and copies ran while one was open for 0% of the time, Pallas kernels for 4%

profile of v1, /device:TPU:1, one launch (start us, length us, event | category | flops | bytes accessed | tf_op | source)
XLA Modules:
  0.0 119.2 jit_solution(114710907943360614)
XLA Ops:
  7.2 0.0 copy-start.5
  7.2 0.0 copy-start.8
  7.2 0.0 copy-start
  7.2 0.0 all-gather.2.cloned.1.call-start
  7.2 0.9 convert_element_type.3
  8.1 0.0 copy-done.5
  8.1 0.0 copy-done.8
  8.2 0.7 pad_maximum_fusion
  8.8 0.0 copy-start.6
  8.8 0.0 all-gather.2.cloned.1.call-update
  9.5 0.1 pad_add_fusion.place
  9.6 0.0 copy-start.7
  9.6 0.0 copy-done
  9.6 0.0 copy-done.6
  9.6 0.6 copy-done.7
  10.3 1.0 copy-done.1
  11.3 1.5 %shard_map.104 = (f32[4,8,256]{2,1,0:T(8,128)S(1)}, f32[4,8,256]{2,1,0:T(8,128)S(1)}, f32[4,8,256]{2,1,0:T(8,128)S(1)}, f32[4,8,256]{2,1,0:T(8,128)S(1)}, f32[512,128]{1,0:T(8,128)}) custom-call(f32[16]{0:T(128)S(1)} %copy-done.7, s32[1]{0:T(128)S(6)} %copy.12.count, s32[2]{0:T(128)S(1)} %pad_add_fusion.place, f32[4,8,256]{2,1,0:T(8,128)S(1)} %copy-done.6, ...), custom_call_target="tpu_custom_call" | custom-call | flops 10000 | bytes 100000 | tf_op jit(solution)/shard_map/pallas_call | solution.py:470
  12.8 11.5 %all-to-all-start = ((f32[128,4,128]{2,1,0:T(4,128)}), f32[128,4,128]{2,1,0:T(4,128)S(1)}, u32[]{:S(2)}, u32[]{:S(2)}) async-start(f32[128,4,128]{2,1,0:T(4,128)} %bitcast.3), calls=%async_computation | async-start | bytes 524288 | tf_op jit(solution)/shard_map/all_to_all | solution.py:457
  24.3 0.0 copy-done.4
  24.3 2.7 %shard_map.105 = (s32[128,128]{1,0:T(8,128)S(1)}, bf16[128,128]{1,0:T(8,128)(2,1)S(1)}) custom-call(s32[128,128]{1,0:T(8,128)S(1)} %bitcast.17), custom_call_target="tpu_custom_call" | custom-call | flops 10000000 | bytes 100000 | tf_op jit(solution)/shard_map/pallas_call | solution.py:475
  27.0 10.2 %all-to-all-done = f32[128,4,128]{2,1,0:T(4,128)S(1)} async-done(((f32[128,4,128]{2,1,0:T(4,128)}), f32[128,4,128]{2,1,0:T(4,128)S(1)}, u32[]{:S(2)}, u32[]{:S(2)}) %all-to-all-start) | async-done | bytes 262176 | tf_op jit(solution)/shard_map/all_to_all | solution.py:457
  37.2 0.4 all-gather.2.cloned.1.call-done.tabs
  37.6 1.2 %copy-done.3 = f32[128,2048]{1,0:T(8,128)S(1)} copy-done((f32[128,2048]{1,0:T(8,128)S(1)}, f32[128,2048]{1,0:T(8,128)}, u32[]{:S(2)}) %copy-start.3) | copy-done | bytes 1048600
  38.8 8.4 %shard_map.106 = (f32[4,8,256]{2,1,0:T(8,128)S(1)}, f32[9,24,256]{2,1,0:T(8,128)S(1)}, f32[8,256]{1,0:T(8,128)S(1)}, f32[7,8,256]{2,1,0:T(8,128)S(1)}, f32[7,8,256]{2,1,0:T(8,128)S(1)}) custom-call(s32[1]{0:T(128)S(6)} %copy.12.count, s32[2]{0:T(128)S(1)} %pad_add_fusion.place, f32[512,128]{1,0:T(8,128)S(1)} %bitcast.12, s32[128,128]{1,0:T(8,128)S(1)} %bitcast.18, ...), custom_call_target="tpu_custom_call" | custom-call | flops 10000 | bytes 100000 | tf_op jit(solution)/shard_map/pallas_call | solution.py:479
  47.2 0.4 collective-permute-start
  47.6 2.0 %collective-permute-start.1 = (f32[7,8,256]{2,1,0:T(8,128)S(1)}, f32[7,8,256]{2,1,0:T(8,128)S(1)}, u32[]{:S(2)}, u32[]{:S(2)}) collective-permute-start(f32[7,8,256]{2,1,0:T(8,128)S(1)} %get-tuple-element.34), channel_id=1, source_target_pairs={{16,32},{32,16},{48,64},{64,48},{80,96},{96,80},{17,33},{33,17},{4... | collective-permute-start | bytes 172040 | tf_op jit(solution)/shard_map/ppermute | solution.py:453
  49.6 0.0 collective-permute-done.xa
  49.6 3.7 %collective-permute-done.1.xb = f32[7,8,256]{2,1,0:T(8,128)S(1)} collective-permute-done((f32[7,8,256]{2,1,0:T(8,128)S(1)}, f32[7,8,256]{2,1,0:T(8,128)S(1)}, u32[]{:S(2)}, u32[]{:S(2)}) %collective-permute-start.1) | collective-permute-done | bytes 57376 | tf_op jit(solution)/shard_map/ppermute | solution.py:453
  53.4 0.6 shard_map.107
  54.0 0.8 collective-permute-start.2
  54.8 0.7 collective-permute-start.3
  55.4 1.7 %collective-permute-done.2.ya = f32[8,8,256]{2,1,0:T(8,128)S(1)} collective-permute-done((f32[8,8,256]{2,1,0:T(8,128)S(1)}, f32[8,8,256]{2,1,0:T(8,128)S(1)}, u32[]{:S(2)}, u32[]{:S(2)}) %collective-permute-start.2) | collective-permute-done | bytes 65568 | tf_op jit(solution)/shard_map/ppermute | solution.py:453
  57.2 0.0 collective-permute-done.3.yb
  57.2 1.0 shard_map.108
  58.1 22.8 %all_to_all.15 = f32[128,2,128]{2,1,0:T(2,128)S(1)} all-to-all(f32[128,2,128]{2,1,0:T(2,128)S(1)} %bitcast.19), channel_id=1, replica_groups=mesh['coarse'=8,'fine'=16] {'coarse','fine'}, dimensions={0} | all-to-all | bytes 262144 | tf_op jit(solution)/shard_map/all_to_all | solution.py:457
  80.9 4.4 %shard_map.109 = (f32[4,8,256]{2,1,0:T(8,128)S(1)}, f32[8,256]{1,0:T(8,128)S(1)}, f32[8,256]{1,0:T(8,128)S(1)}, f32[8,256]{1,0:T(8,128)S(1)}, f32[8,256]{1,0:T(8,128)S(1)}) custom-call(s32[1]{0:T(128)S(6)} %copy.12.count, s32[2]{0:T(128)S(1)} %pad_add_fusion.place, f32[256,128]{1,0:T(8,128)S(1)} %bitcast.14, f32[512,128]{1,0:T(8,128)S(1)} %bitcast.13, ...), custom_call_target="tpu_custom_call" | custom-call | flops 10000 | bytes 100000 | tf_op jit(solution)/shard_map/pallas_call | solution.py:494
  85.3 0.8 collective-permute-start.4
  86.1 2.1 %collective-permute-start.5 = (f32[8,256]{1,0:T(8,128)S(1)}, f32[8,256]{1,0:T(8,128)S(1)}, u32[]{:S(2)}, u32[]{:S(2)}) collective-permute-start(f32[8,256]{1,0:T(8,128)S(1)} %get-tuple-element.44), channel_id=1, source_target_pairs={{16,32},{32,16},{48,64},{64,48},{80,96},{96,80},{17,33},{33,17},{4... | collective-permute-start | bytes 24584 | tf_op jit(solution)/shard_map/ppermute | solution.py:453
  88.2 0.6 collective-permute-start.6
  88.9 0.6 collective-permute-start.7
  89.5 0.0 collective-permute-done.4.xa
  89.5 1.5 %collective-permute-done.5.xb = f32[8,256]{1,0:T(8,128)S(1)} collective-permute-done((f32[8,256]{1,0:T(8,128)S(1)}, f32[8,256]{1,0:T(8,128)S(1)}, u32[]{:S(2)}, u32[]{:S(2)}) %collective-permute-start.5) | collective-permute-done | bytes 8224 | tf_op jit(solution)/shard_map/ppermute | solution.py:453
  91.1 0.0 collective-permute-done.6.ya
  91.1 0.0 collective-permute-done.7.yb
  91.1 0.8 shard_map.110
  91.9 19.1 %all_to_all.16 = f32[128,1,128]{2,1,0:T(1,128)S(1)} all-to-all(f32[128,1,128]{2,1,0:T(1,128)S(1)} %bitcast.15), channel_id=1, replica_groups=mesh['coarse'=8,'fine'=16] {'coarse','fine'}, dimensions={0} | all-to-all | bytes 131072 | tf_op jit(solution)/shard_map/all_to_all | solution.py:457
  111.0 0.0 copy-done.2
  111.0 1.4 %shard_map.111 = (f32[4,8,256]{2,1,0:T(8,128)}, f32[16,4,8,256]{3,2,1,0:T(8,128)}) custom-call(f32[128,128]{1,0:T(8,128)S(1)} %bitcast.16, f32[4,8,256]{2,1,0:T(8,128)S(1)} %get-tuple-element.47.z1, f32[4,8,256]{2,1,0:T(8,128)S(1)} %get-tuple-element.42.p, f32[16,4,8,256]{3,2,1,0:T(8,128)S(1)} %copy-done, f32[16,4,8,256]{3,2,1,0:T(8,128)S(1)} %copy-done.2), custom_call_target="tpu_custom_call" | custom-call | flops 10000 | bytes 100000 | tf_op jit(solution)/shard_map/pallas_call | solution.py:503
  (5 shorter events, 0.0 us)
Async XLA Ops:
  7.2 1.0 copy-start.5
  7.2 1.0 copy-start.8
  7.2 2.4 %copy-start = (f32[16,4,8,256]{3,2,1,0:T(8,128)S(1)}, f32[16,4,8,256]{3,2,1,0:T(8,128)}, u32[]{:S(2)}) copy-start(f32[16,4,8,256]{3,2,1,0:T(8,128)} %s_old.3) | copy-start | bytes 1572868
  7.2 30.4 %all-gather.2.cloned.1.call-start = ((), (), s32[]{:S(2)}) async-start(), calls=%async_computation.3 | async-start | bytes 1179648 | tf_op jit(solution)/shard_map/all_gather | solution.py:467
  8.8 0.8 copy-start.6
  9.6 0.7 copy-start.7
  10.2 1.0 copy-start.1
  12.8 11.5 %copy-start.4 = (s32[16384]{0:T(1024)S(1)}, s32[16384]{0:T(1024)}, u32[]{:S(2)}) copy-start(s32[16384]{0:T(1024)} %param.14) | copy-start | bytes 196612
  12.8 24.4 %all-to-all-start = ((f32[128,4,128]{2,1,0:T(4,128)}), f32[128,4,128]{2,1,0:T(4,128)S(1)}, u32[]{:S(2)}, u32[]{:S(2)}) async-start(f32[128,4,128]{2,1,0:T(4,128)} %bitcast.3), calls=%async_computation | async-start | bytes 524288 | tf_op jit(solution)/shard_map/all_to_all | solution.py:457
  37.6 1.2 %copy-start.3 = (f32[128,2048]{1,0:T(8,128)S(1)}, f32[128,2048]{1,0:T(8,128)}, u32[]{:S(2)}) copy-start(f32[128,2048]{1,0:T(8,128)} %all-gather.2.cloned.1.call-done.tabs) | copy-start | bytes 3145732
  47.2 2.4 %collective-permute-start = (f32[7,8,256]{2,1,0:T(8,128)S(1)}, f32[7,8,256]{2,1,0:T(8,128)S(1)}, u32[]{:S(2)}, u32[]{:S(2)}) collective-permute-start(f32[7,8,256]{2,1,0:T(8,128)S(1)} %get-tuple-element.33), channel_id=1, source_target_pairs={{0,16},{16,0},{32,48},{48,32},{64,80},{80,64},{96,112},{112,96},{1... | collective-permute-start | bytes 172040 | tf_op jit(solution)/shard_map/ppermute | solution.py:453
  47.6 5.8 %collective-permute-start.1 = (f32[7,8,256]{2,1,0:T(8,128)S(1)}, f32[7,8,256]{2,1,0:T(8,128)S(1)}, u32[]{:S(2)}, u32[]{:S(2)}) collective-permute-start(f32[7,8,256]{2,1,0:T(8,128)S(1)} %get-tuple-element.34), channel_id=1, source_target_pairs={{16,32},{32,16},{48,64},{64,48},{80,96},{96,80},{17,33},{33,17},{4... | collective-permute-start | bytes 172040 | tf_op jit(solution)/shard_map/ppermute | solution.py:453
  54.0 3.2 %collective-permute-start.2 = (f32[8,8,256]{2,1,0:T(8,128)S(1)}, f32[8,8,256]{2,1,0:T(8,128)S(1)}, u32[]{:S(2)}, u32[]{:S(2)}) collective-permute-start(f32[8,8,256]{2,1,0:T(8,128)S(1)} %get-tuple-element.35), channel_id=1, source_target_pairs={{0,1},{1,0},{2,3},{3,2},{4,5},{5,4},{6,7},{7,6},{8,9},{9,8},{10,11... | collective-permute-start | bytes 196616 | tf_op jit(solution)/shard_map/ppermute | solution.py:453
  54.8 2.4 %collective-permute-start.3 = (f32[8,8,256]{2,1,0:T(8,128)S(1)}, f32[8,8,256]{2,1,0:T(8,128)S(1)}, u32[]{:S(2)}, u32[]{:S(2)}) collective-permute-start(f32[8,8,256]{2,1,0:T(8,128)S(1)} %get-tuple-element.36), channel_id=1, source_target_pairs={{1,2},{2,1},{3,4},{4,3},{5,6},{6,5},{7,8},{8,7},{9,10},{10,9},{11,... | collective-permute-start | bytes 196616 | tf_op jit(solution)/shard_map/ppermute | solution.py:453
  80.9 30.1 %copy-start.2 = (f32[16,4,8,256]{3,2,1,0:T(8,128)S(1)}, f32[16,4,8,256]{3,2,1,0:T(8,128)}, u32[]{:S(2)}) copy-start(f32[16,4,8,256]{3,2,1,0:T(8,128)} %rate.3) | copy-start | bytes 1572868
  85.3 4.2 %collective-permute-start.4 = (f32[8,256]{1,0:T(8,128)S(1)}, f32[8,256]{1,0:T(8,128)S(1)}, u32[]{:S(2)}, u32[]{:S(2)}) collective-permute-start(f32[8,256]{1,0:T(8,128)S(1)} %get-tuple-element.43), channel_id=1, source_target_pairs={{0,16},{16,0},{32,48},{48,32},{64,80},{80,64},{96,112},{112,96},{1... | collective-permute-start | bytes 24584 | tf_op jit(solution)/shard_map/ppermute | solution.py:453
  86.1 5.0 %collective-permute-start.5 = (f32[8,256]{1,0:T(8,128)S(1)}, f32[8,256]{1,0:T(8,128)S(1)}, u32[]{:S(2)}, u32[]{:S(2)}) collective-permute-start(f32[8,256]{1,0:T(8,128)S(1)} %get-tuple-element.44), channel_id=1, source_target_pairs={{16,32},{32,16},{48,64},{64,48},{80,96},{96,80},{17,33},{33,17},{4... | collective-permute-start | bytes 24584 | tf_op jit(solution)/shard_map/ppermute | solution.py:453
  88.2 2.8 %collective-permute-start.6 = (f32[8,256]{1,0:T(8,128)S(1)}, f32[8,256]{1,0:T(8,128)S(1)}, u32[]{:S(2)}, u32[]{:S(2)}) collective-permute-start(f32[8,256]{1,0:T(8,128)S(1)} %get-tuple-element.45), channel_id=1, source_target_pairs={{0,1},{1,0},{2,3},{3,2},{4,5},{5,4},{6,7},{7,6},{8,9},{9,8},{10,11... | collective-permute-start | bytes 24584 | tf_op jit(solution)/shard_map/ppermute | solution.py:453
  88.9 2.2 %collective-permute-start.7 = (f32[8,256]{1,0:T(8,128)S(1)}, f32[8,256]{1,0:T(8,128)S(1)}, u32[]{:S(2)}, u32[]{:S(2)}) collective-permute-start(f32[8,256]{1,0:T(8,128)S(1)} %get-tuple-element.46), channel_id=1, source_target_pairs={{1,2},{2,1},{3,4},{4,3},{5,6},{6,5},{7,8},{8,7},{9,10},{10,9},{11,... | collective-permute-start | bytes 24584 | tf_op jit(solution)/shard_map/ppermute | solution.py:453
Sparse Core Ops, SparseCore 0:
  9.7 27.7 all-gather.1

commit v2 on v1

--- a/solution.py
+++ b/solution.py
@@ -18,6 +18,11 @@
 F32, BF16, I32 = jnp.float32, jnp.bfloat16, jnp.int32
 VM = pl.BlockSpec(memory_space=pltpu.VMEM)
 SM = pl.BlockSpec(memory_space=pltpu.SMEM)
+HB = pl.BlockSpec(memory_space=pltpu.HBM)
+
+
+def places():
+    return lax.axis_index("coarse").astype(I32), lax.axis_index("fine").astype(I32)
 
 
 def iota(shape, dim):
@@ -91,10 +96,29 @@
     return 8.0 * (left + right + up + down + ahead) + 10.0 * behind
 
 
-def source_kernel(cap, count, place, c_old, s_old, rate, diag, c_out, ic_out, s_out, zs_out, pay):
+def table_kernel(cols, off, diag, after, out):
+    out[0:8, :] = cols[...].astype(F32)
+    out[8:16, :] = off[...] * (0.8 / diag[...])
+
+
+def source_kernel(
+    cap, count, c_old, s_old_hbm, rate_hbm, diag, c_out, ic_out, s_out, zs_out, pay, s_old, rate, sems
+):
+    place = places()
     n = count[0]
+    copies = []
+    for x in range(CX):
+        pair = (
+            pltpu.make_async_copy(rate_hbm.at[:, x], rate.at[:, x], sems.at[0, x]),
+            pltpu.make_async_copy(s_old_hbm.at[:, x], s_old.at[:, x], sems.at[1, x]),
+        )
+        for copy in pair:
+            copy.start()
+        copies.append(pair)
     planes = []
     for x in range(CX):
+        for copy in copies[x]:
+            copy.wait()
         mass = jnp.zeros((CY, CZ), F32)
         extra = jnp.zeros((CY, CZ), F32)
         for k in range(RATES):
@@ -125,7 +149,7 @@
         pay[pl.ds(8 * i, 8), :] = tile
 
 
-def order_kernel(order, inverse_out, blocks_out):
+def order_kernel(order, after, inverse_out, blocks_out):
     numbers = order[...]
     blocks = (iota((LANES, LANES), 0) == (numbers[0:1, :] >> 7)).astype(F32).astype(BF16)
     blocks_out[...] = blocks
@@ -166,9 +190,10 @@
     return lane_take(by_block, inverse)
 
 
-def fetch(table, unknown):
+def fetch(table, unknown, coarse):
     inner = unknown & (SHARD_ROWS - 1)
     shard = unknown >> 11
+    shard = ((((coarse >> 1) - (shard >> 1)) & 3) << 1) | ((shard ^ coarse) & 1)
     found = jnp.zeros((SHARDS * 32, SLOTS), F32)
     for chunk in range(SHARD_ROWS // 256):
         spot = (iota((256, SLOTS), 0) + chunk * 256 == inner).astype(F32).astype(BF16)
@@ -209,9 +234,10 @@
 
 
 def first_kernel(
-    count, place, gathered, order, inverse, blocks, tabs, zs, ic,
+    count, gathered, order, inverse, blocks, tab0, tab1, tab2, tab3, tab4, tab5, tab6, tab7, zs, ic,
     pe_out, plan, own, xa, xb, table,
 ):
+    place = places()
     n = count[0]
     me = place[0] * 16 + place[1]
     counts = gathered[pl.ds(3, DEVICES, stride=4), :]
@@ -223,12 +249,13 @@
     )
     values = 0.8 * sums / gathered[pl.ds(2, DEVICES, stride=4), :]
 
+    tabs = (tab0, tab1, tab2, tab3, tab4, tab5, tab6, tab7)
     for g in range(SHARDS):
-        cols = tabs[16 * g : 16 * g + 8, :]
+        cols = tabs[g][0:8, :]
         high = jnp.floor(cols * (1.0 / 128.0))
         pair = jnp.concatenate([high, cols - 128.0 * high], axis=0)
         table[32 * g : 32 * g + 16, :] = pair.astype(BF16)
-        off = tabs[16 * g + 8 : 16 * g + 16, :]
+        off = tabs[g][8:16, :]
         big = off.astype(BF16).astype(F32)
         table[32 * g + 16 : 32 * g + 32, :] = jnp.concatenate([big, off - big], axis=0).astype(BF16)
 
@@ -248,11 +275,11 @@
     own[0:1, :] = (unknown >> 7).astype(F32)
     own[1:2, :] = (unknown & 127).astype(F32)
 
-    plan_rows(plan, KC, fetch(table, unknown))
+    plan_rows(plan, KC, fetch(table, unknown, place[0]))
 
     def level(k, carry):
         col = 128.0 * plan[KC, pl.ds(k, 1), :] + plan[KC, pl.ds(8 + k, 1), :]
-        plan_rows(plan, k, fetch(table, col.astype(I32)))
+        plan_rows(plan, k, fetch(table, col.astype(I32), place[0]))
         return carry
 
     lax.fori_loop(0, KC, level, 0)
@@ -286,7 +313,8 @@
     return (lambda *i: jnp.where(even, b[i], a[i])), (lambda *i: jnp.where(even, a[i], b[i]))
 
 
-def widen_kernel(place, zs, ic, pe, xa, xb, ya, yb):
+def widen_kernel(zs, ic, pe, xa, xb, ya, yb):
+    place = places()
     below, above = below_above(place[0] & 1, xa, xb)
     own = (zs, ic, pe)
     depth = (3, 2, 2)
@@ -308,7 +336,8 @@
         yb[x + 2] = jnp.where(even, lower, upper)
 
 
-def second_kernel(count, place, zs, ic, pe, c, xa, xb, ya, yb, z1_out, w1_out, sw_out, pay):
+def second_kernel(count, zs, ic, pe, c, xa, xb, ya, yb, z1_out, w1_out, sw_out, pay):
+    place = places()
     below, above = below_above(place[0] & 1, xa, xb)
     near, far = below_above(place[1] & 1, ya, yb)
     own = (zs, ic, pe)
@@ -363,9 +392,10 @@
 
 
 def third_kernel(
-    count, place, sums, gathered, inverse, blocks, plan, own, sw,
+    count, sums, gathered, inverse, blocks, plan, own, sw,
     p_out, xa, xb, ya, yb,
 ):
+    place = places()
     offsets = offsets_of(gathered[pl.ds(3, DEVICES, stride=4), :])
     values = assemble(
         sums[pl.ds(0, DEVICES, stride=2), :],
@@ -387,7 +417,8 @@
     yb[...] = jnp.where(even, lower, upper)
 
 
-def products_kernel(place, s, w1, p, c, xa, xb, ya, yb, pay):
+def products_kernel(s, w1, p, c, xa, xb, ya, yb, pay):
+    place = places()
     even = (place[0] & 1) == 0
     below, above = jnp.where(even, xb[...], xa[...]), jnp.where(even, xa[...], xb[...])
     even = (place[1] & 1) == 0
@@ -461,44 +492,53 @@
 def local(
     c_old, s_old, rate_time, capacity, agg_count, coarse_order, coarse_cols, coarse_off, coarse_diag
 ):
-    place = jnp.stack([lax.axis_index("coarse"), lax.axis_index("fine")]).astype(I32)
-    scaled = 0.8 * coarse_off / coarse_diag[None, :]
-    tab = jnp.concatenate([coarse_cols.astype(F32), scaled], axis=0)
-    tabs = lax.all_gather(tab, "coarse", axis=0, tiled=True)
     order = coarse_order.reshape(LANES, LANES)
 
     c, ic, s, zs, pay = call(
-        source_kernel, [SM, SM, SM, VM, VM, VM, VM],
+        source_kernel, [SM, SM, VM, HB, HB, VM],
         [FIELD, FIELD, FIELD, FIELD, ((4 * DEVICES, LANES), F32)],
-    )(capacity, agg_count, place, c_old, s_old, rate_time, coarse_diag.reshape(16, LANES))
+        scratch=[
+            pltpu.VMEM((RATES, CX, CY, CZ), F32),
+            pltpu.VMEM((RATES, CX, CY, CZ), F32),
+            pltpu.SemaphoreType.DMA((2, CX)),
+        ],
+        vmem=63 << 20,
+    )(capacity, agg_count, c_old, s_old, rate_time, coarse_diag.reshape(16, LANES))
+    (tab,) = call(table_kernel, [VM] * 4, [((16, SHARD_ROWS), F32)], vmem=63 << 20)(
+        coarse_cols, coarse_off, coarse_diag.reshape(1, SHARD_ROWS), ic
+    )
+    tabs = []
+    for hop in (0, 2, 4, 6):
+        mine = lax.ppermute(tab, "coarse", [(i, (i + hop) % 8) for i in range(8)]) if hop else tab
+        tabs += [mine, lax.ppermute(mine, "coarse", [(i, i ^ 1) for i in range(8)])]
     gathered = everyone(pay, 4)
     inverse, blocks = call(
-        order_kernel, [VM], [((LANES, LANES), I32), ((LANES, LANES), BF16)], flops=10_000_000
-    )(order)
+        order_kernel, [VM] * 2, [((LANES, LANES), I32), ((LANES, LANES), BF16)], flops=10_000_000
+    )(order, tab)
 
     pe, plan, own, xa, xb = call(
-        first_kernel, [SM, SM] + [VM] * 7,
+        first_kernel, [SM] + [VM] * 14,
         [FIELD, ((KC + 1, 24, SLOTS), F32), ((8, SLOTS), F32), ((7, CY, CZ), F32), ((7, CY, CZ), F32)],
         scratch=[pltpu.VMEM((SHARDS * 32, SHARD_ROWS), BF16)],
-    )(agg_count, place, gathered, order, inverse, blocks, tabs, zs, ic)
+    )(agg_count, gathered, order, inverse, blocks, *tabs, zs, ic)
     xa, xb = trade(xa, xb, "coarse")
     ya, yb = call(
-        widen_kernel, [SM] + [VM] * 5, [((CX + 4, CY, CZ), F32)] * 2
-    )(place, zs, ic, pe, xa, xb)
+        widen_kernel, [VM] * 5, [((CX + 4, CY, CZ), F32)] * 2
+    )(zs, ic, pe, xa, xb)
     ya, yb = trade(ya, yb, "fine")
     z1, w1, sw, pay = call(
-        second_kernel, [SM, SM] + [VM] * 8, [FIELD, FIELD, FIELD, ((2 * DEVICES, LANES), F32)]
-    )(agg_count, place, zs, ic, pe, c, xa, xb, ya, yb)
+        second_kernel, [SM] + [VM] * 8, [FIELD, FIELD, FIELD, ((2 * DEVICES, LANES), F32)]
+    )(agg_count, zs, ic, pe, c, xa, xb, ya, yb)
     sums = everyone(pay, 2)
 
     p, xa, xb, ya, yb = call(
-        third_kernel, [SM, SM] + [VM] * 7, [FIELD] + [((CY, CZ), F32)] * 4
-    )(agg_count, place, sums, gathered, inverse, blocks, plan, own, sw)
+        third_kernel, [SM] + [VM] * 7, [FIELD] + [((CY, CZ), F32)] * 4
+    )(agg_count, sums, gathered, inverse, blocks, plan, own, sw)
     xa, xb = trade(xa, xb, "coarse")
     ya, yb = trade(ya, yb, "fine")
     (pay,) = call(
-        products_kernel, [SM] + [VM] * 8, [((DEVICES, LANES), F32)]
-    )(place, s, w1, p, c, xa, xb, ya, yb)
+        products_kernel, [VM] * 8, [((DEVICES, LANES), F32)]
+    )(s, w1, p, c, xa, xb, ya, yb)
     parts = everyone(pay, 1)
     mobile, immobile = call(
         update_kernel, [VM] * 5, [FIELD, ((RATES, CX, CY, CZ), F32)]

time: 120 us -> 100 us (0.83)
  between operations: 14.8 us -> 1.44 us
  starting transfers between devices: 19.6 us -> 25.4 us
  waiting for transfers between devices: 17.6 us -> 13.6 us
  blocking collectives: 41.9 us -> 38.3 us
  local copies, waits for them, and re-layouts: 2.94 us -> 0.03 us
  other arithmetic: 1.66 us -> 0 us
    ppermute x0 -> x7, starting transfers between devices: none -> 6.19 us  [the longest x3 4.43 us: local(): lax.ppermute(tab, 'coarse', [(i, (i + hop) % 8) for i in range(8)])]
    all_to_all x2, blocking collectives: 41.9 us -> 38.3 us  [everyone(): moved = lax.all_to_all(pay.reshape(DEVICES, rows, LANES), BOTH, 0, 0)]
    all_to_all x1, waiting for transfers between devices: 10.2 us -> 6.76 us  [everyone(): moved = lax.all_to_all(pay.reshape(DEVICES, rows, LANES), BOTH, 0, 0)]
    unnamed x18 -> x16, local copies, waits for them, and re-layouts: 2.94 us -> 0.03 us
    pallas_call x7 -> x8, Pallas kernels: 19.3 us -> 19.6 us  [the longest x1 7.84 us: local(): call(first_kernel, [SM] + [VM] * 14, [FIELD, ((KC + 1, 24, SLOTS), F32),...]
  transfers between devices with their start and end apart: 10 -> 16, of which waited for: 5 -> 4; matrix products, arithmetic and copies ran while one was open for 0% -> 0% of each run, Pallas kernels for 4% -> 3%
where the time goes in v2:
time: 100 us; the launch traced here: 99.8 us
  blocking collectives  38.3 us (38%)
  starting transfers between devices  25.4 us (25%)
  Pallas kernels  21 us (21%)
  waiting for transfers between devices  13.6 us (14%)
  between operations  1.44 us (1%)
    all_to_all x2, blocking collectives, everyone(): moved = lax.all_to_all(pay.reshape(DEVICES, rows, LANES), BOTH, 0, 0)  38.3 us
    all_to_all x1, starting transfers between devices, everyone(): moved = lax.all_to_all(pay.reshape(DEVICES, rows, LANES), BOTH, 0, 0)  10.8 us
    ppermute x8, starting transfers between devices, trade(): return (lax.ppermute(a, axis, first), lax.ppermute(b, axis, second))  8.36 us
    pallas_call x1, Pallas kernels, local(): call(first_kernel, [SM] + [VM] * 14, [FIELD, ((KC + 1, 24, SLOTS), F32),...  7.84 us
    ppermute x8, waiting for transfers between devices, trade(): return (lax.ppermute(a, axis, first), lax.ppermute(b, axis, second))  6.79 us
    all_to_all x1, waiting for transfers between devices, everyone(): moved = lax.all_to_all(pay.reshape(DEVICES, rows, LANES), BOTH, 0, 0)  6.76 us
    ppermute x3, starting transfers between devices, local(): lax.ppermute(tab, 'coarse', [(i, (i + hop) % 8) for i in range(8)])  4.43 us
    pallas_call x1, Pallas kernels, local(): call(third_kernel, [SM] + [VM] * 7, [FIELD] + [((CY, CZ), F32)] * 4)  3.9 us
  transfers between devices with their start and end apart: 16, of which 4 were waited for; matrix products, arithmetic and copies ran while one was open for 0% of the time, Pallas kernels for 3%

profile of v2, /device:TPU:1, one launch (start us, length us, event | category | flops | bytes accessed | tf_op | source)
XLA Modules:
  0.0 99.8 jit_solution(7799889939400841179)
XLA Ops:
  1.3 3.0 %shard_map.104 = (f32[4,8,256]{2,1,0:T(8,128)}, f32[4,8,256]{2,1,0:T(8,128)}, f32[4,8,256]{2,1,0:T(8,128)}, f32[4,8,256]{2,1,0:T(8,128)}, f32[512,128]{1,0:T(8,128)}) custom-call(f32[16]{0:T(128)} %cap.1, s32[1]{0:T(128)S(6)} %copy.12.count, f32[4,8,256]{2,1,0:T(8,128)} %c_old.1, f32[16,4,8,256]{3,2,1,0:T(8,128)} %s_old.1, f32[16,4,8,256]{3,2,1,0:T(8,128)} %rate.1, ...), custom_call_target="tpu_custom_call" | custom-call | flops 10000 | bytes 100000 | tf_op jit(solution)/shard_map/pallas_call | solution.py:497
  4.3 1.5 %shard_map.105.after.tab0 = f32[16,2048]{1,0:T(8,128)} custom-call(s32[8,2048]{1,0:T(8,128)} %cols.1, f32[8,2048]{1,0:T(8,128)} %off.1, f32[1,2048]{1,0:T(1,128)} %bitcast.20, f32[4,8,256]{2,1,0:T(8,128)} %get-tuple-element.27.after.ic), custom_call_target="tpu_custom_call" | custom-call | flops 10000 | bytes 100000 | tf_op jit(solution)/shard_map/pallas_call | solution.py:507
  5.8 3.3 %collective-permute-start.5 = (f32[16,2048]{1,0:T(8,128)}, f32[16,2048]{1,0:T(8,128)S(1)}, u32[]{:S(2)}, u32[]{:S(2)}) collective-permute-start(f32[16,2048]{1,0:T(8,128)} %shard_map.105.after.tab0), channel_id=1, source_target_pairs={{0,96},{16,112},{32,0},{48,16},{64,32},{80,48},{96,64},{112,80},{1... | collective-permute-start | bytes 393224 | tf_op jit(solution)/shard_map/ppermute | solution.py:512
  9.1 0.5 collective-permute-start.3
  9.7 0.6 collective-permute-start.1
  10.3 10.8 %all-to-all-start = ((f32[128,4,128]{2,1,0:T(4,128)}), f32[128,4,128]{2,1,0:T(4,128)S(1)}, u32[]{:S(2)}, u32[]{:S(2)}) async-start(f32[128,4,128]{2,1,0:T(4,128)} %bitcast.1), calls=%async_computation | async-start | bytes 524288 | tf_op jit(solution)/shard_map/all_to_all | solution.py:488
  21.1 0.0 copy-done.2
  21.1 1.1 %collective-permute-start = (f32[16,2048]{1,0:T(8,128)S(1)}, f32[16,2048]{1,0:T(8,128)S(1)}, u32[]{:S(2)}, u32[]{:S(2)}) collective-permute-start(f32[16,2048]{1,0:T(8,128)S(1)} %copy-done.2), channel_id=1, source_target_pairs={{0,16},{16,0},{32,48},{48,32},{64,80},{80,64},{96,112},{112,96},{1... | collective-permute-start | bytes 393224 | tf_op jit(solution)/shard_map/ppermute | solution.py:513
  22.3 0.0 collective-permute-done.5.tab6
  22.3 0.1 collective-permute-start.6
  22.4 0.0 collective-permute-done.3.tab4
  22.4 0.4 collective-permute-start.4
  22.8 0.0 collective-permute-done.1.tab2
  22.8 0.1 collective-permute-start.2
  22.9 0.0 copy-done.5
  22.9 2.7 %shard_map.106 = (s32[128,128]{1,0:T(8,128)S(1)}, bf16[128,128]{1,0:T(8,128)(2,1)S(1)}) custom-call(s32[128,128]{1,0:T(8,128)S(1)} %bitcast.14, f32[16,2048]{1,0:T(8,128)S(1)} %copy-done.2), custom_call_target="tpu_custom_call" | custom-call | flops 10000000 | bytes 100000 | tf_op jit(solution)/shard_map/pallas_call | solution.py:515
  25.6 0.0 collective-permute-done.tab1
  25.6 6.8 %all-to-all-done = f32[128,4,128]{2,1,0:T(4,128)S(1)} async-done(((f32[128,4,128]{2,1,0:T(4,128)}), f32[128,4,128]{2,1,0:T(4,128)S(1)}, u32[]{:S(2)}, u32[]{:S(2)}) %all-to-all-start) | async-done | bytes 262176 | tf_op jit(solution)/shard_map/all_to_all | solution.py:488
  32.4 0.0 collective-permute-done.6.tab7
  32.4 0.0 collective-permute-done.4.tab5
  32.4 0.0 collective-permute-done.2.tab3
  32.4 0.0 copy-done.3
  32.4 0.0 copy-done.4
  32.4 7.8 %shard_map.107 = (f32[4,8,256]{2,1,0:T(8,128)S(1)}, f32[9,24,256]{2,1,0:T(8,128)S(1)}, f32[8,256]{1,0:T(8,128)S(1)}, f32[7,8,256]{2,1,0:T(8,128)S(1)}, f32[7,8,256]{2,1,0:T(8,128)S(1)}) custom-call(s32[1]{0:T(128)S(6)} %copy.12.count, f32[512,128]{1,0:T(8,128)S(1)} %bitcast.11, s32[128,128]{1,0:T(8,128)S(1)} %bitcast.15, ...), custom_call_target="tpu_custom_call" | custom-call | flops 10000 | bytes 100000 | tf_op jit(solution)/shard_map/pallas_call | solution.py:519
  40.2 0.8 collective-permute-start.7
  41.0 2.1 %collective-permute-start.8 = (f32[7,8,256]{2,1,0:T(8,128)S(1)}, f32[7,8,256]{2,1,0:T(8,128)S(1)}, u32[]{:S(2)}, u32[]{:S(2)}) collective-permute-start(f32[7,8,256]{2,1,0:T(8,128)S(1)} %get-tuple-element.34), channel_id=1, source_target_pairs={{16,32},{32,16},{48,64},{64,48},{80,96},{96,80},{17,33},{33,17},{4... | collective-permute-start | bytes 172040 | tf_op jit(solution)/shard_map/ppermute | solution.py:484
  43.1 0.0 collective-permute-done.7.xa
  43.2 3.3 %collective-permute-done.8.xb = f32[7,8,256]{2,1,0:T(8,128)S(1)} collective-permute-done((f32[7,8,256]{2,1,0:T(8,128)S(1)}, f32[7,8,256]{2,1,0:T(8,128)S(1)}, u32[]{:S(2)}, u32[]{:S(2)}) %collective-permute-start.8) | collective-permute-done | bytes 57376 | tf_op jit(solution)/shard_map/ppermute | solution.py:484
  46.5 0.6 collective-permute-start.9
  47.2 0.7 collective-permute-start.10
  47.8 1.9 %collective-permute-done.9.ya = f32[8,8,256]{2,1,0:T(8,128)S(1)} collective-permute-done((f32[8,8,256]{2,1,0:T(8,128)S(1)}, f32[8,8,256]{2,1,0:T(8,128)S(1)}, u32[]{:S(2)}, u32[]{:S(2)}) %collective-permute-start.9) | collective-permute-done | bytes 65568 | tf_op jit(solution)/shard_map/ppermute | solution.py:484
  49.7 0.0 collective-permute-done.10.yb
  49.7 0.0 copy-done.6
  49.7 0.4 shard_map.109
  50.2 19.2 %all_to_all.15 = f32[128,2,128]{2,1,0:T(2,128)S(1)} all-to-all(f32[128,2,128]{2,1,0:T(2,128)S(1)} %bitcast.18), channel_id=1, replica_groups=mesh['coarse'=8,'fine'=16] {'coarse','fine'}, dimensions={0} | all-to-all | bytes 262144 | tf_op jit(solution)/shard_map/all_to_all | solution.py:488
  69.4 3.9 %shard_map.110 = (f32[4,8,256]{2,1,0:T(8,128)S(1)}, f32[8,256]{1,0:T(8,128)S(1)}, f32[8,256]{1,0:T(8,128)S(1)}, f32[8,256]{1,0:T(8,128)S(1)}, f32[8,256]{1,0:T(8,128)S(1)}) custom-call(s32[1]{0:T(128)S(6)} %copy.12.count, f32[256,128]{1,0:T(8,128)S(1)} %bitcast.13, f32[512,128]{1,0:T(8,128)S(1)} %bitcast.12, s32[128,128]{1,0:T(8,128)S(1)} %get-tuple-element.29.inverse, ...), custom_call_target="tpu_custom_call" | custom-call | flops 10000 | bytes 100000 | tf_op jit(solution)/shard_map/pallas_call | solution.py:534
  73.3 0.8 collective-permute-start.11
  74.1 2.1 %collective-permute-start.12 = (f32[8,256]{1,0:T(8,128)S(1)}, f32[8,256]{1,0:T(8,128)S(1)}, u32[]{:S(2)}, u32[]{:S(2)}) collective-permute-start(f32[8,256]{1,0:T(8,128)S(1)} %get-tuple-element.44), channel_id=1, source_target_pairs={{16,32},{32,16},{48,64},{64,48},{80,96},{96,80},{17,33},{33,17},{4... | collective-permute-start | bytes 24584 | tf_op jit(solution)/shard_map/ppermute | solution.py:484
  76.2 0.6 collective-permute-start.13
  76.8 0.6 collective-permute-start.14
  77.5 0.0 collective-permute-done.11.xa
  77.5 1.5 %collective-permute-done.12.xb = f32[8,256]{1,0:T(8,128)S(1)} collective-permute-done((f32[8,256]{1,0:T(8,128)S(1)}, f32[8,256]{1,0:T(8,128)S(1)}, u32[]{:S(2)}, u32[]{:S(2)}) %collective-permute-start.12) | collective-permute-done | bytes 8224 | tf_op jit(solution)/shard_map/ppermute | solution.py:484
  79.0 0.0 collective-permute-done.13.ya
  79.0 0.0 collective-permute-done.14.yb
  79.0 0.0 copy-done.7
  79.1 0.2 shard_map.111
  79.3 19.1 %all_to_all.16 = f32[128,1,128]{2,1,0:T(1,128)S(1)} all-to-all(f32[128,1,128]{2,1,0:T(1,128)S(1)} %bitcast.16), channel_id=1, replica_groups=mesh['coarse'=8,'fine'=16] {'coarse','fine'}, dimensions={0} | all-to-all | bytes 131072 | tf_op jit(solution)/shard_map/all_to_all | solution.py:488
  98.4 1.4 %shard_map.112 = (f32[4,8,256]{2,1,0:T(8,128)}, f32[16,4,8,256]{3,2,1,0:T(8,128)}) custom-call(f32[128,128]{1,0:T(8,128)S(1)} %bitcast.17, f32[4,8,256]{2,1,0:T(8,128)S(1)} %get-tuple-element.47.z1, f32[4,8,256]{2,1,0:T(8,128)S(1)} %get-tuple-element.42.p, f32[16,4,8,256]{3,2,1,0:T(8,128)S(1)} %copy-done, f32[16,4,8,256]{3,2,1,0:T(8,128)S(1)} %copy-done.1), custom_call_target="tpu_custom_call" | custom-call | flops 10000 | bytes 100000 | tf_op jit(solution)/shard_map/pallas_call | solution.py:543
  (11 shorter events, 0.1 us)
Async XLA Ops:
  5.8 16.4 %collective-permute-start.5 = (f32[16,2048]{1,0:T(8,128)}, f32[16,2048]{1,0:T(8,128)S(1)}, u32[]{:S(2)}, u32[]{:S(2)}) collective-permute-start(f32[16,2048]{1,0:T(8,128)} %shard_map.105.after.tab0), channel_id=1, source_target_pairs={{0,96},{16,112},{32,0},{48,16},{64,32},{80,48},{96,64},{112,80},{1... | collective-permute-start | bytes 393224 | tf_op jit(solution)/shard_map/ppermute | solution.py:512
  9.1 13.2 %collective-permute-start.3 = (f32[16,2048]{1,0:T(8,128)}, f32[16,2048]{1,0:T(8,128)S(1)}, u32[]{:S(2)}, u32[]{:S(2)}) collective-permute-start(f32[16,2048]{1,0:T(8,128)} %shard_map.105.after.tab0), channel_id=1, source_target_pairs={{0,64},{16,80},{32,96},{48,112},{64,0},{80,16},{96,32},{112,48},{1... | collective-permute-start | bytes 393224 | tf_op jit(solution)/shard_map/ppermute | solution.py:512
  9.7 13.1 %collective-permute-start.1 = (f32[16,2048]{1,0:T(8,128)}, f32[16,2048]{1,0:T(8,128)S(1)}, u32[]{:S(2)}, u32[]{:S(2)}) collective-permute-start(f32[16,2048]{1,0:T(8,128)} %shard_map.105.after.tab0), channel_id=1, source_target_pairs={{0,32},{16,48},{32,64},{48,80},{64,96},{80,112},{96,0},{112,16},{1... | collective-permute-start | bytes 393224 | tf_op jit(solution)/shard_map/ppermute | solution.py:512
  10.3 10.8 %copy-start.2 = (f32[16,2048]{1,0:T(8,128)S(1)}, f32[16,2048]{1,0:T(8,128)}, u32[]{:S(2)}) copy-start(f32[16,2048]{1,0:T(8,128)} %shard_map.105.after.tab0) | copy-start | bytes 393220
  10.3 12.6 %copy-start.5 = (s32[16384]{0:T(1024)S(1)}, s32[16384]{0:T(1024)}, u32[]{:S(2)}) copy-start(s32[16384]{0:T(1024)} %param.14) | copy-start | bytes 196612
  10.3 22.1 %all-to-all-start = ((f32[128,4,128]{2,1,0:T(4,128)}), f32[128,4,128]{2,1,0:T(4,128)S(1)}, u32[]{:S(2)}, u32[]{:S(2)}) async-start(f32[128,4,128]{2,1,0:T(4,128)} %bitcast.1), calls=%async_computation | async-start | bytes 524288 | tf_op jit(solution)/shard_map/all_to_all | solution.py:488
  21.1 4.5 %collective-permute-start = (f32[16,2048]{1,0:T(8,128)S(1)}, f32[16,2048]{1,0:T(8,128)S(1)}, u32[]{:S(2)}, u32[]{:S(2)}) collective-permute-start(f32[16,2048]{1,0:T(8,128)S(1)} %copy-done.2), channel_id=1, source_target_pairs={{0,16},{16,0},{32,48},{48,32},{64,80},{80,64},{96,112},{112,96},{1... | collective-permute-start | bytes 393224 | tf_op jit(solution)/shard_map/ppermute | solution.py:513
  22.3 10.1 %collective-permute-start.6 = (f32[16,2048]{1,0:T(8,128)S(1)}, f32[16,2048]{1,0:T(8,128)S(1)}, u32[]{:S(2)}, u32[]{:S(2)}) collective-permute-start(f32[16,2048]{1,0:T(8,128)S(1)} %collective-permute-done.5.tab6), channel_id=1, source_target_pairs={{0,16},{16,0},{32,48},{48,32},{64,80},{80,64},{96,112},{112,96},{1... | collective-permute-start | bytes 393224 | tf_op jit(solution)/shard_map/ppermute | solution.py:513
  22.4 10.0 %collective-permute-start.4 = (f32[16,2048]{1,0:T(8,128)S(1)}, f32[16,2048]{1,0:T(8,128)S(1)}, u32[]{:S(2)}, u32[]{:S(2)}) collective-permute-start(f32[16,2048]{1,0:T(8,128)S(1)} %collective-permute-done.3.tab4), channel_id=1, source_target_pairs={{0,16},{16,0},{32,48},{48,32},{64,80},{80,64},{96,112},{112,96},{1... | collective-permute-start | bytes 393224 | tf_op jit(solution)/shard_map/ppermute | solution.py:513
  22.8 9.6 %collective-permute-start.2 = (f32[16,2048]{1,0:T(8,128)S(1)}, f32[16,2048]{1,0:T(8,128)S(1)}, u32[]{:S(2)}, u32[]{:S(2)}) collective-permute-start(f32[16,2048]{1,0:T(8,128)S(1)} %collective-permute-done.1.tab2), channel_id=1, source_target_pairs={{0,16},{16,0},{32,48},{48,32},{64,80},{80,64},{96,112},{112,96},{1... | collective-permute-start | bytes 393224 | tf_op jit(solution)/shard_map/ppermute | solution.py:513
  22.9 9.5 %copy-start.3 = (f32[4,8,256]{2,1,0:T(8,128)S(1)}, f32[4,8,256]{2,1,0:T(8,128)}, u32[]{:S(2)}) copy-start(f32[4,8,256]{2,1,0:T(8,128)} %get-tuple-element.27.after.ic) | copy-start | bytes 98308
  22.9 9.5 %copy-start.4 = (f32[4,8,256]{2,1,0:T(8,128)S(1)}, f32[4,8,256]{2,1,0:T(8,128)}, u32[]{:S(2)}) copy-start(f32[4,8,256]{2,1,0:T(8,128)} %get-tuple-element.26.zs) | copy-start | bytes 98308
  40.2 2.9 %collective-permute-start.7 = (f32[7,8,256]{2,1,0:T(8,128)S(1)}, f32[7,8,256]{2,1,0:T(8,128)S(1)}, u32[]{:S(2)}, u32[]{:S(2)}) collective-permute-start(f32[7,8,256]{2,1,0:T(8,128)S(1)} %get-tuple-element.33), channel_id=1, source_target_pairs={{0,16},{16,0},{32,48},{48,32},{64,80},{80,64},{96,112},{112,96},{1... | collective-permute-start | bytes 172040 | tf_op jit(solution)/shard_map/ppermute | solution.py:484
  41.0 5.5 %collective-permute-start.8 = (f32[7,8,256]{2,1,0:T(8,128)S(1)}, f32[7,8,256]{2,1,0:T(8,128)S(1)}, u32[]{:S(2)}, u32[]{:S(2)}) collective-permute-start(f32[7,8,256]{2,1,0:T(8,128)S(1)} %get-tuple-element.34), channel_id=1, source_target_pairs={{16,32},{32,16},{48,64},{64,48},{80,96},{96,80},{17,33},{33,17},{4... | collective-permute-start | bytes 172040 | tf_op jit(solution)/shard_map/ppermute | solution.py:484
  46.5 3.2 %copy-start.6 = (f32[4,8,256]{2,1,0:T(8,128)S(1)}, f32[4,8,256]{2,1,0:T(8,128)}, u32[]{:S(2)}) copy-start(f32[4,8,256]{2,1,0:T(8,128)} %get-tuple-element.32.c) | copy-start | bytes 98308
  46.5 3.2 %collective-permute-start.9 = (f32[8,8,256]{2,1,0:T(8,128)S(1)}, f32[8,8,256]{2,1,0:T(8,128)S(1)}, u32[]{:S(2)}, u32[]{:S(2)}) collective-permute-start(f32[8,8,256]{2,1,0:T(8,128)S(1)} %get-tuple-element.35), channel_id=1, source_target_pairs={{0,1},{1,0},{2,3},{3,2},{4,5},{5,4},{6,7},{7,6},{8,9},{9,8},{10,11... | collective-permute-start | bytes 196616 | tf_op jit(solution)/shard_map/ppermute | solution.py:484
  47.2 2.6 %collective-permute-start.10 = (f32[8,8,256]{2,1,0:T(8,128)S(1)}, f32[8,8,256]{2,1,0:T(8,128)S(1)}, u32[]{:S(2)}, u32[]{:S(2)}) collective-permute-start(f32[8,8,256]{2,1,0:T(8,128)S(1)} %get-tuple-element.36), channel_id=1, source_target_pairs={{1,2},{2,1},{3,4},{4,3},{5,6},{6,5},{7,8},{8,7},{9,10},{10,9},{11,... | collective-permute-start | bytes 196616 | tf_op jit(solution)/shard_map/ppermute | solution.py:484
  69.4 9.7 %copy-start.7 = (f32[4,8,256]{2,1,0:T(8,128)S(1)}, f32[4,8,256]{2,1,0:T(8,128)}, u32[]{:S(2)}) copy-start(f32[4,8,256]{2,1,0:T(8,128)} %get-tuple-element.25.s) | copy-start | bytes 98308
  69.4 29.0 %copy-start = (f32[16,4,8,256]{3,2,1,0:T(8,128)S(1)}, f32[16,4,8,256]{3,2,1,0:T(8,128)}, u32[]{:S(2)}) copy-start(f32[16,4,8,256]{3,2,1,0:T(8,128)} %s_old.1) | copy-start | bytes 1572868
  69.4 29.0 %copy-start.1 = (f32[16,4,8,256]{3,2,1,0:T(8,128)S(1)}, f32[16,4,8,256]{3,2,1,0:T(8,128)}, u32[]{:S(2)}) copy-start(f32[16,4,8,256]{3,2,1,0:T(8,128)} %rate.1) | copy-start | bytes 1572868
  73.3 4.2 %collective-permute-start.11 = (f32[8,256]{1,0:T(8,128)S(1)}, f32[8,256]{1,0:T(8,128)S(1)}, u32[]{:S(2)}, u32[]{:S(2)}) collective-permute-start(f32[8,256]{1,0:T(8,128)S(1)} %get-tuple-element.43), channel_id=1, source_target_pairs={{0,16},{16,0},{32,48},{48,32},{64,80},{80,64},{96,112},{112,96},{1... | collective-permute-start | bytes 24584 | tf_op jit(solution)/shard_map/ppermute | solution.py:484
  74.1 5.0 %collective-permute-start.12 = (f32[8,256]{1,0:T(8,128)S(1)}, f32[8,256]{1,0:T(8,128)S(1)}, u32[]{:S(2)}, u32[]{:S(2)}) collective-permute-start(f32[8,256]{1,0:T(8,128)S(1)} %get-tuple-element.44), channel_id=1, source_target_pairs={{16,32},{32,16},{48,64},{64,48},{80,96},{96,80},{17,33},{33,17},{4... | collective-permute-start | bytes 24584 | tf_op jit(solution)/shard_map/ppermute | solution.py:484
  76.2 2.8 %collective-permute-start.13 = (f32[8,256]{1,0:T(8,128)S(1)}, f32[8,256]{1,0:T(8,128)S(1)}, u32[]{:S(2)}, u32[]{:S(2)}) collective-permute-start(f32[8,256]{1,0:T(8,128)S(1)} %get-tuple-element.45), channel_id=1, source_target_pairs={{0,1},{1,0},{2,3},{3,2},{4,5},{5,4},{6,7},{7,6},{8,9},{9,8},{10,11... | collective-permute-start | bytes 24584 | tf_op jit(solution)/shard_map/ppermute | solution.py:484
  76.8 2.2 %collective-permute-start.14 = (f32[8,256]{1,0:T(8,128)S(1)}, f32[8,256]{1,0:T(8,128)S(1)}, u32[]{:S(2)}, u32[]{:S(2)}) collective-permute-start(f32[8,256]{1,0:T(8,128)S(1)} %get-tuple-element.46), channel_id=1, source_target_pairs={{1,2},{2,1},{3,4},{4,3},{5,6},{6,5},{7,8},{8,7},{9,10},{10,9},{11,... | collective-permute-start | bytes 24584 | tf_op jit(solution)/shard_map/ppermute | solution.py:484

commit v3 on v2

--- a/solution.py
+++ b/solution.py
@@ -15,6 +15,7 @@
 SHARDS = 8
 SHARD_ROWS = 2048
 FLOW = 50.0
+UNUSED = 1e30
 F32, BF16, I32 = jnp.float32, jnp.bfloat16, jnp.int32
 VM = pl.BlockSpec(memory_space=pltpu.VMEM)
 SM = pl.BlockSpec(memory_space=pltpu.SMEM)
@@ -44,13 +45,6 @@
 def split2(values):
     high = values.astype(BF16)
     return high, (values - high.astype(F32)).astype(BF16)
-
-
-def split3(values):
-    high = values.astype(BF16)
-    rest = values - high.astype(F32)
-    mid = rest.astype(BF16)
-    return high, mid, (rest - mid.astype(F32)).astype(BF16)
 
 
 def slots_of(plane, half, count):
@@ -96,15 +90,12 @@
     return 8.0 * (left + right + up + down + ahead) + 10.0 * behind
 
 
-def table_kernel(cols, off, diag, after, out):
-    out[0:8, :] = cols[...].astype(F32)
-    out[8:16, :] = off[...] * (0.8 / diag[...])
-
-
 def source_kernel(
-    cap, count, c_old, s_old_hbm, rate_hbm, diag, c_out, ic_out, s_out, zs_out, pay, s_old, rate, sems
+    cap, count, c_old, s_old_hbm, rate_hbm, diag, diag_row, order, cols, off,
+    c_out, ic_out, s_out, zs_out, tile_out, tab, s_old, rate, sems,
 ):
     place = places()
+    me = place[0] * 16 + place[1]
     n = count[0]
     copies = []
     for x in range(CX):
@@ -115,6 +106,12 @@
         for copy in pair:
             copy.start()
         copies.append(pair)
+    tab[0:8, :] = cols[...].astype(F32)
+    tab[8:16, :] = off[...] * (0.8 / diag_row[...])
+    mine = (order[0:1, :] >> 7) == me
+    low = jnp.sum(jnp.where(mine, (order[...] & 127).astype(F32), 0.0), axis=1, keepdims=True)
+    spot = iota((LANES, LANES), 1).astype(F32) == low
+    inverse = jnp.sum(jnp.where(spot, iota((LANES, LANES), 0).astype(F32), 0.0), axis=0, keepdims=True)
     planes = []
     for x in range(CX):
         for copy in copies[x]:
@@ -128,45 +125,47 @@
             extra = extra + weighted * s_old[k, x]
         centre = (1.0 + mass) + FLOW
         source = c_old[x] + extra
-        inverse = 1.0 / centre
+        inv = 1.0 / centre
         c_out[x] = centre
-        ic_out[x] = inverse
+        ic_out[x] = inv
         s_out[x] = source
-        zs_out[x] = 0.8 * source * inverse
+        zs_out[x] = 0.8 * source * inv
         planes.append(source)
-    sums = restrict(planes, n)
+    sums = jnp.where(iota((1, SLOTS), 1) < n, restrict(planes, n), UNUSED)
     kind = iota((8, LANES), 0) & 3
-    rows = [
-        sums[:, :LANES],
-        sums[:, LANES:],
-        diag[pl.ds(place[1], 1), :],
-        jnp.full((1, LANES), n, I32).astype(F32),
-    ]
+    rows = [sums[:, :LANES], sums[:, LANES:], diag[pl.ds(place[1], 1), :], inverse]
     tile = jnp.broadcast_to(rows[3], (8, LANES))
     for k in range(3):
         tile = jnp.where(kind == k, rows[k], tile)
+    tile_out[...] = tile
+
+
+def repeat_kernel(tile, pay):
     for i in range(DEVICES // 2):
-        pay[pl.ds(8 * i, 8), :] = tile
-
-
-def order_kernel(order, after, inverse_out, blocks_out):
-    numbers = order[...]
-    blocks = (iota((LANES, LANES), 0) == (numbers[0:1, :] >> 7)).astype(F32).astype(BF16)
-    blocks_out[...] = blocks
-    lows = nt(blocks, (numbers & 127).astype(F32).astype(BF16)).astype(I32)
-    lane = iota((LANES, LANES), 1)
-    found = jnp.zeros((LANES, LANES), I32)
-    for q in range(LANES):
-        found = jnp.where(lows[:, q : q + 1] == lane, q, found)
-    inverse_out[...] = found
-
-
-def offsets_of(counts):
-    strict = (iota((LANES, LANES), 1) < iota((LANES, LANES), 0)).astype(F32).astype(BF16)
-    by_row = nn(strict, counts.astype(BF16)).astype(I32)
-    later = iota((LANES, LANES), 0) < iota((LANES, LANES), 1)
-    by_lane = jnp.sum(jnp.where(later, counts, 0.0), axis=0, keepdims=True).astype(I32)
+        pay[pl.ds(8 * i, 8), :] = tile[...]
+
+
+def read_sums(gathered):
+    low = gathered[pl.ds(0, DEVICES, stride=4), :]
+    high = gathered[pl.ds(1, DEVICES, stride=4), :]
+    diag = gathered[pl.ds(2, DEVICES, stride=4), :]
+    inverse = gathered[pl.ds(3, DEVICES, stride=4), :].astype(I32)
+    used = ((low < 0.5 * UNUSED).astype(F32) + (high < 0.5 * UNUSED).astype(F32)).astype(BF16)
+    return low, high, diag, inverse, used
+
+
+def offsets_of(used):
+    below = iota((LANES, LANES), 1) < iota((LANES, LANES), 0)
+    ones = jnp.ones((LANES, LANES), BF16)
+    by_row = nn(nn(below.astype(F32).astype(BF16), used).astype(BF16), ones).astype(I32)
+    counts = nt(ones, used)
+    above = iota((LANES, LANES), 0) < iota((LANES, LANES), 1)
+    by_lane = nn(counts[0:8].astype(BF16), above.astype(F32).astype(BF16))[0:1].astype(I32)
     return by_row, by_lane
+
+
+def blocks_of(order):
+    return (iota((LANES, LANES), 0) == (order[0:1, :] >> 7)).astype(F32).astype(BF16)
 
 
 def assemble(low, high, offsets, inverse, blocks):
@@ -179,21 +178,17 @@
     kept = lane >= shift
     rows = (jnp.where(kept, low, 0.0), jnp.where(kept, high, low), jnp.where(kept, 0.0, high))
     start = by_lane >> 7
-    table = jnp.zeros((LANES, LANES), F32)
-    for j in range(3):
-        spot = (iota((LANES, LANES), 0) == start + j).astype(F32).astype(BF16)
-        for part in split3(rows[j]):
-            table = table + nn(spot, part)
-    by_block = jnp.zeros((LANES, LANES), F32)
-    for part in split3(table):
-        by_block = by_block + nt(blocks, part)
-    return lane_take(by_block, inverse)
+    spots = [(iota((LANES, LANES), 0) == start + j).astype(F32).astype(BF16) for j in range(3)]
+    parts = [jnp.concatenate(split2(r), axis=1) for r in rows]
+    table = nn(jnp.concatenate(spots, axis=1), jnp.concatenate(parts, axis=0))
+    by_block = nt(blocks, jnp.concatenate([table[:, :LANES], table[:, LANES:]], axis=0).astype(BF16))
+    return lane_take(by_block[:, :LANES] + by_block[:, LANES:], inverse)
 
 
 def fetch(table, unknown, coarse):
     inner = unknown & (SHARD_ROWS - 1)
     shard = unknown >> 11
-    shard = ((((coarse >> 1) - (shard >> 1)) & 3) << 1) | ((shard ^ coarse) & 1)
+    shard = shard ^ coarse
     found = jnp.zeros((SHARDS * 32, SLOTS), F32)
     for chunk in range(SHARD_ROWS // 256):
         spot = (iota((256, SLOTS), 0) + chunk * 256 == inner).astype(F32).astype(BF16)
@@ -234,20 +229,25 @@
 
 
 def first_kernel(
-    count, gathered, order, inverse, blocks, tab0, tab1, tab2, tab3, tab4, tab5, tab6, tab7, zs, ic,
-    pe_out, plan, own, xa, xb, table,
+    count, gathered, order, tab0, tab1, tab2, tab3, tab4, tab5, tab6, tab7, zs, ic,
+    pe_out, plan, own, beside, xa, xb, table,
 ):
     place = places()
     n = count[0]
     me = place[0] * 16 + place[1]
-    counts = gathered[pl.ds(3, DEVICES, stride=4), :]
-    offsets = offsets_of(counts)
+    low, high, diag, inverse, used = read_sums(gathered)
+    offsets = offsets_of(used)
     sums = assemble(
-        gathered[pl.ds(0, DEVICES, stride=4), :],
-        gathered[pl.ds(1, DEVICES, stride=4), :],
-        offsets, inverse[...], blocks[...],
+        jnp.where(low < 0.5 * UNUSED, low, 0.0), jnp.where(high < 0.5 * UNUSED, high, 0.0),
+        offsets, inverse, blocks_of(order),
     )
-    values = 0.8 * sums / gathered[pl.ds(2, DEVICES, stride=4), :]
+    values = 0.8 * sums / diag
+    counts = nn(used, jnp.ones((LANES, LANES), BF16))
+    wanted = me + jnp.where(iota((8, LANES), 0) < 4, -1, 1)
+    row = iota((LANES, LANES), 0)
+    before = jnp.sum(jnp.where(row == me - 1, counts, 0.0), axis=0, keepdims=True)
+    after = jnp.sum(jnp.where(row == me + 1, counts, 0.0), axis=0, keepdims=True)
+    beside[...] = jnp.where(wanted < me, before, after).astype(I32)
 
     tabs = (tab0, tab1, tab2, tab3, tab4, tab5, tab6, tab7)
     for g in range(SHARDS):
@@ -259,7 +259,6 @@
         big = off.astype(BF16).astype(F32)
         table[32 * g + 16 : 32 * g + 32, :] = jnp.concatenate([big, off - big], axis=0).astype(BF16)
 
-    row = iota((LANES, LANES), 0)
     mine = jnp.sum(jnp.where(row == me, offsets[0].astype(F32), 0.0), axis=0, keepdims=True).astype(I32)
     numbers = order[...].astype(F32)
     start = mine >> 7
@@ -308,15 +307,32 @@
         message(xb, True)
 
 
-def below_above(parity, a, b):
-    even = parity == 0
-    return (lambda *i: jnp.where(even, b[i], a[i])), (lambda *i: jnp.where(even, a[i], b[i]))
-
-
-def widen_kernel(zs, ic, pe, xa, xb, ya, yb):
-    place = places()
-    below, above = below_above(place[0] & 1, xa, xb)
-    own = (zs, ic, pe)
+def below_above(index, count, a, b):
+    even = (index & 1) == 0
+    inner = jnp.logical_and(index > 0, index < count - 1)
+
+    def near(i):
+        return a[i], jnp.where(inner, b[i], 0.0)
+
+    def below(i):
+        first, second = near(i)
+        return jnp.where(even, second, first)
+
+    def above(i):
+        first, second = near(i)
+        return jnp.where(even, first, second)
+
+    return below, above
+
+
+def ghost_rows(field, x):
+    return max(0, (4, 3, 3)[field] - max(0, -x, x - CX + 1))
+
+
+PACKED = [(f, x, k) for f in range(3) for x in range(-3, CX + 3) for k in range(ghost_rows(f, x))]
+
+
+def wide_plane(own, below, above):
     depth = (3, 2, 2)
     base = (0, 3, 5)
 
@@ -327,39 +343,45 @@
             return above(base[field] + x - CX)
         return own[field][x]
 
+    return plane
+
+
+def widen_kernel(zs, ic, pe, xa, xb, ya, yb):
+    place = places()
+    plane = wide_plane((zs, ic, pe), *below_above(place[0], 8, xa, xb))
     even = (place[1] & 1) == 0
-    for x in range(-2, CX + 2):
-        fields = [plane(f, x) for f in range(3)]
-        upper = jnp.concatenate([fields[f][CY - depth[f] :] for f in range(3)] + [fields[0][0:1]], axis=0)
-        lower = jnp.concatenate([fields[f][: depth[f]] for f in range(3)] + [fields[0][0:1]], axis=0)
-        ya[x + 2] = jnp.where(even, upper, lower)
-        yb[x + 2] = jnp.where(even, lower, upper)
-
-
-def second_kernel(count, zs, ic, pe, c, xa, xb, ya, yb, z1_out, w1_out, sw_out, pay):
+    upper, lower = [], []
+    for f in range(3):
+        for x in range(-3, CX + 3):
+            d = ghost_rows(f, x)
+            if d:
+                here = plane(f, x)
+                upper.append(here[CY - d :])
+                lower.append(here[:d])
+    upper, lower = jnp.concatenate(upper, axis=0), jnp.concatenate(lower, axis=0)
+    ya[...] = jnp.where(even, upper, lower)
+    yb[...] = jnp.where(even, lower, upper)
+
+
+def second_kernel(
+    count, zs, ic, pe, c, xa, xb, ya, yb, z1_out, w1_out, sw_out, sw_ghost, s_ghost, w_ghost, pay
+):
     place = places()
-    below, above = below_above(place[0] & 1, xa, xb)
-    near, far = below_above(place[1] & 1, ya, yb)
-    own = (zs, ic, pe)
-    depth = (3, 2, 2)
-    base = (0, 3, 5)
+    middle = wide_plane((zs, ic, pe), *below_above(place[0], 8, xa, xb))
+    near, far = [side(...) for side in below_above(place[1], 16, ya, yb)]
 
     def plane(field, x):
-        if x < 0:
-            middle = below(base[field] + depth[field] + x)
-        elif x >= CX:
-            middle = above(base[field] + x - CX)
-        else:
-            middle = own[field][x]
-        d = depth[field]
-        if -2 <= x < CX + 2:
-            low = near(x + 2)[base[field] : base[field] + d]
-            high = far(x + 2)[base[field] : base[field] + d]
-        else:
-            low = jnp.zeros((d, CZ), F32)
-            high = low
-        blank = jnp.zeros((8 - d, CZ), F32)
-        return jnp.concatenate([blank, low, middle, high, blank], axis=0)
+        d = ghost_rows(field, x)
+        here = middle(field, x)
+        if not d:
+            blank = jnp.zeros((8, CZ), F32)
+            return jnp.concatenate([blank, here, blank], axis=0)
+        at = PACKED.index((field, x, 0))
+        parts = [near[at : at + d], here, far[at : at + d]]
+        if d < 8:
+            blank = jnp.zeros((8 - d, CZ), F32)
+            parts = [blank] + parts + [blank]
+        return jnp.concatenate(parts, axis=0)
 
     def neighbours(get, x):
         mid = get(x)
@@ -384,6 +406,12 @@
     for x in range(CX):
         smooth = 1.2 * zw[x] + 0.8 * inv[x] * neighbours(zw.get, x)
         sw_out[x] = smooth[8:16]
+        for at, row in ((x, 7), (CX + x, 16)):
+            iv = inv[x][row : row + 1]
+            scale = jnp.where(iv > 0.0, 1.25 / jnp.where(iv > 0.0, iv, 1.0), 0.0)
+            sw_ghost[at : at + 1, :] = smooth[row : row + 1]
+            s_ghost[at : at + 1, :] = z[x][row : row + 1] * scale
+            w_ghost[at : at + 1, :] = zw[x][row : row + 1] * scale
     sums = restrict(image, count[0])
     kind = iota((8, LANES), 0) & 1
     tile = jnp.where(kind == 0, sums[:, :LANES], sums[:, LANES:])
@@ -391,61 +419,82 @@
         pay[pl.ds(8 * i, 8), :] = tile
 
 
-def third_kernel(
-    count, sums, gathered, inverse, blocks, plan, own, sw,
-    p_out, xa, xb, ya, yb,
-):
+def third_kernel(count, sums, gathered, order, plan, own, sw, p_out, pe_face, e_face, xa, xb):
     place = places()
-    offsets = offsets_of(gathered[pl.ds(3, DEVICES, stride=4), :])
+    n = count[0]
+    _, _, diag, inverse, used = read_sums(gathered)
     values = assemble(
-        sums[pl.ds(0, DEVICES, stride=2), :],
-        sums[pl.ds(1, DEVICES, stride=2), :],
-        offsets, inverse[...], blocks[...],
+        sums[pl.ds(0, DEVICES, stride=2), :], sums[pl.ds(1, DEVICES, stride=2), :],
+        offsets_of(used), inverse, blocks_of(order),
     )
-    values = 0.8 * values / gathered[pl.ds(2, DEVICES, stride=4), :]
-    pe = prolong(coarse_solve(values, plan, own), count[0])
+    entries = coarse_solve(0.8 * values / diag, plan, own)
+    pe = prolong(entries, n)
     p = [sw[x] + pe[x] for x in range(CX)]
     for x in range(CX):
         p_out[x] = p[x]
+        pe_face[x : x + 1, :] = pe[x][0:1]
+        pe_face[CX + x : CX + x + 1, :] = pe[x][CY - 1 : CY]
     even = (place[0] & 1) == 0
     xa[...] = jnp.where(even, p[CX - 1], p[0])
     xb[...] = jnp.where(even, p[0], p[CX - 1])
-    even = (place[1] & 1) == 0
-    upper = jnp.concatenate([p[x][CY - 1 : CY] for x in range(CX)] * 2, axis=0)
-    lower = jnp.concatenate([p[x][0:1] for x in range(CX)] * 2, axis=0)
-    ya[...] = jnp.where(even, upper, lower)
-    yb[...] = jnp.where(even, lower, upper)
-
-
-def products_kernel(s, w1, p, c, xa, xb, ya, yb, pay):
+    lane = iota((8, LANES), 1)
+    group = lane >> 4
+    cells = ((group & 3) * CY + jnp.where(group < 4, 0, CY - 1)) * CZ
+    slot = jnp.minimum(((cells * n) >> 13) + (lane & 15), SLOTS - 1)
+    low = jnp.broadcast_to(entries[:, :LANES], (8, LANES))
+    high = jnp.broadcast_to(entries[:, LANES:], (8, LANES))
+    e_face[...] = jnp.where(slot < LANES, lane_take(low, slot & 127), lane_take(high, slot & 127))
+
+
+def products_kernel(s, w1, p, c, xa, xb, sw_ghost, s_ghost, w_ghost, pe_face, e_face, beside, pay):
     place = places()
-    even = (place[0] & 1) == 0
-    below, above = jnp.where(even, xb[...], xa[...]), jnp.where(even, xa[...], xb[...])
-    even = (place[1] & 1) == 0
-    near, far = jnp.where(even, yb[...], ya[...]), jnp.where(even, ya[...], yb[...])
+    below, above = [side(...) for side in below_above(place[0], 8, xa, xb)]
     sums = [jnp.zeros((CY, CZ), F32) for _ in range(6)]
     row = iota((CY, CZ), 0)
+    rims = [None] * (2 * CX)
     for x in range(CX):
         mid = p[x]
         left = p[x - 1] if x else below
         right = p[x + 1] if x + 1 < CX else above
-        up = jnp.where(row == 0, near[x : x + 1], pltpu.roll(mid, 1, 0))
-        down = jnp.where(row == CY - 1, far[x : x + 1], pltpu.roll(mid, CY - 1, 0))
+        up = jnp.where(row == 0, sw_ghost[x : x + 1, :], pltpu.roll(mid, 1, 0))
+        down = jnp.where(row == CY - 1, sw_ghost[CX + x : CX + x + 1, :], pltpu.roll(mid, CY - 1, 0))
         q = c[x] * mid - couple(left, mid, right, up, down)
+        rims[x], rims[CX + x] = q[0:1], q[CY - 1 : CY]
         a, b = s[x], w1[x]
         for k, term in enumerate((a * a, a * b, a * q, b * b, b * q, q * q)):
             sums[k] = sums[k] + term
+    exists = jnp.where(row < 4, place[1], 15 - place[1]) > 0
+    face = pe_face[...]
+    sums[2] = sums[2] - 8.0 * face * s_ghost[...]
+    sums[4] = sums[4] - 8.0 * face * w_ghost[...]
+    sums[5] = sums[5] + jnp.where(exists, 64.0 * face * face, 0.0)
+    rim = jnp.where(exists, jnp.concatenate(rims, axis=0), 0.0)
+    n = jnp.concatenate([beside[...], beside[...]], axis=1)
+    cells = ((row & 3) * CY + jnp.where(row < 4, CY - 1, 0)) * CZ
+    member = (((cells + iota((CY, CZ), 1)) * n) >> 13) - ((cells * n) >> 13)
     lane = iota((8, LANES), 1)
-    tile = jnp.zeros((8, LANES), F32)
+    start = iota((8, LANES), 0) * 16
+    spread = jnp.zeros((8, LANES), F32)
+    for k in range(9):
+        part = jnp.sum(jnp.where(member == k, rim, 0.0), axis=1, keepdims=True)
+        spread = spread + jnp.where(lane == start + k, part, 0.0)
+    top = jnp.broadcast_to(jnp.sum(spread, axis=0, keepdims=True), (8, LANES))
     for k in range(6):
-        tile = tile + jnp.where(lane == k, jnp.sum(sums[k], keepdims=True), 0.0)
-    for i in range(DEVICES // 8):
+        top = top + jnp.where(lane == 9 + k, jnp.sum(sums[k], keepdims=True), 0.0)
+    tile = jnp.where((iota((8, LANES), 0) & 1) == 0, top, e_face[...])
+    for i in range(DEVICES // 4):
         pay[pl.ds(8 * i, 8), :] = tile
 
 
 def update_kernel(parts, z1, p, s_old, rate, mobile, immobile):
-    total = jnp.sum(parts[...], axis=0, keepdims=True)
-    ss, sw, sq, ww, wq, qq = [total[:, k : k + 1] for k in range(6)]
+    top = parts[pl.ds(0, DEVICES, stride=2), :]
+    face = pltpu.roll(parts[pl.ds(1, DEVICES, stride=2), :], LANES // 2, 1)
+    lane = iota((DEVICES, LANES), 1)
+    other = jnp.where(lane < LANES // 2, pltpu.roll(face, 1, 0), pltpu.roll(face, DEVICES - 1, 0))
+    cross = jnp.sum(jnp.where((lane & 15) < 9, top * other, 0.0), keepdims=True)
+    total = jnp.sum(top, axis=0, keepdims=True)
+    ss, sw, sq, ww, wq, qq = [total[:, 9 + k : 10 + k] for k in range(6)]
+    qq = qq - 16.0 * cross
     factor = wq / ww
     y2 = (sq - factor * sw) / (qq - factor * wq)
     y1 = (sw - wq * y2) / ww
@@ -473,15 +522,22 @@
 FIELD = ((CX, CY, CZ), F32)
 
 
-def swaps(count):
-    first = [(i, i ^ 1) for i in range(count)]
-    second = [(i, ((i - 1) ^ 1) + 1) for i in range(1, count - 1)]
-    return first, second
-
-
 def trade(a, b, axis):
-    first, second = swaps(lax.axis_size(axis))
-    return lax.ppermute(a, axis, first), lax.ppermute(b, axis, second)
+    n, m = lax.axis_size("coarse"), lax.axis_size("fine")
+    inside, between = [], []
+    for c in range(n):
+        for f in range(m):
+            me = c * m + f
+            at, count, step = (c, n, m) if axis == "coarse" else (f, m, 1)
+            inside.append((me, me + ((at ^ 1) - at) * step))
+            if 0 < at < count - 1:
+                between.append((me, me + (((at - 1) ^ 1) + 1 - at) * step))
+            elif axis == "fine":
+                between.append((me, (c ^ 1) * m + f))
+            else:
+                between.append((me, (n - 1 - c) * m + f))
+    b = lax.ppermute(b, BOTH, between)
+    return lax.ppermute(a, BOTH, inside), b
 
 
 def everyone(pay, rows):
@@ -493,53 +549,54 @@
     c_old, s_old, rate_time, capacity, agg_count, coarse_order, coarse_cols, coarse_off, coarse_diag
 ):
     order = coarse_order.reshape(LANES, LANES)
-
-    c, ic, s, zs, pay = call(
-        source_kernel, [SM, SM, VM, HB, HB, VM],
-        [FIELD, FIELD, FIELD, FIELD, ((4 * DEVICES, LANES), F32)],
+    c, ic, s, zs, tile, tab = call(
+        source_kernel, [SM, SM, VM, HB, HB] + [VM] * 5,
+        [FIELD, FIELD, FIELD, FIELD, ((8, LANES), F32), ((16, SHARD_ROWS), F32)],
         scratch=[
             pltpu.VMEM((RATES, CX, CY, CZ), F32),
             pltpu.VMEM((RATES, CX, CY, CZ), F32),
             pltpu.SemaphoreType.DMA((2, CX)),
         ],
         vmem=63 << 20,
-    )(capacity, agg_count, c_old, s_old, rate_time, coarse_diag.reshape(16, LANES))
-    (tab,) = call(table_kernel, [VM] * 4, [((16, SHARD_ROWS), F32)], vmem=63 << 20)(
-        coarse_cols, coarse_off, coarse_diag.reshape(1, SHARD_ROWS), ic
+    )(
+        capacity, agg_count, c_old, s_old, rate_time, coarse_diag.reshape(16, LANES),
+        coarse_diag.reshape(1, SHARD_ROWS), order, coarse_cols, coarse_off,
     )
     tabs = []
     for hop in (0, 2, 4, 6):
-        mine = lax.ppermute(tab, "coarse", [(i, (i + hop) % 8) for i in range(8)]) if hop else tab
-        tabs += [mine, lax.ppermute(mine, "coarse", [(i, i ^ 1) for i in range(8)])]
+        shard = lax.ppermute(tab, "coarse", [(i, i ^ hop) for i in range(8)]) if hop else tab
+        tabs += [shard, lax.ppermute(shard, "coarse", [(i, i ^ 1) for i in range(8)])]
+    (pay,) = call(repeat_kernel, [VM], [((4 * DEVICES, LANES), F32)])(tile)
     gathered = everyone(pay, 4)
-    inverse, blocks = call(
-        order_kernel, [VM] * 2, [((LANES, LANES), I32), ((LANES, LANES), BF16)], flops=10_000_000
-    )(order, tab)
-
-    pe, plan, own, xa, xb = call(
-        first_kernel, [SM] + [VM] * 14,
-        [FIELD, ((KC + 1, 24, SLOTS), F32), ((8, SLOTS), F32), ((7, CY, CZ), F32), ((7, CY, CZ), F32)],
+
+    pe, plan, own, beside, xa, xb = call(
+        first_kernel, [SM] + [VM] * 12,
+        [
+            FIELD, ((KC + 1, 24, SLOTS), F32), ((8, SLOTS), F32), ((8, LANES), I32),
+            ((7, CY, CZ), F32), ((7, CY, CZ), F32),
+        ],
         scratch=[pltpu.VMEM((SHARDS * 32, SHARD_ROWS), BF16)],
-    )(agg_count, gathered, order, inverse, blocks, *tabs, zs, ic)
+    )(agg_count, gathered, order, *tabs, zs, ic)
     xa, xb = trade(xa, xb, "coarse")
     ya, yb = call(
-        widen_kernel, [VM] * 5, [((CX + 4, CY, CZ), F32)] * 2
+        widen_kernel, [VM] * 5, [((len(PACKED), CZ), F32)] * 2
     )(zs, ic, pe, xa, xb)
     ya, yb = trade(ya, yb, "fine")
-    z1, w1, sw, pay = call(
-        second_kernel, [SM] + [VM] * 8, [FIELD, FIELD, FIELD, ((2 * DEVICES, LANES), F32)]
+    z1, w1, sw, sw_ghost, s_ghost, w_ghost, pay = call(
+        second_kernel, [SM] + [VM] * 8,
+        [FIELD, FIELD, FIELD] + [((CY, CZ), F32)] * 3 + [((2 * DEVICES, LANES), F32)],
     )(agg_count, zs, ic, pe, c, xa, xb, ya, yb)
     sums = everyone(pay, 2)
 
-    p, xa, xb, ya, yb = call(
-        third_kernel, [SM] + [VM] * 7, [FIELD] + [((CY, CZ), F32)] * 4
-    )(agg_count, sums, gathered, inverse, blocks, plan, own, sw)
+    p, pe_face, e_face, xa, xb = call(
+        third_kernel, [SM] + [VM] * 6,
+        [FIELD, ((CY, CZ), F32), ((8, LANES), F32), ((CY, CZ), F32), ((CY, CZ), F32)],
+    )(agg_count, sums, gathered, order, plan, own, sw)
     xa, xb = trade(xa, xb, "coarse")
-    ya, yb = trade(ya, yb, "fine")
     (pay,) = call(
-        products_kernel, [VM] * 8, [((DEVICES, LANES), F32)]
-    )(s, w1, p, c, xa, xb, ya, yb)
-    parts = everyone(pay, 1)
+        products_kernel, [VM] * 12, [((2 * DEVICES, LANES), F32)]
+    )(s, w1, p, c, xa, xb, sw_ghost, s_ghost, w_ghost, pe_face, e_face, beside)
+    parts = everyone(pay, 2)
     mobile, immobile = call(
         update_kernel, [VM] * 5, [FIELD, ((RATES, CX, CY, CZ), F32)]
     )(parts, z1, p, s_old, rate_time)

time: 100 us -> 90.3 us (0.903)
  blocking collectives: 38.3 us -> 31.5 us
  starting transfers between devices: 25.4 us -> 21.5 us
  waiting for transfers between devices: 13.6 us -> 17.1 us
  Pallas kernels: 21 us -> 17.7 us
    all_to_all x2, blocking collectives: 38.3 us -> 31.5 us  [everyone(): moved = lax.all_to_all(pay.reshape(DEVICES, rows, LANES), BOTH, 0, 0)]
    ppermute x15 -> x13, starting transfers between devices: 14.6 us -> 9.87 us  [the longest x3 4.06 us: local(): lax.ppermute(tab, 'coarse', [(i, i ^ hop) for i in range(8)])]
    pallas_call x8 -> x7, Pallas kernels: 19.6 us -> 16.3 us  [the longest x1 7.85 us: local(): call(first_kernel, [SM] + [VM] * 12, [FIELD, ((KC + 1, 24, SLOTS), F32),...]
    all_to_all x1, waiting for transfers between devices: 6.76 us -> 9.1 us  [everyone(): moved = lax.all_to_all(pay.reshape(DEVICES, rows, LANES), BOTH, 0, 0)]
    ppermute x15 -> x13, waiting for transfers between devices: 6.81 us -> 8.05 us  [the longest x3 5.26 us: trade(): b = lax.ppermute(b, BOTH, between)]
  transfers between devices with their start and end apart: 16 -> 14, of which waited for: 4 -> 7; matrix products, arithmetic and copies ran while one was open for 0% -> 0% of each run, Pallas kernels for 3% -> 1%
where the time goes in v3:
time: 90.3 us; the launch traced here: 89.9 us
  blocking collectives  31.5 us (35%)
  starting transfers between devices  21.5 us (24%)
  Pallas kernels  17.7 us (20%)
  waiting for transfers between devices  17.1 us (19%)
  between operations  1.39 us (2%)
    all_to_all x2, blocking collectives, everyone(): moved = lax.all_to_all(pay.reshape(DEVICES, rows, LANES), BOTH, 0, 0)  31.5 us
    all_to_all x1, starting transfers between devices, everyone(): moved = lax.all_to_all(pay.reshape(DEVICES, rows, LANES), BOTH, 0, 0)  11.6 us
    all_to_all x1, waiting for transfers between devices, everyone(): moved = lax.all_to_all(pay.reshape(DEVICES, rows, LANES), BOTH, 0, 0)  9.1 us
    pallas_call x1, Pallas kernels, local(): call(first_kernel, [SM] + [VM] * 12, [FIELD, ((KC + 1, 24, SLOTS), F32),...  7.85 us
    ppermute x3, waiting for transfers between devices, trade(): b = lax.ppermute(b, BOTH, between)  5.26 us
    ppermute x3, starting transfers between devices, local(): lax.ppermute(tab, 'coarse', [(i, i ^ hop) for i in range(8)])  4.06 us
    pallas_call x1, Pallas kernels, local(): call(third_kernel, [SM] + [VM] * 6, [FIELD, ((CY, CZ), F32), ((8, LANES),...  3.89 us
    pallas_call x1, Pallas kernels, local(): call(source_kernel, [SM, SM, VM, HB, HB] + [VM] * 5, [FIELD, FIELD, FIELD...  3.09 us
  transfers between devices with their start and end apart: 14, of which 7 were waited for; matrix products, arithmetic and copies ran while one was open for 0% of the time, Pallas kernels for 1%

profile of v3, /device:TPU:1, one launch (start us, length us, event | category | flops | bytes accessed | tf_op | source)
XLA Modules:
  0.0 89.9 jit_solution(10922470198584321931)
XLA Ops:
  1.3 3.1 %shard_map.104 = (f32[4,8,256]{2,1,0:T(8,128)}, f32[4,8,256]{2,1,0:T(8,128)}, f32[4,8,256]{2,1,0:T(8,128)}, f32[4,8,256]{2,1,0:T(8,128)}, f32[8,128]{1,0:T(8,128)}, /*index=5*/f32[16,2048]{1,0:T(8,128)}) custom-call(f32[16]{0:T(128)} %cap.1, s32[1]{0:T(128)S(6)} %copy.11.count, f32[4,8,256]{2,1,0:T(8,128)} %c_old.1, f32[16,4,8,256]{3,2,1,0:T(8,128)} %s_old.1, ...), custom_call_target="tpu_custom_call" | custom-call | flops 10000 | bytes 100000 | tf_op jit(solution)/shard_map/pallas_call | solution.py:552
  4.4 3.4 %collective-permute-start.5 = (f32[16,2048]{1,0:T(8,128)}, f32[16,2048]{1,0:T(8,128)S(1)}, u32[]{:S(2)}, u32[]{:S(2)}) collective-permute-start(f32[16,2048]{1,0:T(8,128)} %get-tuple-element.32.tab0), channel_id=1, source_target_pairs={{0,96},{16,112},{32,64},{48,80},{64,32},{80,48},{96,0},{112,16},{1... | collective-permute-start | bytes 393224 | tf_op jit(solution)/shard_map/ppermute | solution.py:567
  7.8 0.5 collective-permute-start.3
  8.3 0.1 collective-permute-start.1
  8.4 0.0 copy-start.8
  8.4 0.7 copy-done.8
  9.1 0.7 shard_map.105
  9.8 0.0 copy-start.6
  9.8 11.6 %all-to-all-start = ((f32[128,4,128]{2,1,0:T(4,128)}), f32[128,4,128]{2,1,0:T(4,128)S(1)}, u32[]{:S(2)}, u32[]{:S(2)}) async-start(f32[128,4,128]{2,1,0:T(4,128)} %bitcast.3), calls=%async_computation | async-start | bytes 524288 | tf_op jit(solution)/shard_map/all_to_all | solution.py:544
  21.5 0.0 copy-done.6
  21.5 1.1 %collective-permute-start = (f32[16,2048]{1,0:T(8,128)S(1)}, f32[16,2048]{1,0:T(8,128)S(1)}, u32[]{:S(2)}, u32[]{:S(2)}) collective-permute-start(f32[16,2048]{1,0:T(8,128)S(1)} %copy-done.6), channel_id=1, source_target_pairs={{0,16},{16,0},{32,48},{48,32},{64,80},{80,64},{96,112},{112,96},{1... | collective-permute-start | bytes 393224 | tf_op jit(solution)/shard_map/ppermute | solution.py:568
  22.6 0.0 collective-permute-done.5.tab6
  22.6 0.1 collective-permute-start.6
  22.7 0.0 collective-permute-done.3.tab4
  22.7 0.4 collective-permute-start.4
  23.2 0.0 collective-permute-done.1.tab2
  23.2 0.1 collective-permute-start.2
  23.3 0.4 collective-permute-done.tab1
  23.6 9.1 %all-to-all-done = f32[128,4,128]{2,1,0:T(4,128)S(1)} async-done(((f32[128,4,128]{2,1,0:T(4,128)}), f32[128,4,128]{2,1,0:T(4,128)S(1)}, u32[]{:S(2)}, u32[]{:S(2)}) %all-to-all-start) | async-done | bytes 262176 | tf_op jit(solution)/shard_map/all_to_all | solution.py:544
  32.7 0.0 collective-permute-done.6.tab7
  32.7 0.0 collective-permute-done.4.tab5
  32.7 0.0 collective-permute-done.2.tab3
  32.7 0.0 copy-done.2
  32.7 0.0 copy-done.3
  32.8 0.0 copy-done.4
  32.8 7.9 %shard_map.106 = (f32[4,8,256]{2,1,0:T(8,128)S(1)}, f32[9,24,256]{2,1,0:T(8,128)S(1)}, f32[8,256]{1,0:T(8,128)S(1)}, s32[8,128]{1,0:T(8,128)S(1)}, f32[7,8,256]{2,1,0:T(8,128)S(1)}, /*index=5*/f32[7,8,256]{2,1,0:T(8,128)S(1)}) custom-call(s32[1]{0:T(128)S(6)} %copy.11.count, f32[512,128]{1,0:T(8,128)S(1)} %bitcast.9, s32[128,128]{1,0:T(8,128)S(1)} %bitcast.12, ...), custom_call_target="tpu_custom_call" | custom-call | flops 10000 | bytes 100000 | tf_op jit(solution)/shard_map/pallas_call | solution.py:572
  40.6 0.8 collective-permute-start.7
  41.4 0.3 collective-permute-start.8
  41.7 0.6 collective-permute-done.7.xa
  42.3 3.0 %collective-permute-done.8.xb = f32[7,8,256]{2,1,0:T(8,128)S(1)} collective-permute-done((f32[7,8,256]{2,1,0:T(8,128)S(1)}, f32[7,8,256]{2,1,0:T(8,128)S(1)}, u32[]{:S(2)}, u32[]{:S(2)}) %collective-permute-start.8) | collective-permute-done | bytes 57376 | tf_op jit(solution)/shard_map/ppermute | solution.py:539
  45.3 0.6 collective-permute-start.9
  46.0 1.3 %collective-permute-start.10 = (f32[64,256]{1,0:T(8,128)S(1)}, f32[64,256]{1,0:T(8,128)S(1)}, u32[]{:S(2)}, u32[]{:S(2)}) collective-permute-start(f32[64,256]{1,0:T(8,128)S(1)} %get-tuple-element.38), channel_id=1, source_target_pairs={{0,16},{1,2},{2,1},{3,4},{4,3},{5,6},{6,5},{7,8},{8,7},{9,10},{10,... | collective-permute-start | bytes 196616 | tf_op jit(solution)/shard_map/ppermute | solution.py:539
  47.3 1.3 %collective-permute-done.9.ya = f32[64,256]{1,0:T(8,128)S(1)} collective-permute-done((f32[64,256]{1,0:T(8,128)S(1)}, f32[64,256]{1,0:T(8,128)S(1)}, u32[]{:S(2)}, u32[]{:S(2)}) %collective-permute-start.9) | collective-permute-done | bytes 65568 | tf_op jit(solution)/shard_map/ppermute | solution.py:540
  48.5 0.0 collective-permute-done.10.yb
  48.5 0.0 copy-done.5
  48.5 0.4 shard_map.108
  49.0 17.1 %all_to_all.15 = f32[128,2,128]{2,1,0:T(2,128)S(1)} all-to-all(f32[128,2,128]{2,1,0:T(2,128)S(1)} %bitcast.17), channel_id=1, replica_groups=mesh['coarse'=8,'fine'=16] {'coarse','fine'}, dimensions={0} | all-to-all | bytes 262144 | tf_op jit(solution)/shard_map/all_to_all | solution.py:544
  66.1 3.9 %shard_map.109 = (f32[4,8,256]{2,1,0:T(8,128)S(1)}, f32[8,256]{1,0:T(8,128)S(1)}, f32[8,128]{1,0:T(8,128)S(1)}, f32[8,256]{1,0:T(8,128)S(1)}, f32[8,256]{1,0:T(8,128)S(1)}) custom-call(s32[1]{0:T(128)S(6)} %copy.11.count, f32[256,128]{1,0:T(8,128)S(1)} %bitcast.14, f32[512,128]{1,0:T(8,128)S(1)} %bitcast.10, s32[128,128]{1,0:T(8,128)S(1)} %bitcast.13, ...), custom_call_target="tpu_custom_call" | custom-call | flops 10000 | bytes 100000 | tf_op jit(solution)/shard_map/pallas_call | solution.py:591
  70.0 0.8 collective-permute-start.11
  70.8 0.3 collective-permute-start.12
  71.1 0.6 collective-permute-done.11.xa
  71.6 2.2 %collective-permute-done.12.xb = f32[8,256]{1,0:T(8,128)S(1)} collective-permute-done((f32[8,256]{1,0:T(8,128)S(1)}, f32[8,256]{1,0:T(8,128)S(1)}, u32[]{:S(2)}, u32[]{:S(2)}) %collective-permute-start.12) | collective-permute-done | bytes 8224 | tf_op jit(solution)/shard_map/ppermute | solution.py:539
  73.9 0.0 copy-done.7
  73.9 0.2 shard_map.110
  74.1 14.4 %all_to_all.16 = f32[128,2,128]{2,1,0:T(2,128)S(1)} all-to-all(f32[128,2,128]{2,1,0:T(2,128)S(1)} %bitcast.16), channel_id=1, replica_groups=mesh['coarse'=8,'fine'=16] {'coarse','fine'}, dimensions={0} | all-to-all | bytes 262144 | tf_op jit(solution)/shard_map/all_to_all | solution.py:544
  88.5 0.0 copy-done
  88.5 0.0 copy-done.1
  88.5 1.4 %shard_map.111 = (f32[4,8,256]{2,1,0:T(8,128)}, f32[16,4,8,256]{3,2,1,0:T(8,128)}) custom-call(f32[256,128]{1,0:T(8,128)S(1)} %bitcast.15, f32[4,8,256]{2,1,0:T(8,128)S(1)} %get-tuple-element.53.z1, f32[4,8,256]{2,1,0:T(8,128)S(1)} %get-tuple-element.44.p, f32[16,4,8,256]{3,2,1,0:T(8,128)S(1)} %copy-done, f32[16,4,8,256]{3,2,1,0:T(8,128)S(1)} %copy-done.1), custom_call_target="tpu_custom_call" | custom-call | flops 10000 | bytes 100000 | tf_op jit(solution)/shard_map/pallas_call | solution.py:600
  (8 shorter events, 0.1 us)
Async XLA Ops:
  4.4 18.3 %collective-permute-start.5 = (f32[16,2048]{1,0:T(8,128)}, f32[16,2048]{1,0:T(8,128)S(1)}, u32[]{:S(2)}, u32[]{:S(2)}) collective-permute-start(f32[16,2048]{1,0:T(8,128)} %get-tuple-element.32.tab0), channel_id=1, source_target_pairs={{0,96},{16,112},{32,64},{48,80},{64,32},{80,48},{96,0},{112,16},{1... | collective-permute-start | bytes 393224 | tf_op jit(solution)/shard_map/ppermute | solution.py:567
  7.8 15.0 %collective-permute-start.3 = (f32[16,2048]{1,0:T(8,128)}, f32[16,2048]{1,0:T(8,128)S(1)}, u32[]{:S(2)}, u32[]{:S(2)}) collective-permute-start(f32[16,2048]{1,0:T(8,128)} %get-tuple-element.32.tab0), channel_id=1, source_target_pairs={{0,64},{16,80},{32,96},{48,112},{64,0},{80,16},{96,32},{112,48},{1... | collective-permute-start | bytes 393224 | tf_op jit(solution)/shard_map/ppermute | solution.py:567
  8.3 14.9 %collective-permute-start.1 = (f32[16,2048]{1,0:T(8,128)}, f32[16,2048]{1,0:T(8,128)S(1)}, u32[]{:S(2)}, u32[]{:S(2)}) collective-permute-start(f32[16,2048]{1,0:T(8,128)} %get-tuple-element.32.tab0), channel_id=1, source_target_pairs={{0,32},{16,48},{32,0},{48,16},{64,96},{80,112},{96,64},{112,80},{1... | collective-permute-start | bytes 393224 | tf_op jit(solution)/shard_map/ppermute | solution.py:567
  8.4 0.7 copy-start.8
  9.8 11.6 %copy-start.6 = (f32[16,2048]{1,0:T(8,128)S(1)}, f32[16,2048]{1,0:T(8,128)}, u32[]{:S(2)}) copy-start(f32[16,2048]{1,0:T(8,128)} %get-tuple-element.32.tab0) | copy-start | bytes 393220
  9.8 22.9 %copy-start.2 = (s32[16384]{0:T(1024)S(1)}, s32[16384]{0:T(1024)}, u32[]{:S(2)}) copy-start(s32[16384]{0:T(1024)} %param.14) | copy-start | bytes 196612
  9.8 22.9 %copy-start.3 = (f32[4,8,256]{2,1,0:T(8,128)S(1)}, f32[4,8,256]{2,1,0:T(8,128)}, u32[]{:S(2)}) copy-start(f32[4,8,256]{2,1,0:T(8,128)} %get-tuple-element.30.ic) | copy-start | bytes 98308
  9.8 22.9 %copy-start.4 = (f32[4,8,256]{2,1,0:T(8,128)S(1)}, f32[4,8,256]{2,1,0:T(8,128)}, u32[]{:S(2)}) copy-start(f32[4,8,256]{2,1,0:T(8,128)} %get-tuple-element.29.zs) | copy-start | bytes 98308
  9.8 22.9 %all-to-all-start = ((f32[128,4,128]{2,1,0:T(4,128)}), f32[128,4,128]{2,1,0:T(4,128)S(1)}, u32[]{:S(2)}, u32[]{:S(2)}) async-start(f32[128,4,128]{2,1,0:T(4,128)} %bitcast.3), calls=%async_computation | async-start | bytes 524288 | tf_op jit(solution)/shard_map/all_to_all | solution.py:544
  21.5 2.1 %collective-permute-start = (f32[16,2048]{1,0:T(8,128)S(1)}, f32[16,2048]{1,0:T(8,128)S(1)}, u32[]{:S(2)}, u32[]{:S(2)}) collective-permute-start(f32[16,2048]{1,0:T(8,128)S(1)} %copy-done.6), channel_id=1, source_target_pairs={{0,16},{16,0},{32,48},{48,32},{64,80},{80,64},{96,112},{112,96},{1... | collective-permute-start | bytes 393224 | tf_op jit(solution)/shard_map/ppermute | solution.py:568
  22.6 10.1 %collective-permute-start.6 = (f32[16,2048]{1,0:T(8,128)S(1)}, f32[16,2048]{1,0:T(8,128)S(1)}, u32[]{:S(2)}, u32[]{:S(2)}) collective-permute-start(f32[16,2048]{1,0:T(8,128)S(1)} %collective-permute-done.5.tab6), channel_id=1, source_target_pairs={{0,16},{16,0},{32,48},{48,32},{64,80},{80,64},{96,112},{112,96},{1... | collective-permute-start | bytes 393224 | tf_op jit(solution)/shard_map/ppermute | solution.py:568
  22.7 10.0 %collective-permute-start.4 = (f32[16,2048]{1,0:T(8,128)S(1)}, f32[16,2048]{1,0:T(8,128)S(1)}, u32[]{:S(2)}, u32[]{:S(2)}) collective-permute-start(f32[16,2048]{1,0:T(8,128)S(1)} %collective-permute-done.3.tab4), channel_id=1, source_target_pairs={{0,16},{16,0},{32,48},{48,32},{64,80},{80,64},{96,112},{112,96},{1... | collective-permute-start | bytes 393224 | tf_op jit(solution)/shard_map/ppermute | solution.py:568
  23.2 9.6 %collective-permute-start.2 = (f32[16,2048]{1,0:T(8,128)S(1)}, f32[16,2048]{1,0:T(8,128)S(1)}, u32[]{:S(2)}, u32[]{:S(2)}) collective-permute-start(f32[16,2048]{1,0:T(8,128)S(1)} %collective-permute-done.1.tab2), channel_id=1, source_target_pairs={{0,16},{16,0},{32,48},{48,32},{64,80},{80,64},{96,112},{112,96},{1... | collective-permute-start | bytes 393224 | tf_op jit(solution)/shard_map/ppermute | solution.py:568
  40.6 1.7 %collective-permute-start.7 = (f32[7,8,256]{2,1,0:T(8,128)S(1)}, f32[7,8,256]{2,1,0:T(8,128)S(1)}, u32[]{:S(2)}, u32[]{:S(2)}) collective-permute-start(f32[7,8,256]{2,1,0:T(8,128)S(1)} %get-tuple-element.35), channel_id=1, source_target_pairs={{0,16},{1,17},{2,18},{3,19},{4,20},{5,21},{6,22},{7,23},{8,24},{9,... | collective-permute-start | bytes 172040 | tf_op jit(solution)/shard_map/ppermute | solution.py:540
  41.4 3.9 %collective-permute-start.8 = (f32[7,8,256]{2,1,0:T(8,128)S(1)}, f32[7,8,256]{2,1,0:T(8,128)S(1)}, u32[]{:S(2)}, u32[]{:S(2)}) collective-permute-start(f32[7,8,256]{2,1,0:T(8,128)S(1)} %get-tuple-element.36), channel_id=1, source_target_pairs={{0,112},{1,113},{2,114},{3,115},{4,116},{5,117},{6,118},{7,119},{8... | collective-permute-start | bytes 172040 | tf_op jit(solution)/shard_map/ppermute | solution.py:539
  45.3 3.3 %copy-start.5 = (f32[4,8,256]{2,1,0:T(8,128)S(1)}, f32[4,8,256]{2,1,0:T(8,128)}, u32[]{:S(2)}) copy-start(f32[4,8,256]{2,1,0:T(8,128)} %get-tuple-element.34.c) | copy-start | bytes 98308
  45.3 3.2 %collective-permute-start.9 = (f32[64,256]{1,0:T(8,128)S(1)}, f32[64,256]{1,0:T(8,128)S(1)}, u32[]{:S(2)}, u32[]{:S(2)}) collective-permute-start(f32[64,256]{1,0:T(8,128)S(1)} %get-tuple-element.37), channel_id=1, source_target_pairs={{0,1},{1,0},{2,3},{3,2},{4,5},{5,4},{6,7},{7,6},{8,9},{9,8},{10,11... | collective-permute-start | bytes 196616 | tf_op jit(solution)/shard_map/ppermute | solution.py:540
  46.0 2.6 %collective-permute-start.10 = (f32[64,256]{1,0:T(8,128)S(1)}, f32[64,256]{1,0:T(8,128)S(1)}, u32[]{:S(2)}, u32[]{:S(2)}) collective-permute-start(f32[64,256]{1,0:T(8,128)S(1)} %get-tuple-element.38), channel_id=1, source_target_pairs={{0,16},{1,2},{2,1},{3,4},{4,3},{5,6},{6,5},{7,8},{8,7},{9,10},{10,... | collective-permute-start | bytes 196616 | tf_op jit(solution)/shard_map/ppermute | solution.py:539
  66.1 7.8 %copy-start.7 = (f32[4,8,256]{2,1,0:T(8,128)S(1)}, f32[4,8,256]{2,1,0:T(8,128)}, u32[]{:S(2)}) copy-start(f32[4,8,256]{2,1,0:T(8,128)} %get-tuple-element.28.s) | copy-start | bytes 98308
  66.1 22.4 %copy-start = (f32[16,4,8,256]{3,2,1,0:T(8,128)S(1)}, f32[16,4,8,256]{3,2,1,0:T(8,128)}, u32[]{:S(2)}) copy-start(f32[16,4,8,256]{3,2,1,0:T(8,128)} %s_old.1) | copy-start | bytes 1572868
  66.1 22.4 %copy-start.1 = (f32[16,4,8,256]{3,2,1,0:T(8,128)S(1)}, f32[16,4,8,256]{3,2,1,0:T(8,128)}, u32[]{:S(2)}) copy-start(f32[16,4,8,256]{3,2,1,0:T(8,128)} %rate.1) | copy-start | bytes 1572868
  70.0 1.6 %collective-permute-start.11 = (f32[8,256]{1,0:T(8,128)S(1)}, f32[8,256]{1,0:T(8,128)S(1)}, u32[]{:S(2)}, u32[]{:S(2)}) collective-permute-start(f32[8,256]{1,0:T(8,128)S(1)} %get-tuple-element.45), channel_id=1, source_target_pairs={{0,16},{1,17},{2,18},{3,19},{4,20},{5,21},{6,22},{7,23},{8,24},{9,... | collective-permute-start | bytes 24584 | tf_op jit(solution)/shard_map/ppermute | solution.py:540
  70.8 3.1 %collective-permute-start.12 = (f32[8,256]{1,0:T(8,128)S(1)}, f32[8,256]{1,0:T(8,128)S(1)}, u32[]{:S(2)}, u32[]{:S(2)}) collective-permute-start(f32[8,256]{1,0:T(8,128)S(1)} %get-tuple-element.46), channel_id=1, source_target_pairs={{0,112},{1,113},{2,114},{3,115},{4,116},{5,117},{6,118},{7,119},{8... | collective-permute-start | bytes 24584 | tf_op jit(solution)/shard_map/ppermute | solution.py:539

commit v4 on v3

--- a/solution.py
+++ b/solution.py
@@ -15,6 +15,7 @@
 SHARDS = 8
 SHARD_ROWS = 2048
 FLOW = 50.0
+TABLE_ROWS = 128
 UNUSED = 1e30
 F32, BF16, I32 = jnp.float32, jnp.bfloat16, jnp.int32
 VM = pl.BlockSpec(memory_space=pltpu.VMEM)
@@ -52,20 +53,43 @@
     return ((row * LANES + iota((CY, LANES), 1)) * count) >> 13
 
 
+def restrict_plane(values, plane, count, total, base):
+    slot = iota(total.shape, 1) + base
+    for half in range(2):
+        part_of = values[:, half * LANES : (half + 1) * LANES]
+        row = (plane * CY + iota((CY, 1), 0)) * 2 + half
+        first = (row * count) >> 6
+        member = slots_of(plane, half, count) - first
+        relative = slot - first
+        for k in range(5):
+            part = jnp.sum(jnp.where(member == k, part_of, 0.0), axis=1, keepdims=True)
+            total = total + jnp.where(relative == k, part, 0.0)
+    return total
+
+
 def restrict(cells, count):
-    slot = iota((CY, SLOTS), 1)
     total = jnp.zeros((CY, SLOTS), F32)
     for plane in range(CX):
-        for half in range(2):
-            values = cells[plane][:, half * LANES : (half + 1) * LANES]
-            row = (plane * CY + iota((CY, 1), 0)) * 2 + half
-            first = (row * count) >> 6
-            member = slots_of(plane, half, count) - first
-            relative = slot - first
-            for k in range(5):
-                part = jnp.sum(jnp.where(member == k, values, 0.0), axis=1, keepdims=True)
-                total = total + jnp.where(relative == k, part, 0.0)
+        total = restrict_plane(cells[plane], plane, count, total, 0)
     return jnp.sum(total, axis=0, keepdims=True)
+
+
+def rim_restrict(rim, count):
+    n = jnp.concatenate([count, count], axis=1)
+    row = iota((CY, CZ), 0)
+    cells = ((row & 3) * CY + jnp.where(row < 4, CY - 1, 0)) * CZ
+    member = (((cells + iota((CY, CZ), 1)) * n) >> 13) - ((cells * n) >> 13)
+    lane = iota((8, LANES), 1)
+    start = iota((8, LANES), 0) * 16
+    spread = jnp.zeros((8, LANES), F32)
+    for k in range(9):
+        part = jnp.sum(jnp.where(member == k, rim, 0.0), axis=1, keepdims=True)
+        spread = spread + jnp.where(lane == start + k, part, 0.0)
+    return jnp.sum(spread, axis=0, keepdims=True)
+
+
+def rim_exists(index):
+    return jnp.where(iota((CY, CZ), 0) < 4, index, 15 - index) > 0
 
 
 def prolong(entries, count):
@@ -91,12 +115,9 @@
 
 
 def source_kernel(
-    cap, count, c_old, s_old_hbm, rate_hbm, diag, diag_row, order, cols, off,
-    c_out, ic_out, s_out, zs_out, tile_out, tab, s_old, rate, sems,
+    cap, c_old, s_old_hbm, rate_hbm, diag, cols, off,
+    c_out, ic_out, s_out, zs_out, tab, both, xb, ya, yb, s_old, rate, sems,
 ):
-    place = places()
-    me = place[0] * 16 + place[1]
-    n = count[0]
     copies = []
     for x in range(CX):
         pair = (
@@ -106,13 +127,12 @@
         for copy in pair:
             copy.start()
         copies.append(pair)
-    tab[0:8, :] = cols[...].astype(F32)
-    tab[8:16, :] = off[...] * (0.8 / diag_row[...])
-    mine = (order[0:1, :] >> 7) == me
-    low = jnp.sum(jnp.where(mine, (order[...] & 127).astype(F32), 0.0), axis=1, keepdims=True)
-    spot = iota((LANES, LANES), 1).astype(F32) == low
-    inverse = jnp.sum(jnp.where(spot, iota((LANES, LANES), 0).astype(F32), 0.0), axis=0, keepdims=True)
-    planes = []
+    for j in range(SHARD_ROWS // 256):
+        at = slice(256 * j, 256 * j + 256)
+        part = jnp.concatenate([cols[:, at].astype(F32), off[:, at] * (0.8 / diag[:, at])], axis=0)
+        tab[16 * j : 16 * j + 16, :] = part
+        both[16 * j : 16 * j + 16, :] = part
+    smooth, inverse = [], []
     for x in range(CX):
         for copy in copies[x]:
             copy.wait()
@@ -130,19 +150,45 @@
         ic_out[x] = inv
         s_out[x] = source
         zs_out[x] = 0.8 * source * inv
-        planes.append(source)
-    sums = jnp.where(iota((1, SLOTS), 1) < n, restrict(planes, n), UNUSED)
+        smooth.append(0.8 * source * inv)
+        inverse.append(inv)
+    xa, xb[...] = send_planes([(smooth, 3), (inverse, 2)])
+    both[TABLE_ROWS:, :] = xa
+    ya[...], yb[...] = send_rims(smooth)
+
+
+def send_planes(fields):
+    even = (places()[0] & 1) == 0
+    upper = jnp.concatenate([p for planes, depth in fields for p in planes[CX - depth :]], axis=0)
+    lower = jnp.concatenate([p for planes, depth in fields for p in planes[:depth]], axis=0)
+    return jnp.where(even, upper, lower), jnp.where(even, lower, upper)
+
+
+def send_rims(planes):
+    even = (places()[1] & 1) == 0
+    upper = jnp.concatenate([p[CY - 1 : CY] for p in planes] * 2, axis=0)
+    lower = jnp.concatenate([p[0:1] for p in planes] * 2, axis=0)
+    return jnp.where(even, upper, lower), jnp.where(even, lower, upper)
+
+
+def sums_kernel(count, s, diag, order, pay):
+    place = places()
+    n = count[0]
+    mine = (order[0:1, :] >> 7) == place[0] * 16 + place[1]
+    low = jnp.sum(jnp.where(mine, (order[...] & 127).astype(F32), 0.0), axis=1, keepdims=True)
+    spot = iota((LANES, LANES), 1).astype(F32) == low
+    inverse = jnp.sum(jnp.where(spot, iota((LANES, LANES), 0).astype(F32), 0.0), axis=0, keepdims=True)
+    sums = jnp.where(iota((1, SLOTS), 1) < n, restrict([s[x] for x in range(CX)], n), UNUSED)
+    repeat4(pay, [sums[:, :LANES], sums[:, LANES:], diag[pl.ds(place[1], 1), :], inverse])
+
+
+def repeat4(pay, rows):
     kind = iota((8, LANES), 0) & 3
-    rows = [sums[:, :LANES], sums[:, LANES:], diag[pl.ds(place[1], 1), :], inverse]
     tile = jnp.broadcast_to(rows[3], (8, LANES))
     for k in range(3):
         tile = jnp.where(kind == k, rows[k], tile)
-    tile_out[...] = tile
-
-
-def repeat_kernel(tile, pay):
     for i in range(DEVICES // 2):
-        pay[pl.ds(8 * i, 8), :] = tile[...]
+        pay[pl.ds(8 * i, 8), :] = tile
 
 
 def read_sums(gathered):
@@ -229,35 +275,40 @@
 
 
 def first_kernel(
-    count, gathered, order, tab0, tab1, tab2, tab3, tab4, tab5, tab6, tab7, zs, ic,
-    pe_out, plan, own, beside, xa, xb, table,
+    count, gathered, order, tab0, tab1, tab2, tab3, tab4, tab5, tab6, tab7,
+    pe_out, plan, own, beside, across, at_row, at_lane, counts_out, xa, xb, table,
 ):
     place = places()
     n = count[0]
     me = place[0] * 16 + place[1]
     low, high, diag, inverse, used = read_sums(gathered)
     offsets = offsets_of(used)
+    at_row[...] = offsets[0]
+    at_lane[...] = jnp.broadcast_to(offsets[1], (8, LANES))
     sums = assemble(
         jnp.where(low < 0.5 * UNUSED, low, 0.0), jnp.where(high < 0.5 * UNUSED, high, 0.0),
         offsets, inverse, blocks_of(order),
     )
     values = 0.8 * sums / diag
     counts = nn(used, jnp.ones((LANES, LANES), BF16))
-    wanted = me + jnp.where(iota((8, LANES), 0) < 4, -1, 1)
+    counts_out[...] = counts.astype(I32)
     row = iota((LANES, LANES), 0)
-    before = jnp.sum(jnp.where(row == me - 1, counts, 0.0), axis=0, keepdims=True)
-    after = jnp.sum(jnp.where(row == me + 1, counts, 0.0), axis=0, keepdims=True)
-    beside[...] = jnp.where(wanted < me, before, after).astype(I32)
+    before = iota((8, LANES), 0) < 4
+    for out, step in ((beside, 1), (across, 16)):
+        sides = [jnp.sum(jnp.where(row == me + d, counts, 0.0), axis=0, keepdims=True) for d in (-step, step)]
+        out[...] = jnp.where(before, sides[0], sides[1]).astype(I32)
 
     tabs = (tab0, tab1, tab2, tab3, tab4, tab5, tab6, tab7)
     for g in range(SHARDS):
-        cols = tabs[g][0:8, :]
-        high = jnp.floor(cols * (1.0 / 128.0))
-        pair = jnp.concatenate([high, cols - 128.0 * high], axis=0)
-        table[32 * g : 32 * g + 16, :] = pair.astype(BF16)
-        off = tabs[g][8:16, :]
-        big = off.astype(BF16).astype(F32)
-        table[32 * g + 16 : 32 * g + 32, :] = jnp.concatenate([big, off - big], axis=0).astype(BF16)
+        for j in range(SHARD_ROWS // 256):
+            at = slice(256 * j, 256 * j + 256)
+            cols = tabs[g][16 * j : 16 * j + 8, :]
+            big = jnp.floor(cols * (1.0 / 128.0))
+            pair = jnp.concatenate([big, cols - 128.0 * big], axis=0)
+            table[32 * g : 32 * g + 16, at] = pair.astype(BF16)
+            off = tabs[g][16 * j + 8 : 16 * j + 16, :]
+            big = off.astype(BF16).astype(F32)
+            table[32 * g + 16 : 32 * g + 32, at] = jnp.concatenate([big, off - big], axis=0).astype(BF16)
 
     mine = jnp.sum(jnp.where(row == me, offsets[0].astype(F32), 0.0), axis=0, keepdims=True).astype(I32)
     numbers = order[...].astype(F32)
@@ -287,24 +338,7 @@
     for x in range(CX):
         pe_out[x] = pe[x]
 
-    def message(out, upper):
-        for k in range(3):
-            out[k] = zs[CX - 3 + k] if upper else zs[k]
-        for k in range(2):
-            out[3 + k] = ic[CX - 2 + k] if upper else ic[k]
-            out[5 + k] = pe[CX - 2 + k] if upper else pe[k]
-
-    even = (place[0] & 1) == 0
-
-    @pl.when(even)
-    def _():
-        message(xa, True)
-        message(xb, False)
-
-    @pl.when(jnp.logical_not(even))
-    def _():
-        message(xa, False)
-        message(xb, True)
+    xa[...], xb[...] = send_planes([(pe, 2)])
 
 
 def below_above(index, count, a, b):
@@ -312,6 +346,8 @@
     inner = jnp.logical_and(index > 0, index < count - 1)
 
     def near(i):
+        if i is not ...:
+            i = slice(CY * i, CY * i + CY)
         return a[i], jnp.where(inner, b[i], 0.0)
 
     def below(i):
@@ -329,27 +365,47 @@
     return max(0, (4, 3, 3)[field] - max(0, -x, x - CX + 1))
 
 
-PACKED = [(f, x, k) for f in range(3) for x in range(-3, CX + 3) for k in range(ghost_rows(f, x))]
-
-
-def wide_plane(own, below, above):
-    depth = (3, 2, 2)
-    base = (0, 3, 5)
-
+def packed(fields):
+    return [(f, x, k) for f in fields for x in range(-3, CX + 3) for k in range(ghost_rows(f, x))]
+
+
+PACKED = packed((0, 1, 2))
+
+
+def with_ghosts(own, messages):
     def plane(field, x):
-        if x < 0:
-            return below(base[field] + depth[field] + x)
-        if x >= CX:
-            return above(base[field] + x - CX)
-        return own[field][x]
+        if 0 <= x < CX:
+            return own[field][x]
+        below, above, base, depth = messages[field]
+        return below(base + depth + x) if x < 0 else above(base + x - CX)
 
     return plane
 
 
-def widen_kernel(zs, ic, pe, xa, xb, ya, yb):
-    place = places()
-    plane = wide_plane((zs, ic, pe), *below_above(place[0], 8, xa, xb))
-    even = (place[1] & 1) == 0
+def widen(plane, fields, ya, yb):
+    even = (places()[1] & 1) == 0
+    upper, lower = [], []
+    for f in fields:
+        for x in range(-3, CX + 3):
+            d = ghost_rows(f, x)
+            if d:
+                here = plane(f, x)
+                upper.append(here[CY - d :])
+                lower.append(here[:d])
+    upper, lower = jnp.concatenate(upper, axis=0), jnp.concatenate(lower, axis=0)
+    ya[...] = jnp.where(even, upper, lower)
+    yb[...] = jnp.where(even, lower, upper)
+
+
+def all_ghosts(own, x0a, x0b, x1a, x1b):
+    early = below_above(places()[0], 8, x0a.at[TABLE_ROWS:], x0b)
+    late = below_above(places()[0], 8, x1a, x1b)
+    return with_ghosts(own, ((*early, 0, 3), (*early, 3, 2), (*late, 0, 2)))
+
+
+def widen_kernel(zs, ic, pe, x0a, x0b, x1a, x1b, ya, yb):
+    plane = all_ghosts((zs, ic, pe), x0a, x0b, x1a, x1b)
+    even = (places()[1] & 1) == 0
     upper, lower = [], []
     for f in range(3):
         for x in range(-3, CX + 3):
@@ -363,11 +419,95 @@
     yb[...] = jnp.where(even, lower, upper)
 
 
-def second_kernel(
-    count, zs, ic, pe, c, xa, xb, ya, yb, z1_out, w1_out, sw_out, sw_ghost, s_ghost, w_ghost, pay
+def early_kernel(count, beside, across, zs, ic, pe, c, xa, xb, ya, yb, pay):
+    place = places()
+    n = count[0]
+    below, above = below_above(place[0], 8, xa.at[TABLE_ROWS:], xb)
+    near, far = [side(...) for side in below_above(place[1], 16, ya, yb)]
+    row = iota((CY, CZ), 0)
+    z1 = []
+    for x in range(CX):
+        mid = zs[x]
+        left = zs[x - 1] if x else below(2)
+        right = zs[x + 1] if x + 1 < CX else above(0)
+        up = jnp.where(row == 0, near[x : x + 1], pltpu.roll(mid, 1, 0))
+        down = jnp.where(row == CY - 1, far[x : x + 1], pltpu.roll(mid, CY - 1, 0))
+        z1.append(1.2 * mid + 0.8 * ic[x] * couple(left, mid, right, up, down) + pe[x])
+    image = []
+    zero = jnp.zeros((CY, CZ), F32)
+    for x in range(CX):
+        mid = z1[x]
+        up = jnp.where(row == 0, 0.0, pltpu.roll(mid, 1, 0))
+        down = jnp.where(row == CY - 1, 0.0, pltpu.roll(mid, CY - 1, 0))
+        left = z1[x - 1] if x else zero
+        right = z1[x + 1] if x + 1 < CX else zero
+        image.append(c[x] * mid - couple(left, mid, right, up, down))
+    sums = restrict(image, n)
+    blank = jnp.zeros((CY, LANES), F32)
+    lane = iota((1, LANES), 1)
+    under, over = across[0:1, 0:1], across[4:5, 0:1]
+    down_x = restrict_plane(-8.0 * z1[0], CX - 1, under, blank, (3 * under) >> 2)
+    up_x = restrict_plane(-8.0 * z1[CX - 1], 0, over, blank, 0)
+    down_x = jnp.where(place[0] > 0, jnp.sum(down_x, axis=0, keepdims=True), 0.0)
+    up_x = jnp.where(place[0] < 7, jnp.sum(up_x, axis=0, keepdims=True), 0.0)
+    along_x = jnp.where(lane < 64, down_x, pltpu.roll(jnp.broadcast_to(up_x, (8, LANES)), 64, 1)[0:1])
+    rims = jnp.concatenate([z[0:1] for z in z1] + [z[CY - 1 : CY] for z in z1], axis=0)
+    along_y = rim_restrict(jnp.where(rim_exists(place[1]), -8.0 * rims, 0.0), beside[...])
+    repeat4(pay, [sums[:, :LANES], sums[:, LANES:], along_x, along_y])
+
+
+def add_neighbours(low, high, from_x, from_y, counts):
+    lane = iota((DEVICES, LANES), 1)
+
+    def place(window, base, shift, length):
+        nonlocal low, high
+        relative = lane - base
+        moved = lane_take(window, (relative + shift) & 127)
+        low = low + jnp.where(jnp.logical_and(relative >= 0, relative < length), moved, 0.0)
+        relative = relative + LANES
+        high = high + jnp.where(jnp.logical_and(relative >= 0, relative < length), moved, 0.0)
+
+    low = low + jnp.where(lane < 64, pltpu.roll(pltpu.roll(from_x, 16, 0), 64, 1), 0.0)
+    place(pltpu.roll(from_x, DEVICES - 16, 0), (3 * counts) >> 2, 0, 64)
+    both = jnp.where(lane < 64, pltpu.roll(from_y, DEVICES - 1, 0), pltpu.roll(from_y, 1, 0))
+    for g in range(2 * CX):
+        cells = ((g & 3) * CY + (CY - 1 if g < CX else 0)) * CZ
+        place(both, (cells * counts) >> 13, 16 * g, 9)
+    return low, high
+
+
+def second_solve_kernel(
+    count, sums, gathered, order, plan, own, at_row, at_lane, counts, pe_out, pe_face, e_face
+):
+    n = count[0]
+    low, high = add_neighbours(
+        sums[pl.ds(0, DEVICES, stride=4), :], sums[pl.ds(1, DEVICES, stride=4), :],
+        sums[pl.ds(2, DEVICES, stride=4), :], sums[pl.ds(3, DEVICES, stride=4), :], counts[...],
+    )
+    diag = gathered[pl.ds(2, DEVICES, stride=4), :]
+    inverse = gathered[pl.ds(3, DEVICES, stride=4), :].astype(I32)
+    values = assemble(low, high, (at_row[...], at_lane[0:1, :]), inverse, blocks_of(order))
+    entries = coarse_solve(0.8 * values / diag, plan, own)
+    pe = prolong(entries, n)
+    for x in range(CX):
+        pe_out[x] = pe[x]
+        pe_face[x : x + 1, :] = pe[x][0:1]
+        pe_face[CX + x : CX + x + 1, :] = pe[x][CY - 1 : CY]
+    lane = iota((8, LANES), 1)
+    group = lane >> 4
+    cells = ((group & 3) * CY + jnp.where(group < 4, 0, CY - 1)) * CZ
+    slot = jnp.minimum(((cells * n) >> 13) + (lane & 15), SLOTS - 1)
+    low = jnp.broadcast_to(entries[:, :LANES], (8, LANES))
+    high = jnp.broadcast_to(entries[:, LANES:], (8, LANES))
+    e_face[...] = jnp.where(slot < LANES, lane_take(low, slot & 127), lane_take(high, slot & 127))
+
+
+def direction_kernel(
+    zs, ic, pe, c, x0a, x0b, x1a, x1b, ya, yb, pe2,
+    z1_out, w1_out, p_out, sw_ghost, s_ghost, w_ghost, xa, xb,
 ):
     place = places()
-    middle = wide_plane((zs, ic, pe), *below_above(place[0], 8, xa, xb))
+    middle = all_ghosts((zs, ic, pe), x0a, x0b, x1a, x1b)
     near, far = [side(...) for side in below_above(place[1], 16, ya, yb)]
 
     def plane(field, x):
@@ -385,8 +525,8 @@
 
     def neighbours(get, x):
         mid = get(x)
-        rows = mid.shape[0]
-        return couple(get(x - 1), mid, get(x + 1), pltpu.roll(mid, 1, 0), pltpu.roll(mid, rows - 1, 0))
+        count = mid.shape[0]
+        return couple(get(x - 1), mid, get(x + 1), pltpu.roll(mid, 1, 0), pltpu.roll(mid, count - 1, 0))
 
     z = {x: plane(0, x) for x in range(-3, CX + 3)}
     inv = {x: plane(1, x) for x in range(-2, CX + 2)}
@@ -394,56 +534,26 @@
     for x in range(-2, CX + 2):
         first[x] = 1.2 * z[x] + 0.8 * inv[x] * neighbours(z.get, x) + plane(2, x)
     zw = {}
-    image = []
     for x in range(-1, CX + 1):
         beside = neighbours(first.get, x)
         zw[x] = 0.8 * (first[x] - inv[x] * beside)
         if 0 <= x < CX:
-            here = c[x] * first[x][8:16] - beside[8:16]
-            image.append(here)
             z1_out[x] = first[x][8:16]
-            w1_out[x] = here
+            w1_out[x] = c[x] * first[x][8:16] - beside[8:16]
+    p = []
     for x in range(CX):
         smooth = 1.2 * zw[x] + 0.8 * inv[x] * neighbours(zw.get, x)
-        sw_out[x] = smooth[8:16]
+        p.append(smooth[8:16] + pe2[x])
+        p_out[x] = p[x]
         for at, row in ((x, 7), (CX + x, 16)):
             iv = inv[x][row : row + 1]
             scale = jnp.where(iv > 0.0, 1.25 / jnp.where(iv > 0.0, iv, 1.0), 0.0)
             sw_ghost[at : at + 1, :] = smooth[row : row + 1]
             s_ghost[at : at + 1, :] = z[x][row : row + 1] * scale
             w_ghost[at : at + 1, :] = zw[x][row : row + 1] * scale
-    sums = restrict(image, count[0])
-    kind = iota((8, LANES), 0) & 1
-    tile = jnp.where(kind == 0, sums[:, :LANES], sums[:, LANES:])
-    for i in range(DEVICES // 4):
-        pay[pl.ds(8 * i, 8), :] = tile
-
-
-def third_kernel(count, sums, gathered, order, plan, own, sw, p_out, pe_face, e_face, xa, xb):
-    place = places()
-    n = count[0]
-    _, _, diag, inverse, used = read_sums(gathered)
-    values = assemble(
-        sums[pl.ds(0, DEVICES, stride=2), :], sums[pl.ds(1, DEVICES, stride=2), :],
-        offsets_of(used), inverse, blocks_of(order),
-    )
-    entries = coarse_solve(0.8 * values / diag, plan, own)
-    pe = prolong(entries, n)
-    p = [sw[x] + pe[x] for x in range(CX)]
-    for x in range(CX):
-        p_out[x] = p[x]
-        pe_face[x : x + 1, :] = pe[x][0:1]
-        pe_face[CX + x : CX + x + 1, :] = pe[x][CY - 1 : CY]
     even = (place[0] & 1) == 0
     xa[...] = jnp.where(even, p[CX - 1], p[0])
     xb[...] = jnp.where(even, p[0], p[CX - 1])
-    lane = iota((8, LANES), 1)
-    group = lane >> 4
-    cells = ((group & 3) * CY + jnp.where(group < 4, 0, CY - 1)) * CZ
-    slot = jnp.minimum(((cells * n) >> 13) + (lane & 15), SLOTS - 1)
-    low = jnp.broadcast_to(entries[:, :LANES], (8, LANES))
-    high = jnp.broadcast_to(entries[:, LANES:], (8, LANES))
-    e_face[...] = jnp.where(slot < LANES, lane_take(low, slot & 127), lane_take(high, slot & 127))
 
 
 def products_kernel(s, w1, p, c, xa, xb, sw_ghost, s_ghost, w_ghost, pe_face, e_face, beside, pay):
@@ -463,22 +573,14 @@
         a, b = s[x], w1[x]
         for k, term in enumerate((a * a, a * b, a * q, b * b, b * q, q * q)):
             sums[k] = sums[k] + term
-    exists = jnp.where(row < 4, place[1], 15 - place[1]) > 0
+    exists = rim_exists(place[1])
     face = pe_face[...]
     sums[2] = sums[2] - 8.0 * face * s_ghost[...]
     sums[4] = sums[4] - 8.0 * face * w_ghost[...]
     sums[5] = sums[5] + jnp.where(exists, 64.0 * face * face, 0.0)
     rim = jnp.where(exists, jnp.concatenate(rims, axis=0), 0.0)
-    n = jnp.concatenate([beside[...], beside[...]], axis=1)
-    cells = ((row & 3) * CY + jnp.where(row < 4, CY - 1, 0)) * CZ
-    member = (((cells + iota((CY, CZ), 1)) * n) >> 13) - ((cells * n) >> 13)
     lane = iota((8, LANES), 1)
-    start = iota((8, LANES), 0) * 16
-    spread = jnp.zeros((8, LANES), F32)
-    for k in range(9):
-        part = jnp.sum(jnp.where(member == k, rim, 0.0), axis=1, keepdims=True)
-        spread = spread + jnp.where(lane == start + k, part, 0.0)
-    top = jnp.broadcast_to(jnp.sum(spread, axis=0, keepdims=True), (8, LANES))
+    top = jnp.broadcast_to(rim_restrict(rim, beside[...]), (8, LANES))
     for k in range(6):
         top = top + jnp.where(lane == 9 + k, jnp.sum(sums[k], keepdims=True), 0.0)
     tile = jnp.where((iota((8, LANES), 0) & 1) == 0, top, e_face[...])
@@ -520,9 +622,10 @@
 
 
 FIELD = ((CX, CY, CZ), F32)
-
-
-def trade(a, b, axis):
+SOURCE_VMEM = 63 << 20
+
+
+def swap_pairs(axis):
     n, m = lax.axis_size("coarse"), lax.axis_size("fine")
     inside, between = [], []
     for c in range(n):
@@ -536,8 +639,16 @@
                 between.append((me, (c ^ 1) * m + f))
             else:
                 between.append((me, (n - 1 - c) * m + f))
-    b = lax.ppermute(b, BOTH, between)
-    return lax.ppermute(a, BOTH, inside), b
+    return inside, between
+
+
+def swap_between(b, axis):
+    return lax.ppermute(b, BOTH, swap_pairs(axis)[1])
+
+
+def trade(a, b, axis):
+    b = swap_between(b, axis)
+    return lax.ppermute(a, BOTH, swap_pairs(axis)[0]), b
 
 
 def everyone(pay, rows):
@@ -549,49 +660,57 @@
     c_old, s_old, rate_time, capacity, agg_count, coarse_order, coarse_cols, coarse_off, coarse_diag
 ):
     order = coarse_order.reshape(LANES, LANES)
-    c, ic, s, zs, tile, tab = call(
-        source_kernel, [SM, SM, VM, HB, HB] + [VM] * 5,
-        [FIELD, FIELD, FIELD, FIELD, ((8, LANES), F32), ((16, SHARD_ROWS), F32)],
+    c, ic, s, zs, tab, both, x0b, y0a, y0b = call(
+        source_kernel, [SM, VM, HB, HB] + [VM] * 3,
+        [
+            FIELD, FIELD, FIELD, FIELD, ((TABLE_ROWS, 256), F32), ((TABLE_ROWS + 40, 256), F32),
+            ((40, CZ), F32), ((CY, CZ), F32), ((CY, CZ), F32),
+        ],
         scratch=[
             pltpu.VMEM((RATES, CX, CY, CZ), F32),
             pltpu.VMEM((RATES, CX, CY, CZ), F32),
             pltpu.SemaphoreType.DMA((2, CX)),
         ],
-        vmem=63 << 20,
+        vmem=SOURCE_VMEM,
     )(
-        capacity, agg_count, c_old, s_old, rate_time, coarse_diag.reshape(16, LANES),
-        coarse_diag.reshape(1, SHARD_ROWS), order, coarse_cols, coarse_off,
+        capacity, c_old, s_old, rate_time, coarse_diag.reshape(1, SHARD_ROWS), coarse_cols, coarse_off,
     )
-    tabs = []
-    for hop in (0, 2, 4, 6):
-        shard = lax.ppermute(tab, "coarse", [(i, i ^ hop) for i in range(8)]) if hop else tab
-        tabs += [shard, lax.ppermute(shard, "coarse", [(i, i ^ 1) for i in range(8)])]
-    (pay,) = call(repeat_kernel, [VM], [((4 * DEVICES, LANES), F32)])(tile)
+    other_core = [(i, i ^ 1) for i in range(8)]
+    both = lax.ppermute(both, "coarse", other_core)
+    tabs = [tab, both]
+    for hop in (2, 4, 6):
+        shard = lax.ppermute(tab, "coarse", [(i, i ^ hop) for i in range(8)])
+        tabs += [shard, lax.ppermute(shard, "coarse", other_core)]
+    x0b = swap_between(x0b, "coarse")
+    y0a, y0b = trade(y0a, y0b, "fine")
+    (pay,) = call(sums_kernel, [SM] + [VM] * 3, [((4 * DEVICES, LANES), F32)])(
+        agg_count, s, coarse_diag.reshape(16, LANES), order
+    )
     gathered = everyone(pay, 4)
 
-    pe, plan, own, beside, xa, xb = call(
-        first_kernel, [SM] + [VM] * 12,
+    pe, plan, own, beside, across, at_row, at_lane, counts, x1a, x1b = call(
+        first_kernel, [SM] + [VM] * 10,
         [
-            FIELD, ((KC + 1, 24, SLOTS), F32), ((8, SLOTS), F32), ((8, LANES), I32),
-            ((7, CY, CZ), F32), ((7, CY, CZ), F32),
+            FIELD, ((KC + 1, 24, SLOTS), F32), ((8, SLOTS), F32), ((8, LANES), I32), ((8, LANES), I32),
+            ((LANES, LANES), I32), ((8, LANES), I32), ((LANES, LANES), I32),
+            ((2 * CY, CZ), F32), ((2 * CY, CZ), F32),
         ],
         scratch=[pltpu.VMEM((SHARDS * 32, SHARD_ROWS), BF16)],
-    )(agg_count, gathered, order, *tabs, zs, ic)
-    xa, xb = trade(xa, xb, "coarse")
-    ya, yb = call(
-        widen_kernel, [VM] * 5, [((len(PACKED), CZ), F32)] * 2
-    )(zs, ic, pe, xa, xb)
+    )(agg_count, gathered, order, *tabs)
+    x1a, x1b = trade(x1a, x1b, "coarse")
+    (pay,) = call(early_kernel, [SM] + [VM] * 10, [((4 * DEVICES, LANES), F32)])(
+        agg_count, beside, across, zs, ic, pe, c, both, x0b, y0a, y0b
+    )
+    sums = everyone(pay, 4)
+    ya, yb = call(widen_kernel, [VM] * 7, [((len(PACKED), CZ), F32)] * 2)(zs, ic, pe, both, x0b, x1a, x1b)
     ya, yb = trade(ya, yb, "fine")
-    z1, w1, sw, sw_ghost, s_ghost, w_ghost, pay = call(
-        second_kernel, [SM] + [VM] * 8,
-        [FIELD, FIELD, FIELD] + [((CY, CZ), F32)] * 3 + [((2 * DEVICES, LANES), F32)],
-    )(agg_count, zs, ic, pe, c, xa, xb, ya, yb)
-    sums = everyone(pay, 2)
-
-    p, pe_face, e_face, xa, xb = call(
-        third_kernel, [SM] + [VM] * 6,
-        [FIELD, ((CY, CZ), F32), ((8, LANES), F32), ((CY, CZ), F32), ((CY, CZ), F32)],
-    )(agg_count, sums, gathered, order, plan, own, sw)
+
+    pe2, pe_face, e_face = call(
+        second_solve_kernel, [SM] + [VM] * 8, [FIELD, ((CY, CZ), F32), ((8, LANES), F32)], flops=100_000_000
+    )(agg_count, sums, gathered, order, plan, own, at_row, at_lane, counts)
+    z1, w1, p, sw_ghost, s_ghost, w_ghost, xa, xb = call(
+        direction_kernel, [VM] * 11, [FIELD, FIELD, FIELD] + [((CY, CZ), F32)] * 5,
+    )(zs, ic, pe, c, both, x0b, x1a, x1b, ya, yb, pe2)
     xa, xb = trade(xa, xb, "coarse")
     (pay,) = call(
         products_kernel, [VM] * 12, [((2 * DEVICES, LANES), F32)]

time: 90.3 us -> 84.2 us (0.932)
  blocking collectives: 31.5 us -> 16 us
  starting transfers between devices: 21.5 us -> 31.2 us
  waiting for transfers between devices: 17.1 us -> 15.2 us
  Pallas kernels: 17.7 us -> 19.1 us
    all_to_all x2 -> x1, blocking collectives: 31.5 us -> 16 us  [everyone(): moved = lax.all_to_all(pay.reshape(DEVICES, rows, LANES), BOTH, 0, 0)]
    ppermute x13 -> x16, starting transfers between devices: 9.87 us -> 15.4 us  [the longest x5 4.81 us: swap_between(): return lax.ppermute(b, BOTH, swap_pairs(axis)[1])]
    all_to_all x1 -> x2, starting transfers between devices: 11.6 us -> 15.8 us  [everyone(): moved = lax.all_to_all(pay.reshape(DEVICES, rows, LANES), BOTH, 0, 0)]
    ppermute x13 -> x16, waiting for transfers between devices: 8.05 us -> 6.07 us  [the longest x5 5.16 us: swap_between(): return lax.ppermute(b, BOTH, swap_pairs(axis)[1])]
    pallas_call x6 -> x7, Pallas kernels: 16 us -> 17.5 us  [the longest x1 7.87 us: local(): call(first_kernel, [SM] + [VM] * 10, [FIELD, ((KC + 1, 24, SLOTS), F32),...]
    all_to_all x1 -> x2, waiting for transfers between devices: 9.1 us -> 9.12 us  [everyone(): moved = lax.all_to_all(pay.reshape(DEVICES, rows, LANES), BOTH, 0, 0)]
  transfers between devices with their start and end apart: 14 -> 18, of which waited for: 7 -> 6; matrix products, arithmetic and copies ran while one was open for 0% -> 0% of each run, Pallas kernels for 1% -> 15%
where the time goes in v4:
time: 84.2 us; the launch traced here: 83.8 us
  starting transfers between devices  31.2 us (37%)
  Pallas kernels  19.1 us (23%)
  blocking collectives  16 us (19%)
  waiting for transfers between devices  15.2 us (18%)
  between operations  1.53 us (2%)
    all_to_all x1, blocking collectives, everyone(): moved = lax.all_to_all(pay.reshape(DEVICES, rows, LANES), BOTH, 0, 0)  16 us
    all_to_all x2, starting transfers between devices, everyone(): moved = lax.all_to_all(pay.reshape(DEVICES, rows, LANES), BOTH, 0, 0)  15.8 us
    all_to_all x2, waiting for transfers between devices, everyone(): moved = lax.all_to_all(pay.reshape(DEVICES, rows, LANES), BOTH, 0, 0)  9.12 us
    pallas_call x1, Pallas kernels, local(): call(first_kernel, [SM] + [VM] * 10, [FIELD, ((KC + 1, 24, SLOTS), F32),...  7.87 us
    ppermute x5, waiting for transfers between devices, swap_between(): return lax.ppermute(b, BOTH, swap_pairs(axis)[1])  5.16 us
    ppermute x5, starting transfers between devices, swap_between(): return lax.ppermute(b, BOTH, swap_pairs(axis)[1])  4.81 us
    ppermute x4, starting transfers between devices, trade(): return (lax.ppermute(a, BOTH, swap_pairs(axis)[0]), b)  4.77 us
    pallas_call x1, Pallas kernels, local(): call(second_solve_kernel, [SM] + [VM] * 8, [FIELD, ((CY, CZ), F32), ((8,...  4.12 us
  transfers between devices with their start and end apart: 18, of which 6 were waited for; matrix products, arithmetic and copies ran while one was open for 0% of the time, Pallas kernels for 15%

profile of v4, /device:TPU:1, one launch (start us, length us, event | category | flops | bytes accessed | tf_op | source)
XLA Modules:
  0.0 83.8 jit_solution(7827690949930938665)
XLA Ops:
  0.6 3.1 %shard_map.104 = (f32[4,8,256]{2,1,0:T(8,128)}, f32[4,8,256]{2,1,0:T(8,128)}, f32[4,8,256]{2,1,0:T(8,128)}, f32[4,8,256]{2,1,0:T(8,128)}, f32[128,256]{1,0:T(8,1...) custom-call(f32[16]{0:T(128)} %cap.1, f32[4,8,256]{2,1,0:T(8,128)} %c_old.1, ...), custom_call_target="tpu_custom_call" | custom-call | flops 10000 | bytes 100000 | tf_op jit(solution)/shard_map/pallas_call | solution.py:663
  3.8 0.0 copy-start.9
  3.8 3.4 %collective-permute-start.5 = (f32[128,256]{1,0:T(8,128)}, f32[128,256]{1,0:T(8,128)S(1)}, u32[]{:S(2)}, u32[]{:S(2)}) collective-permute-start(f32[128,256]{1,0:T(8,128)} %get-tuple-element.37.tab0), channel_id=1, source_target_pairs={{0,96},{16,112},{32,64},{48,80},{64,32},{80,48},{96,0},{112,16},{1... | collective-permute-start | bytes 393224 | tf_op jit(solution)/shard_map/ppermute | solution.py:682
  7.2 0.5 collective-permute-start.3
  7.7 0.1 collective-permute-start.1
  8.5 0.7 copy-done.7
  9.3 0.9 %shard_map.105 = f32[512,128]{1,0:T(8,128)} custom-call(s32[1]{0:T(128)S(6)} %copy.11.count, f32[4,8,256]{2,1,0:T(8,128)S(1)} %copy-done.7, f32[16,128]{1,0:T(8,128)S(1)} %bitcast.18, s32[128,128]{1,0:T(8,128)S(1)} %bitcast.12), custom_call_target="tpu_custom_call" | custom-call | flops 10000 | bytes 100000 | tf_op jit(solution)/shard_map/pallas_call | solution.py:686
  10.2 11.6 %all-to-all-start = ((f32[128,4,128]{2,1,0:T(4,128)}), f32[128,4,128]{2,1,0:T(4,128)S(1)}, u32[]{:S(2)}, u32[]{:S(2)}) async-start(f32[128,4,128]{2,1,0:T(4,128)} %bitcast.3), calls=%async_computation | async-start | bytes 524288 | tf_op jit(solution)/shard_map/all_to_all | solution.py:655
  21.8 1.1 %collective-permute-start = (f32[168,256]{1,0:T(8,128)S(1)}, f32[168,256]{1,0:T(8,128)S(1)}, u32[]{:S(2)}, u32[]{:S(2)}) collective-permute-start(f32[168,256]{1,0:T(8,128)S(1)} %copy-done.10), channel_id=1, source_target_pairs={{0,16},{16,0},{32,48},{48,32},{64,80},{80,64},{96,112},{112,96},{1... | collective-permute-start | bytes 516104 | tf_op jit(solution)/shard_map/ppermute | solution.py:679
  22.9 0.0 collective-permute-done.5.tab6
  22.9 0.1 collective-permute-start.6
  23.0 0.0 collective-permute-done.3.tab4
  23.1 0.4 collective-permute-start.4
  23.5 0.0 collective-permute-done.1.tab2
  23.5 0.1 collective-permute-start.2
  23.6 1.0 %collective-permute-start.7 = (f32[40,256]{1,0:T(8,128)S(1)}, f32[40,256]{1,0:T(8,128)S(1)}, u32[]{:S(2)}, u32[]{:S(2)}) collective-permute-start(f32[40,256]{1,0:T(8,128)S(1)} %copy-done.11), channel_id=1, source_target_pairs={{0,112},{1,113},{2,114},{3,115},{4,116},{5,117},{6,118},{7,119},{8... | collective-permute-start | bytes 122888 | tf_op jit(solution)/shard_map/ppermute | solution.py:646
  24.5 0.0 collective-permute-done.tab1.x0a.xa
  24.5 1.3 %collective-permute-start.12 = (f32[8,256]{1,0:T(8,128)S(1)}, f32[8,256]{1,0:T(8,128)S(1)}, u32[]{:S(2)}, u32[]{:S(2)}) collective-permute-start(f32[8,256]{1,0:T(8,128)S(1)} %copy-done.13), channel_id=1, source_target_pairs={{0,1},{1,0},{2,3},{3,2},{4,5},{5,4},{6,7},{7,6},{8,9},{9,8},{10,11... | collective-permute-start | bytes 24584 | tf_op jit(solution)/shard_map/ppermute | solution.py:651
  25.9 0.0 collective-permute-done.6.tab7
  25.9 1.7 %collective-permute-start.13 = (f32[8,256]{1,0:T(8,128)S(1)}, f32[8,256]{1,0:T(8,128)S(1)}, u32[]{:S(2)}, u32[]{:S(2)}) collective-permute-start(f32[8,256]{1,0:T(8,128)S(1)} %copy-done.12), channel_id=1, source_target_pairs={{0,16},{1,2},{2,1},{3,4},{4,3},{5,6},{6,5},{7,8},{8,7},{9,10},{10,... | collective-permute-start | bytes 24584 | tf_op jit(solution)/shard_map/ppermute | solution.py:646
  27.6 5.5 %all-to-all-done = f32[128,4,128]{2,1,0:T(4,128)S(1)} async-done(((f32[128,4,128]{2,1,0:T(4,128)}), f32[128,4,128]{2,1,0:T(4,128)S(1)}, u32[]{:S(2)}, u32[]{:S(2)}) %all-to-all-start) | async-done | bytes 262176 | tf_op jit(solution)/shard_map/all_to_all | solution.py:655
  33.0 0.0 collective-permute-done.4.tab5
  33.0 0.0 collective-permute-done.2.tab3
  33.0 0.0 copy-start.3
  33.1 7.9 %shard_map.106 = (f32[4,8,256]{2,1,0:T(8,128)S(1)}, f32[9,24,256]{2,1,0:T(8,128)S(1)}, f32[8,256]{1,0:T(8,128)S(1)}, s32[8,128]{1,0:T(8,128)S(1)}, s32[8,128]{1,...) custom-call(s32[1]{0:T(128)S(6)} %copy.11.count, ...), custom_call_target="tpu_custom_call" | custom-call | flops 10000 | bytes 100000 | tf_op jit(solution)/shard_map/pallas_call | solution.py:691
  41.0 0.0 collective-permute-done.12.ya
  41.0 0.0 collective-permute-done.13.yb
  41.0 1.1 %shard_map.108 = f32[512,128]{1,0:T(8,128)} custom-call(s32[1]{0:T(128)S(6)} %copy.11.count, s32[8,128]{1,0:T(8,128)S(1)} %get-tuple-element.46.beside, s32[8,128]{1,0:T(8,128)S(1)} %get-tuple-element.47.across, f32[4,8,256]{2,1,0:T(8,128)S(1)} %copy-done.5, f32[4,8,256]{2,1,0:T(8,128)S(1)} %copy-done.4, f32[4,8,256]{2,1,0:T(8,128)S(1)} %get-tuple-element.39.pe, ...), custom_call_target="tpu_custom_call" | custom-call | flops 10000 | bytes 100000 | tf_op jit(solution)/shard_map/pallas_call | solution.py:701
  42.1 4.2 %all-to-all-start.1 = ((f32[128,4,128]{2,1,0:T(4,128)}), f32[128,4,128]{2,1,0:T(4,128)S(1)}, u32[]{:S(2)}, u32[]{:S(2)}) async-start(f32[128,4,128]{2,1,0:T(4,128)} %bitcast.5), calls=%async_computation.1 | async-start | bytes 524288 | tf_op jit(solution)/shard_map/all_to_all | solution.py:655
  46.3 1.2 %collective-permute-start.8 = (f32[16,256]{1,0:T(8,128)S(1)}, f32[16,256]{1,0:T(8,128)S(1)}, u32[]{:S(2)}, u32[]{:S(2)}) collective-permute-start(f32[16,256]{1,0:T(8,128)S(1)} %get-tuple-element.42), channel_id=1, source_target_pairs={{0,16},{1,17},{2,18},{3,19},{4,20},{5,21},{6,22},{7,23},{8,24},{9,... | collective-permute-start | bytes 49160 | tf_op jit(solution)/shard_map/ppermute | solution.py:651
  47.5 0.7 collective-permute-start.9
  48.2 0.2 collective-permute-done.8.x1a
  48.3 2.9 %collective-permute-done.9.x1b = f32[16,256]{1,0:T(8,128)S(1)} collective-permute-done((f32[16,256]{1,0:T(8,128)S(1)}, f32[16,256]{1,0:T(8,128)S(1)}, u32[]{:S(2)}, u32[]{:S(2)}) %collective-permute-start.9) | collective-permute-done | bytes 16416 | tf_op jit(solution)/shard_map/ppermute | solution.py:646
  51.3 1.5 %collective-permute-start.10 = (f32[64,256]{1,0:T(8,128)S(1)}, f32[64,256]{1,0:T(8,128)S(1)}, u32[]{:S(2)}, u32[]{:S(2)}) collective-permute-start(f32[64,256]{1,0:T(8,128)S(1)} %get-tuple-element.44), channel_id=1, source_target_pairs={{0,1},{1,0},{2,3},{3,2},{4,5},{5,4},{6,7},{7,6},{8,9},{9,8},{10,11... | collective-permute-start | bytes 196616 | tf_op jit(solution)/shard_map/ppermute | solution.py:651
  52.8 1.4 %collective-permute-start.11 = (f32[64,256]{1,0:T(8,128)S(1)}, f32[64,256]{1,0:T(8,128)S(1)}, u32[]{:S(2)}, u32[]{:S(2)}) collective-permute-start(f32[64,256]{1,0:T(8,128)S(1)} %get-tuple-element.45), channel_id=1, source_target_pairs={{0,16},{1,2},{2,1},{3,4},{4,3},{5,6},{6,5},{7,8},{8,7},{9,10},{10,... | collective-permute-start | bytes 196616 | tf_op jit(solution)/shard_map/ppermute | solution.py:646
  54.1 3.6 %all-to-all-done.1 = f32[128,4,128]{2,1,0:T(4,128)S(1)} async-done(((f32[128,4,128]{2,1,0:T(4,128)}), f32[128,4,128]{2,1,0:T(4,128)S(1)}, u32[]{:S(2)}, u32[]{:S(2)}) %all-to-all-start.1) | async-done | bytes 262176 | tf_op jit(solution)/shard_map/all_to_all | solution.py:655
  57.8 4.1 %shard_map.109 = (f32[4,8,256]{2,1,0:T(8,128)S(1)}, f32[8,256]{1,0:T(8,128)S(1)}, f32[8,128]{1,0:T(8,128)S(1)}) custom-call(s32[1]{0:T(128)S(6)} %copy.11.count, f32[512,128]{1,0:T(8,128)S(1)} %bitcast.11, f32[512,128]{1,0:T(8,128)S(1)} %bitcast.10, s32[128,128]{1,0:T(8,128)S(1)} %bitcast.14, f32[9,24,256]{2,1,0:T(8,128)S(1)} %get-tuple-element.50.plan, ...), custom_call_target="tpu_custom_call" | custom-call | flops 100000000 | bytes 100000 | tf_op jit(solution)/shard_map/pallas_call | solution.py:708
  61.9 0.0 collective-permute-done.11.yb
  61.9 0.0 copy-start
  61.9 0.0 copy-start.1
  62.0 0.4 shard_map.110
  62.4 0.8 collective-permute-start.14
  63.1 0.1 collective-permute-start.15
  63.3 0.7 collective-permute-done.14.xa
  64.0 2.2 %collective-permute-done.15.xb = f32[8,256]{1,0:T(8,128)S(1)} collective-permute-done((f32[8,256]{1,0:T(8,128)S(1)}, f32[8,256]{1,0:T(8,128)S(1)}, u32[]{:S(2)}, u32[]{:S(2)}) %collective-permute-start.15) | collective-permute-done | bytes 8224 | tf_op jit(solution)/shard_map/ppermute | solution.py:646
  66.2 0.2 shard_map.111
  66.4 16.0 %all_to_all.15 = f32[128,2,128]{2,1,0:T(2,128)S(1)} all-to-all(f32[128,2,128]{2,1,0:T(2,128)S(1)} %bitcast.16), channel_id=1, replica_groups=mesh['coarse'=8,'fine'=16] {'coarse','fine'}, dimensions={0} | all-to-all | bytes 262144 | tf_op jit(solution)/shard_map/all_to_all | solution.py:655
  82.4 1.4 %shard_map.112 = (f32[4,8,256]{2,1,0:T(8,128)}, f32[16,4,8,256]{3,2,1,0:T(8,128)}) custom-call(f32[256,128]{1,0:T(8,128)S(1)} %bitcast.15, f32[4,8,256]{2,1,0:T(8,128)S(1)} %get-tuple-element.65.z1, f32[4,8,256]{2,1,0:T(8,128)S(1)} %get-tuple-element.57.p, f32[16,4,8,256]{3,2,1,0:T(8,128)S(1)} %copy-done, f32[16,4,8,256]{3,2,1,0:T(8,128)S(1)} %copy-done.1), custom_call_target="tpu_custom_call" | custom-call | flops 10000 | bytes 100000 | tf_op jit(solution)/shard_map/pallas_call | solution.py:719
  (26 shorter events, 0.1 us)
Async XLA Ops:
  0.6 7.9 %copy-start.2 = (s32[16384]{0:T(1024)S(1)}, s32[16384]{0:T(1024)}, u32[]{:S(2)}) copy-start(s32[16384]{0:T(1024)} %param.14) | copy-start | bytes 196612
  3.8 4.7 %copy-start.9 = (f32[2048]{0:T(1024)S(1)}, f32[2048]{0:T(1024)}, u32[]{:S(2)}) copy-start(f32[2048]{0:T(1024)} %param.17) | copy-start | bytes 24580
  3.8 19.2 %collective-permute-start.5 = (f32[128,256]{1,0:T(8,128)}, f32[128,256]{1,0:T(8,128)S(1)}, u32[]{:S(2)}, u32[]{:S(2)}) collective-permute-start(f32[128,256]{1,0:T(8,128)} %get-tuple-element.37.tab0), channel_id=1, source_target_pairs={{0,96},{16,112},{32,64},{48,80},{64,32},{80,48},{96,0},{112,16},{1... | collective-permute-start | bytes 393224 | tf_op jit(solution)/shard_map/ppermute | solution.py:682
  7.2 15.9 %collective-permute-start.3 = (f32[128,256]{1,0:T(8,128)}, f32[128,256]{1,0:T(8,128)S(1)}, u32[]{:S(2)}, u32[]{:S(2)}) collective-permute-start(f32[128,256]{1,0:T(8,128)} %get-tuple-element.37.tab0), channel_id=1, source_target_pairs={{0,64},{16,80},{32,96},{48,112},{64,0},{80,16},{96,32},{112,48},{1... | collective-permute-start | bytes 393224 | tf_op jit(solution)/shard_map/ppermute | solution.py:682
  7.7 15.8 %collective-permute-start.1 = (f32[128,256]{1,0:T(8,128)}, f32[128,256]{1,0:T(8,128)S(1)}, u32[]{:S(2)}, u32[]{:S(2)}) collective-permute-start(f32[128,256]{1,0:T(8,128)} %get-tuple-element.37.tab0), channel_id=1, source_target_pairs={{0,32},{16,48},{32,0},{48,16},{64,96},{80,112},{96,64},{112,80},{1... | collective-permute-start | bytes 393224 | tf_op jit(solution)/shard_map/ppermute | solution.py:682
  8.5 0.8 copy-start.7
  10.1 11.7 %copy-start.10 = (f32[168,256]{1,0:T(8,128)S(1)}, f32[168,256]{1,0:T(8,128)}, u32[]{:S(2)}) copy-start(f32[168,256]{1,0:T(8,128)} %get-tuple-element.38) | copy-start | bytes 516100
  10.1 13.4 %copy-start.11 = (f32[40,256]{1,0:T(8,128)S(1)}, f32[40,256]{1,0:T(8,128)}, u32[]{:S(2)}) copy-start(f32[40,256]{1,0:T(8,128)} %get-tuple-element.41) | copy-start | bytes 122884
  10.1 14.4 %copy-start.13 = (f32[8,256]{1,0:T(8,128)S(1)}, f32[8,256]{1,0:T(8,128)}, u32[]{:S(2)}) copy-start(f32[8,256]{1,0:T(8,128)} %get-tuple-element.48) | copy-start | bytes 24580
  10.1 15.7 %copy-start.12 = (f32[8,256]{1,0:T(8,128)S(1)}, f32[8,256]{1,0:T(8,128)}, u32[]{:S(2)}) copy-start(f32[8,256]{1,0:T(8,128)} %get-tuple-element.49) | copy-start | bytes 24580
  10.1 22.9 %copy-start.6 = (f32[128,256]{1,0:T(8,128)S(1)}, f32[128,256]{1,0:T(8,128)}, u32[]{:S(2)}) copy-start(f32[128,256]{1,0:T(8,128)} %get-tuple-element.37.tab0) | copy-start | bytes 393220
  10.2 22.9 %all-to-all-start = ((f32[128,4,128]{2,1,0:T(4,128)}), f32[128,4,128]{2,1,0:T(4,128)S(1)}, u32[]{:S(2)}, u32[]{:S(2)}) async-start(f32[128,4,128]{2,1,0:T(4,128)} %bitcast.3), calls=%async_computation | async-start | bytes 524288 | tf_op jit(solution)/shard_map/all_to_all | solution.py:655
  21.8 2.8 %collective-permute-start = (f32[168,256]{1,0:T(8,128)S(1)}, f32[168,256]{1,0:T(8,128)S(1)}, u32[]{:S(2)}, u32[]{:S(2)}) collective-permute-start(f32[168,256]{1,0:T(8,128)S(1)} %copy-done.10), channel_id=1, source_target_pairs={{0,16},{16,0},{32,48},{48,32},{64,80},{80,64},{96,112},{112,96},{1... | collective-permute-start | bytes 516104 | tf_op jit(solution)/shard_map/ppermute | solution.py:679
  22.9 2.9 %collective-permute-start.6 = (f32[128,256]{1,0:T(8,128)S(1)}, f32[128,256]{1,0:T(8,128)S(1)}, u32[]{:S(2)}, u32[]{:S(2)}) collective-permute-start(f32[128,256]{1,0:T(8,128)S(1)} %collective-permute-done.5.tab6), channel_id=1, source_target_pairs={{0,16},{16,0},{32,48},{48,32},{64,80},{80,64},{96,112},{112,96},{1... | collective-permute-start | bytes 393224 | tf_op jit(solution)/shard_map/ppermute | solution.py:683
  23.1 10.0 %collective-permute-start.4 = (f32[128,256]{1,0:T(8,128)S(1)}, f32[128,256]{1,0:T(8,128)S(1)}, u32[]{:S(2)}, u32[]{:S(2)}) collective-permute-start(f32[128,256]{1,0:T(8,128)S(1)} %collective-permute-done.3.tab4), channel_id=1, source_target_pairs={{0,16},{16,0},{32,48},{48,32},{64,80},{80,64},{96,112},{112,96},{1... | collective-permute-start | bytes 393224 | tf_op jit(solution)/shard_map/ppermute | solution.py:683
  23.5 9.6 %collective-permute-start.2 = (f32[128,256]{1,0:T(8,128)S(1)}, f32[128,256]{1,0:T(8,128)S(1)}, u32[]{:S(2)}, u32[]{:S(2)}) collective-permute-start(f32[128,256]{1,0:T(8,128)S(1)} %collective-permute-done.1.tab2), channel_id=1, source_target_pairs={{0,16},{16,0},{32,48},{48,32},{64,80},{80,64},{96,112},{112,96},{1... | collective-permute-start | bytes 393224 | tf_op jit(solution)/shard_map/ppermute | solution.py:683
  23.6 17.4 %collective-permute-start.7 = (f32[40,256]{1,0:T(8,128)S(1)}, f32[40,256]{1,0:T(8,128)S(1)}, u32[]{:S(2)}, u32[]{:S(2)}) collective-permute-start(f32[40,256]{1,0:T(8,128)S(1)} %copy-done.11), channel_id=1, source_target_pairs={{0,112},{1,113},{2,114},{3,115},{4,116},{5,117},{6,118},{7,119},{8... | collective-permute-start | bytes 122888 | tf_op jit(solution)/shard_map/ppermute | solution.py:646
  24.5 16.4 %collective-permute-start.12 = (f32[8,256]{1,0:T(8,128)S(1)}, f32[8,256]{1,0:T(8,128)S(1)}, u32[]{:S(2)}, u32[]{:S(2)}) collective-permute-start(f32[8,256]{1,0:T(8,128)S(1)} %copy-done.13), channel_id=1, source_target_pairs={{0,1},{1,0},{2,3},{3,2},{4,5},{5,4},{6,7},{7,6},{8,9},{9,8},{10,11... | collective-permute-start | bytes 24584 | tf_op jit(solution)/shard_map/ppermute | solution.py:651
  25.9 15.1 %collective-permute-start.13 = (f32[8,256]{1,0:T(8,128)S(1)}, f32[8,256]{1,0:T(8,128)S(1)}, u32[]{:S(2)}, u32[]{:S(2)}) collective-permute-start(f32[8,256]{1,0:T(8,128)S(1)} %copy-done.12), channel_id=1, source_target_pairs={{0,16},{1,2},{2,1},{3,4},{4,3},{5,6},{6,5},{7,8},{8,7},{9,10},{10,... | collective-permute-start | bytes 24584 | tf_op jit(solution)/shard_map/ppermute | solution.py:646
  33.0 7.9 %copy-start.3 = (f32[4,8,256]{2,1,0:T(8,128)S(1)}, f32[4,8,256]{2,1,0:T(8,128)}, u32[]{:S(2)}) copy-start(f32[4,8,256]{2,1,0:T(8,128)} %get-tuple-element.40.c) | copy-start | bytes 98308
  33.1 7.9 %copy-start.4 = (f32[4,8,256]{2,1,0:T(8,128)S(1)}, f32[4,8,256]{2,1,0:T(8,128)}, u32[]{:S(2)}) copy-start(f32[4,8,256]{2,1,0:T(8,128)} %get-tuple-element.36.ic) | copy-start | bytes 98308
  33.1 7.9 %copy-start.5 = (f32[4,8,256]{2,1,0:T(8,128)S(1)}, f32[4,8,256]{2,1,0:T(8,128)}, u32[]{:S(2)}) copy-start(f32[4,8,256]{2,1,0:T(8,128)} %get-tuple-element.35.zs) | copy-start | bytes 98308
  42.1 15.7 %all-to-all-start.1 = ((f32[128,4,128]{2,1,0:T(4,128)}), f32[128,4,128]{2,1,0:T(4,128)S(1)}, u32[]{:S(2)}, u32[]{:S(2)}) async-start(f32[128,4,128]{2,1,0:T(4,128)} %bitcast.5), calls=%async_computation.1 | async-start | bytes 524288 | tf_op jit(solution)/shard_map/all_to_all | solution.py:655
  46.3 2.0 %collective-permute-start.8 = (f32[16,256]{1,0:T(8,128)S(1)}, f32[16,256]{1,0:T(8,128)S(1)}, u32[]{:S(2)}, u32[]{:S(2)}) collective-permute-start(f32[16,256]{1,0:T(8,128)S(1)} %get-tuple-element.42), channel_id=1, source_target_pairs={{0,16},{1,17},{2,18},{3,19},{4,20},{5,21},{6,22},{7,23},{8,24},{9,... | collective-permute-start | bytes 49160 | tf_op jit(solution)/shard_map/ppermute | solution.py:651
  47.5 3.7 %collective-permute-start.9 = (f32[16,256]{1,0:T(8,128)S(1)}, f32[16,256]{1,0:T(8,128)S(1)}, u32[]{:S(2)}, u32[]{:S(2)}) collective-permute-start(f32[16,256]{1,0:T(8,128)S(1)} %get-tuple-element.43), channel_id=1, source_target_pairs={{0,112},{1,113},{2,114},{3,115},{4,116},{5,117},{6,118},{7,119},{8... | collective-permute-start | bytes 49160 | tf_op jit(solution)/shard_map/ppermute | solution.py:646
  51.3 10.6 %collective-permute-start.10 = (f32[64,256]{1,0:T(8,128)S(1)}, f32[64,256]{1,0:T(8,128)S(1)}, u32[]{:S(2)}, u32[]{:S(2)}) collective-permute-start(f32[64,256]{1,0:T(8,128)S(1)} %get-tuple-element.44), channel_id=1, source_target_pairs={{0,1},{1,0},{2,3},{3,2},{4,5},{5,4},{6,7},{7,6},{8,9},{9,8},{10,11... | collective-permute-start | bytes 196616 | tf_op jit(solution)/shard_map/ppermute | solution.py:651
  52.8 9.2 %collective-permute-start.11 = (f32[64,256]{1,0:T(8,128)S(1)}, f32[64,256]{1,0:T(8,128)S(1)}, u32[]{:S(2)}, u32[]{:S(2)}) collective-permute-start(f32[64,256]{1,0:T(8,128)S(1)} %get-tuple-element.45), channel_id=1, source_target_pairs={{0,16},{1,2},{2,1},{3,4},{4,3},{5,6},{6,5},{7,8},{8,7},{9,10},{10,... | collective-permute-start | bytes 196616 | tf_op jit(solution)/shard_map/ppermute | solution.py:646
  61.9 4.3 %copy-start.8 = (f32[4,8,256]{2,1,0:T(8,128)S(1)}, f32[4,8,256]{2,1,0:T(8,128)}, u32[]{:S(2)}) copy-start(f32[4,8,256]{2,1,0:T(8,128)} %get-tuple-element.34.s) | copy-start | bytes 98308
  61.9 20.5 %copy-start = (f32[16,4,8,256]{3,2,1,0:T(8,128)S(1)}, f32[16,4,8,256]{3,2,1,0:T(8,128)}, u32[]{:S(2)}) copy-start(f32[16,4,8,256]{3,2,1,0:T(8,128)} %s_old.1) | copy-start | bytes 1572868
  61.9 20.5 %copy-start.1 = (f32[16,4,8,256]{3,2,1,0:T(8,128)S(1)}, f32[16,4,8,256]{3,2,1,0:T(8,128)}, u32[]{:S(2)}) copy-start(f32[16,4,8,256]{3,2,1,0:T(8,128)} %rate.1) | copy-start | bytes 1572868
  62.4 1.6 %collective-permute-start.14 = (f32[8,256]{1,0:T(8,128)S(1)}, f32[8,256]{1,0:T(8,128)S(1)}, u32[]{:S(2)}, u32[]{:S(2)}) collective-permute-start(f32[8,256]{1,0:T(8,128)S(1)} %get-tuple-element.58), channel_id=1, source_target_pairs={{0,16},{1,17},{2,18},{3,19},{4,20},{5,21},{6,22},{7,23},{8,24},{9,... | collective-permute-start | bytes 24584 | tf_op jit(solution)/shard_map/ppermute | solution.py:651
  63.1 3.1 %collective-permute-start.15 = (f32[8,256]{1,0:T(8,128)S(1)}, f32[8,256]{1,0:T(8,128)S(1)}, u32[]{:S(2)}, u32[]{:S(2)}) collective-permute-start(f32[8,256]{1,0:T(8,128)S(1)} %get-tuple-element.59), channel_id=1, source_target_pairs={{0,112},{1,113},{2,114},{3,115},{4,116},{5,117},{6,118},{7,119},{8... | collective-permute-start | bytes 24584 | tf_op jit(solution)/shard_map/ppermute | solution.py:646

commit v5 on v4

--- a/solution.py
+++ b/solution.py
@@ -196,18 +196,16 @@
     high = gathered[pl.ds(1, DEVICES, stride=4), :]
     diag = gathered[pl.ds(2, DEVICES, stride=4), :]
     inverse = gathered[pl.ds(3, DEVICES, stride=4), :].astype(I32)
-    used = ((low < 0.5 * UNUSED).astype(F32) + (high < 0.5 * UNUSED).astype(F32)).astype(BF16)
-    return low, high, diag, inverse, used
-
-
-def offsets_of(used):
-    below = iota((LANES, LANES), 1) < iota((LANES, LANES), 0)
-    ones = jnp.ones((LANES, LANES), BF16)
-    by_row = nn(nn(below.astype(F32).astype(BF16), used).astype(BF16), ones).astype(I32)
-    counts = nt(ones, used)
-    above = iota((LANES, LANES), 0) < iota((LANES, LANES), 1)
-    by_lane = nn(counts[0:8].astype(BF16), above.astype(F32).astype(BF16))[0:1].astype(I32)
-    return by_row, by_lane
+    used = jnp.where(low < 0.5 * UNUSED, 1.0, 0.0) + jnp.where(high < 0.5 * UNUSED, 1.0, 0.0)
+    return low, high, diag, inverse, jnp.sum(used, axis=1, keepdims=True)
+
+
+def offsets_of(counts):
+    row, lane = iota((LANES, LANES), 0), iota((LANES, LANES), 1)
+    by_lane = jnp.sum(jnp.where(row < lane, counts, 0.0), axis=0, keepdims=True)
+    across = jnp.sum(jnp.where(row == lane, counts, 0.0), axis=0, keepdims=True)
+    by_row = jnp.sum(jnp.where(lane < row, across, 0.0), axis=1, keepdims=True)
+    return jnp.broadcast_to(by_row, (LANES, LANES)).astype(I32), by_lane.astype(I32)
 
 
 def blocks_of(order):
@@ -231,40 +229,57 @@
     return lane_take(by_block[:, :LANES] + by_block[:, LANES:], inverse)
 
 
+def one_hot(row16, index):
+    return jnp.where(row16 == index.astype(BF16), jnp.ones(row16.shape, BF16), jnp.zeros(row16.shape, BF16))
+
+
 def fetch(table, unknown, coarse):
     inner = unknown & (SHARD_ROWS - 1)
-    shard = unknown >> 11
-    shard = shard ^ coarse
+    shard = (unknown >> 11) ^ coarse
+    row16 = iota((256, SLOTS), 0).astype(F32).astype(BF16)
     found = jnp.zeros((SHARDS * 32, SLOTS), F32)
     for chunk in range(SHARD_ROWS // 256):
-        spot = (iota((256, SLOTS), 0) + chunk * 256 == inner).astype(F32).astype(BF16)
+        spot = one_hot(row16, (inner - chunk * 256).astype(F32))
         found = found + nn(table[:, chunk * 256 : (chunk + 1) * 256], spot)
     found = found.reshape(SHARDS, 32, SLOTS)
-    picked = jnp.zeros((32, SLOTS), F32)
-    for g in range(SHARDS):
-        picked = picked + jnp.where(shard == g, found[g], 0.0)
+    picked = found[0]
+    for g in range(1, SHARDS):
+        picked = jnp.where(shard == g, found[g], picked)
     return picked[0:8], picked[8:16], picked[16:24] + picked[24:32]
 
 
-def coarse_solve(values, plan, own):
+def gatherer(values):
     high, low = split2(values.T)
     table = jnp.concatenate([high, low], axis=1)
     row = iota((LANES, SLOTS), 0).astype(F32)
+    row16 = row.astype(BF16)
 
     def gather(block, inner):
-        spot = (row == block).astype(F32).astype(BF16)
+        spot = one_hot(row16, block)
         found = nn(table, jnp.concatenate([spot, spot], axis=0))
-        return jnp.sum(jnp.where(row == inner, found, 0.0).reshape(16, 8, SLOTS), axis=0)
-
-    def entry(k, total):
-        part = -1.4 * gather(plan[KC, pl.ds(k, 1), :], plan[KC, pl.ds(8 + k, 1), :])
-        for j in range(KC):
-            weight = plan[k, 16 + j : 17 + j, :]
-            part = part + weight * gather(plan[k, j : j + 1, :], plan[k, 8 + j : 9 + j, :])
-        return total + plan[KC, pl.ds(16 + k, 1), :] * part
-
-    total = 1.24 * gather(own[0:1, :], own[1:2, :])
-    total = lax.fori_loop(0, KC, entry, total)
+        kept = jnp.zeros((8, SLOTS), F32)
+        for b in range(0, LANES, 8):
+            kept = jnp.where(row[b : b + 8] == inner, found[b : b + 8], kept)
+        return kept
+
+    return gather
+
+
+def solve_entry(gather, first, parts):
+    total = -1.4 * gather(first[0], first[1])
+    for j in range(KC):
+        total = total + parts[2][j : j + 1] * gather(parts[0][j : j + 1], parts[1][j : j + 1])
+    return first[2] * total
+
+
+def coarse_solve(values, plan, own):
+    gather = gatherer(values)
+
+    def column(k, total):
+        first = [plan[KC, pl.ds(8 * i + k, 1), :] for i in range(3)]
+        return total + solve_entry(gather, first, [plan[k, 8 * i : 8 * i + 8, :] for i in range(3)])
+
+    total = lax.fori_loop(0, KC, column, 1.24 * gather(own[0:1, :], own[1:2, :]), unroll=SECOND_UNROLL)
     return jnp.sum(total, axis=0, keepdims=True)
 
 
@@ -281,8 +296,8 @@
     place = places()
     n = count[0]
     me = place[0] * 16 + place[1]
-    low, high, diag, inverse, used = read_sums(gathered)
-    offsets = offsets_of(used)
+    low, high, diag, inverse, counts = read_sums(gathered)
+    offsets = offsets_of(counts)
     at_row[...] = offsets[0]
     at_lane[...] = jnp.broadcast_to(offsets[1], (8, LANES))
     sums = assemble(
@@ -290,7 +305,7 @@
         offsets, inverse, blocks_of(order),
     )
     values = 0.8 * sums / diag
-    counts = nn(used, jnp.ones((LANES, LANES), BF16))
+    counts = jnp.broadcast_to(counts, (LANES, LANES))
     counts_out[...] = counts.astype(I32)
     row = iota((LANES, LANES), 0)
     before = iota((8, LANES), 0) < 4
@@ -324,16 +339,14 @@
     )[0:1].astype(I32)
     own[0:1, :] = (unknown >> 7).astype(F32)
     own[1:2, :] = (unknown & 127).astype(F32)
-
     plan_rows(plan, KC, fetch(table, unknown, place[0]))
 
-    def level(k, carry):
+    def column(k, carry):
         col = 128.0 * plan[KC, pl.ds(k, 1), :] + plan[KC, pl.ds(8 + k, 1), :]
         plan_rows(plan, k, fetch(table, col.astype(I32), place[0]))
         return carry
 
-    lax.fori_loop(0, KC, level, 0)
-
+    lax.fori_loop(0, KC, column, 0, unroll=FIRST_UNROLL)
     pe = prolong(coarse_solve(values, plan, own), n)
     for x in range(CX):
         pe_out[x] = pe[x]
@@ -623,6 +636,8 @@
 
 FIELD = ((CX, CY, CZ), F32)
 SOURCE_VMEM = 63 << 20
+FIRST_UNROLL = 8
+SECOND_UNROLL = 8
 
 
 def swap_pairs(axis):

time: 84.2 us -> 81.6 us (0.969)
  Pallas kernels: 19.1 us -> 15.1 us
  blocking collectives: 16 us -> 17.4 us
    pallas_call x1, Pallas kernels: 7.87 us -> 5.28 us  [local(): call(first_kernel, [SM] + [VM] * 10, [FIELD, ((KC + 1, 24, SLOTS), F32),...]
    pallas_call x1, Pallas kernels: 4.12 us -> 2.67 us  [local(): call(second_solve_kernel, [SM] + [VM] * 8, [FIELD, ((CY, CZ), F32), ((8,...]
    all_to_all x1, blocking collectives: 16 us -> 17.4 us  [everyone(): moved = lax.all_to_all(pay.reshape(DEVICES, rows, LANES), BOTH, 0, 0)]
  transfers between devices with their start and end apart: 18 -> 18, of which waited for: 6 -> 6; matrix products, arithmetic and copies ran while one was open for 0% -> 0% of each run, Pallas kernels for 15% -> 11%
where the time goes in v5:
time: 81.6 us; the launch traced here: 81.3 us
  starting transfers between devices  31.2 us (38%)
  blocking collectives  17.4 us (21%)
  waiting for transfers between devices  15.2 us (19%)
  Pallas kernels  15.1 us (19%)
  between operations  1.54 us (2%)
    all_to_all x1, blocking collectives, everyone(): moved = lax.all_to_all(pay.reshape(DEVICES, rows, LANES), BOTH, 0, 0)  17.4 us
    all_to_all x2, starting transfers between devices, everyone(): moved = lax.all_to_all(pay.reshape(DEVICES, rows, LANES), BOTH, 0, 0)  15.8 us
    all_to_all x2, waiting for transfers between devices, everyone(): moved = lax.all_to_all(pay.reshape(DEVICES, rows, LANES), BOTH, 0, 0)  9.12 us
    pallas_call x1, Pallas kernels, local(): call(first_kernel, [SM] + [VM] * 10, [FIELD, ((KC + 1, 24, SLOTS), F32),...  5.28 us
    ppermute x5, waiting for transfers between devices, swap_between(): return lax.ppermute(b, BOTH, swap_pairs(axis)[1])  5.15 us
    ppermute x5, starting transfers between devices, swap_between(): return lax.ppermute(b, BOTH, swap_pairs(axis)[1])  4.8 us
    ppermute x4, starting transfers between devices, trade(): return (lax.ppermute(a, BOTH, swap_pairs(axis)[0]), b)  4.79 us
    ppermute x3, starting transfers between devices, local(): shard = lax.ppermute(tab, 'coarse', [(i, i ^ hop) for i in range(8)])  4.06 us
  transfers between devices with their start and end apart: 18, of which 6 were waited for; matrix products, arithmetic and copies ran while one was open for 0% of the time, Pallas kernels for 11%

profile of v5, /device:TPU:1, one launch (start us, length us, event | category | flops | bytes accessed | tf_op | source)
XLA Modules:
  0.0 81.3 jit_solution(14491827072375067711)
XLA Ops:
  0.6 3.1 %shard_map.104 = (f32[4,8,256]{2,1,0:T(8,128)}, f32[4,8,256]{2,1,0:T(8,128)}, f32[4,8,256]{2,1,0:T(8,128)}, f32[4,8,256]{2,1,0:T(8,128)}, f32[128,256]{1,0:T(8,1...) custom-call(f32[16]{0:T(128)} %cap.1, f32[4,8,256]{2,1,0:T(8,128)} %c_old.1, ...), custom_call_target="tpu_custom_call" | custom-call | flops 10000 | bytes 100000 | tf_op jit(solution)/shard_map/pallas_call | solution.py:678
  3.8 0.0 copy-start.9
  3.8 3.4 %collective-permute-start.5 = (f32[128,256]{1,0:T(8,128)}, f32[128,256]{1,0:T(8,128)S(1)}, u32[]{:S(2)}, u32[]{:S(2)}) collective-permute-start(f32[128,256]{1,0:T(8,128)} %get-tuple-element.37.tab0), channel_id=1, source_target_pairs={{0,96},{16,112},{32,64},{48,80},{64,32},{80,48},{96,0},{112,16},{1... | collective-permute-start | bytes 393224 | tf_op jit(solution)/shard_map/ppermute | solution.py:697
  7.2 0.5 collective-permute-start.3
  7.7 0.1 collective-permute-start.1
  8.5 0.7 copy-done.7
  9.3 0.9 %shard_map.105 = f32[512,128]{1,0:T(8,128)} custom-call(s32[1]{0:T(128)S(6)} %copy.11.count, f32[4,8,256]{2,1,0:T(8,128)S(1)} %copy-done.7, f32[16,128]{1,0:T(8,128)S(1)} %bitcast.18, s32[128,128]{1,0:T(8,128)S(1)} %bitcast.12), custom_call_target="tpu_custom_call" | custom-call | flops 10000 | bytes 100000 | tf_op jit(solution)/shard_map/pallas_call | solution.py:701
  10.2 11.6 %all-to-all-start = ((f32[128,4,128]{2,1,0:T(4,128)}), f32[128,4,128]{2,1,0:T(4,128)S(1)}, u32[]{:S(2)}, u32[]{:S(2)}) async-start(f32[128,4,128]{2,1,0:T(4,128)} %bitcast.3), calls=%async_computation | async-start | bytes 524288 | tf_op jit(solution)/shard_map/all_to_all | solution.py:670
  21.8 1.1 %collective-permute-start = (f32[168,256]{1,0:T(8,128)S(1)}, f32[168,256]{1,0:T(8,128)S(1)}, u32[]{:S(2)}, u32[]{:S(2)}) collective-permute-start(f32[168,256]{1,0:T(8,128)S(1)} %copy-done.10), channel_id=1, source_target_pairs={{0,16},{16,0},{32,48},{48,32},{64,80},{80,64},{96,112},{112,96},{1... | collective-permute-start | bytes 516104 | tf_op jit(solution)/shard_map/ppermute | solution.py:694
  22.9 0.0 collective-permute-done.5.tab6
  22.9 0.1 collective-permute-start.6
  23.0 0.0 collective-permute-done.3.tab4
  23.1 0.4 collective-permute-start.4
  23.5 0.0 collective-permute-done.1.tab2
  23.5 0.1 collective-permute-start.2
  23.6 1.0 %collective-permute-start.7 = (f32[40,256]{1,0:T(8,128)S(1)}, f32[40,256]{1,0:T(8,128)S(1)}, u32[]{:S(2)}, u32[]{:S(2)}) collective-permute-start(f32[40,256]{1,0:T(8,128)S(1)} %copy-done.11), channel_id=1, source_target_pairs={{0,112},{1,113},{2,114},{3,115},{4,116},{5,117},{6,118},{7,119},{8... | collective-permute-start | bytes 122888 | tf_op jit(solution)/shard_map/ppermute | solution.py:661
  24.5 0.0 collective-permute-done.tab1.x0a.xa
  24.5 1.3 %collective-permute-start.12 = (f32[8,256]{1,0:T(8,128)S(1)}, f32[8,256]{1,0:T(8,128)S(1)}, u32[]{:S(2)}, u32[]{:S(2)}) collective-permute-start(f32[8,256]{1,0:T(8,128)S(1)} %copy-done.13), channel_id=1, source_target_pairs={{0,1},{1,0},{2,3},{3,2},{4,5},{5,4},{6,7},{7,6},{8,9},{9,8},{10,11... | collective-permute-start | bytes 24584 | tf_op jit(solution)/shard_map/ppermute | solution.py:666
  25.9 0.0 collective-permute-done.6.tab7
  25.9 1.7 %collective-permute-start.13 = (f32[8,256]{1,0:T(8,128)S(1)}, f32[8,256]{1,0:T(8,128)S(1)}, u32[]{:S(2)}, u32[]{:S(2)}) collective-permute-start(f32[8,256]{1,0:T(8,128)S(1)} %copy-done.12), channel_id=1, source_target_pairs={{0,16},{1,2},{2,1},{3,4},{4,3},{5,6},{6,5},{7,8},{8,7},{9,10},{10,... | collective-permute-start | bytes 24584 | tf_op jit(solution)/shard_map/ppermute | solution.py:661
  27.6 5.5 %all-to-all-done = f32[128,4,128]{2,1,0:T(4,128)S(1)} async-done(((f32[128,4,128]{2,1,0:T(4,128)}), f32[128,4,128]{2,1,0:T(4,128)S(1)}, u32[]{:S(2)}, u32[]{:S(2)}) %all-to-all-start) | async-done | bytes 262176 | tf_op jit(solution)/shard_map/all_to_all | solution.py:670
  33.0 0.0 collective-permute-done.4.tab5
  33.0 0.0 collective-permute-done.2.tab3
  33.0 0.0 copy-start.3
  33.1 5.3 %shard_map.106 = (f32[4,8,256]{2,1,0:T(8,128)S(1)}, f32[9,24,256]{2,1,0:T(8,128)S(1)}, f32[8,256]{1,0:T(8,128)S(1)}, s32[8,128]{1,0:T(8,128)S(1)}, s32[8,128]{1,...) custom-call(s32[1]{0:T(128)S(6)} %copy.11.count, ...), custom_call_target="tpu_custom_call" | custom-call | flops 10000 | bytes 100000 | tf_op jit(solution)/shard_map/pallas_call | solution.py:706
  38.4 0.0 collective-permute-done.12.ya
  38.4 0.0 collective-permute-done.13.yb
  38.4 1.1 %shard_map.108 = f32[512,128]{1,0:T(8,128)} custom-call(s32[1]{0:T(128)S(6)} %copy.11.count, s32[8,128]{1,0:T(8,128)S(1)} %get-tuple-element.46.beside, s32[8,128]{1,0:T(8,128)S(1)} %get-tuple-element.47.across, f32[4,8,256]{2,1,0:T(8,128)S(1)} %copy-done.5, f32[4,8,256]{2,1,0:T(8,128)S(1)} %copy-done.4, f32[4,8,256]{2,1,0:T(8,128)S(1)} %get-tuple-element.39.pe, ...), custom_call_target="tpu_custom_call" | custom-call | flops 10000 | bytes 100000 | tf_op jit(solution)/shard_map/pallas_call | solution.py:716
  39.5 4.2 %all-to-all-start.1 = ((f32[128,4,128]{2,1,0:T(4,128)}), f32[128,4,128]{2,1,0:T(4,128)S(1)}, u32[]{:S(2)}, u32[]{:S(2)}) async-start(f32[128,4,128]{2,1,0:T(4,128)} %bitcast.5), calls=%async_computation.1 | async-start | bytes 524288 | tf_op jit(solution)/shard_map/all_to_all | solution.py:670
  43.7 1.2 %collective-permute-start.8 = (f32[16,256]{1,0:T(8,128)S(1)}, f32[16,256]{1,0:T(8,128)S(1)}, u32[]{:S(2)}, u32[]{:S(2)}) collective-permute-start(f32[16,256]{1,0:T(8,128)S(1)} %get-tuple-element.42), channel_id=1, source_target_pairs={{0,16},{1,17},{2,18},{3,19},{4,20},{5,21},{6,22},{7,23},{8,24},{9,... | collective-permute-start | bytes 49160 | tf_op jit(solution)/shard_map/ppermute | solution.py:666
  44.9 0.6 collective-permute-start.9
  45.6 0.2 collective-permute-done.8.x1a
  45.8 2.9 %collective-permute-done.9.x1b = f32[16,256]{1,0:T(8,128)S(1)} collective-permute-done((f32[16,256]{1,0:T(8,128)S(1)}, f32[16,256]{1,0:T(8,128)S(1)}, u32[]{:S(2)}, u32[]{:S(2)}) %collective-permute-start.9) | collective-permute-done | bytes 16416 | tf_op jit(solution)/shard_map/ppermute | solution.py:661
  48.7 1.5 %collective-permute-start.10 = (f32[64,256]{1,0:T(8,128)S(1)}, f32[64,256]{1,0:T(8,128)S(1)}, u32[]{:S(2)}, u32[]{:S(2)}) collective-permute-start(f32[64,256]{1,0:T(8,128)S(1)} %get-tuple-element.44), channel_id=1, source_target_pairs={{0,1},{1,0},{2,3},{3,2},{4,5},{5,4},{6,7},{7,6},{8,9},{9,8},{10,11... | collective-permute-start | bytes 196616 | tf_op jit(solution)/shard_map/ppermute | solution.py:666
  50.2 1.4 %collective-permute-start.11 = (f32[64,256]{1,0:T(8,128)S(1)}, f32[64,256]{1,0:T(8,128)S(1)}, u32[]{:S(2)}, u32[]{:S(2)}) collective-permute-start(f32[64,256]{1,0:T(8,128)S(1)} %get-tuple-element.45), channel_id=1, source_target_pairs={{0,16},{1,2},{2,1},{3,4},{4,3},{5,6},{6,5},{7,8},{8,7},{9,10},{10,... | collective-permute-start | bytes 196616 | tf_op jit(solution)/shard_map/ppermute | solution.py:661
  51.5 3.6 %all-to-all-done.1 = f32[128,4,128]{2,1,0:T(4,128)S(1)} async-done(((f32[128,4,128]{2,1,0:T(4,128)}), f32[128,4,128]{2,1,0:T(4,128)S(1)}, u32[]{:S(2)}, u32[]{:S(2)}) %all-to-all-start.1) | async-done | bytes 262176 | tf_op jit(solution)/shard_map/all_to_all | solution.py:670
  55.2 2.7 %shard_map.109 = (f32[4,8,256]{2,1,0:T(8,128)S(1)}, f32[8,256]{1,0:T(8,128)S(1)}, f32[8,128]{1,0:T(8,128)S(1)}) custom-call(s32[1]{0:T(128)S(6)} %copy.11.count, f32[512,128]{1,0:T(8,128)S(1)} %bitcast.11, f32[512,128]{1,0:T(8,128)S(1)} %bitcast.10, s32[128,128]{1,0:T(8,128)S(1)} %bitcast.14, f32[9,24,256]{2,1,0:T(8,128)S(1)} %get-tuple-element.50.plan, ...), custom_call_target="tpu_custom_call" | custom-call | flops 100000000 | bytes 100000 | tf_op jit(solution)/shard_map/pallas_call | solution.py:723
  57.9 0.0 collective-permute-done.11.yb
  57.9 0.0 copy-start
  57.9 0.0 copy-start.1
  57.9 0.4 shard_map.110
  58.3 0.8 collective-permute-start.14
  59.1 0.1 collective-permute-start.15
  59.2 0.7 collective-permute-done.14.xa
  59.9 2.2 %collective-permute-done.15.xb = f32[8,256]{1,0:T(8,128)S(1)} collective-permute-done((f32[8,256]{1,0:T(8,128)S(1)}, f32[8,256]{1,0:T(8,128)S(1)}, u32[]{:S(2)}, u32[]{:S(2)}) %collective-permute-start.15) | collective-permute-done | bytes 8224 | tf_op jit(solution)/shard_map/ppermute | solution.py:661
  62.2 0.2 shard_map.111
  62.4 17.4 %all_to_all.15 = f32[128,2,128]{2,1,0:T(2,128)S(1)} all-to-all(f32[128,2,128]{2,1,0:T(2,128)S(1)} %bitcast.16), channel_id=1, replica_groups=mesh['coarse'=8,'fine'=16] {'coarse','fine'}, dimensions={0} | all-to-all | bytes 262144 | tf_op jit(solution)/shard_map/all_to_all | solution.py:670
  79.8 1.4 %shard_map.112 = (f32[4,8,256]{2,1,0:T(8,128)}, f32[16,4,8,256]{3,2,1,0:T(8,128)}) custom-call(f32[256,128]{1,0:T(8,128)S(1)} %bitcast.15, f32[4,8,256]{2,1,0:T(8,128)S(1)} %get-tuple-element.65.z1, f32[4,8,256]{2,1,0:T(8,128)S(1)} %get-tuple-element.57.p, f32[16,4,8,256]{3,2,1,0:T(8,128)S(1)} %copy-done, f32[16,4,8,256]{3,2,1,0:T(8,128)S(1)} %copy-done.1), custom_call_target="tpu_custom_call" | custom-call | flops 10000 | bytes 100000 | tf_op jit(solution)/shard_map/pallas_call | solution.py:734
  (26 shorter events, 0.1 us)
Async XLA Ops:
  0.6 7.9 %copy-start.2 = (s32[16384]{0:T(1024)S(1)}, s32[16384]{0:T(1024)}, u32[]{:S(2)}) copy-start(s32[16384]{0:T(1024)} %param.14) | copy-start | bytes 196612
  3.8 4.7 %copy-start.9 = (f32[2048]{0:T(1024)S(1)}, f32[2048]{0:T(1024)}, u32[]{:S(2)}) copy-start(f32[2048]{0:T(1024)} %param.17) | copy-start | bytes 24580
  3.8 19.2 %collective-permute-start.5 = (f32[128,256]{1,0:T(8,128)}, f32[128,256]{1,0:T(8,128)S(1)}, u32[]{:S(2)}, u32[]{:S(2)}) collective-permute-start(f32[128,256]{1,0:T(8,128)} %get-tuple-element.37.tab0), channel_id=1, source_target_pairs={{0,96},{16,112},{32,64},{48,80},{64,32},{80,48},{96,0},{112,16},{1... | collective-permute-start | bytes 393224 | tf_op jit(solution)/shard_map/ppermute | solution.py:697
  7.2 15.9 %collective-permute-start.3 = (f32[128,256]{1,0:T(8,128)}, f32[128,256]{1,0:T(8,128)S(1)}, u32[]{:S(2)}, u32[]{:S(2)}) collective-permute-start(f32[128,256]{1,0:T(8,128)} %get-tuple-element.37.tab0), channel_id=1, source_target_pairs={{0,64},{16,80},{32,96},{48,112},{64,0},{80,16},{96,32},{112,48},{1... | collective-permute-start | bytes 393224 | tf_op jit(solution)/shard_map/ppermute | solution.py:697
  7.7 15.8 %collective-permute-start.1 = (f32[128,256]{1,0:T(8,128)}, f32[128,256]{1,0:T(8,128)S(1)}, u32[]{:S(2)}, u32[]{:S(2)}) collective-permute-start(f32[128,256]{1,0:T(8,128)} %get-tuple-element.37.tab0), channel_id=1, source_target_pairs={{0,32},{16,48},{32,0},{48,16},{64,96},{80,112},{96,64},{112,80},{1... | collective-permute-start | bytes 393224 | tf_op jit(solution)/shard_map/ppermute | solution.py:697
  8.5 0.8 copy-start.7
  10.1 11.7 %copy-start.10 = (f32[168,256]{1,0:T(8,128)S(1)}, f32[168,256]{1,0:T(8,128)}, u32[]{:S(2)}) copy-start(f32[168,256]{1,0:T(8,128)} %get-tuple-element.38) | copy-start | bytes 516100
  10.1 13.4 %copy-start.11 = (f32[40,256]{1,0:T(8,128)S(1)}, f32[40,256]{1,0:T(8,128)}, u32[]{:S(2)}) copy-start(f32[40,256]{1,0:T(8,128)} %get-tuple-element.41) | copy-start | bytes 122884
  10.1 14.4 %copy-start.13 = (f32[8,256]{1,0:T(8,128)S(1)}, f32[8,256]{1,0:T(8,128)}, u32[]{:S(2)}) copy-start(f32[8,256]{1,0:T(8,128)} %get-tuple-element.48) | copy-start | bytes 24580
  10.1 15.7 %copy-start.12 = (f32[8,256]{1,0:T(8,128)S(1)}, f32[8,256]{1,0:T(8,128)}, u32[]{:S(2)}) copy-start(f32[8,256]{1,0:T(8,128)} %get-tuple-element.49) | copy-start | bytes 24580
  10.1 22.9 %copy-start.6 = (f32[128,256]{1,0:T(8,128)S(1)}, f32[128,256]{1,0:T(8,128)}, u32[]{:S(2)}) copy-start(f32[128,256]{1,0:T(8,128)} %get-tuple-element.37.tab0) | copy-start | bytes 393220
  10.2 22.9 %all-to-all-start = ((f32[128,4,128]{2,1,0:T(4,128)}), f32[128,4,128]{2,1,0:T(4,128)S(1)}, u32[]{:S(2)}, u32[]{:S(2)}) async-start(f32[128,4,128]{2,1,0:T(4,128)} %bitcast.3), calls=%async_computation | async-start | bytes 524288 | tf_op jit(solution)/shard_map/all_to_all | solution.py:670
  21.8 2.8 %collective-permute-start = (f32[168,256]{1,0:T(8,128)S(1)}, f32[168,256]{1,0:T(8,128)S(1)}, u32[]{:S(2)}, u32[]{:S(2)}) collective-permute-start(f32[168,256]{1,0:T(8,128)S(1)} %copy-done.10), channel_id=1, source_target_pairs={{0,16},{16,0},{32,48},{48,32},{64,80},{80,64},{96,112},{112,96},{1... | collective-permute-start | bytes 516104 | tf_op jit(solution)/shard_map/ppermute | solution.py:694
  22.9 2.9 %collective-permute-start.6 = (f32[128,256]{1,0:T(8,128)S(1)}, f32[128,256]{1,0:T(8,128)S(1)}, u32[]{:S(2)}, u32[]{:S(2)}) collective-permute-start(f32[128,256]{1,0:T(8,128)S(1)} %collective-permute-done.5.tab6), channel_id=1, source_target_pairs={{0,16},{16,0},{32,48},{48,32},{64,80},{80,64},{96,112},{112,96},{1... | collective-permute-start | bytes 393224 | tf_op jit(solution)/shard_map/ppermute | solution.py:698
  23.1 10.0 %collective-permute-start.4 = (f32[128,256]{1,0:T(8,128)S(1)}, f32[128,256]{1,0:T(8,128)S(1)}, u32[]{:S(2)}, u32[]{:S(2)}) collective-permute-start(f32[128,256]{1,0:T(8,128)S(1)} %collective-permute-done.3.tab4), channel_id=1, source_target_pairs={{0,16},{16,0},{32,48},{48,32},{64,80},{80,64},{96,112},{112,96},{1... | collective-permute-start | bytes 393224 | tf_op jit(solution)/shard_map/ppermute | solution.py:698
  23.5 9.6 %collective-permute-start.2 = (f32[128,256]{1,0:T(8,128)S(1)}, f32[128,256]{1,0:T(8,128)S(1)}, u32[]{:S(2)}, u32[]{:S(2)}) collective-permute-start(f32[128,256]{1,0:T(8,128)S(1)} %collective-permute-done.1.tab2), channel_id=1, source_target_pairs={{0,16},{16,0},{32,48},{48,32},{64,80},{80,64},{96,112},{112,96},{1... | collective-permute-start | bytes 393224 | tf_op jit(solution)/shard_map/ppermute | solution.py:698
  23.6 14.8 %collective-permute-start.7 = (f32[40,256]{1,0:T(8,128)S(1)}, f32[40,256]{1,0:T(8,128)S(1)}, u32[]{:S(2)}, u32[]{:S(2)}) collective-permute-start(f32[40,256]{1,0:T(8,128)S(1)} %copy-done.11), channel_id=1, source_target_pairs={{0,112},{1,113},{2,114},{3,115},{4,116},{5,117},{6,118},{7,119},{8... | collective-permute-start | bytes 122888 | tf_op jit(solution)/shard_map/ppermute | solution.py:661
  24.5 13.8 %collective-permute-start.12 = (f32[8,256]{1,0:T(8,128)S(1)}, f32[8,256]{1,0:T(8,128)S(1)}, u32[]{:S(2)}, u32[]{:S(2)}) collective-permute-start(f32[8,256]{1,0:T(8,128)S(1)} %copy-done.13), channel_id=1, source_target_pairs={{0,1},{1,0},{2,3},{3,2},{4,5},{5,4},{6,7},{7,6},{8,9},{9,8},{10,11... | collective-permute-start | bytes 24584 | tf_op jit(solution)/shard_map/ppermute | solution.py:666
  25.9 12.5 %collective-permute-start.13 = (f32[8,256]{1,0:T(8,128)S(1)}, f32[8,256]{1,0:T(8,128)S(1)}, u32[]{:S(2)}, u32[]{:S(2)}) collective-permute-start(f32[8,256]{1,0:T(8,128)S(1)} %copy-done.12), channel_id=1, source_target_pairs={{0,16},{1,2},{2,1},{3,4},{4,3},{5,6},{6,5},{7,8},{8,7},{9,10},{10,... | collective-permute-start | bytes 24584 | tf_op jit(solution)/shard_map/ppermute | solution.py:661
  33.0 5.4 %copy-start.3 = (f32[4,8,256]{2,1,0:T(8,128)S(1)}, f32[4,8,256]{2,1,0:T(8,128)}, u32[]{:S(2)}) copy-start(f32[4,8,256]{2,1,0:T(8,128)} %get-tuple-element.40.c) | copy-start | bytes 98308
  33.1 5.3 %copy-start.4 = (f32[4,8,256]{2,1,0:T(8,128)S(1)}, f32[4,8,256]{2,1,0:T(8,128)}, u32[]{:S(2)}) copy-start(f32[4,8,256]{2,1,0:T(8,128)} %get-tuple-element.36.ic) | copy-start | bytes 98308
  33.1 5.3 %copy-start.5 = (f32[4,8,256]{2,1,0:T(8,128)S(1)}, f32[4,8,256]{2,1,0:T(8,128)}, u32[]{:S(2)}) copy-start(f32[4,8,256]{2,1,0:T(8,128)} %get-tuple-element.35.zs) | copy-start | bytes 98308
  39.5 15.7 %all-to-all-start.1 = ((f32[128,4,128]{2,1,0:T(4,128)}), f32[128,4,128]{2,1,0:T(4,128)S(1)}, u32[]{:S(2)}, u32[]{:S(2)}) async-start(f32[128,4,128]{2,1,0:T(4,128)} %bitcast.5), calls=%async_computation.1 | async-start | bytes 524288 | tf_op jit(solution)/shard_map/all_to_all | solution.py:670
  43.7 2.1 %collective-permute-start.8 = (f32[16,256]{1,0:T(8,128)S(1)}, f32[16,256]{1,0:T(8,128)S(1)}, u32[]{:S(2)}, u32[]{:S(2)}) collective-permute-start(f32[16,256]{1,0:T(8,128)S(1)} %get-tuple-element.42), channel_id=1, source_target_pairs={{0,16},{1,17},{2,18},{3,19},{4,20},{5,21},{6,22},{7,23},{8,24},{9,... | collective-permute-start | bytes 49160 | tf_op jit(solution)/shard_map/ppermute | solution.py:666
  44.9 3.7 %collective-permute-start.9 = (f32[16,256]{1,0:T(8,128)S(1)}, f32[16,256]{1,0:T(8,128)S(1)}, u32[]{:S(2)}, u32[]{:S(2)}) collective-permute-start(f32[16,256]{1,0:T(8,128)S(1)} %get-tuple-element.43), channel_id=1, source_target_pairs={{0,112},{1,113},{2,114},{3,115},{4,116},{5,117},{6,118},{7,119},{8... | collective-permute-start | bytes 49160 | tf_op jit(solution)/shard_map/ppermute | solution.py:661
  48.7 9.2 %collective-permute-start.10 = (f32[64,256]{1,0:T(8,128)S(1)}, f32[64,256]{1,0:T(8,128)S(1)}, u32[]{:S(2)}, u32[]{:S(2)}) collective-permute-start(f32[64,256]{1,0:T(8,128)S(1)} %get-tuple-element.44), channel_id=1, source_target_pairs={{0,1},{1,0},{2,3},{3,2},{4,5},{5,4},{6,7},{7,6},{8,9},{9,8},{10,11... | collective-permute-start | bytes 196616 | tf_op jit(solution)/shard_map/ppermute | solution.py:666
  50.2 7.7 %collective-permute-start.11 = (f32[64,256]{1,0:T(8,128)S(1)}, f32[64,256]{1,0:T(8,128)S(1)}, u32[]{:S(2)}, u32[]{:S(2)}) collective-permute-start(f32[64,256]{1,0:T(8,128)S(1)} %get-tuple-element.45), channel_id=1, source_target_pairs={{0,16},{1,2},{2,1},{3,4},{4,3},{5,6},{6,5},{7,8},{8,7},{9,10},{10,... | collective-permute-start | bytes 196616 | tf_op jit(solution)/shard_map/ppermute | solution.py:661
  57.9 4.3 %copy-start.8 = (f32[4,8,256]{2,1,0:T(8,128)S(1)}, f32[4,8,256]{2,1,0:T(8,128)}, u32[]{:S(2)}) copy-start(f32[4,8,256]{2,1,0:T(8,128)} %get-tuple-element.34.s) | copy-start | bytes 98308
  57.9 21.9 %copy-start = (f32[16,4,8,256]{3,2,1,0:T(8,128)S(1)}, f32[16,4,8,256]{3,2,1,0:T(8,128)}, u32[]{:S(2)}) copy-start(f32[16,4,8,256]{3,2,1,0:T(8,128)} %s_old.1) | copy-start | bytes 1572868
  57.9 21.9 %copy-start.1 = (f32[16,4,8,256]{3,2,1,0:T(8,128)S(1)}, f32[16,4,8,256]{3,2,1,0:T(8,128)}, u32[]{:S(2)}) copy-start(f32[16,4,8,256]{3,2,1,0:T(8,128)} %rate.1) | copy-start | bytes 1572868
  58.3 1.6 %collective-permute-start.14 = (f32[8,256]{1,0:T(8,128)S(1)}, f32[8,256]{1,0:T(8,128)S(1)}, u32[]{:S(2)}, u32[]{:S(2)}) collective-permute-start(f32[8,256]{1,0:T(8,128)S(1)} %get-tuple-element.58), channel_id=1, source_target_pairs={{0,16},{1,17},{2,18},{3,19},{4,20},{5,21},{6,22},{7,23},{8,24},{9,... | collective-permute-start | bytes 24584 | tf_op jit(solution)/shard_map/ppermute | solution.py:666
  59.1 3.1 %collective-permute-start.15 = (f32[8,256]{1,0:T(8,128)S(1)}, f32[8,256]{1,0:T(8,128)S(1)}, u32[]{:S(2)}, u32[]{:S(2)}) collective-permute-start(f32[8,256]{1,0:T(8,128)S(1)} %get-tuple-element.59), channel_id=1, source_target_pairs={{0,112},{1,113},{2,114},{3,115},{4,116},{5,117},{6,118},{7,119},{8... | collective-permute-start | bytes 24584 | tf_op jit(solution)/shard_map/ppermute | solution.py:661

commit v6 on v5

--- a/solution.py
+++ b/solution.py
@@ -152,9 +152,9 @@
         zs_out[x] = 0.8 * source * inv
         smooth.append(0.8 * source * inv)
         inverse.append(inv)
-    xa, xb[...] = send_planes([(smooth, 3), (inverse, 2)])
+    xa, xb[...] = send_planes([(smooth, 4), (inverse, 3)])
     both[TABLE_ROWS:, :] = xa
-    ya[...], yb[...] = send_rims(smooth)
+    ya[...], yb[...] = send_rows(EARLY_ROWS, lambda f, x: (smooth, inverse)[f][x])
 
 
 def send_planes(fields):
@@ -164,10 +164,26 @@
     return jnp.where(even, upper, lower), jnp.where(even, lower, upper)
 
 
-def send_rims(planes):
+def ghost_rows(field, x):
+    return max(0, (4, 3, 3)[field] - max(0, -x, x - CX + 1))
+
+
+EARLY_ROWS = [(f, x) for f in range(2) for x in range(CX)]
+LATE_ROWS = [(f, x) for f in range(3) for x in range(-3, CX + 3) if ghost_rows(f, x) and (f, x) not in EARLY_ROWS]
+
+
+def row_of(rows, which):
+    return sum(ghost_rows(*w) for w in rows[: rows.index(which)])
+
+
+def row_count(rows):
+    return sum(ghost_rows(*w) for w in rows)
+
+
+def send_rows(rows, plane):
     even = (places()[1] & 1) == 0
-    upper = jnp.concatenate([p[CY - 1 : CY] for p in planes] * 2, axis=0)
-    lower = jnp.concatenate([p[0:1] for p in planes] * 2, axis=0)
+    upper = jnp.concatenate([plane(*w)[CY - ghost_rows(*w) :] for w in rows], axis=0)
+    lower = jnp.concatenate([plane(*w)[: ghost_rows(*w)] for w in rows], axis=0)
     return jnp.where(even, upper, lower), jnp.where(even, lower, upper)
 
 
@@ -351,7 +367,7 @@
     for x in range(CX):
         pe_out[x] = pe[x]
 
-    xa[...], xb[...] = send_planes([(pe, 2)])
+    xa[...], xb[...] = send_planes([(pe, 3)])
 
 
 def below_above(index, count, a, b):
@@ -372,17 +388,6 @@
         return jnp.where(even, first, second)
 
     return below, above
-
-
-def ghost_rows(field, x):
-    return max(0, (4, 3, 3)[field] - max(0, -x, x - CX + 1))
-
-
-def packed(fields):
-    return [(f, x, k) for f in fields for x in range(-3, CX + 3) for k in range(ghost_rows(f, x))]
-
-
-PACKED = packed((0, 1, 2))
 
 
 def with_ghosts(own, messages):
@@ -413,23 +418,12 @@
 def all_ghosts(own, x0a, x0b, x1a, x1b):
     early = below_above(places()[0], 8, x0a.at[TABLE_ROWS:], x0b)
     late = below_above(places()[0], 8, x1a, x1b)
-    return with_ghosts(own, ((*early, 0, 3), (*early, 3, 2), (*late, 0, 2)))
+    return with_ghosts(own, ((*early, 0, 4), (*early, 4, 3), (*late, 0, 3)))
 
 
 def widen_kernel(zs, ic, pe, x0a, x0b, x1a, x1b, ya, yb):
     plane = all_ghosts((zs, ic, pe), x0a, x0b, x1a, x1b)
-    even = (places()[1] & 1) == 0
-    upper, lower = [], []
-    for f in range(3):
-        for x in range(-3, CX + 3):
-            d = ghost_rows(f, x)
-            if d:
-                here = plane(f, x)
-                upper.append(here[CY - d :])
-                lower.append(here[:d])
-    upper, lower = jnp.concatenate(upper, axis=0), jnp.concatenate(lower, axis=0)
-    ya[...] = jnp.where(even, upper, lower)
-    yb[...] = jnp.where(even, lower, upper)
+    ya[...], yb[...] = send_rows(LATE_ROWS, plane)
 
 
 def early_kernel(count, beside, across, zs, ic, pe, c, xa, xb, ya, yb, pay):
@@ -441,10 +435,12 @@
     z1 = []
     for x in range(CX):
         mid = zs[x]
-        left = zs[x - 1] if x else below(2)
+        left = zs[x - 1] if x else below(3)
         right = zs[x + 1] if x + 1 < CX else above(0)
-        up = jnp.where(row == 0, near[x : x + 1], pltpu.roll(mid, 1, 0))
-        down = jnp.where(row == CY - 1, far[x : x + 1], pltpu.roll(mid, CY - 1, 0))
+        at = row_of(EARLY_ROWS, (0, x))
+        last = at + ghost_rows(0, x) - 1
+        up = jnp.where(row == 0, near[last : last + 1], pltpu.roll(mid, 1, 0))
+        down = jnp.where(row == CY - 1, far[at : at + 1], pltpu.roll(mid, CY - 1, 0))
         z1.append(1.2 * mid + 0.8 * ic[x] * couple(left, mid, right, up, down) + pe[x])
     image = []
     zero = jnp.zeros((CY, CZ), F32)
@@ -490,7 +486,7 @@
 
 
 def second_solve_kernel(
-    count, sums, gathered, order, plan, own, at_row, at_lane, counts, pe_out, pe_face, e_face
+    count, sums, gathered, order, plan, own, at_row, at_lane, counts, pe_out, pe_face, e_face, xa, xb
 ):
     n = count[0]
     low, high = add_neighbours(
@@ -506,6 +502,7 @@
         pe_out[x] = pe[x]
         pe_face[x : x + 1, :] = pe[x][0:1]
         pe_face[CX + x : CX + x + 1, :] = pe[x][CY - 1 : CY]
+    xa[...], xb[...] = send_planes([(pe, 1)])
     lane = iota((8, LANES), 1)
     group = lane >> 4
     cells = ((group & 3) * CY + jnp.where(group < 4, 0, CY - 1)) * CZ
@@ -516,12 +513,13 @@
 
 
 def direction_kernel(
-    zs, ic, pe, c, x0a, x0b, x1a, x1b, ya, yb, pe2,
-    z1_out, w1_out, p_out, sw_ghost, s_ghost, w_ghost, xa, xb,
+    zs, ic, pe, c, x0a, x0b, x1a, x1b, y0a, y0b, y1a, y1b, after,
+    z1_out, w1_out, sw_out, sw_beside, sw_ghost, s_ghost, w_ghost,
 ):
     place = places()
     middle = all_ghosts((zs, ic, pe), x0a, x0b, x1a, x1b)
-    near, far = [side(...) for side in below_above(place[1], 16, ya, yb)]
+    early = [side(...) for side in below_above(place[1], 16, y0a, y0b)]
+    late = [side(...) for side in below_above(place[1], 16, y1a, y1b)]
 
     def plane(field, x):
         d = ghost_rows(field, x)
@@ -529,56 +527,53 @@
         if not d:
             blank = jnp.zeros((8, CZ), F32)
             return jnp.concatenate([blank, here, blank], axis=0)
-        at = PACKED.index((field, x, 0))
-        parts = [near[at : at + d], here, far[at : at + d]]
-        if d < 8:
-            blank = jnp.zeros((8 - d, CZ), F32)
-            parts = [blank] + parts + [blank]
-        return jnp.concatenate(parts, axis=0)
+        rows, (near, far) = (EARLY_ROWS, early) if (field, x) in EARLY_ROWS else (LATE_ROWS, late)
+        at = row_of(rows, (field, x))
+        blank = jnp.zeros((8 - d, CZ), F32)
+        return jnp.concatenate([blank, near[at : at + d], here, far[at : at + d], blank], axis=0)
 
     def neighbours(get, x):
         mid = get(x)
         count = mid.shape[0]
         return couple(get(x - 1), mid, get(x + 1), pltpu.roll(mid, 1, 0), pltpu.roll(mid, count - 1, 0))
 
-    z = {x: plane(0, x) for x in range(-3, CX + 3)}
-    inv = {x: plane(1, x) for x in range(-2, CX + 2)}
+    z = {x: plane(0, x) for x in range(-4, CX + 4)}
+    inv = {x: plane(1, x) for x in range(-3, CX + 3)}
     first = {}
-    for x in range(-2, CX + 2):
+    for x in range(-3, CX + 3):
         first[x] = 1.2 * z[x] + 0.8 * inv[x] * neighbours(z.get, x) + plane(2, x)
     zw = {}
-    for x in range(-1, CX + 1):
+    for x in range(-2, CX + 2):
         beside = neighbours(first.get, x)
         zw[x] = 0.8 * (first[x] - inv[x] * beside)
         if 0 <= x < CX:
             z1_out[x] = first[x][8:16]
             w1_out[x] = c[x] * first[x][8:16] - beside[8:16]
-    p = []
-    for x in range(CX):
+    for x in range(-1, CX + 1):
         smooth = 1.2 * zw[x] + 0.8 * inv[x] * neighbours(zw.get, x)
-        p.append(smooth[8:16] + pe2[x])
-        p_out[x] = p[x]
+        if not 0 <= x < CX:
+            sw_beside[0 if x < 0 else 1] = smooth[8:16]
+            continue
+        sw_out[x] = smooth[8:16]
         for at, row in ((x, 7), (CX + x, 16)):
             iv = inv[x][row : row + 1]
             scale = jnp.where(iv > 0.0, 1.25 / jnp.where(iv > 0.0, iv, 1.0), 0.0)
             sw_ghost[at : at + 1, :] = smooth[row : row + 1]
             s_ghost[at : at + 1, :] = z[x][row : row + 1] * scale
             w_ghost[at : at + 1, :] = zw[x][row : row + 1] * scale
-    even = (place[0] & 1) == 0
-    xa[...] = jnp.where(even, p[CX - 1], p[0])
-    xb[...] = jnp.where(even, p[0], p[CX - 1])
-
-
-def products_kernel(s, w1, p, c, xa, xb, sw_ghost, s_ghost, w_ghost, pe_face, e_face, beside, pay):
+
+
+def products_kernel(
+    s, w1, sw, pe2, c, xa, xb, sw_beside, sw_ghost, s_ghost, w_ghost, pe_face, e_face, beside, pay
+):
     place = places()
     below, above = [side(...) for side in below_above(place[0], 8, xa, xb)]
     sums = [jnp.zeros((CY, CZ), F32) for _ in range(6)]
     row = iota((CY, CZ), 0)
     rims = [None] * (2 * CX)
+    p = [below + sw_beside[0], *(sw[x] + pe2[x] for x in range(CX)), above + sw_beside[1]]
     for x in range(CX):
-        mid = p[x]
-        left = p[x - 1] if x else below
-        right = p[x + 1] if x + 1 < CX else above
+        left, mid, right = p[x : x + 3]
         up = jnp.where(row == 0, sw_ghost[x : x + 1, :], pltpu.roll(mid, 1, 0))
         down = jnp.where(row == CY - 1, sw_ghost[CX + x : CX + x + 1, :], pltpu.roll(mid, CY - 1, 0))
         q = c[x] * mid - couple(left, mid, right, up, down)
@@ -601,7 +596,7 @@
         pay[pl.ds(8 * i, 8), :] = tile
 
 
-def update_kernel(parts, z1, p, s_old, rate, mobile, immobile):
+def update_kernel(parts, z1, smooth, pe2, s_old, rate, mobile, immobile):
     top = parts[pl.ds(0, DEVICES, stride=2), :]
     face = pltpu.roll(parts[pl.ds(1, DEVICES, stride=2), :], LANES // 2, 1)
     lane = iota((DEVICES, LANES), 1)
@@ -614,7 +609,7 @@
     y2 = (sq - factor * sw) / (qq - factor * wq)
     y1 = (sw - wq * y2) / ww
     for x in range(CX):
-        new = y1 * z1[x] + y2 * p[x]
+        new = y1 * z1[x] + y2 * (smooth[x] + pe2[x])
         mobile[x] = new
         for k in range(RATES):
             r = rate[k, x]
@@ -678,8 +673,8 @@
     c, ic, s, zs, tab, both, x0b, y0a, y0b = call(
         source_kernel, [SM, VM, HB, HB] + [VM] * 3,
         [
-            FIELD, FIELD, FIELD, FIELD, ((TABLE_ROWS, 256), F32), ((TABLE_ROWS + 40, 256), F32),
-            ((40, CZ), F32), ((CY, CZ), F32), ((CY, CZ), F32),
+            FIELD, FIELD, FIELD, FIELD, ((TABLE_ROWS, 256), F32), ((TABLE_ROWS + 7 * CY, 256), F32),
+            ((7 * CY, CZ), F32), ((row_count(EARLY_ROWS), CZ), F32), ((row_count(EARLY_ROWS), CZ), F32),
         ],
         scratch=[
             pltpu.VMEM((RATES, CX, CY, CZ), F32),
@@ -708,7 +703,7 @@
         [
             FIELD, ((KC + 1, 24, SLOTS), F32), ((8, SLOTS), F32), ((8, LANES), I32), ((8, LANES), I32),
             ((LANES, LANES), I32), ((8, LANES), I32), ((LANES, LANES), I32),
-            ((2 * CY, CZ), F32), ((2 * CY, CZ), F32),
+            ((3 * CY, CZ), F32), ((3 * CY, CZ), F32),
         ],
         scratch=[pltpu.VMEM((SHARDS * 32, SHARD_ROWS), BF16)],
     )(agg_count, gathered, order, *tabs)
@@ -717,23 +712,26 @@
         agg_count, beside, across, zs, ic, pe, c, both, x0b, y0a, y0b
     )
     sums = everyone(pay, 4)
-    ya, yb = call(widen_kernel, [VM] * 7, [((len(PACKED), CZ), F32)] * 2)(zs, ic, pe, both, x0b, x1a, x1b)
-    ya, yb = trade(ya, yb, "fine")
-
-    pe2, pe_face, e_face = call(
-        second_solve_kernel, [SM] + [VM] * 8, [FIELD, ((CY, CZ), F32), ((8, LANES), F32)], flops=100_000_000
+    y1a, y1b = call(widen_kernel, [VM] * 7, [((row_count(LATE_ROWS), CZ), F32)] * 2)(
+        zs, ic, pe, both, x0b, x1a, x1b
+    )
+    y1a, y1b = trade(y1a, y1b, "fine")
+
+    pe2, pe_face, e_face, xa, xb = call(
+        second_solve_kernel, [SM] + [VM] * 8,
+        [FIELD, ((CY, CZ), F32), ((8, LANES), F32), ((CY, CZ), F32), ((CY, CZ), F32)], flops=100_000_000,
     )(agg_count, sums, gathered, order, plan, own, at_row, at_lane, counts)
-    z1, w1, p, sw_ghost, s_ghost, w_ghost, xa, xb = call(
-        direction_kernel, [VM] * 11, [FIELD, FIELD, FIELD] + [((CY, CZ), F32)] * 5,
-    )(zs, ic, pe, c, both, x0b, x1a, x1b, ya, yb, pe2)
     xa, xb = trade(xa, xb, "coarse")
+    z1, w1, sw, sw_beside, sw_ghost, s_ghost, w_ghost = call(
+        direction_kernel, [VM] * 13, [FIELD, FIELD, FIELD, ((2, CY, CZ), F32)] + [((CY, CZ), F32)] * 3,
+    )(zs, ic, pe, c, both, x0b, x1a, x1b, y0a, y0b, y1a, y1b, e_face)
     (pay,) = call(
-        products_kernel, [VM] * 12, [((2 * DEVICES, LANES), F32)]
-    )(s, w1, p, c, xa, xb, sw_ghost, s_ghost, w_ghost, pe_face, e_face, beside)
+        products_kernel, [VM] * 14, [((2 * DEVICES, LANES), F32)]
+    )(s, w1, sw, pe2, c, xa, xb, sw_beside, sw_ghost, s_ghost, w_ghost, pe_face, e_face, beside)
     parts = everyone(pay, 2)
     mobile, immobile = call(
-        update_kernel, [VM] * 5, [FIELD, ((RATES, CX, CY, CZ), F32)]
-    )(parts, z1, p, s_old, rate_time)
+        update_kernel, [VM] * 6, [FIELD, ((RATES, CX, CY, CZ), F32)]
+    )(parts, z1, sw, pe2, s_old, rate_time)
     return mobile, immobile
 
 

time: 81.6 us -> 79.1 us (0.969)
  blocking collectives: 17.4 us -> 15.2 us
    all_to_all x1, blocking collectives: 17.4 us -> 15.2 us  [everyone(): moved = lax.all_to_all(pay.reshape(DEVICES, rows, LANES), BOTH, 0, 0)]
  transfers between devices with their start and end apart: 18 -> 18, of which waited for: 6 -> 6; matrix products, arithmetic and copies ran while one was open for 0% -> 0% of each run, Pallas kernels for 11% -> 12%
where the time goes in v6:
time: 79.1 us; the launch traced here: 78.7 us
  starting transfers between devices  31.3 us (40%)
  blocking collectives  15.2 us (19%)
  Pallas kernels  15.1 us (19%)
  waiting for transfers between devices  14.7 us (19%)
  between operations  1.51 us (2%)
  local copies, waits for them, and re-layouts  0.81 us (1%)
    all_to_all x2, starting transfers between devices, everyone(): moved = lax.all_to_all(pay.reshape(DEVICES, rows, LANES), BOTH, 0, 0)  15.8 us
    all_to_all x1, blocking collectives, everyone(): moved = lax.all_to_all(pay.reshape(DEVICES, rows, LANES), BOTH, 0, 0)  15.2 us
    all_to_all x2, waiting for transfers between devices, everyone(): moved = lax.all_to_all(pay.reshape(DEVICES, rows, LANES), BOTH, 0, 0)  8.94 us
    pallas_call x1, Pallas kernels, local(): call(first_kernel, [SM] + [VM] * 10, [FIELD, ((KC + 1, 24, SLOTS), F32),...  5.28 us
    ppermute x5, waiting for transfers between devices, swap_between(): return lax.ppermute(b, BOTH, swap_pairs(axis)[1])  5.24 us
    ppermute x5, starting transfers between devices, swap_between(): return lax.ppermute(b, BOTH, swap_pairs(axis)[1])  4.91 us
    ppermute x4, starting transfers between devices, trade(): return (lax.ppermute(a, BOTH, swap_pairs(axis)[0]), b)  4.77 us
    ppermute x3, starting transfers between devices, local(): shard = lax.ppermute(tab, 'coarse', [(i, i ^ hop) for i in range(8)])  4.06 us
  transfers between devices with their start and end apart: 18, of which 6 were waited for; matrix products, arithmetic and copies ran while one was open for 0% of the time, Pallas kernels for 12%

profile of v6, /device:TPU:1, one launch (start us, length us, event | category | flops | bytes accessed | tf_op | source)
XLA Modules:
  0.0 78.7 jit_solution(11635171365265782193)
XLA Ops:
  0.6 3.1 %shard_map.104 = (f32[4,8,256]{2,1,0:T(8,128)}, f32[4,8,256]{2,1,0:T(8,128)}, f32[4,8,256]{2,1,0:T(8,128)}, f32[4,8,256]{2,1,0:T(8,128)}, f32[128,256]{1,0:T(8,1...) custom-call(f32[16]{0:T(128)} %cap.1, f32[4,8,256]{2,1,0:T(8,128)} %c_old.1, ...), custom_call_target="tpu_custom_call" | custom-call | flops 10000 | bytes 100000 | tf_op jit(solution)/shard_map/pallas_call | solution.py:673
  3.8 0.0 copy-start.9
  3.8 3.4 %collective-permute-start.5 = (f32[128,256]{1,0:T(8,128)}, f32[128,256]{1,0:T(8,128)S(1)}, u32[]{:S(2)}, u32[]{:S(2)}) collective-permute-start(f32[128,256]{1,0:T(8,128)} %get-tuple-element.38.tab0), channel_id=1, source_target_pairs={{0,96},{16,112},{32,64},{48,80},{64,32},{80,48},{96,0},{112,16},{1... | collective-permute-start | bytes 393224 | tf_op jit(solution)/shard_map/ppermute | solution.py:692
  7.2 0.5 collective-permute-start.3
  7.7 0.1 collective-permute-start.1
  8.5 0.7 copy-done.6
  9.3 0.9 %shard_map.105 = f32[512,128]{1,0:T(8,128)} custom-call(s32[1]{0:T(128)S(6)} %copy.11.count, f32[4,8,256]{2,1,0:T(8,128)S(1)} %copy-done.6, f32[16,128]{1,0:T(8,128)S(1)} %bitcast.18, s32[128,128]{1,0:T(8,128)S(1)} %bitcast.12), custom_call_target="tpu_custom_call" | custom-call | flops 10000 | bytes 100000 | tf_op jit(solution)/shard_map/pallas_call | solution.py:696
  10.2 11.6 %all-to-all-start = ((f32[128,4,128]{2,1,0:T(4,128)}), f32[128,4,128]{2,1,0:T(4,128)S(1)}, u32[]{:S(2)}, u32[]{:S(2)}) async-start(f32[128,4,128]{2,1,0:T(4,128)} %bitcast.3), calls=%async_computation | async-start | bytes 524288 | tf_op jit(solution)/shard_map/all_to_all | solution.py:665
  21.8 1.1 %collective-permute-start = (f32[184,256]{1,0:T(8,128)S(1)}, f32[184,256]{1,0:T(8,128)S(1)}, u32[]{:S(2)}, u32[]{:S(2)}) collective-permute-start(f32[184,256]{1,0:T(8,128)S(1)} %copy-done.10), channel_id=1, source_target_pairs={{0,16},{16,0},{32,48},{48,32},{64,80},{80,64},{96,112},{112,96},{1... | collective-permute-start | bytes 565256 | tf_op jit(solution)/shard_map/ppermute | solution.py:689
  23.0 0.0 collective-permute-done.5.tab6
  23.0 0.1 collective-permute-start.6
  23.1 0.0 collective-permute-done.3.tab4
  23.1 0.4 collective-permute-start.4
  23.5 0.0 collective-permute-done.1.tab2
  23.5 0.1 collective-permute-start.2
  23.6 1.0 %collective-permute-start.7 = (f32[56,256]{1,0:T(8,128)S(1)}, f32[56,256]{1,0:T(8,128)S(1)}, u32[]{:S(2)}, u32[]{:S(2)}) collective-permute-start(f32[56,256]{1,0:T(8,128)S(1)} %copy-done.11), channel_id=1, source_target_pairs={{0,112},{1,113},{2,114},{3,115},{4,116},{5,117},{6,118},{7,119},{8... | collective-permute-start | bytes 172040 | tf_op jit(solution)/shard_map/ppermute | solution.py:656
  24.6 0.0 collective-permute-done.tab1.x0a.xa
  24.6 1.3 %collective-permute-start.10 = (f32[28,256]{1,0:T(8,128)S(1)}, f32[28,256]{1,0:T(8,128)S(1)}, u32[]{:S(2)}, u32[]{:S(2)}) collective-permute-start(f32[28,256]{1,0:T(8,128)S(1)} %copy-done.13), channel_id=1, source_target_pairs={{0,1},{1,0},{2,3},{3,2},{4,5},{5,4},{6,7},{7,6},{8,9},{9,8},{10,11... | collective-permute-start | bytes 86024 | tf_op jit(solution)/shard_map/ppermute | solution.py:661
  25.9 0.0 collective-permute-done.6.tab7
  25.9 1.7 %collective-permute-start.11 = (f32[28,256]{1,0:T(8,128)S(1)}, f32[28,256]{1,0:T(8,128)S(1)}, u32[]{:S(2)}, u32[]{:S(2)}) collective-permute-start(f32[28,256]{1,0:T(8,128)S(1)} %copy-done.12), channel_id=1, source_target_pairs={{0,16},{1,2},{2,1},{3,4},{4,3},{5,6},{6,5},{7,8},{8,7},{9,10},{10,... | collective-permute-start | bytes 86024 | tf_op jit(solution)/shard_map/ppermute | solution.py:656
  27.6 5.5 %all-to-all-done = f32[128,4,128]{2,1,0:T(4,128)S(1)} async-done(((f32[128,4,128]{2,1,0:T(4,128)}), f32[128,4,128]{2,1,0:T(4,128)S(1)}, u32[]{:S(2)}, u32[]{:S(2)}) %all-to-all-start) | async-done | bytes 262176 | tf_op jit(solution)/shard_map/all_to_all | solution.py:665
  33.1 0.0 collective-permute-done.4.tab5
  33.1 0.0 collective-permute-done.2.tab3
  33.1 0.0 copy-start.3
  33.1 5.3 %shard_map.106 = (f32[4,8,256]{2,1,0:T(8,128)S(1)}, f32[9,24,256]{2,1,0:T(8,128)S(1)}, f32[8,256]{1,0:T(8,128)S(1)}, s32[8,128]{1,0:T(8,128)S(1)}, s32[8,128]{1,...) custom-call(s32[1]{0:T(128)S(6)} %copy.11.count, ...), custom_call_target="tpu_custom_call" | custom-call | flops 10000 | bytes 100000 | tf_op jit(solution)/shard_map/pallas_call | solution.py:701
  38.4 0.0 collective-permute-done.7.x0b.xb
  38.5 1.1 %shard_map.108 = f32[512,128]{1,0:T(8,128)} custom-call(s32[1]{0:T(128)S(6)} %copy.11.count, s32[8,128]{1,0:T(8,128)S(1)} %get-tuple-element.49.beside, s32[8,128]{1,0:T(8,128)S(1)} %get-tuple-element.50.across, f32[4,8,256]{2,1,0:T(8,128)S(1)} %copy-done.5, f32[4,8,256]{2,1,0:T(8,128)S(1)} %copy-done.4, f32[4,8,256]{2,1,0:T(8,128)S(1)} %get-tuple-element.40.pe, ...), custom_call_target="tpu_custom_call" | custom-call | flops 10000 | bytes 100000 | tf_op jit(solution)/shard_map/pallas_call | solution.py:711
  39.5 4.2 %all-to-all-start.1 = ((f32[128,4,128]{2,1,0:T(4,128)}), f32[128,4,128]{2,1,0:T(4,128)S(1)}, u32[]{:S(2)}, u32[]{:S(2)}) async-start(f32[128,4,128]{2,1,0:T(4,128)} %bitcast.5), calls=%async_computation.1 | async-start | bytes 524288 | tf_op jit(solution)/shard_map/all_to_all | solution.py:665
  43.7 1.2 %collective-permute-start.8 = (f32[24,256]{1,0:T(8,128)S(1)}, f32[24,256]{1,0:T(8,128)S(1)}, u32[]{:S(2)}, u32[]{:S(2)}) collective-permute-start(f32[24,256]{1,0:T(8,128)S(1)} %get-tuple-element.43), channel_id=1, source_target_pairs={{0,16},{1,17},{2,18},{3,19},{4,20},{5,21},{6,22},{7,23},{8,24},{9,... | collective-permute-start | bytes 73736 | tf_op jit(solution)/shard_map/ppermute | solution.py:661
  44.9 0.7 collective-permute-start.9
  45.6 0.2 collective-permute-done.8.x1a
  45.8 3.0 %collective-permute-done.9.x1b = f32[24,256]{1,0:T(8,128)S(1)} collective-permute-done((f32[24,256]{1,0:T(8,128)S(1)}, f32[24,256]{1,0:T(8,128)S(1)}, u32[]{:S(2)}, u32[]{:S(2)}) %collective-permute-start.9) | collective-permute-done | bytes 24608 | tf_op jit(solution)/shard_map/ppermute | solution.py:656
  48.8 1.5 %collective-permute-start.12 = (f32[36,256]{1,0:T(8,128)S(1)}, f32[36,256]{1,0:T(8,128)S(1)}, u32[]{:S(2)}, u32[]{:S(2)}) collective-permute-start(f32[36,256]{1,0:T(8,128)S(1)} %get-tuple-element.47), channel_id=1, source_target_pairs={{0,1},{1,0},{2,3},{3,2},{4,5},{5,4},{6,7},{7,6},{8,9},{9,8},{10,11... | collective-permute-start | bytes 110600 | tf_op jit(solution)/shard_map/ppermute | solution.py:661
  50.3 1.6 %collective-permute-start.13 = (f32[36,256]{1,0:T(8,128)S(1)}, f32[36,256]{1,0:T(8,128)S(1)}, u32[]{:S(2)}, u32[]{:S(2)}) collective-permute-start(f32[36,256]{1,0:T(8,128)S(1)} %get-tuple-element.48), channel_id=1, source_target_pairs={{0,16},{1,2},{2,1},{3,4},{4,3},{5,6},{6,5},{7,8},{8,7},{9,10},{10,... | collective-permute-start | bytes 110600 | tf_op jit(solution)/shard_map/ppermute | solution.py:656
  51.8 3.5 %all-to-all-done.1 = f32[128,4,128]{2,1,0:T(4,128)S(1)} async-done(((f32[128,4,128]{2,1,0:T(4,128)}), f32[128,4,128]{2,1,0:T(4,128)S(1)}, u32[]{:S(2)}, u32[]{:S(2)}) %all-to-all-start.1) | async-done | bytes 262176 | tf_op jit(solution)/shard_map/all_to_all | solution.py:665
  55.3 2.7 %shard_map.109 = (f32[4,8,256]{2,1,0:T(8,128)S(1)}, f32[8,256]{1,0:T(8,128)S(1)}, f32[8,128]{1,0:T(8,128)S(1)}, f32[8,256]{1,0:T(8,128)S(1)}, f32[8,256]{1,0:T(8,128)S(1)}) custom-call(s32[1]{0:T(128)S(6)} %copy.11.count, f32[512,128]{1,0:T(8,128)S(1)} %bitcast.11, f32[512,128]{1,0:T(8,128)S(1)} %bitcast.10, s32[128,128]{1,0:T(8,128)S(1)} %bitcast.14, ...), custom_call_target="tpu_custom_call" | custom-call | flops 100000000 | bytes 100000 | tf_op jit(solution)/shard_map/pallas_call | solution.py:720
  58.0 0.8 %collective-permute-start.14 = (f32[8,256]{1,0:T(8,128)S(1)}, f32[8,256]{1,0:T(8,128)S(1)}, u32[]{:S(2)}, u32[]{:S(2)}) collective-permute-start(f32[8,256]{1,0:T(8,128)S(1)} %get-tuple-element.60), channel_id=1, source_target_pairs={{0,16},{1,17},{2,18},{3,19},{4,20},{5,21},{6,22},{7,23},{8,24},{9,... | collective-permute-start | bytes 24584 | tf_op jit(solution)/shard_map/ppermute | solution.py:661
  58.8 0.0 collective-permute-start.15
  58.8 0.0 collective-permute-done.12.y1a
  58.8 0.0 collective-permute-done.13.y1b
  58.8 0.0 copy-start
  58.8 0.0 copy-start.1
  58.9 0.4 shard_map.110
  59.3 0.3 collective-permute-done.14.xa
  59.6 2.2 %collective-permute-done.15.xb = f32[8,256]{1,0:T(8,128)S(1)} collective-permute-done((f32[8,256]{1,0:T(8,128)S(1)}, f32[8,256]{1,0:T(8,128)S(1)}, u32[]{:S(2)}, u32[]{:S(2)}) %collective-permute-start.15) | collective-permute-done | bytes 8224 | tf_op jit(solution)/shard_map/ppermute | solution.py:656
  61.9 0.2 shard_map.111
  62.1 15.2 %all_to_all.15 = f32[128,2,128]{2,1,0:T(2,128)S(1)} all-to-all(f32[128,2,128]{2,1,0:T(2,128)S(1)} %bitcast.15), channel_id=1, replica_groups=mesh['coarse'=8,'fine'=16] {'coarse','fine'}, dimensions={0} | all-to-all | bytes 262144 | tf_op jit(solution)/shard_map/all_to_all | solution.py:665
  77.3 1.4 %shard_map.112 = (f32[4,8,256]{2,1,0:T(8,128)}, f32[16,4,8,256]{3,2,1,0:T(8,128)}) custom-call(f32[256,128]{1,0:T(8,128)S(1)} %bitcast.16, f32[4,8,256]{2,1,0:T(8,128)S(1)} %get-tuple-element.67.z1, f32[4,8,256]{2,1,0:T(8,128)S(1)} %get-tuple-element.58.sw.smooth, f32[4,8,256]{2,1,0:T(8,128)S(1)} %get-tuple-element.59.pe2, f32[16,4,8,256]{3,2,1,0:T(8,128)S(1)} %copy-done, ...), custom_call_target="tpu_custom_call" | custom-call | flops 10000 | bytes 100000 | tf_op jit(solution)/shard_map/pallas_call | solution.py:732
  (26 shorter events, 0.1 us)
Async XLA Ops:
  0.6 7.9 %copy-start.2 = (s32[16384]{0:T(1024)S(1)}, s32[16384]{0:T(1024)}, u32[]{:S(2)}) copy-start(s32[16384]{0:T(1024)} %param.14) | copy-start | bytes 196612
  3.8 4.7 %copy-start.9 = (f32[2048]{0:T(1024)S(1)}, f32[2048]{0:T(1024)}, u32[]{:S(2)}) copy-start(f32[2048]{0:T(1024)} %param.17) | copy-start | bytes 24580
  3.8 19.2 %collective-permute-start.5 = (f32[128,256]{1,0:T(8,128)}, f32[128,256]{1,0:T(8,128)S(1)}, u32[]{:S(2)}, u32[]{:S(2)}) collective-permute-start(f32[128,256]{1,0:T(8,128)} %get-tuple-element.38.tab0), channel_id=1, source_target_pairs={{0,96},{16,112},{32,64},{48,80},{64,32},{80,48},{96,0},{112,16},{1... | collective-permute-start | bytes 393224 | tf_op jit(solution)/shard_map/ppermute | solution.py:692
  7.2 15.9 %collective-permute-start.3 = (f32[128,256]{1,0:T(8,128)}, f32[128,256]{1,0:T(8,128)S(1)}, u32[]{:S(2)}, u32[]{:S(2)}) collective-permute-start(f32[128,256]{1,0:T(8,128)} %get-tuple-element.38.tab0), channel_id=1, source_target_pairs={{0,64},{16,80},{32,96},{48,112},{64,0},{80,16},{96,32},{112,48},{1... | collective-permute-start | bytes 393224 | tf_op jit(solution)/shard_map/ppermute | solution.py:692
  7.7 15.8 %collective-permute-start.1 = (f32[128,256]{1,0:T(8,128)}, f32[128,256]{1,0:T(8,128)S(1)}, u32[]{:S(2)}, u32[]{:S(2)}) collective-permute-start(f32[128,256]{1,0:T(8,128)} %get-tuple-element.38.tab0), channel_id=1, source_target_pairs={{0,32},{16,48},{32,0},{48,16},{64,96},{80,112},{96,64},{112,80},{1... | collective-permute-start | bytes 393224 | tf_op jit(solution)/shard_map/ppermute | solution.py:692
  8.5 0.8 copy-start.6
  10.2 11.7 %copy-start.10 = (f32[184,256]{1,0:T(8,128)S(1)}, f32[184,256]{1,0:T(8,128)}, u32[]{:S(2)}) copy-start(f32[184,256]{1,0:T(8,128)} %get-tuple-element.39) | copy-start | bytes 565252
  10.2 13.4 %copy-start.11 = (f32[56,256]{1,0:T(8,128)S(1)}, f32[56,256]{1,0:T(8,128)}, u32[]{:S(2)}) copy-start(f32[56,256]{1,0:T(8,128)} %get-tuple-element.42) | copy-start | bytes 172036
  10.2 14.4 %copy-start.13 = (f32[28,256]{1,0:T(8,128)S(1)}, f32[28,256]{1,0:T(8,128)}, u32[]{:S(2)}) copy-start(f32[28,256]{1,0:T(8,128)} %get-tuple-element.45) | copy-start | bytes 86020
  10.2 15.7 %copy-start.12 = (f32[28,256]{1,0:T(8,128)S(1)}, f32[28,256]{1,0:T(8,128)}, u32[]{:S(2)}) copy-start(f32[28,256]{1,0:T(8,128)} %get-tuple-element.46) | copy-start | bytes 86020
  10.2 22.9 %copy-start.8 = (f32[128,256]{1,0:T(8,128)S(1)}, f32[128,256]{1,0:T(8,128)}, u32[]{:S(2)}) copy-start(f32[128,256]{1,0:T(8,128)} %get-tuple-element.38.tab0) | copy-start | bytes 393220
  10.2 22.9 %all-to-all-start = ((f32[128,4,128]{2,1,0:T(4,128)}), f32[128,4,128]{2,1,0:T(4,128)S(1)}, u32[]{:S(2)}, u32[]{:S(2)}) async-start(f32[128,4,128]{2,1,0:T(4,128)} %bitcast.3), calls=%async_computation | async-start | bytes 524288 | tf_op jit(solution)/shard_map/all_to_all | solution.py:665
  21.8 2.8 %collective-permute-start = (f32[184,256]{1,0:T(8,128)S(1)}, f32[184,256]{1,0:T(8,128)S(1)}, u32[]{:S(2)}, u32[]{:S(2)}) collective-permute-start(f32[184,256]{1,0:T(8,128)S(1)} %copy-done.10), channel_id=1, source_target_pairs={{0,16},{16,0},{32,48},{48,32},{64,80},{80,64},{96,112},{112,96},{1... | collective-permute-start | bytes 565256 | tf_op jit(solution)/shard_map/ppermute | solution.py:689
  23.0 2.9 %collective-permute-start.6 = (f32[128,256]{1,0:T(8,128)S(1)}, f32[128,256]{1,0:T(8,128)S(1)}, u32[]{:S(2)}, u32[]{:S(2)}) collective-permute-start(f32[128,256]{1,0:T(8,128)S(1)} %collective-permute-done.5.tab6), channel_id=1, source_target_pairs={{0,16},{16,0},{32,48},{48,32},{64,80},{80,64},{96,112},{112,96},{1... | collective-permute-start | bytes 393224 | tf_op jit(solution)/shard_map/ppermute | solution.py:693
  23.1 10.0 %collective-permute-start.4 = (f32[128,256]{1,0:T(8,128)S(1)}, f32[128,256]{1,0:T(8,128)S(1)}, u32[]{:S(2)}, u32[]{:S(2)}) collective-permute-start(f32[128,256]{1,0:T(8,128)S(1)} %collective-permute-done.3.tab4), channel_id=1, source_target_pairs={{0,16},{16,0},{32,48},{48,32},{64,80},{80,64},{96,112},{112,96},{1... | collective-permute-start | bytes 393224 | tf_op jit(solution)/shard_map/ppermute | solution.py:693
  23.5 9.6 %collective-permute-start.2 = (f32[128,256]{1,0:T(8,128)S(1)}, f32[128,256]{1,0:T(8,128)S(1)}, u32[]{:S(2)}, u32[]{:S(2)}) collective-permute-start(f32[128,256]{1,0:T(8,128)S(1)} %collective-permute-done.1.tab2), channel_id=1, source_target_pairs={{0,16},{16,0},{32,48},{48,32},{64,80},{80,64},{96,112},{112,96},{1... | collective-permute-start | bytes 393224 | tf_op jit(solution)/shard_map/ppermute | solution.py:693
  23.6 14.8 %collective-permute-start.7 = (f32[56,256]{1,0:T(8,128)S(1)}, f32[56,256]{1,0:T(8,128)S(1)}, u32[]{:S(2)}, u32[]{:S(2)}) collective-permute-start(f32[56,256]{1,0:T(8,128)S(1)} %copy-done.11), channel_id=1, source_target_pairs={{0,112},{1,113},{2,114},{3,115},{4,116},{5,117},{6,118},{7,119},{8... | collective-permute-start | bytes 172040 | tf_op jit(solution)/shard_map/ppermute | solution.py:656
  24.6 13.8 %collective-permute-start.10 = (f32[28,256]{1,0:T(8,128)S(1)}, f32[28,256]{1,0:T(8,128)S(1)}, u32[]{:S(2)}, u32[]{:S(2)}) collective-permute-start(f32[28,256]{1,0:T(8,128)S(1)} %copy-done.13), channel_id=1, source_target_pairs={{0,1},{1,0},{2,3},{3,2},{4,5},{5,4},{6,7},{7,6},{8,9},{9,8},{10,11... | collective-permute-start | bytes 86024 | tf_op jit(solution)/shard_map/ppermute | solution.py:661
  25.9 12.5 %collective-permute-start.11 = (f32[28,256]{1,0:T(8,128)S(1)}, f32[28,256]{1,0:T(8,128)S(1)}, u32[]{:S(2)}, u32[]{:S(2)}) collective-permute-start(f32[28,256]{1,0:T(8,128)S(1)} %copy-done.12), channel_id=1, source_target_pairs={{0,16},{1,2},{2,1},{3,4},{4,3},{5,6},{6,5},{7,8},{8,7},{9,10},{10,... | collective-permute-start | bytes 86024 | tf_op jit(solution)/shard_map/ppermute | solution.py:656
  33.1 5.3 %copy-start.3 = (f32[4,8,256]{2,1,0:T(8,128)S(1)}, f32[4,8,256]{2,1,0:T(8,128)}, u32[]{:S(2)}) copy-start(f32[4,8,256]{2,1,0:T(8,128)} %get-tuple-element.41.c) | copy-start | bytes 98308
  33.1 5.3 %copy-start.4 = (f32[4,8,256]{2,1,0:T(8,128)S(1)}, f32[4,8,256]{2,1,0:T(8,128)}, u32[]{:S(2)}) copy-start(f32[4,8,256]{2,1,0:T(8,128)} %get-tuple-element.37.ic) | copy-start | bytes 98308
  33.1 5.3 %copy-start.5 = (f32[4,8,256]{2,1,0:T(8,128)S(1)}, f32[4,8,256]{2,1,0:T(8,128)}, u32[]{:S(2)}) copy-start(f32[4,8,256]{2,1,0:T(8,128)} %get-tuple-element.36.zs) | copy-start | bytes 98308
  39.5 15.8 %all-to-all-start.1 = ((f32[128,4,128]{2,1,0:T(4,128)}), f32[128,4,128]{2,1,0:T(4,128)S(1)}, u32[]{:S(2)}, u32[]{:S(2)}) async-start(f32[128,4,128]{2,1,0:T(4,128)} %bitcast.5), calls=%async_computation.1 | async-start | bytes 524288 | tf_op jit(solution)/shard_map/all_to_all | solution.py:665
  43.7 2.1 %collective-permute-start.8 = (f32[24,256]{1,0:T(8,128)S(1)}, f32[24,256]{1,0:T(8,128)S(1)}, u32[]{:S(2)}, u32[]{:S(2)}) collective-permute-start(f32[24,256]{1,0:T(8,128)S(1)} %get-tuple-element.43), channel_id=1, source_target_pairs={{0,16},{1,17},{2,18},{3,19},{4,20},{5,21},{6,22},{7,23},{8,24},{9,... | collective-permute-start | bytes 73736 | tf_op jit(solution)/shard_map/ppermute | solution.py:661
  44.9 3.8 %collective-permute-start.9 = (f32[24,256]{1,0:T(8,128)S(1)}, f32[24,256]{1,0:T(8,128)S(1)}, u32[]{:S(2)}, u32[]{:S(2)}) collective-permute-start(f32[24,256]{1,0:T(8,128)S(1)} %get-tuple-element.44), channel_id=1, source_target_pairs={{0,112},{1,113},{2,114},{3,115},{4,116},{5,117},{6,118},{7,119},{8... | collective-permute-start | bytes 73736 | tf_op jit(solution)/shard_map/ppermute | solution.py:656
  48.8 10.0 %collective-permute-start.12 = (f32[36,256]{1,0:T(8,128)S(1)}, f32[36,256]{1,0:T(8,128)S(1)}, u32[]{:S(2)}, u32[]{:S(2)}) collective-permute-start(f32[36,256]{1,0:T(8,128)S(1)} %get-tuple-element.47), channel_id=1, source_target_pairs={{0,1},{1,0},{2,3},{3,2},{4,5},{5,4},{6,7},{7,6},{8,9},{9,8},{10,11... | collective-permute-start | bytes 110600 | tf_op jit(solution)/shard_map/ppermute | solution.py:661
  50.3 8.5 %collective-permute-start.13 = (f32[36,256]{1,0:T(8,128)S(1)}, f32[36,256]{1,0:T(8,128)S(1)}, u32[]{:S(2)}, u32[]{:S(2)}) collective-permute-start(f32[36,256]{1,0:T(8,128)S(1)} %get-tuple-element.48), channel_id=1, source_target_pairs={{0,16},{1,2},{2,1},{3,4},{4,3},{5,6},{6,5},{7,8},{8,7},{9,10},{10,... | collective-permute-start | bytes 110600 | tf_op jit(solution)/shard_map/ppermute | solution.py:656
  58.0 1.6 %collective-permute-start.14 = (f32[8,256]{1,0:T(8,128)S(1)}, f32[8,256]{1,0:T(8,128)S(1)}, u32[]{:S(2)}, u32[]{:S(2)}) collective-permute-start(f32[8,256]{1,0:T(8,128)S(1)} %get-tuple-element.60), channel_id=1, source_target_pairs={{0,16},{1,17},{2,18},{3,19},{4,20},{5,21},{6,22},{7,23},{8,24},{9,... | collective-permute-start | bytes 24584 | tf_op jit(solution)/shard_map/ppermute | solution.py:661
  58.8 3.1 %collective-permute-start.15 = (f32[8,256]{1,0:T(8,128)S(1)}, f32[8,256]{1,0:T(8,128)S(1)}, u32[]{:S(2)}, u32[]{:S(2)}) collective-permute-start(f32[8,256]{1,0:T(8,128)S(1)} %get-tuple-element.61), channel_id=1, source_target_pairs={{0,112},{1,113},{2,114},{3,115},{4,116},{5,117},{6,118},{7,119},{8... | collective-permute-start | bytes 24584 | tf_op jit(solution)/shard_map/ppermute | solution.py:656
  58.8 3.0 %copy-start.7 = (f32[4,8,256]{2,1,0:T(8,128)S(1)}, f32[4,8,256]{2,1,0:T(8,128)}, u32[]{:S(2)}) copy-start(f32[4,8,256]{2,1,0:T(8,128)} %get-tuple-element.35.s) | copy-start | bytes 98308
  58.8 18.5 %copy-start = (f32[16,4,8,256]{3,2,1,0:T(8,128)S(1)}, f32[16,4,8,256]{3,2,1,0:T(8,128)}, u32[]{:S(2)}) copy-start(f32[16,4,8,256]{3,2,1,0:T(8,128)} %s_old.1) | copy-start | bytes 1572868
  58.8 18.5 %copy-start.1 = (f32[16,4,8,256]{3,2,1,0:T(8,128)S(1)}, f32[16,4,8,256]{3,2,1,0:T(8,128)}, u32[]{:S(2)}) copy-start(f32[16,4,8,256]{3,2,1,0:T(8,128)} %rate.1) | copy-start | bytes 1572868

commit v7 on v6

--- a/solution.py
+++ b/solution.py
@@ -53,25 +53,25 @@
     return ((row * LANES + iota((CY, LANES), 1)) * count) >> 13
 
 
-def restrict_plane(values, plane, count, total, base):
-    slot = iota(total.shape, 1) + base
+def restrict_plane(values, plane, count, totals, base):
+    lane = iota((CY, LANES), 1)
     for half in range(2):
         part_of = values[:, half * LANES : (half + 1) * LANES]
-        row = (plane * CY + iota((CY, 1), 0)) * 2 + half
+        row = (plane * CY + iota((CY, LANES), 0)) * 2 + half
         first = (row * count) >> 6
         member = slots_of(plane, half, count) - first
-        relative = slot - first
+        relative = lane + (base - first)
         for k in range(5):
             part = jnp.sum(jnp.where(member == k, part_of, 0.0), axis=1, keepdims=True)
-            total = total + jnp.where(relative == k, part, 0.0)
-    return total
+            totals = [t + jnp.where(relative == k - LANES * i, part, 0.0) for i, t in enumerate(totals)]
+    return totals
 
 
 def restrict(cells, count):
-    total = jnp.zeros((CY, SLOTS), F32)
+    totals = [jnp.zeros((CY, LANES), F32)] * 2
     for plane in range(CX):
-        total = restrict_plane(cells[plane], plane, count, total, 0)
-    return jnp.sum(total, axis=0, keepdims=True)
+        totals = restrict_plane(cells[plane], plane, count, totals, 0)
+    return [jnp.sum(t, axis=0, keepdims=True) for t in totals]
 
 
 def rim_restrict(rim, count):
@@ -115,8 +115,8 @@
 
 
 def source_kernel(
-    cap, c_old, s_old_hbm, rate_hbm, diag, cols, off,
-    c_out, ic_out, s_out, zs_out, tab, both, xb, ya, yb, s_old, rate, sems,
+    cap, count, c_old, s_old_hbm, rate_hbm, diag, cols, off, diag_rows, order,
+    c_out, ic_out, s_out, zs_out, tab, both, xb, ya, yb, pay, s_old, rate, sems,
 ):
     copies = []
     for x in range(CX):
@@ -132,7 +132,14 @@
         part = jnp.concatenate([cols[:, at].astype(F32), off[:, at] * (0.8 / diag[:, at])], axis=0)
         tab[16 * j : 16 * j + 16, :] = part
         both[16 * j : 16 * j + 16, :] = part
-    smooth, inverse = [], []
+    place = places()
+    n = jnp.full((CY, LANES), count[0], I32)
+    mine = (order[0:1, :] >> 7) == place[0] * 16 + place[1]
+    low = jnp.sum(jnp.where(mine, (order[...] & 127).astype(F32), 0.0), axis=1, keepdims=True)
+    spot = iota((LANES, LANES), 1).astype(F32) == low
+    at_place = jnp.sum(jnp.where(spot, iota((LANES, LANES), 0).astype(F32), 0.0), axis=0, keepdims=True)
+    shares = [jnp.broadcast_to(cap[0:1, k : k + 1], (CY, CZ)) for k in range(RATES)]
+    smooth, inverse, sources = [], [], []
     for x in range(CX):
         for copy in copies[x]:
             copy.wait()
@@ -140,7 +147,7 @@
         extra = jnp.zeros((CY, CZ), F32)
         for k in range(RATES):
             r = rate[k, x]
-            weighted = cap[k] * (r / (1.0 + r))
+            weighted = shares[k] * (r / (1.0 + r))
             mass = mass + weighted
             extra = extra + weighted * s_old[k, x]
         centre = (1.0 + mass) + FLOW
@@ -152,9 +159,13 @@
         zs_out[x] = 0.8 * source * inv
         smooth.append(0.8 * source * inv)
         inverse.append(inv)
+        sources.append(source)
     xa, xb[...] = send_planes([(smooth, 4), (inverse, 3)])
     both[TABLE_ROWS:, :] = xa
     ya[...], yb[...] = send_rows(EARLY_ROWS, lambda f, x: (smooth, inverse)[f][x])
+    slot = iota((1, LANES), 1)
+    sums = [jnp.where(slot + LANES * i < n[0:1], t, UNUSED) for i, t in enumerate(restrict(sources, n))]
+    repeat4(pay, [*sums, diag_rows[pl.ds(place[1], 1), :], at_place])
 
 
 def send_planes(fields):
@@ -185,17 +196,6 @@
     upper = jnp.concatenate([plane(*w)[CY - ghost_rows(*w) :] for w in rows], axis=0)
     lower = jnp.concatenate([plane(*w)[: ghost_rows(*w)] for w in rows], axis=0)
     return jnp.where(even, upper, lower), jnp.where(even, lower, upper)
-
-
-def sums_kernel(count, s, diag, order, pay):
-    place = places()
-    n = count[0]
-    mine = (order[0:1, :] >> 7) == place[0] * 16 + place[1]
-    low = jnp.sum(jnp.where(mine, (order[...] & 127).astype(F32), 0.0), axis=1, keepdims=True)
-    spot = iota((LANES, LANES), 1).astype(F32) == low
-    inverse = jnp.sum(jnp.where(spot, iota((LANES, LANES), 0).astype(F32), 0.0), axis=0, keepdims=True)
-    sums = jnp.where(iota((1, SLOTS), 1) < n, restrict([s[x] for x in range(CX)], n), UNUSED)
-    repeat4(pay, [sums[:, :LANES], sums[:, LANES:], diag[pl.ds(place[1], 1), :], inverse])
 
 
 def repeat4(pay, rows):
@@ -306,11 +306,10 @@
 
 
 def first_kernel(
-    count, gathered, order, tab0, tab1, tab2, tab3, tab4, tab5, tab6, tab7,
-    pe_out, plan, own, beside, across, at_row, at_lane, counts_out, xa, xb, table,
+    gathered, order, tab0, tab1, tab2, tab3, tab4, tab5, tab6, tab7,
+    pe_out, plan, own, own_count, beside, across, at_row, at_lane, counts_out, xa, xb, table,
 ):
     place = places()
-    n = count[0]
     me = place[0] * 16 + place[1]
     low, high, diag, inverse, counts = read_sums(gathered)
     offsets = offsets_of(counts)
@@ -324,10 +323,16 @@
     counts = jnp.broadcast_to(counts, (LANES, LANES))
     counts_out[...] = counts.astype(I32)
     row = iota((LANES, LANES), 0)
-    before = iota((8, LANES), 0) < 4
-    for out, step in ((beside, 1), (across, 16)):
-        sides = [jnp.sum(jnp.where(row == me + d, counts, 0.0), axis=0, keepdims=True) for d in (-step, step)]
-        out[...] = jnp.where(before, sides[0], sides[1]).astype(I32)
+
+    def count_of(device):
+        found = jnp.sum(jnp.where(row == device, counts, 0.0), axis=0, keepdims=True)
+        return jnp.broadcast_to(found, (8, LANES)).astype(I32)
+
+    n = count_of(me)
+    own_count[...] = n
+    beside[...] = jnp.where(iota((8, LANES), 0) < 4, count_of(me - 1), count_of(me + 1))
+    across[0] = count_of(me - 16)
+    across[1] = count_of(me + 16)
 
     tabs = (tab0, tab1, tab2, tab3, tab4, tab5, tab6, tab7)
     for g in range(SHARDS):
@@ -428,7 +433,7 @@
 
 def early_kernel(count, beside, across, zs, ic, pe, c, xa, xb, ya, yb, pay):
     place = places()
-    n = count[0]
+    n = count[...]
     below, above = below_above(place[0], 8, xa.at[TABLE_ROWS:], xb)
     near, far = [side(...) for side in below_above(place[1], 16, ya, yb)]
     row = iota((CY, CZ), 0)
@@ -452,17 +457,17 @@
         right = z1[x + 1] if x + 1 < CX else zero
         image.append(c[x] * mid - couple(left, mid, right, up, down))
     sums = restrict(image, n)
-    blank = jnp.zeros((CY, LANES), F32)
+    blank = [jnp.zeros((CY, LANES), F32)]
     lane = iota((1, LANES), 1)
-    under, over = across[0:1, 0:1], across[4:5, 0:1]
-    down_x = restrict_plane(-8.0 * z1[0], CX - 1, under, blank, (3 * under) >> 2)
-    up_x = restrict_plane(-8.0 * z1[CX - 1], 0, over, blank, 0)
+    under, over = across[0], across[1]
+    (down_x,) = restrict_plane(-8.0 * z1[0], CX - 1, under, blank, (3 * under) >> 2)
+    (up_x,) = restrict_plane(-8.0 * z1[CX - 1], 0, over, blank, 0)
     down_x = jnp.where(place[0] > 0, jnp.sum(down_x, axis=0, keepdims=True), 0.0)
     up_x = jnp.where(place[0] < 7, jnp.sum(up_x, axis=0, keepdims=True), 0.0)
     along_x = jnp.where(lane < 64, down_x, pltpu.roll(jnp.broadcast_to(up_x, (8, LANES)), 64, 1)[0:1])
     rims = jnp.concatenate([z[0:1] for z in z1] + [z[CY - 1 : CY] for z in z1], axis=0)
     along_y = rim_restrict(jnp.where(rim_exists(place[1]), -8.0 * rims, 0.0), beside[...])
-    repeat4(pay, [sums[:, :LANES], sums[:, LANES:], along_x, along_y])
+    repeat4(pay, [*sums, along_x, along_y])
 
 
 def add_neighbours(low, high, from_x, from_y, counts):
@@ -488,7 +493,7 @@
 def second_solve_kernel(
     count, sums, gathered, order, plan, own, at_row, at_lane, counts, pe_out, pe_face, e_face, xa, xb
 ):
-    n = count[0]
+    n = count[...]
     low, high = add_neighbours(
         sums[pl.ds(0, DEVICES, stride=4), :], sums[pl.ds(1, DEVICES, stride=4), :],
         sums[pl.ds(2, DEVICES, stride=4), :], sums[pl.ds(3, DEVICES, stride=4), :], counts[...],
@@ -670,11 +675,12 @@
     c_old, s_old, rate_time, capacity, agg_count, coarse_order, coarse_cols, coarse_off, coarse_diag
 ):
     order = coarse_order.reshape(LANES, LANES)
-    c, ic, s, zs, tab, both, x0b, y0a, y0b = call(
-        source_kernel, [SM, VM, HB, HB] + [VM] * 3,
+    c, ic, s, zs, tab, both, x0b, y0a, y0b, pay = call(
+        source_kernel, [VM, SM, VM, HB, HB] + [VM] * 5,
         [
             FIELD, FIELD, FIELD, FIELD, ((TABLE_ROWS, 256), F32), ((TABLE_ROWS + 7 * CY, 256), F32),
             ((7 * CY, CZ), F32), ((row_count(EARLY_ROWS), CZ), F32), ((row_count(EARLY_ROWS), CZ), F32),
+            ((4 * DEVICES, LANES), F32),
         ],
         scratch=[
             pltpu.VMEM((RATES, CX, CY, CZ), F32),
@@ -683,7 +689,8 @@
         ],
         vmem=SOURCE_VMEM,
     )(
-        capacity, c_old, s_old, rate_time, coarse_diag.reshape(1, SHARD_ROWS), coarse_cols, coarse_off,
+        capacity.reshape(1, RATES), agg_count, c_old, s_old, rate_time, coarse_diag.reshape(1, SHARD_ROWS), coarse_cols, coarse_off,
+        coarse_diag.reshape(16, LANES), order,
     )
     other_core = [(i, i ^ 1) for i in range(8)]
     both = lax.ppermute(both, "coarse", other_core)
@@ -693,23 +700,21 @@
         tabs += [shard, lax.ppermute(shard, "coarse", other_core)]
     x0b = swap_between(x0b, "coarse")
     y0a, y0b = trade(y0a, y0b, "fine")
-    (pay,) = call(sums_kernel, [SM] + [VM] * 3, [((4 * DEVICES, LANES), F32)])(
-        agg_count, s, coarse_diag.reshape(16, LANES), order
-    )
+    pay, x0b = lax.optimization_barrier((pay, x0b))
     gathered = everyone(pay, 4)
 
-    pe, plan, own, beside, across, at_row, at_lane, counts, x1a, x1b = call(
-        first_kernel, [SM] + [VM] * 10,
+    pe, plan, own, own_count, beside, across, at_row, at_lane, counts, x1a, x1b = call(
+        first_kernel, [VM] * 10,
         [
-            FIELD, ((KC + 1, 24, SLOTS), F32), ((8, SLOTS), F32), ((8, LANES), I32), ((8, LANES), I32),
+            FIELD, ((KC + 1, 24, SLOTS), F32), ((8, SLOTS), F32), ((8, LANES), I32), ((8, LANES), I32), ((2, 8, LANES), I32),
             ((LANES, LANES), I32), ((8, LANES), I32), ((LANES, LANES), I32),
             ((3 * CY, CZ), F32), ((3 * CY, CZ), F32),
         ],
         scratch=[pltpu.VMEM((SHARDS * 32, SHARD_ROWS), BF16)],
-    )(agg_count, gathered, order, *tabs)
+    )(gathered, order, *tabs)
     x1a, x1b = trade(x1a, x1b, "coarse")
-    (pay,) = call(early_kernel, [SM] + [VM] * 10, [((4 * DEVICES, LANES), F32)])(
-        agg_count, beside, across, zs, ic, pe, c, both, x0b, y0a, y0b
+    (pay,) = call(early_kernel, [VM] * 11, [((4 * DEVICES, LANES), F32)])(
+        own_count, beside, across, zs, ic, pe, c, both, x0b, y0a, y0b
     )
     sums = everyone(pay, 4)
     y1a, y1b = call(widen_kernel, [VM] * 7, [((row_count(LATE_ROWS), CZ), F32)] * 2)(
@@ -718,9 +723,9 @@
     y1a, y1b = trade(y1a, y1b, "fine")
 
     pe2, pe_face, e_face, xa, xb = call(
-        second_solve_kernel, [SM] + [VM] * 8,
+        second_solve_kernel, [VM] * 9,
         [FIELD, ((CY, CZ), F32), ((8, LANES), F32), ((CY, CZ), F32), ((CY, CZ), F32)], flops=100_000_000,
-    )(agg_count, sums, gathered, order, plan, own, at_row, at_lane, counts)
+    )(own_count, sums, gathered, order, plan, own, at_row, at_lane, counts)
     xa, xb = trade(xa, xb, "coarse")
     z1, w1, sw, sw_beside, sw_ghost, s_ghost, w_ghost = call(
         direction_kernel, [VM] * 13, [FIELD, FIELD, FIELD, ((2, CY, CZ), F32)] + [((CY, CZ), F32)] * 3,

time: 79.1 us -> 78 us (0.986)
  waiting for transfers between devices: 14.7 us -> 17.2 us
  starting transfers between devices: 31.3 us -> 29.4 us
    all_to_all x2, waiting for transfers between devices: 8.94 us -> 11.4 us  [everyone(): moved = lax.all_to_all(pay.reshape(DEVICES, rows, LANES), BOTH, 0, 0)]
    all_to_all x2, starting transfers between devices: 15.8 us -> 14.5 us  [everyone(): moved = lax.all_to_all(pay.reshape(DEVICES, rows, LANES), BOTH, 0, 0)]
    ppermute x3, starting transfers between devices: 4.06 us -> 3.25 us  [local(): shard = lax.ppermute(tab, 'coarse', [(i, i ^ hop) for i in range(8)])]
    pallas_call x5 -> x4, Pallas kernels: 13.1 us -> 12.3 us  [the longest x1 5.29 us: local(): call(first_kernel, [VM] * 10, [FIELD, ((KC + 1, 24, SLOTS), F32), ((8, SL...]
  transfers between devices with their start and end apart: 18 -> 18, of which waited for: 6 -> 6; matrix products, arithmetic and copies ran while one was open for 0% -> 0% of each run, Pallas kernels for 12% -> 11%
where the time goes in v7:
time: 78 us; the launch traced here: 77.7 us
  starting transfers between devices  29.4 us (38%)
  waiting for transfers between devices  17.2 us (22%)
  blocking collectives  15.2 us (19%)
  Pallas kernels  14.4 us (18%)
  between operations  1.46 us (2%)
    all_to_all x1, blocking collectives, everyone(): moved = lax.all_to_all(pay.reshape(DEVICES, rows, LANES), BOTH, 0, 0)  15.2 us
    all_to_all x2, starting transfers between devices, everyone(): moved = lax.all_to_all(pay.reshape(DEVICES, rows, LANES), BOTH, 0, 0)  14.5 us
    all_to_all x2, waiting for transfers between devices, everyone(): moved = lax.all_to_all(pay.reshape(DEVICES, rows, LANES), BOTH, 0, 0)  11.4 us
    ppermute x5, starting transfers between devices, swap_between(): return lax.ppermute(b, BOTH, swap_pairs(axis)[1])  5.58 us
    pallas_call x1, Pallas kernels, local(): call(first_kernel, [VM] * 10, [FIELD, ((KC + 1, 24, SLOTS), F32), ((8, SL...  5.29 us
    ppermute x5, waiting for transfers between devices, swap_between(): return lax.ppermute(b, BOTH, swap_pairs(axis)[1])  5.24 us
    ppermute x4, starting transfers between devices, trade(): return (lax.ppermute(a, BOTH, swap_pairs(axis)[0]), b)  4.31 us
    pallas_call x1, Pallas kernels, local(): call(source_kernel, [VM, SM, VM, HB, HB] + [VM] * 5, [FIELD, FIELD, FIELD...  3.3 us
  transfers between devices with their start and end apart: 18, of which 6 were waited for; matrix products, arithmetic and copies ran while one was open for 0% of the time, Pallas kernels for 11%

profile of v7, /device:TPU:1, one launch (start us, length us, event | category | flops | bytes accessed | tf_op | source)
XLA Modules:
  0.0 77.7 jit_solution(4978634692345989708)
XLA Ops:
  1.3 3.3 %shard_map.104 = (f32[4,8,256]{2,1,0:T(8,128)}, f32[4,8,256]{2,1,0:T(8,128)}, f32[4,8,256]{2,1,0:T(8,128)}, f32[4,8,256]{2,1,0:T(8,128)}, f32[128,256]{1,0:T(8,1...) custom-call(f32[1,16]{1,0:T(1,128)} %bitcast.21, ...), custom_call_target="tpu_custom_call" | custom-call | flops 10000 | bytes 100000 | tf_op jit(solution)/shard_map/pallas_call | solution.py:678
  4.6 2.7 %collective-permute-start = (f32[56,256]{1,0:T(8,128)}, f32[56,256]{1,0:T(8,128)S(1)}, u32[]{:S(2)}, u32[]{:S(2)}) collective-permute-start(f32[56,256]{1,0:T(8,128)} %get-tuple-element.43), channel_id=1, source_target_pairs={{0,112},{1,113},{2,114},{3,115},{4,116},{5,117},{6,118},{7,119},{8... | collective-permute-start | bytes 172040 | tf_op jit(solution)/shard_map/ppermute | solution.py:661
  7.3 1.4 %collective-permute-start.6 = (f32[128,256]{1,0:T(8,128)}, f32[128,256]{1,0:T(8,128)S(1)}, u32[]{:S(2)}, u32[]{:S(2)}) collective-permute-start(f32[128,256]{1,0:T(8,128)} %get-tuple-element.45.tab0), channel_id=1, source_target_pairs={{0,96},{16,112},{32,64},{48,80},{64,32},{80,48},{96,0},{112,16},{1... | collective-permute-start | bytes 393224 | tf_op jit(solution)/shard_map/ppermute | solution.py:699
  8.7 1.6 %collective-permute-start.4 = (f32[128,256]{1,0:T(8,128)}, f32[128,256]{1,0:T(8,128)S(1)}, u32[]{:S(2)}, u32[]{:S(2)}) collective-permute-start(f32[128,256]{1,0:T(8,128)} %get-tuple-element.45.tab0), channel_id=1, source_target_pairs={{0,64},{16,80},{32,96},{48,112},{64,0},{80,16},{96,32},{112,48},{1... | collective-permute-start | bytes 393224 | tf_op jit(solution)/shard_map/ppermute | solution.py:699
  10.3 0.3 collective-permute-start.2
  10.5 0.0 collective-permute-done.x0b.xb
  10.5 0.0 copy-start.2
  10.5 0.0 copy-start.6
  10.6 10.3 %all-to-all-start = ((f32[128,4,128]{2,1,0:T(4,128)}), f32[128,4,128]{2,1,0:T(4,128)S(1)}, u32[]{:S(2)}, u32[]{:S(2)}) async-start(f32[128,4,128]{2,1,0:T(4,128)} %bitcast.18), calls=%async_computation | async-start | bytes 524288 | tf_op jit(solution)/shard_map/all_to_all | solution.py:670
  20.8 1.1 %collective-permute-start.1 = (f32[184,256]{1,0:T(8,128)S(1)}, f32[184,256]{1,0:T(8,128)S(1)}, u32[]{:S(2)}, u32[]{:S(2)}) collective-permute-start(f32[184,256]{1,0:T(8,128)S(1)} %copy-done.8), channel_id=1, source_target_pairs={{0,16},{16,0},{32,48},{48,32},{64,80},{80,64},{96,112},{112,96},{1... | collective-permute-start | bytes 565256 | tf_op jit(solution)/shard_map/ppermute | solution.py:696
  22.0 0.0 collective-permute-done.6.tab6
  22.0 0.1 collective-permute-start.7
  22.1 0.0 collective-permute-done.4.tab4
  22.1 0.4 collective-permute-start.5
  22.5 0.0 collective-permute-done.2.tab2
  22.5 0.1 collective-permute-start.3
  22.6 0.8 %collective-permute-start.10 = (f32[28,256]{1,0:T(8,128)S(1)}, f32[28,256]{1,0:T(8,128)S(1)}, u32[]{:S(2)}, u32[]{:S(2)}) collective-permute-start(f32[28,256]{1,0:T(8,128)S(1)} %copy-done.10), channel_id=1, source_target_pairs={{0,1},{1,0},{2,3},{3,2},{4,5},{5,4},{6,7},{7,6},{8,9},{9,8},{10,11... | collective-permute-start | bytes 86024 | tf_op jit(solution)/shard_map/ppermute | solution.py:666
  23.5 0.0 collective-permute-done.1.tab1.x0a.xa
  23.5 0.6 collective-permute-start.11
  24.1 0.0 collective-permute-done.7.tab7
  24.1 0.0 collective-permute-done.5.tab5
  24.1 0.0 collective-permute-done.3.tab3
  24.1 8.0 %all-to-all-done = f32[128,4,128]{2,1,0:T(4,128)S(1)} async-done(((f32[128,4,128]{2,1,0:T(4,128)}), f32[128,4,128]{2,1,0:T(4,128)S(1)}, u32[]{:S(2)}, u32[]{:S(2)}) %all-to-all-start) | async-done | bytes 262176 | tf_op jit(solution)/shard_map/all_to_all | solution.py:670
  32.1 5.3 %shard_map.105 = (f32[4,8,256]{2,1,0:T(8,128)S(1)}, f32[9,24,256]{2,1,0:T(8,128)S(1)}, f32[8,256]{1,0:T(8,128)S(1)}, s32[8,128]{1,0:T(8,128)S(1)}, s32[8,128]{1,...) custom-call(f32[512,128]{1,0:T(8,128)S(1)} %bitcast.10, ...), custom_call_target="tpu_custom_call" | custom-call | flops 10000 | bytes 100000 | tf_op jit(solution)/shard_map/pallas_call | solution.py:706
  37.4 0.0 collective-permute-done.10.ya.y0a
  37.4 0.0 collective-permute-done.11.yb.y0b
  37.4 1.0 %shard_map.107 = f32[512,128]{1,0:T(8,128)} custom-call(s32[8,128]{1,0:T(8,128)S(1)} %get-tuple-element.56.count, s32[8,128]{1,0:T(8,128)S(1)} %get-tuple-element.57.beside, s32[2,8,128]{2,1,0:T(8,128)S(1)} %get-tuple-element.58.across, f32[4,8,256]{2,1,0:T(8,128)S(1)} %copy-done.5, f32[4,8,256]{2,1,0:T(8,128)S(1)} %copy-done.4, ...), custom_call_target="tpu_custom_call" | custom-call | flops 10000 | bytes 100000 | tf_op jit(solution)/shard_map/pallas_call | solution.py:716
  38.5 4.2 %all-to-all-start.1 = ((f32[128,4,128]{2,1,0:T(4,128)}), f32[128,4,128]{2,1,0:T(4,128)S(1)}, u32[]{:S(2)}, u32[]{:S(2)}) async-start(f32[128,4,128]{2,1,0:T(4,128)} %bitcast.6), calls=%async_computation.1 | async-start | bytes 524288 | tf_op jit(solution)/shard_map/all_to_all | solution.py:670
  42.7 1.2 %collective-permute-start.8 = (f32[24,256]{1,0:T(8,128)S(1)}, f32[24,256]{1,0:T(8,128)S(1)}, u32[]{:S(2)}, u32[]{:S(2)}) collective-permute-start(f32[24,256]{1,0:T(8,128)S(1)} %get-tuple-element.50), channel_id=1, source_target_pairs={{0,16},{1,17},{2,18},{3,19},{4,20},{5,21},{6,22},{7,23},{8,24},{9,... | collective-permute-start | bytes 73736 | tf_op jit(solution)/shard_map/ppermute | solution.py:666
  43.9 0.7 collective-permute-start.9
  44.5 0.2 collective-permute-done.8.x1a
  44.7 3.0 %collective-permute-done.9.x1b = f32[24,256]{1,0:T(8,128)S(1)} collective-permute-done((f32[24,256]{1,0:T(8,128)S(1)}, f32[24,256]{1,0:T(8,128)S(1)}, u32[]{:S(2)}, u32[]{:S(2)}) %collective-permute-start.9) | collective-permute-done | bytes 24608 | tf_op jit(solution)/shard_map/ppermute | solution.py:661
  47.7 1.5 %collective-permute-start.12 = (f32[36,256]{1,0:T(8,128)S(1)}, f32[36,256]{1,0:T(8,128)S(1)}, u32[]{:S(2)}, u32[]{:S(2)}) collective-permute-start(f32[36,256]{1,0:T(8,128)S(1)} %get-tuple-element.54), channel_id=1, source_target_pairs={{0,1},{1,0},{2,3},{3,2},{4,5},{5,4},{6,7},{7,6},{8,9},{9,8},{10,11... | collective-permute-start | bytes 110600 | tf_op jit(solution)/shard_map/ppermute | solution.py:666
  49.2 1.6 %collective-permute-start.13 = (f32[36,256]{1,0:T(8,128)S(1)}, f32[36,256]{1,0:T(8,128)S(1)}, u32[]{:S(2)}, u32[]{:S(2)}) collective-permute-start(f32[36,256]{1,0:T(8,128)S(1)} %get-tuple-element.55), channel_id=1, source_target_pairs={{0,16},{1,2},{2,1},{3,4},{4,3},{5,6},{6,5},{7,8},{8,7},{9,10},{10,... | collective-permute-start | bytes 110600 | tf_op jit(solution)/shard_map/ppermute | solution.py:661
  50.8 3.5 %all-to-all-done.1 = f32[128,4,128]{2,1,0:T(4,128)S(1)} async-done(((f32[128,4,128]{2,1,0:T(4,128)}), f32[128,4,128]{2,1,0:T(4,128)S(1)}, u32[]{:S(2)}, u32[]{:S(2)}) %all-to-all-start.1) | async-done | bytes 262176 | tf_op jit(solution)/shard_map/all_to_all | solution.py:670
  54.2 2.7 %shard_map.108 = (f32[4,8,256]{2,1,0:T(8,128)S(1)}, f32[8,256]{1,0:T(8,128)S(1)}, f32[8,128]{1,0:T(8,128)S(1)}, f32[8,256]{1,0:T(8,128)S(1)}, f32[8,256]{1,0:T(8,128)S(1)}) custom-call(s32[8,128]{1,0:T(8,128)S(1)} %get-tuple-element.56.count, f32[512,128]{1,0:T(8,128)S(1)} %bitcast.12, f32[512,128]{1,0:T(8,128)S(1)} %bitcast.11, s32[128,128]{1,0:T(8,128)S(1)} %bitcast.15, ...), custom_call_target="tpu_custom_call" | custom-call | flops 100000000 | bytes 100000 | tf_op jit(solution)/shard_map/pallas_call | solution.py:725
  56.9 0.8 %collective-permute-start.14 = (f32[8,256]{1,0:T(8,128)S(1)}, f32[8,256]{1,0:T(8,128)S(1)}, u32[]{:S(2)}, u32[]{:S(2)}) collective-permute-start(f32[8,256]{1,0:T(8,128)S(1)} %get-tuple-element.68), channel_id=1, source_target_pairs={{0,16},{1,17},{2,18},{3,19},{4,20},{5,21},{6,22},{7,23},{8,24},{9,... | collective-permute-start | bytes 24584 | tf_op jit(solution)/shard_map/ppermute | solution.py:666
  57.7 0.0 collective-permute-start.15
  57.8 0.0 collective-permute-done.12.y1a
  57.8 0.0 collective-permute-done.13.y1b
  57.8 0.0 copy-start
  57.8 0.0 copy-start.1
  57.8 0.4 shard_map.109
  58.2 0.3 collective-permute-done.14.xa
  58.5 2.2 %collective-permute-done.15.xb = f32[8,256]{1,0:T(8,128)S(1)} collective-permute-done((f32[8,256]{1,0:T(8,128)S(1)}, f32[8,256]{1,0:T(8,128)S(1)}, u32[]{:S(2)}, u32[]{:S(2)}) %collective-permute-start.15) | collective-permute-done | bytes 8224 | tf_op jit(solution)/shard_map/ppermute | solution.py:661
  60.8 0.2 shard_map.110
  61.0 15.2 %all_to_all.15 = f32[128,2,128]{2,1,0:T(2,128)S(1)} all-to-all(f32[128,2,128]{2,1,0:T(2,128)S(1)} %bitcast.16), channel_id=1, replica_groups=mesh['coarse'=8,'fine'=16] {'coarse','fine'}, dimensions={0} | all-to-all | bytes 262144 | tf_op jit(solution)/shard_map/all_to_all | solution.py:670
  76.3 1.4 %shard_map.111 = (f32[4,8,256]{2,1,0:T(8,128)}, f32[16,4,8,256]{3,2,1,0:T(8,128)}) custom-call(f32[256,128]{1,0:T(8,128)S(1)} %bitcast.17, f32[4,8,256]{2,1,0:T(8,128)S(1)} %get-tuple-element.75.z1, f32[4,8,256]{2,1,0:T(8,128)S(1)} %get-tuple-element.66.sw.smooth, f32[4,8,256]{2,1,0:T(8,128)S(1)} %get-tuple-element.67.pe2, f32[16,4,8,256]{3,2,1,0:T(8,128)S(1)} %copy-done, ...), custom_call_target="tpu_custom_call" | custom-call | flops 10000 | bytes 100000 | tf_op jit(solution)/shard_map/pallas_call | solution.py:737
  (19 shorter events, 0.1 us)
Async XLA Ops:
  4.6 5.9 %collective-permute-start = (f32[56,256]{1,0:T(8,128)}, f32[56,256]{1,0:T(8,128)S(1)}, u32[]{:S(2)}, u32[]{:S(2)}) collective-permute-start(f32[56,256]{1,0:T(8,128)} %get-tuple-element.43), channel_id=1, source_target_pairs={{0,112},{1,113},{2,114},{3,115},{4,116},{5,117},{6,118},{7,119},{8... | collective-permute-start | bytes 172040 | tf_op jit(solution)/shard_map/ppermute | solution.py:661
  7.3 14.7 %collective-permute-start.6 = (f32[128,256]{1,0:T(8,128)}, f32[128,256]{1,0:T(8,128)S(1)}, u32[]{:S(2)}, u32[]{:S(2)}) collective-permute-start(f32[128,256]{1,0:T(8,128)} %get-tuple-element.45.tab0), channel_id=1, source_target_pairs={{0,96},{16,112},{32,64},{48,80},{64,32},{80,48},{96,0},{112,16},{1... | collective-permute-start | bytes 393224 | tf_op jit(solution)/shard_map/ppermute | solution.py:699
  8.7 13.4 %collective-permute-start.4 = (f32[128,256]{1,0:T(8,128)}, f32[128,256]{1,0:T(8,128)S(1)}, u32[]{:S(2)}, u32[]{:S(2)}) collective-permute-start(f32[128,256]{1,0:T(8,128)} %get-tuple-element.45.tab0), channel_id=1, source_target_pairs={{0,64},{16,80},{32,96},{48,112},{64,0},{80,16},{96,32},{112,48},{1... | collective-permute-start | bytes 393224 | tf_op jit(solution)/shard_map/ppermute | solution.py:699
  10.3 12.2 %collective-permute-start.2 = (f32[128,256]{1,0:T(8,128)}, f32[128,256]{1,0:T(8,128)S(1)}, u32[]{:S(2)}, u32[]{:S(2)}) collective-permute-start(f32[128,256]{1,0:T(8,128)} %get-tuple-element.45.tab0), channel_id=1, source_target_pairs={{0,32},{16,48},{32,0},{48,16},{64,96},{80,112},{96,64},{112,80},{1... | collective-permute-start | bytes 393224 | tf_op jit(solution)/shard_map/ppermute | solution.py:699
  10.5 10.3 %copy-start.8 = (f32[184,256]{1,0:T(8,128)S(1)}, f32[184,256]{1,0:T(8,128)}, u32[]{:S(2)}) copy-start(f32[184,256]{1,0:T(8,128)} %get-tuple-element.46) | copy-start | bytes 565252
  10.5 12.1 %copy-start.10 = (f32[28,256]{1,0:T(8,128)S(1)}, f32[28,256]{1,0:T(8,128)}, u32[]{:S(2)}) copy-start(f32[28,256]{1,0:T(8,128)} %get-tuple-element.52) | copy-start | bytes 86020
  10.5 12.9 %copy-start.9 = (f32[28,256]{1,0:T(8,128)S(1)}, f32[28,256]{1,0:T(8,128)}, u32[]{:S(2)}) copy-start(f32[28,256]{1,0:T(8,128)} %get-tuple-element.53) | copy-start | bytes 86020
  10.5 21.5 %copy-start.2 = (s32[16384]{0:T(1024)S(1)}, s32[16384]{0:T(1024)}, u32[]{:S(2)}) copy-start(s32[16384]{0:T(1024)} %param.14) | copy-start | bytes 196612
  10.5 21.5 %copy-start.6 = (f32[128,256]{1,0:T(8,128)S(1)}, f32[128,256]{1,0:T(8,128)}, u32[]{:S(2)}) copy-start(f32[128,256]{1,0:T(8,128)} %get-tuple-element.45.tab0) | copy-start | bytes 393220
  10.6 21.5 %all-to-all-start = ((f32[128,4,128]{2,1,0:T(4,128)}), f32[128,4,128]{2,1,0:T(4,128)S(1)}, u32[]{:S(2)}, u32[]{:S(2)}) async-start(f32[128,4,128]{2,1,0:T(4,128)} %bitcast.18), calls=%async_computation | async-start | bytes 524288 | tf_op jit(solution)/shard_map/all_to_all | solution.py:670
  20.8 2.6 %collective-permute-start.1 = (f32[184,256]{1,0:T(8,128)S(1)}, f32[184,256]{1,0:T(8,128)S(1)}, u32[]{:S(2)}, u32[]{:S(2)}) collective-permute-start(f32[184,256]{1,0:T(8,128)S(1)} %copy-done.8), channel_id=1, source_target_pairs={{0,16},{16,0},{32,48},{48,32},{64,80},{80,64},{96,112},{112,96},{1... | collective-permute-start | bytes 565256 | tf_op jit(solution)/shard_map/ppermute | solution.py:696
  22.0 2.1 %collective-permute-start.7 = (f32[128,256]{1,0:T(8,128)S(1)}, f32[128,256]{1,0:T(8,128)S(1)}, u32[]{:S(2)}, u32[]{:S(2)}) collective-permute-start(f32[128,256]{1,0:T(8,128)S(1)} %collective-permute-done.6.tab6), channel_id=1, source_target_pairs={{0,16},{16,0},{32,48},{48,32},{64,80},{80,64},{96,112},{112,96},{1... | collective-permute-start | bytes 393224 | tf_op jit(solution)/shard_map/ppermute | solution.py:700
  22.1 2.0 %collective-permute-start.5 = (f32[128,256]{1,0:T(8,128)S(1)}, f32[128,256]{1,0:T(8,128)S(1)}, u32[]{:S(2)}, u32[]{:S(2)}) collective-permute-start(f32[128,256]{1,0:T(8,128)S(1)} %collective-permute-done.4.tab4), channel_id=1, source_target_pairs={{0,16},{16,0},{32,48},{48,32},{64,80},{80,64},{96,112},{112,96},{1... | collective-permute-start | bytes 393224 | tf_op jit(solution)/shard_map/ppermute | solution.py:700
  22.5 1.6 %collective-permute-start.3 = (f32[128,256]{1,0:T(8,128)S(1)}, f32[128,256]{1,0:T(8,128)S(1)}, u32[]{:S(2)}, u32[]{:S(2)}) collective-permute-start(f32[128,256]{1,0:T(8,128)S(1)} %collective-permute-done.2.tab2), channel_id=1, source_target_pairs={{0,16},{16,0},{32,48},{48,32},{64,80},{80,64},{96,112},{112,96},{1... | collective-permute-start | bytes 393224 | tf_op jit(solution)/shard_map/ppermute | solution.py:700
  22.6 14.8 %collective-permute-start.10 = (f32[28,256]{1,0:T(8,128)S(1)}, f32[28,256]{1,0:T(8,128)S(1)}, u32[]{:S(2)}, u32[]{:S(2)}) collective-permute-start(f32[28,256]{1,0:T(8,128)S(1)} %copy-done.10), channel_id=1, source_target_pairs={{0,1},{1,0},{2,3},{3,2},{4,5},{5,4},{6,7},{7,6},{8,9},{9,8},{10,11... | collective-permute-start | bytes 86024 | tf_op jit(solution)/shard_map/ppermute | solution.py:666
  23.5 13.9 %collective-permute-start.11 = (f32[28,256]{1,0:T(8,128)S(1)}, f32[28,256]{1,0:T(8,128)S(1)}, u32[]{:S(2)}, u32[]{:S(2)}) collective-permute-start(f32[28,256]{1,0:T(8,128)S(1)} %copy-done.9), channel_id=1, source_target_pairs={{0,16},{1,2},{2,1},{3,4},{4,3},{5,6},{6,5},{7,8},{8,7},{9,10},{10,... | collective-permute-start | bytes 86024 | tf_op jit(solution)/shard_map/ppermute | solution.py:661
  32.1 5.3 %copy-start.3 = (f32[4,8,256]{2,1,0:T(8,128)S(1)}, f32[4,8,256]{2,1,0:T(8,128)}, u32[]{:S(2)}) copy-start(f32[4,8,256]{2,1,0:T(8,128)} %get-tuple-element.48.c) | copy-start | bytes 98308
  32.1 5.3 %copy-start.4 = (f32[4,8,256]{2,1,0:T(8,128)S(1)}, f32[4,8,256]{2,1,0:T(8,128)}, u32[]{:S(2)}) copy-start(f32[4,8,256]{2,1,0:T(8,128)} %get-tuple-element.41.ic) | copy-start | bytes 98308
  32.1 5.3 %copy-start.5 = (f32[4,8,256]{2,1,0:T(8,128)S(1)}, f32[4,8,256]{2,1,0:T(8,128)}, u32[]{:S(2)}) copy-start(f32[4,8,256]{2,1,0:T(8,128)} %get-tuple-element.40.zs) | copy-start | bytes 98308
  38.5 15.8 %all-to-all-start.1 = ((f32[128,4,128]{2,1,0:T(4,128)}), f32[128,4,128]{2,1,0:T(4,128)S(1)}, u32[]{:S(2)}, u32[]{:S(2)}) async-start(f32[128,4,128]{2,1,0:T(4,128)} %bitcast.6), calls=%async_computation.1 | async-start | bytes 524288 | tf_op jit(solution)/shard_map/all_to_all | solution.py:670
  42.7 2.1 %collective-permute-start.8 = (f32[24,256]{1,0:T(8,128)S(1)}, f32[24,256]{1,0:T(8,128)S(1)}, u32[]{:S(2)}, u32[]{:S(2)}) collective-permute-start(f32[24,256]{1,0:T(8,128)S(1)} %get-tuple-element.50), channel_id=1, source_target_pairs={{0,16},{1,17},{2,18},{3,19},{4,20},{5,21},{6,22},{7,23},{8,24},{9,... | collective-permute-start | bytes 73736 | tf_op jit(solution)/shard_map/ppermute | solution.py:666
  43.9 3.8 %collective-permute-start.9 = (f32[24,256]{1,0:T(8,128)S(1)}, f32[24,256]{1,0:T(8,128)S(1)}, u32[]{:S(2)}, u32[]{:S(2)}) collective-permute-start(f32[24,256]{1,0:T(8,128)S(1)} %get-tuple-element.51), channel_id=1, source_target_pairs={{0,112},{1,113},{2,114},{3,115},{4,116},{5,117},{6,118},{7,119},{8... | collective-permute-start | bytes 73736 | tf_op jit(solution)/shard_map/ppermute | solution.py:661
  47.7 10.0 %collective-permute-start.12 = (f32[36,256]{1,0:T(8,128)S(1)}, f32[36,256]{1,0:T(8,128)S(1)}, u32[]{:S(2)}, u32[]{:S(2)}) collective-permute-start(f32[36,256]{1,0:T(8,128)S(1)} %get-tuple-element.54), channel_id=1, source_target_pairs={{0,1},{1,0},{2,3},{3,2},{4,5},{5,4},{6,7},{7,6},{8,9},{9,8},{10,11... | collective-permute-start | bytes 110600 | tf_op jit(solution)/shard_map/ppermute | solution.py:666
  49.2 8.6 %collective-permute-start.13 = (f32[36,256]{1,0:T(8,128)S(1)}, f32[36,256]{1,0:T(8,128)S(1)}, u32[]{:S(2)}, u32[]{:S(2)}) collective-permute-start(f32[36,256]{1,0:T(8,128)S(1)} %get-tuple-element.55), channel_id=1, source_target_pairs={{0,16},{1,2},{2,1},{3,4},{4,3},{5,6},{6,5},{7,8},{8,7},{9,10},{10,... | collective-permute-start | bytes 110600 | tf_op jit(solution)/shard_map/ppermute | solution.py:661
  56.9 1.6 %collective-permute-start.14 = (f32[8,256]{1,0:T(8,128)S(1)}, f32[8,256]{1,0:T(8,128)S(1)}, u32[]{:S(2)}, u32[]{:S(2)}) collective-permute-start(f32[8,256]{1,0:T(8,128)S(1)} %get-tuple-element.68), channel_id=1, source_target_pairs={{0,16},{1,17},{2,18},{3,19},{4,20},{5,21},{6,22},{7,23},{8,24},{9,... | collective-permute-start | bytes 24584 | tf_op jit(solution)/shard_map/ppermute | solution.py:666
  57.7 3.1 %collective-permute-start.15 = (f32[8,256]{1,0:T(8,128)S(1)}, f32[8,256]{1,0:T(8,128)S(1)}, u32[]{:S(2)}, u32[]{:S(2)}) collective-permute-start(f32[8,256]{1,0:T(8,128)S(1)} %get-tuple-element.69), channel_id=1, source_target_pairs={{0,112},{1,113},{2,114},{3,115},{4,116},{5,117},{6,118},{7,119},{8... | collective-permute-start | bytes 24584 | tf_op jit(solution)/shard_map/ppermute | solution.py:661
  57.8 3.0 %copy-start.7 = (f32[4,8,256]{2,1,0:T(8,128)S(1)}, f32[4,8,256]{2,1,0:T(8,128)}, u32[]{:S(2)}) copy-start(f32[4,8,256]{2,1,0:T(8,128)} %get-tuple-element.39.s) | copy-start | bytes 98308
  57.8 18.5 %copy-start = (f32[16,4,8,256]{3,2,1,0:T(8,128)S(1)}, f32[16,4,8,256]{3,2,1,0:T(8,128)}, u32[]{:S(2)}) copy-start(f32[16,4,8,256]{3,2,1,0:T(8,128)} %s_old.1) | copy-start | bytes 1572868
  57.8 18.5 %copy-start.1 = (f32[16,4,8,256]{3,2,1,0:T(8,128)S(1)}, f32[16,4,8,256]{3,2,1,0:T(8,128)}, u32[]{:S(2)}) copy-start(f32[16,4,8,256]{3,2,1,0:T(8,128)} %rate.1) | copy-start | bytes 1572868

commit v8 on v7

--- a/solution.py
+++ b/solution.py
@@ -694,13 +694,14 @@
     )
     other_core = [(i, i ^ 1) for i in range(8)]
     both = lax.ppermute(both, "coarse", other_core)
-    tabs = [tab, both]
+    tabs = []
     for hop in (2, 4, 6):
         shard = lax.ppermute(tab, "coarse", [(i, i ^ hop) for i in range(8)])
         tabs += [shard, lax.ppermute(shard, "coarse", other_core)]
     x0b = swap_between(x0b, "coarse")
     y0a, y0b = trade(y0a, y0b, "fine")
-    pay, x0b = lax.optimization_barrier((pay, x0b))
+    pay, both = lax.optimization_barrier((pay, both))
+    tabs = [tab, both] + tabs
     gathered = everyone(pay, 4)
 
     pe, plan, own, own_count, beside, across, at_row, at_lane, counts, x1a, x1b = call(

time: 78 us -> 77.7 us (level)
  waiting for transfers between devices: 17.2 us -> 14.9 us
  starting transfers between devices: 29.4 us -> 31.3 us
    all_to_all x2, waiting for transfers between devices: 11.4 us -> 9.09 us  [everyone(): moved = lax.all_to_all(pay.reshape(DEVICES, rows, LANES), BOTH, 0, 0)]
    ppermute x3, starting transfers between devices: 0.61 us -> 1.66 us  [local(): tabs += [shard, lax.ppermute(shard, 'coarse', other_core)]]
    ppermute x5, starting transfers between devices: 5.58 us -> 4.78 us  [swap_between(): return lax.ppermute(b, BOTH, swap_pairs(axis)[1])]
where the time goes in v8:
time: 77.7 us; the launch traced here: 77.4 us
  starting transfers between devices  31.3 us (40%)
  blocking collectives  15.2 us (20%)
  waiting for transfers between devices  14.9 us (19%)
  Pallas kernels  14.4 us (19%)
  between operations  1.46 us (2%)
    all_to_all x1, blocking collectives, everyone(): moved = lax.all_to_all(pay.reshape(DEVICES, rows, LANES), BOTH, 0, 0)  15.2 us
    all_to_all x2, starting transfers between devices, everyone(): moved = lax.all_to_all(pay.reshape(DEVICES, rows, LANES), BOTH, 0, 0)  15.2 us
    all_to_all x2, waiting for transfers between devices, everyone(): moved = lax.all_to_all(pay.reshape(DEVICES, rows, LANES), BOTH, 0, 0)  9.09 us
    pallas_call x1, Pallas kernels, local(): call(first_kernel, [VM] * 10, [FIELD, ((KC + 1, 24, SLOTS), F32), ((8, SL...  5.29 us
    ppermute x5, waiting for transfers between devices, swap_between(): return lax.ppermute(b, BOTH, swap_pairs(axis)[1])  5.17 us
    ppermute x4, starting transfers between devices, trade(): return (lax.ppermute(a, BOTH, swap_pairs(axis)[0]), b)  4.93 us
    ppermute x5, starting transfers between devices, swap_between(): return lax.ppermute(b, BOTH, swap_pairs(axis)[1])  4.78 us
    pallas_call x1, Pallas kernels, local(): call(source_kernel, [VM, SM, VM, HB, HB] + [VM] * 5, [FIELD, FIELD, FIELD...  3.3 us
  transfers between devices with their start and end apart: 18, of which 6 were waited for; matrix products, arithmetic and copies ran while one was open for 0% of the time, Pallas kernels for 11%

profile of v8, /device:TPU:1, one launch (start us, length us, event | category | flops | bytes accessed | tf_op | source)
XLA Modules:
  0.0 77.4 jit_solution(3283594814228003530)
XLA Ops:
  1.3 3.3 %shard_map.104 = (f32[4,8,256]{2,1,0:T(8,128)}, f32[4,8,256]{2,1,0:T(8,128)}, f32[4,8,256]{2,1,0:T(8,128)}, f32[4,8,256]{2,1,0:T(8,128)}, f32[128,256]{1,0:T(8,1...) custom-call(f32[1,16]{1,0:T(1,128)} %bitcast.21, ...), custom_call_target="tpu_custom_call" | custom-call | flops 10000 | bytes 100000 | tf_op jit(solution)/shard_map/pallas_call | solution.py:678
  4.6 1.5 %collective-permute-start = (f32[184,256]{1,0:T(8,128)}, f32[184,256]{1,0:T(8,128)S(1)}, u32[]{:S(2)}, u32[]{:S(2)}) collective-permute-start(f32[184,256]{1,0:T(8,128)} %get-tuple-element.43), channel_id=1, source_target_pairs={{0,16},{16,0},{32,48},{48,32},{64,80},{80,64},{96,112},{112,96},{1... | collective-permute-start | bytes 565256 | tf_op jit(solution)/shard_map/ppermute | solution.py:696
  6.1 2.6 %collective-permute-start.5 = (f32[128,256]{1,0:T(8,128)}, f32[128,256]{1,0:T(8,128)S(1)}, u32[]{:S(2)}, u32[]{:S(2)}) collective-permute-start(f32[128,256]{1,0:T(8,128)} %get-tuple-element.45.tab0), channel_id=1, source_target_pairs={{0,96},{16,112},{32,64},{48,80},{64,32},{80,48},{96,0},{112,16},{1... | collective-permute-start | bytes 393224 | tf_op jit(solution)/shard_map/ppermute | solution.py:699
  8.7 0.5 collective-permute-start.3
  9.2 0.2 collective-permute-start.1
  9.4 0.0 collective-permute-done.tab1.x0a.xa
  9.4 0.0 copy-start.2
  9.4 11.0 %all-to-all-start = ((f32[128,4,128]{2,1,0:T(4,128)}), f32[128,4,128]{2,1,0:T(4,128)S(1)}, u32[]{:S(2)}, u32[]{:S(2)}) async-start(f32[128,4,128]{2,1,0:T(4,128)} %bitcast.18), calls=%async_computation | async-start | bytes 524288 | tf_op jit(solution)/shard_map/all_to_all | solution.py:670
  20.4 0.0 collective-permute-done.5.tab6
  20.4 1.1 %collective-permute-start.6 = (f32[128,256]{1,0:T(8,128)S(1)}, f32[128,256]{1,0:T(8,128)S(1)}, u32[]{:S(2)}, u32[]{:S(2)}) collective-permute-start(f32[128,256]{1,0:T(8,128)S(1)} %collective-permute-done.5.tab6), channel_id=1, source_target_pairs={{0,16},{16,0},{32,48},{48,32},{64,80},{80,64},{96,112},{112,96},{1... | collective-permute-start | bytes 393224 | tf_op jit(solution)/shard_map/ppermute | solution.py:700
  21.6 0.0 collective-permute-done.3.tab4
  21.6 0.1 collective-permute-start.4
  21.7 0.0 collective-permute-done.1.tab2
  21.7 0.4 collective-permute-start.2
  22.1 0.7 collective-permute-start.7
  22.8 1.3 %collective-permute-start.10 = (f32[28,256]{1,0:T(8,128)S(1)}, f32[28,256]{1,0:T(8,128)S(1)}, u32[]{:S(2)}, u32[]{:S(2)}) collective-permute-start(f32[28,256]{1,0:T(8,128)S(1)} %copy-done.10), channel_id=1, source_target_pairs={{0,1},{1,0},{2,3},{3,2},{4,5},{5,4},{6,7},{7,6},{8,9},{9,8},{10,11... | collective-permute-start | bytes 86024 | tf_op jit(solution)/shard_map/ppermute | solution.py:666
  24.1 0.0 collective-permute-done.6.tab7
  24.1 0.0 copy-done.9
  24.1 1.9 %collective-permute-start.11 = (f32[28,256]{1,0:T(8,128)S(1)}, f32[28,256]{1,0:T(8,128)S(1)}, u32[]{:S(2)}, u32[]{:S(2)}) collective-permute-start(f32[28,256]{1,0:T(8,128)S(1)} %copy-done.9), channel_id=1, source_target_pairs={{0,16},{1,2},{2,1},{3,4},{4,3},{5,6},{6,5},{7,8},{8,7},{9,10},{10,... | collective-permute-start | bytes 86024 | tf_op jit(solution)/shard_map/ppermute | solution.py:661
  26.0 0.0 collective-permute-done.4.tab5
  26.0 0.0 collective-permute-done.2.tab3
  26.0 5.6 %all-to-all-done = f32[128,4,128]{2,1,0:T(4,128)S(1)} async-done(((f32[128,4,128]{2,1,0:T(4,128)}), f32[128,4,128]{2,1,0:T(4,128)S(1)}, u32[]{:S(2)}, u32[]{:S(2)}) %all-to-all-start) | async-done | bytes 262176 | tf_op jit(solution)/shard_map/all_to_all | solution.py:670
  31.7 5.3 %shard_map.105 = (f32[4,8,256]{2,1,0:T(8,128)S(1)}, f32[9,24,256]{2,1,0:T(8,128)S(1)}, f32[8,256]{1,0:T(8,128)S(1)}, s32[8,128]{1,0:T(8,128)S(1)}, s32[8,128]{1,...) custom-call(f32[512,128]{1,0:T(8,128)S(1)} %bitcast.10, ...), custom_call_target="tpu_custom_call" | custom-call | flops 10000 | bytes 100000 | tf_op jit(solution)/shard_map/pallas_call | solution.py:707
  37.0 0.0 collective-permute-done.10.ya.y0a
  37.0 0.0 collective-permute-done.11.yb.y0b
  37.0 0.0 collective-permute-done.7.x0b.xb
  37.0 1.0 %shard_map.107 = f32[512,128]{1,0:T(8,128)} custom-call(s32[8,128]{1,0:T(8,128)S(1)} %get-tuple-element.56.count, s32[8,128]{1,0:T(8,128)S(1)} %get-tuple-element.57.beside, s32[2,8,128]{2,1,0:T(8,128)S(1)} %get-tuple-element.58.across, f32[4,8,256]{2,1,0:T(8,128)S(1)} %copy-done.5, f32[4,8,256]{2,1,0:T(8,128)S(1)} %copy-done.4, ...), custom_call_target="tpu_custom_call" | custom-call | flops 10000 | bytes 100000 | tf_op jit(solution)/shard_map/pallas_call | solution.py:717
  38.1 4.2 %all-to-all-start.1 = ((f32[128,4,128]{2,1,0:T(4,128)}), f32[128,4,128]{2,1,0:T(4,128)S(1)}, u32[]{:S(2)}, u32[]{:S(2)}) async-start(f32[128,4,128]{2,1,0:T(4,128)} %bitcast.6), calls=%async_computation.1 | async-start | bytes 524288 | tf_op jit(solution)/shard_map/all_to_all | solution.py:670
  42.3 1.3 %collective-permute-start.8 = (f32[24,256]{1,0:T(8,128)S(1)}, f32[24,256]{1,0:T(8,128)S(1)}, u32[]{:S(2)}, u32[]{:S(2)}) collective-permute-start(f32[24,256]{1,0:T(8,128)S(1)} %get-tuple-element.50), channel_id=1, source_target_pairs={{0,16},{1,17},{2,18},{3,19},{4,20},{5,21},{6,22},{7,23},{8,24},{9,... | collective-permute-start | bytes 73736 | tf_op jit(solution)/shard_map/ppermute | solution.py:666
  43.6 0.6 collective-permute-start.9
  44.1 0.3 collective-permute-done.8.x1a
  44.4 2.9 %collective-permute-done.9.x1b = f32[24,256]{1,0:T(8,128)S(1)} collective-permute-done((f32[24,256]{1,0:T(8,128)S(1)}, f32[24,256]{1,0:T(8,128)S(1)}, u32[]{:S(2)}, u32[]{:S(2)}) %collective-permute-start.9) | collective-permute-done | bytes 24608 | tf_op jit(solution)/shard_map/ppermute | solution.py:661
  47.3 1.5 %collective-permute-start.12 = (f32[36,256]{1,0:T(8,128)S(1)}, f32[36,256]{1,0:T(8,128)S(1)}, u32[]{:S(2)}, u32[]{:S(2)}) collective-permute-start(f32[36,256]{1,0:T(8,128)S(1)} %get-tuple-element.54), channel_id=1, source_target_pairs={{0,1},{1,0},{2,3},{3,2},{4,5},{5,4},{6,7},{7,6},{8,9},{9,8},{10,11... | collective-permute-start | bytes 110600 | tf_op jit(solution)/shard_map/ppermute | solution.py:666
  48.9 1.6 %collective-permute-start.13 = (f32[36,256]{1,0:T(8,128)S(1)}, f32[36,256]{1,0:T(8,128)S(1)}, u32[]{:S(2)}, u32[]{:S(2)}) collective-permute-start(f32[36,256]{1,0:T(8,128)S(1)} %get-tuple-element.55), channel_id=1, source_target_pairs={{0,16},{1,2},{2,1},{3,4},{4,3},{5,6},{6,5},{7,8},{8,7},{9,10},{10,... | collective-permute-start | bytes 110600 | tf_op jit(solution)/shard_map/ppermute | solution.py:661
  50.5 3.5 %all-to-all-done.1 = f32[128,4,128]{2,1,0:T(4,128)S(1)} async-done(((f32[128,4,128]{2,1,0:T(4,128)}), f32[128,4,128]{2,1,0:T(4,128)S(1)}, u32[]{:S(2)}, u32[]{:S(2)}) %all-to-all-start.1) | async-done | bytes 262176 | tf_op jit(solution)/shard_map/all_to_all | solution.py:670
  53.9 2.7 %shard_map.108 = (f32[4,8,256]{2,1,0:T(8,128)S(1)}, f32[8,256]{1,0:T(8,128)S(1)}, f32[8,128]{1,0:T(8,128)S(1)}, f32[8,256]{1,0:T(8,128)S(1)}, f32[8,256]{1,0:T(8,128)S(1)}) custom-call(s32[8,128]{1,0:T(8,128)S(1)} %get-tuple-element.56.count, f32[512,128]{1,0:T(8,128)S(1)} %bitcast.12, f32[512,128]{1,0:T(8,128)S(1)} %bitcast.11, s32[128,128]{1,0:T(8,128)S(1)} %bitcast.15, ...), custom_call_target="tpu_custom_call" | custom-call | flops 100000000 | bytes 100000 | tf_op jit(solution)/shard_map/pallas_call | solution.py:726
  56.6 0.8 %collective-permute-start.14 = (f32[8,256]{1,0:T(8,128)S(1)}, f32[8,256]{1,0:T(8,128)S(1)}, u32[]{:S(2)}, u32[]{:S(2)}) collective-permute-start(f32[8,256]{1,0:T(8,128)S(1)} %get-tuple-element.68), channel_id=1, source_target_pairs={{0,16},{1,17},{2,18},{3,19},{4,20},{5,21},{6,22},{7,23},{8,24},{9,... | collective-permute-start | bytes 24584 | tf_op jit(solution)/shard_map/ppermute | solution.py:666
  57.4 0.0 collective-permute-start.15
  57.4 0.0 collective-permute-done.12.y1a
  57.4 0.0 collective-permute-done.13.y1b
  57.4 0.0 copy-start
  57.5 0.0 copy-start.1
  57.5 0.4 shard_map.109
  57.9 0.3 collective-permute-done.14.xa
  58.2 2.2 %collective-permute-done.15.xb = f32[8,256]{1,0:T(8,128)S(1)} collective-permute-done((f32[8,256]{1,0:T(8,128)S(1)}, f32[8,256]{1,0:T(8,128)S(1)}, u32[]{:S(2)}, u32[]{:S(2)}) %collective-permute-start.15) | collective-permute-done | bytes 8224 | tf_op jit(solution)/shard_map/ppermute | solution.py:661
  60.5 0.2 shard_map.110
  60.7 15.2 %all_to_all.15 = f32[128,2,128]{2,1,0:T(2,128)S(1)} all-to-all(f32[128,2,128]{2,1,0:T(2,128)S(1)} %bitcast.16), channel_id=1, replica_groups=mesh['coarse'=8,'fine'=16] {'coarse','fine'}, dimensions={0} | all-to-all | bytes 262144 | tf_op jit(solution)/shard_map/all_to_all | solution.py:670
  75.9 1.4 %shard_map.111 = (f32[4,8,256]{2,1,0:T(8,128)}, f32[16,4,8,256]{3,2,1,0:T(8,128)}) custom-call(f32[256,128]{1,0:T(8,128)S(1)} %bitcast.17, f32[4,8,256]{2,1,0:T(8,128)S(1)} %get-tuple-element.75.z1, f32[4,8,256]{2,1,0:T(8,128)S(1)} %get-tuple-element.66.sw.smooth, f32[4,8,256]{2,1,0:T(8,128)S(1)} %get-tuple-element.67.pe2, f32[16,4,8,256]{3,2,1,0:T(8,128)S(1)} %copy-done, ...), custom_call_target="tpu_custom_call" | custom-call | flops 10000 | bytes 100000 | tf_op jit(solution)/shard_map/pallas_call | solution.py:738
  (19 shorter events, 0.1 us)
Async XLA Ops:
  4.6 4.8 %collective-permute-start = (f32[184,256]{1,0:T(8,128)}, f32[184,256]{1,0:T(8,128)S(1)}, u32[]{:S(2)}, u32[]{:S(2)}) collective-permute-start(f32[184,256]{1,0:T(8,128)} %get-tuple-element.43), channel_id=1, source_target_pairs={{0,16},{16,0},{32,48},{48,32},{64,80},{80,64},{96,112},{112,96},{1... | collective-permute-start | bytes 565256 | tf_op jit(solution)/shard_map/ppermute | solution.py:696
  6.1 14.3 %collective-permute-start.5 = (f32[128,256]{1,0:T(8,128)}, f32[128,256]{1,0:T(8,128)S(1)}, u32[]{:S(2)}, u32[]{:S(2)}) collective-permute-start(f32[128,256]{1,0:T(8,128)} %get-tuple-element.45.tab0), channel_id=1, source_target_pairs={{0,96},{16,112},{32,64},{48,80},{64,32},{80,48},{96,0},{112,16},{1... | collective-permute-start | bytes 393224 | tf_op jit(solution)/shard_map/ppermute | solution.py:699
  8.7 12.9 %collective-permute-start.3 = (f32[128,256]{1,0:T(8,128)}, f32[128,256]{1,0:T(8,128)S(1)}, u32[]{:S(2)}, u32[]{:S(2)}) collective-permute-start(f32[128,256]{1,0:T(8,128)} %get-tuple-element.45.tab0), channel_id=1, source_target_pairs={{0,64},{16,80},{32,96},{48,112},{64,0},{80,16},{96,32},{112,48},{1... | collective-permute-start | bytes 393224 | tf_op jit(solution)/shard_map/ppermute | solution.py:699
  9.2 12.5 %collective-permute-start.1 = (f32[128,256]{1,0:T(8,128)}, f32[128,256]{1,0:T(8,128)S(1)}, u32[]{:S(2)}, u32[]{:S(2)}) collective-permute-start(f32[128,256]{1,0:T(8,128)} %get-tuple-element.45.tab0), channel_id=1, source_target_pairs={{0,32},{16,48},{32,0},{48,16},{64,96},{80,112},{96,64},{112,80},{1... | collective-permute-start | bytes 393224 | tf_op jit(solution)/shard_map/ppermute | solution.py:699
  9.4 12.7 %copy-start.8 = (f32[56,256]{1,0:T(8,128)S(1)}, f32[56,256]{1,0:T(8,128)}, u32[]{:S(2)}) copy-start(f32[56,256]{1,0:T(8,128)} %get-tuple-element.49) | copy-start | bytes 172036
  9.4 13.4 %copy-start.10 = (f32[28,256]{1,0:T(8,128)S(1)}, f32[28,256]{1,0:T(8,128)}, u32[]{:S(2)}) copy-start(f32[28,256]{1,0:T(8,128)} %get-tuple-element.52) | copy-start | bytes 86020
  9.4 14.8 %copy-start.9 = (f32[28,256]{1,0:T(8,128)S(1)}, f32[28,256]{1,0:T(8,128)}, u32[]{:S(2)}) copy-start(f32[28,256]{1,0:T(8,128)} %get-tuple-element.53) | copy-start | bytes 86020
  9.4 22.3 %copy-start.2 = (s32[16384]{0:T(1024)S(1)}, s32[16384]{0:T(1024)}, u32[]{:S(2)}) copy-start(s32[16384]{0:T(1024)} %param.14) | copy-start | bytes 196612
  9.4 22.3 %copy-start.6 = (f32[128,256]{1,0:T(8,128)S(1)}, f32[128,256]{1,0:T(8,128)}, u32[]{:S(2)}) copy-start(f32[128,256]{1,0:T(8,128)} %get-tuple-element.45.tab0) | copy-start | bytes 393220
  9.4 22.3 %all-to-all-start = ((f32[128,4,128]{2,1,0:T(4,128)}), f32[128,4,128]{2,1,0:T(4,128)S(1)}, u32[]{:S(2)}, u32[]{:S(2)}) async-start(f32[128,4,128]{2,1,0:T(4,128)} %bitcast.18), calls=%async_computation | async-start | bytes 524288 | tf_op jit(solution)/shard_map/all_to_all | solution.py:670
  20.4 3.7 %collective-permute-start.6 = (f32[128,256]{1,0:T(8,128)S(1)}, f32[128,256]{1,0:T(8,128)S(1)}, u32[]{:S(2)}, u32[]{:S(2)}) collective-permute-start(f32[128,256]{1,0:T(8,128)S(1)} %collective-permute-done.5.tab6), channel_id=1, source_target_pairs={{0,16},{16,0},{32,48},{48,32},{64,80},{80,64},{96,112},{112,96},{1... | collective-permute-start | bytes 393224 | tf_op jit(solution)/shard_map/ppermute | solution.py:700
  21.6 4.5 %collective-permute-start.4 = (f32[128,256]{1,0:T(8,128)S(1)}, f32[128,256]{1,0:T(8,128)S(1)}, u32[]{:S(2)}, u32[]{:S(2)}) collective-permute-start(f32[128,256]{1,0:T(8,128)S(1)} %collective-permute-done.3.tab4), channel_id=1, source_target_pairs={{0,16},{16,0},{32,48},{48,32},{64,80},{80,64},{96,112},{112,96},{1... | collective-permute-start | bytes 393224 | tf_op jit(solution)/shard_map/ppermute | solution.py:700
  21.7 4.3 %collective-permute-start.2 = (f32[128,256]{1,0:T(8,128)S(1)}, f32[128,256]{1,0:T(8,128)S(1)}, u32[]{:S(2)}, u32[]{:S(2)}) collective-permute-start(f32[128,256]{1,0:T(8,128)S(1)} %collective-permute-done.1.tab2), channel_id=1, source_target_pairs={{0,16},{16,0},{32,48},{48,32},{64,80},{80,64},{96,112},{112,96},{1... | collective-permute-start | bytes 393224 | tf_op jit(solution)/shard_map/ppermute | solution.py:700
  22.1 14.9 %collective-permute-start.7 = (f32[56,256]{1,0:T(8,128)S(1)}, f32[56,256]{1,0:T(8,128)S(1)}, u32[]{:S(2)}, u32[]{:S(2)}) collective-permute-start(f32[56,256]{1,0:T(8,128)S(1)} %copy-done.8), channel_id=1, source_target_pairs={{0,112},{1,113},{2,114},{3,115},{4,116},{5,117},{6,118},{7,119},{8... | collective-permute-start | bytes 172040 | tf_op jit(solution)/shard_map/ppermute | solution.py:661
  22.8 14.2 %collective-permute-start.10 = (f32[28,256]{1,0:T(8,128)S(1)}, f32[28,256]{1,0:T(8,128)S(1)}, u32[]{:S(2)}, u32[]{:S(2)}) collective-permute-start(f32[28,256]{1,0:T(8,128)S(1)} %copy-done.10), channel_id=1, source_target_pairs={{0,1},{1,0},{2,3},{3,2},{4,5},{5,4},{6,7},{7,6},{8,9},{9,8},{10,11... | collective-permute-start | bytes 86024 | tf_op jit(solution)/shard_map/ppermute | solution.py:666
  24.1 12.9 %collective-permute-start.11 = (f32[28,256]{1,0:T(8,128)S(1)}, f32[28,256]{1,0:T(8,128)S(1)}, u32[]{:S(2)}, u32[]{:S(2)}) collective-permute-start(f32[28,256]{1,0:T(8,128)S(1)} %copy-done.9), channel_id=1, source_target_pairs={{0,16},{1,2},{2,1},{3,4},{4,3},{5,6},{6,5},{7,8},{8,7},{9,10},{10,... | collective-permute-start | bytes 86024 | tf_op jit(solution)/shard_map/ppermute | solution.py:661
  31.6 5.3 %copy-start.3 = (f32[4,8,256]{2,1,0:T(8,128)S(1)}, f32[4,8,256]{2,1,0:T(8,128)}, u32[]{:S(2)}) copy-start(f32[4,8,256]{2,1,0:T(8,128)} %get-tuple-element.48.c) | copy-start | bytes 98308
  31.7 5.4 %copy-start.4 = (f32[4,8,256]{2,1,0:T(8,128)S(1)}, f32[4,8,256]{2,1,0:T(8,128)}, u32[]{:S(2)}) copy-start(f32[4,8,256]{2,1,0:T(8,128)} %get-tuple-element.41.ic) | copy-start | bytes 98308
  31.7 5.4 %copy-start.5 = (f32[4,8,256]{2,1,0:T(8,128)S(1)}, f32[4,8,256]{2,1,0:T(8,128)}, u32[]{:S(2)}) copy-start(f32[4,8,256]{2,1,0:T(8,128)} %get-tuple-element.40.zs) | copy-start | bytes 98308
  38.1 15.9 %all-to-all-start.1 = ((f32[128,4,128]{2,1,0:T(4,128)}), f32[128,4,128]{2,1,0:T(4,128)S(1)}, u32[]{:S(2)}, u32[]{:S(2)}) async-start(f32[128,4,128]{2,1,0:T(4,128)} %bitcast.6), calls=%async_computation.1 | async-start | bytes 524288 | tf_op jit(solution)/shard_map/all_to_all | solution.py:670
  42.3 2.1 %collective-permute-start.8 = (f32[24,256]{1,0:T(8,128)S(1)}, f32[24,256]{1,0:T(8,128)S(1)}, u32[]{:S(2)}, u32[]{:S(2)}) collective-permute-start(f32[24,256]{1,0:T(8,128)S(1)} %get-tuple-element.50), channel_id=1, source_target_pairs={{0,16},{1,17},{2,18},{3,19},{4,20},{5,21},{6,22},{7,23},{8,24},{9,... | collective-permute-start | bytes 73736 | tf_op jit(solution)/shard_map/ppermute | solution.py:666
  43.6 3.8 %collective-permute-start.9 = (f32[24,256]{1,0:T(8,128)S(1)}, f32[24,256]{1,0:T(8,128)S(1)}, u32[]{:S(2)}, u32[]{:S(2)}) collective-permute-start(f32[24,256]{1,0:T(8,128)S(1)} %get-tuple-element.51), channel_id=1, source_target_pairs={{0,112},{1,113},{2,114},{3,115},{4,116},{5,117},{6,118},{7,119},{8... | collective-permute-start | bytes 73736 | tf_op jit(solution)/shard_map/ppermute | solution.py:661
  47.3 10.1 %collective-permute-start.12 = (f32[36,256]{1,0:T(8,128)S(1)}, f32[36,256]{1,0:T(8,128)S(1)}, u32[]{:S(2)}, u32[]{:S(2)}) collective-permute-start(f32[36,256]{1,0:T(8,128)S(1)} %get-tuple-element.54), channel_id=1, source_target_pairs={{0,1},{1,0},{2,3},{3,2},{4,5},{5,4},{6,7},{7,6},{8,9},{9,8},{10,11... | collective-permute-start | bytes 110600 | tf_op jit(solution)/shard_map/ppermute | solution.py:666
  48.9 8.6 %collective-permute-start.13 = (f32[36,256]{1,0:T(8,128)S(1)}, f32[36,256]{1,0:T(8,128)S(1)}, u32[]{:S(2)}, u32[]{:S(2)}) collective-permute-start(f32[36,256]{1,0:T(8,128)S(1)} %get-tuple-element.55), channel_id=1, source_target_pairs={{0,16},{1,2},{2,1},{3,4},{4,3},{5,6},{6,5},{7,8},{8,7},{9,10},{10,... | collective-permute-start | bytes 110600 | tf_op jit(solution)/shard_map/ppermute | solution.py:661
  56.6 1.6 %collective-permute-start.14 = (f32[8,256]{1,0:T(8,128)S(1)}, f32[8,256]{1,0:T(8,128)S(1)}, u32[]{:S(2)}, u32[]{:S(2)}) collective-permute-start(f32[8,256]{1,0:T(8,128)S(1)} %get-tuple-element.68), channel_id=1, source_target_pairs={{0,16},{1,17},{2,18},{3,19},{4,20},{5,21},{6,22},{7,23},{8,24},{9,... | collective-permute-start | bytes 24584 | tf_op jit(solution)/shard_map/ppermute | solution.py:666
  57.4 3.1 %collective-permute-start.15 = (f32[8,256]{1,0:T(8,128)S(1)}, f32[8,256]{1,0:T(8,128)S(1)}, u32[]{:S(2)}, u32[]{:S(2)}) collective-permute-start(f32[8,256]{1,0:T(8,128)S(1)} %get-tuple-element.69), channel_id=1, source_target_pairs={{0,112},{1,113},{2,114},{3,115},{4,116},{5,117},{6,118},{7,119},{8... | collective-permute-start | bytes 24584 | tf_op jit(solution)/shard_map/ppermute | solution.py:661
  57.4 3.0 %copy-start.7 = (f32[4,8,256]{2,1,0:T(8,128)S(1)}, f32[4,8,256]{2,1,0:T(8,128)}, u32[]{:S(2)}) copy-start(f32[4,8,256]{2,1,0:T(8,128)} %get-tuple-element.39.s) | copy-start | bytes 98308
  57.4 18.5 %copy-start = (f32[16,4,8,256]{3,2,1,0:T(8,128)S(1)}, f32[16,4,8,256]{3,2,1,0:T(8,128)}, u32[]{:S(2)}) copy-start(f32[16,4,8,256]{3,2,1,0:T(8,128)} %s_old.1) | copy-start | bytes 1572868
  57.5 18.5 %copy-start.1 = (f32[16,4,8,256]{3,2,1,0:T(8,128)S(1)}, f32[16,4,8,256]{3,2,1,0:T(8,128)}, u32[]{:S(2)}) copy-start(f32[16,4,8,256]{3,2,1,0:T(8,128)} %rate.1) | copy-start | bytes 1572868

commit v9 on v8

--- a/solution.py
+++ b/solution.py
@@ -717,6 +717,7 @@
     (pay,) = call(early_kernel, [VM] * 11, [((4 * DEVICES, LANES), F32)])(
         own_count, beside, across, zs, ic, pe, c, both, x0b, y0a, y0b
     )
+    pay, x1a = lax.optimization_barrier((pay, x1a))
     sums = everyone(pay, 4)
     y1a, y1b = call(widen_kernel, [VM] * 7, [((row_count(LATE_ROWS), CZ), F32)] * 2)(
         zs, ic, pe, both, x0b, x1a, x1b

time: 77.7 us -> 77.5 us (level)
    ppermute x5, starting transfers between devices: 4.78 us -> 5.91 us  [swap_between(): return lax.ppermute(b, BOTH, swap_pairs(axis)[1])]
  transfers between devices with their start and end apart: 18 -> 18, of which waited for: 6 -> 5; matrix products, arithmetic and copies ran while one was open for 0% -> 0% of each run, Pallas kernels for 11% -> 12%
where the time goes in v9:
time: 77.5 us; the launch traced here: 77.2 us
  starting transfers between devices  31.4 us (41%)
  waiting for transfers between devices  15 us (19%)
  blocking collectives  14.9 us (19%)
  Pallas kernels  14.4 us (19%)
  between operations  1.44 us (2%)
    all_to_all x1, blocking collectives, everyone(): moved = lax.all_to_all(pay.reshape(DEVICES, rows, LANES), BOTH, 0, 0)  14.9 us
    all_to_all x2, starting transfers between devices, everyone(): moved = lax.all_to_all(pay.reshape(DEVICES, rows, LANES), BOTH, 0, 0)  14.6 us
    all_to_all x2, waiting for transfers between devices, everyone(): moved = lax.all_to_all(pay.reshape(DEVICES, rows, LANES), BOTH, 0, 0)  9.09 us
    ppermute x5, starting transfers between devices, swap_between(): return lax.ppermute(b, BOTH, swap_pairs(axis)[1])  5.91 us
    ppermute x5, waiting for transfers between devices, swap_between(): return lax.ppermute(b, BOTH, swap_pairs(axis)[1])  5.58 us
    pallas_call x1, Pallas kernels, local(): call(first_kernel, [VM] * 10, [FIELD, ((KC + 1, 24, SLOTS), F32), ((8, SL...  5.29 us
    ppermute x4, starting transfers between devices, trade(): return (lax.ppermute(a, BOTH, swap_pairs(axis)[0]), b)  4.48 us
    pallas_call x1, Pallas kernels, local(): call(source_kernel, [VM, SM, VM, HB, HB] + [VM] * 5, [FIELD, FIELD, FIELD...  3.3 us
  transfers between devices with their start and end apart: 18, of which 5 were waited for; matrix products, arithmetic and copies ran while one was open for 0% of the time, Pallas kernels for 12%

profile of v9, /device:TPU:1, one launch (start us, length us, event | category | flops | bytes accessed | tf_op | source)
XLA Modules:
  0.0 77.2 jit_solution(13965803473211788584)
XLA Ops:
  1.3 3.3 %shard_map.104 = (f32[4,8,256]{2,1,0:T(8,128)}, f32[4,8,256]{2,1,0:T(8,128)}, f32[4,8,256]{2,1,0:T(8,128)}, f32[4,8,256]{2,1,0:T(8,128)}, f32[128,256]{1,0:T(8,1...) custom-call(f32[1,16]{1,0:T(1,128)} %bitcast.21, ...), custom_call_target="tpu_custom_call" | custom-call | flops 10000 | bytes 100000 | tf_op jit(solution)/shard_map/pallas_call | solution.py:678
  4.6 1.5 %collective-permute-start = (f32[184,256]{1,0:T(8,128)}, f32[184,256]{1,0:T(8,128)S(1)}, u32[]{:S(2)}, u32[]{:S(2)}) collective-permute-start(f32[184,256]{1,0:T(8,128)} %get-tuple-element.45), channel_id=1, source_target_pairs={{0,16},{16,0},{32,48},{48,32},{64,80},{80,64},{96,112},{112,96},{1... | collective-permute-start | bytes 565256 | tf_op jit(solution)/shard_map/ppermute | solution.py:696
  6.1 2.6 %collective-permute-start.5 = (f32[128,256]{1,0:T(8,128)}, f32[128,256]{1,0:T(8,128)S(1)}, u32[]{:S(2)}, u32[]{:S(2)}) collective-permute-start(f32[128,256]{1,0:T(8,128)} %get-tuple-element.47.tab0), channel_id=1, source_target_pairs={{0,96},{16,112},{32,64},{48,80},{64,32},{80,48},{96,0},{112,16},{1... | collective-permute-start | bytes 393224 | tf_op jit(solution)/shard_map/ppermute | solution.py:699
  8.7 0.5 collective-permute-start.3
  9.2 0.2 collective-permute-start.1
  9.4 0.0 collective-permute-done.tab1.xa.x0a
  9.4 0.0 copy-start.2
  9.4 11.0 %all-to-all-start = ((f32[128,4,128]{2,1,0:T(4,128)}), f32[128,4,128]{2,1,0:T(4,128)S(1)}, u32[]{:S(2)}, u32[]{:S(2)}) async-start(f32[128,4,128]{2,1,0:T(4,128)} %bitcast.18), calls=%async_computation | async-start | bytes 524288 | tf_op jit(solution)/shard_map/all_to_all | solution.py:670
  20.4 0.0 collective-permute-done.5.tab6
  20.4 1.1 %collective-permute-start.6 = (f32[128,256]{1,0:T(8,128)S(1)}, f32[128,256]{1,0:T(8,128)S(1)}, u32[]{:S(2)}, u32[]{:S(2)}) collective-permute-start(f32[128,256]{1,0:T(8,128)S(1)} %collective-permute-done.5.tab6), channel_id=1, source_target_pairs={{0,16},{16,0},{32,48},{48,32},{64,80},{80,64},{96,112},{112,96},{1... | collective-permute-start | bytes 393224 | tf_op jit(solution)/shard_map/ppermute | solution.py:700
  21.6 0.0 collective-permute-done.3.tab4
  21.6 0.1 collective-permute-start.4
  21.7 0.0 collective-permute-done.1.tab2
  21.7 0.4 collective-permute-start.2
  22.1 0.7 collective-permute-start.7
  22.8 1.3 %collective-permute-start.8 = (f32[28,256]{1,0:T(8,128)S(1)}, f32[28,256]{1,0:T(8,128)S(1)}, u32[]{:S(2)}, u32[]{:S(2)}) collective-permute-start(f32[28,256]{1,0:T(8,128)S(1)} %copy-done.10), channel_id=1, source_target_pairs={{0,1},{1,0},{2,3},{3,2},{4,5},{5,4},{6,7},{7,6},{8,9},{9,8},{10,11... | collective-permute-start | bytes 86024 | tf_op jit(solution)/shard_map/ppermute | solution.py:666
  24.1 0.0 collective-permute-done.6.tab7
  24.1 0.0 copy-done.9
  24.1 1.9 %collective-permute-start.9 = (f32[28,256]{1,0:T(8,128)S(1)}, f32[28,256]{1,0:T(8,128)S(1)}, u32[]{:S(2)}, u32[]{:S(2)}) collective-permute-start(f32[28,256]{1,0:T(8,128)S(1)} %copy-done.9), channel_id=1, source_target_pairs={{0,16},{1,2},{2,1},{3,4},{4,3},{5,6},{6,5},{7,8},{8,7},{9,10},{10,... | collective-permute-start | bytes 86024 | tf_op jit(solution)/shard_map/ppermute | solution.py:661
  26.0 0.0 collective-permute-done.4.tab5
  26.0 0.0 collective-permute-done.2.tab3
  26.0 5.6 %all-to-all-done = f32[128,4,128]{2,1,0:T(4,128)S(1)} async-done(((f32[128,4,128]{2,1,0:T(4,128)}), f32[128,4,128]{2,1,0:T(4,128)S(1)}, u32[]{:S(2)}, u32[]{:S(2)}) %all-to-all-start) | async-done | bytes 262176 | tf_op jit(solution)/shard_map/all_to_all | solution.py:670
  31.7 5.3 %shard_map.105 = (f32[4,8,256]{2,1,0:T(8,128)S(1)}, f32[9,24,256]{2,1,0:T(8,128)S(1)}, f32[8,256]{1,0:T(8,128)S(1)}, s32[8,128]{1,0:T(8,128)S(1)}, s32[8,128]{1,...) custom-call(f32[512,128]{1,0:T(8,128)S(1)} %bitcast.10, ...), custom_call_target="tpu_custom_call" | custom-call | flops 10000 | bytes 100000 | tf_op jit(solution)/shard_map/pallas_call | solution.py:707
  37.0 0.9 %collective-permute-start.10 = (f32[24,256]{1,0:T(8,128)S(1)}, f32[24,256]{1,0:T(8,128)S(1)}, u32[]{:S(2)}, u32[]{:S(2)}) collective-permute-start(f32[24,256]{1,0:T(8,128)S(1)} %get-tuple-element.57), channel_id=1, source_target_pairs={{0,16},{1,17},{2,18},{3,19},{4,20},{5,21},{6,22},{7,23},{8,24},{9,... | collective-permute-start | bytes 73736 | tf_op jit(solution)/shard_map/ppermute | solution.py:666
  37.8 0.0 collective-permute-done.8.ya.y0a
  37.8 0.0 collective-permute-done.9.yb.y0b
  37.8 0.0 collective-permute-done.7.xb.x0b
  37.9 1.0 %shard_map.106 = f32[512,128]{1,0:T(8,128)} custom-call(s32[8,128]{1,0:T(8,128)S(1)} %get-tuple-element.52.count, s32[8,128]{1,0:T(8,128)S(1)} %get-tuple-element.53.beside, s32[2,8,128]{2,1,0:T(8,128)S(1)} %get-tuple-element.54.across, f32[4,8,256]{2,1,0:T(8,128)S(1)} %copy-done.5, f32[4,8,256]{2,1,0:T(8,128)S(1)} %copy-done.4, ...), custom_call_target="tpu_custom_call" | custom-call | flops 10000 | bytes 100000 | tf_op jit(solution)/shard_map/pallas_call | solution.py:717
  38.9 0.0 collective-permute-done.10.x1a
  38.9 3.6 %all-to-all-start.1 = ((f32[128,4,128]{2,1,0:T(4,128)}), f32[128,4,128]{2,1,0:T(4,128)S(1)}, u32[]{:S(2)}, u32[]{:S(2)}) async-start(f32[128,4,128]{2,1,0:T(4,128)} %bitcast.6), calls=%async_computation.1 | async-start | bytes 524288 | tf_op jit(solution)/shard_map/all_to_all | solution.py:670
  42.5 1.7 %collective-permute-start.11 = (f32[24,256]{1,0:T(8,128)S(1)}, f32[24,256]{1,0:T(8,128)S(1)}, u32[]{:S(2)}, u32[]{:S(2)}) collective-permute-start(f32[24,256]{1,0:T(8,128)S(1)} %get-tuple-element.59), channel_id=1, source_target_pairs={{0,112},{1,113},{2,114},{3,115},{4,116},{5,117},{6,118},{7,119},{8... | collective-permute-start | bytes 73736 | tf_op jit(solution)/shard_map/ppermute | solution.py:661
  44.2 3.3 %collective-permute-done.11.x1b = f32[24,256]{1,0:T(8,128)S(1)} collective-permute-done((f32[24,256]{1,0:T(8,128)S(1)}, f32[24,256]{1,0:T(8,128)S(1)}, u32[]{:S(2)}, u32[]{:S(2)}) %collective-permute-start.11) | collective-permute-done | bytes 24608 | tf_op jit(solution)/shard_map/ppermute | solution.py:661
  47.5 1.5 %collective-permute-start.12 = (f32[36,256]{1,0:T(8,128)S(1)}, f32[36,256]{1,0:T(8,128)S(1)}, u32[]{:S(2)}, u32[]{:S(2)}) collective-permute-start(f32[36,256]{1,0:T(8,128)S(1)} %get-tuple-element.60), channel_id=1, source_target_pairs={{0,1},{1,0},{2,3},{3,2},{4,5},{5,4},{6,7},{7,6},{8,9},{9,8},{10,11... | collective-permute-start | bytes 110600 | tf_op jit(solution)/shard_map/ppermute | solution.py:666
  49.1 1.6 %collective-permute-start.13 = (f32[36,256]{1,0:T(8,128)S(1)}, f32[36,256]{1,0:T(8,128)S(1)}, u32[]{:S(2)}, u32[]{:S(2)}) collective-permute-start(f32[36,256]{1,0:T(8,128)S(1)} %get-tuple-element.61), channel_id=1, source_target_pairs={{0,16},{1,2},{2,1},{3,4},{4,3},{5,6},{6,5},{7,8},{8,7},{9,10},{10,... | collective-permute-start | bytes 110600 | tf_op jit(solution)/shard_map/ppermute | solution.py:661
  50.6 3.5 %all-to-all-done.1 = f32[128,4,128]{2,1,0:T(4,128)S(1)} async-done(((f32[128,4,128]{2,1,0:T(4,128)}), f32[128,4,128]{2,1,0:T(4,128)S(1)}, u32[]{:S(2)}, u32[]{:S(2)}) %all-to-all-start.1) | async-done | bytes 262176 | tf_op jit(solution)/shard_map/all_to_all | solution.py:670
  54.1 2.7 %shard_map.108 = (f32[4,8,256]{2,1,0:T(8,128)S(1)}, f32[8,256]{1,0:T(8,128)S(1)}, f32[8,128]{1,0:T(8,128)S(1)}, f32[8,256]{1,0:T(8,128)S(1)}, f32[8,256]{1,0:T(8,128)S(1)}) custom-call(s32[8,128]{1,0:T(8,128)S(1)} %get-tuple-element.52.count, f32[512,128]{1,0:T(8,128)S(1)} %bitcast.12, f32[512,128]{1,0:T(8,128)S(1)} %bitcast.11, s32[128,128]{1,0:T(8,128)S(1)} %bitcast.15, ...), custom_call_target="tpu_custom_call" | custom-call | flops 100000000 | bytes 100000 | tf_op jit(solution)/shard_map/pallas_call | solution.py:727
  56.8 0.8 %collective-permute-start.14 = (f32[8,256]{1,0:T(8,128)S(1)}, f32[8,256]{1,0:T(8,128)S(1)}, u32[]{:S(2)}, u32[]{:S(2)}) collective-permute-start(f32[8,256]{1,0:T(8,128)S(1)} %get-tuple-element.72), channel_id=1, source_target_pairs={{0,16},{1,17},{2,18},{3,19},{4,20},{5,21},{6,22},{7,23},{8,24},{9,... | collective-permute-start | bytes 24584 | tf_op jit(solution)/shard_map/ppermute | solution.py:666
  57.6 0.0 collective-permute-start.15
  57.6 0.0 collective-permute-done.12.y1a
  57.6 0.0 collective-permute-done.13.y1b
  57.6 0.0 copy-start
  57.6 0.0 copy-start.1
  57.6 0.4 shard_map.109
  58.1 0.3 collective-permute-done.14.xa
  58.4 2.2 %collective-permute-done.15.xb = f32[8,256]{1,0:T(8,128)S(1)} collective-permute-done((f32[8,256]{1,0:T(8,128)S(1)}, f32[8,256]{1,0:T(8,128)S(1)}, u32[]{:S(2)}, u32[]{:S(2)}) %collective-permute-start.15) | collective-permute-done | bytes 8224 | tf_op jit(solution)/shard_map/ppermute | solution.py:661
  60.6 0.2 shard_map.110
  60.9 14.9 %all_to_all.15 = f32[128,2,128]{2,1,0:T(2,128)S(1)} all-to-all(f32[128,2,128]{2,1,0:T(2,128)S(1)} %bitcast.16), channel_id=1, replica_groups=mesh['coarse'=8,'fine'=16] {'coarse','fine'}, dimensions={0} | all-to-all | bytes 262144 | tf_op jit(solution)/shard_map/all_to_all | solution.py:670
  75.8 1.4 %shard_map.111 = (f32[4,8,256]{2,1,0:T(8,128)}, f32[16,4,8,256]{3,2,1,0:T(8,128)}) custom-call(f32[256,128]{1,0:T(8,128)S(1)} %bitcast.17, f32[4,8,256]{2,1,0:T(8,128)S(1)} %get-tuple-element.79.z1, f32[4,8,256]{2,1,0:T(8,128)S(1)} %get-tuple-element.70.sw.smooth, f32[4,8,256]{2,1,0:T(8,128)S(1)} %get-tuple-element.71.pe2, f32[16,4,8,256]{3,2,1,0:T(8,128)S(1)} %copy-done, ...), custom_call_target="tpu_custom_call" | custom-call | flops 10000 | bytes 100000 | tf_op jit(solution)/shard_map/pallas_call | solution.py:739
  (19 shorter events, 0.1 us)
Async XLA Ops:
  4.6 4.8 %collective-permute-start = (f32[184,256]{1,0:T(8,128)}, f32[184,256]{1,0:T(8,128)S(1)}, u32[]{:S(2)}, u32[]{:S(2)}) collective-permute-start(f32[184,256]{1,0:T(8,128)} %get-tuple-element.45), channel_id=1, source_target_pairs={{0,16},{16,0},{32,48},{48,32},{64,80},{80,64},{96,112},{112,96},{1... | collective-permute-start | bytes 565256 | tf_op jit(solution)/shard_map/ppermute | solution.py:696
  6.1 14.3 %collective-permute-start.5 = (f32[128,256]{1,0:T(8,128)}, f32[128,256]{1,0:T(8,128)S(1)}, u32[]{:S(2)}, u32[]{:S(2)}) collective-permute-start(f32[128,256]{1,0:T(8,128)} %get-tuple-element.47.tab0), channel_id=1, source_target_pairs={{0,96},{16,112},{32,64},{48,80},{64,32},{80,48},{96,0},{112,16},{1... | collective-permute-start | bytes 393224 | tf_op jit(solution)/shard_map/ppermute | solution.py:699
  8.7 12.9 %collective-permute-start.3 = (f32[128,256]{1,0:T(8,128)}, f32[128,256]{1,0:T(8,128)S(1)}, u32[]{:S(2)}, u32[]{:S(2)}) collective-permute-start(f32[128,256]{1,0:T(8,128)} %get-tuple-element.47.tab0), channel_id=1, source_target_pairs={{0,64},{16,80},{32,96},{48,112},{64,0},{80,16},{96,32},{112,48},{1... | collective-permute-start | bytes 393224 | tf_op jit(solution)/shard_map/ppermute | solution.py:699
  9.2 12.5 %collective-permute-start.1 = (f32[128,256]{1,0:T(8,128)}, f32[128,256]{1,0:T(8,128)S(1)}, u32[]{:S(2)}, u32[]{:S(2)}) collective-permute-start(f32[128,256]{1,0:T(8,128)} %get-tuple-element.47.tab0), channel_id=1, source_target_pairs={{0,32},{16,48},{32,0},{48,16},{64,96},{80,112},{96,64},{112,80},{1... | collective-permute-start | bytes 393224 | tf_op jit(solution)/shard_map/ppermute | solution.py:699
  9.4 12.7 %copy-start.8 = (f32[56,256]{1,0:T(8,128)S(1)}, f32[56,256]{1,0:T(8,128)}, u32[]{:S(2)}) copy-start(f32[56,256]{1,0:T(8,128)} %get-tuple-element.51) | copy-start | bytes 172036
  9.4 13.4 %copy-start.10 = (f32[28,256]{1,0:T(8,128)S(1)}, f32[28,256]{1,0:T(8,128)}, u32[]{:S(2)}) copy-start(f32[28,256]{1,0:T(8,128)} %get-tuple-element.55) | copy-start | bytes 86020
  9.4 14.8 %copy-start.9 = (f32[28,256]{1,0:T(8,128)S(1)}, f32[28,256]{1,0:T(8,128)}, u32[]{:S(2)}) copy-start(f32[28,256]{1,0:T(8,128)} %get-tuple-element.56) | copy-start | bytes 86020
  9.4 22.3 %copy-start.2 = (s32[16384]{0:T(1024)S(1)}, s32[16384]{0:T(1024)}, u32[]{:S(2)}) copy-start(s32[16384]{0:T(1024)} %param.14) | copy-start | bytes 196612
  9.4 22.3 %copy-start.6 = (f32[128,256]{1,0:T(8,128)S(1)}, f32[128,256]{1,0:T(8,128)}, u32[]{:S(2)}) copy-start(f32[128,256]{1,0:T(8,128)} %get-tuple-element.47.tab0) | copy-start | bytes 393220
  9.4 22.3 %all-to-all-start = ((f32[128,4,128]{2,1,0:T(4,128)}), f32[128,4,128]{2,1,0:T(4,128)S(1)}, u32[]{:S(2)}, u32[]{:S(2)}) async-start(f32[128,4,128]{2,1,0:T(4,128)} %bitcast.18), calls=%async_computation | async-start | bytes 524288 | tf_op jit(solution)/shard_map/all_to_all | solution.py:670
  20.4 3.7 %collective-permute-start.6 = (f32[128,256]{1,0:T(8,128)S(1)}, f32[128,256]{1,0:T(8,128)S(1)}, u32[]{:S(2)}, u32[]{:S(2)}) collective-permute-start(f32[128,256]{1,0:T(8,128)S(1)} %collective-permute-done.5.tab6), channel_id=1, source_target_pairs={{0,16},{16,0},{32,48},{48,32},{64,80},{80,64},{96,112},{112,96},{1... | collective-permute-start | bytes 393224 | tf_op jit(solution)/shard_map/ppermute | solution.py:700
  21.6 4.5 %collective-permute-start.4 = (f32[128,256]{1,0:T(8,128)S(1)}, f32[128,256]{1,0:T(8,128)S(1)}, u32[]{:S(2)}, u32[]{:S(2)}) collective-permute-start(f32[128,256]{1,0:T(8,128)S(1)} %collective-permute-done.3.tab4), channel_id=1, source_target_pairs={{0,16},{16,0},{32,48},{48,32},{64,80},{80,64},{96,112},{112,96},{1... | collective-permute-start | bytes 393224 | tf_op jit(solution)/shard_map/ppermute | solution.py:700
  21.7 4.3 %collective-permute-start.2 = (f32[128,256]{1,0:T(8,128)S(1)}, f32[128,256]{1,0:T(8,128)S(1)}, u32[]{:S(2)}, u32[]{:S(2)}) collective-permute-start(f32[128,256]{1,0:T(8,128)S(1)} %collective-permute-done.1.tab2), channel_id=1, source_target_pairs={{0,16},{16,0},{32,48},{48,32},{64,80},{80,64},{96,112},{112,96},{1... | collective-permute-start | bytes 393224 | tf_op jit(solution)/shard_map/ppermute | solution.py:700
  22.1 15.8 %collective-permute-start.7 = (f32[56,256]{1,0:T(8,128)S(1)}, f32[56,256]{1,0:T(8,128)S(1)}, u32[]{:S(2)}, u32[]{:S(2)}) collective-permute-start(f32[56,256]{1,0:T(8,128)S(1)} %copy-done.8), channel_id=1, source_target_pairs={{0,112},{1,113},{2,114},{3,115},{4,116},{5,117},{6,118},{7,119},{8... | collective-permute-start | bytes 172040 | tf_op jit(solution)/shard_map/ppermute | solution.py:661
  22.8 15.0 %collective-permute-start.8 = (f32[28,256]{1,0:T(8,128)S(1)}, f32[28,256]{1,0:T(8,128)S(1)}, u32[]{:S(2)}, u32[]{:S(2)}) collective-permute-start(f32[28,256]{1,0:T(8,128)S(1)} %copy-done.10), channel_id=1, source_target_pairs={{0,1},{1,0},{2,3},{3,2},{4,5},{5,4},{6,7},{7,6},{8,9},{9,8},{10,11... | collective-permute-start | bytes 86024 | tf_op jit(solution)/shard_map/ppermute | solution.py:666
  24.1 13.7 %collective-permute-start.9 = (f32[28,256]{1,0:T(8,128)S(1)}, f32[28,256]{1,0:T(8,128)S(1)}, u32[]{:S(2)}, u32[]{:S(2)}) collective-permute-start(f32[28,256]{1,0:T(8,128)S(1)} %copy-done.9), channel_id=1, source_target_pairs={{0,16},{1,2},{2,1},{3,4},{4,3},{5,6},{6,5},{7,8},{8,7},{9,10},{10,... | collective-permute-start | bytes 86024 | tf_op jit(solution)/shard_map/ppermute | solution.py:661
  31.6 6.2 %copy-start.3 = (f32[4,8,256]{2,1,0:T(8,128)S(1)}, f32[4,8,256]{2,1,0:T(8,128)}, u32[]{:S(2)}) copy-start(f32[4,8,256]{2,1,0:T(8,128)} %get-tuple-element.50.c) | copy-start | bytes 98308
  31.7 6.2 %copy-start.4 = (f32[4,8,256]{2,1,0:T(8,128)S(1)}, f32[4,8,256]{2,1,0:T(8,128)}, u32[]{:S(2)}) copy-start(f32[4,8,256]{2,1,0:T(8,128)} %get-tuple-element.43.ic) | copy-start | bytes 98308
  31.7 6.2 %copy-start.5 = (f32[4,8,256]{2,1,0:T(8,128)S(1)}, f32[4,8,256]{2,1,0:T(8,128)}, u32[]{:S(2)}) copy-start(f32[4,8,256]{2,1,0:T(8,128)} %get-tuple-element.42.zs) | copy-start | bytes 98308
  37.0 1.9 %collective-permute-start.10 = (f32[24,256]{1,0:T(8,128)S(1)}, f32[24,256]{1,0:T(8,128)S(1)}, u32[]{:S(2)}, u32[]{:S(2)}) collective-permute-start(f32[24,256]{1,0:T(8,128)S(1)} %get-tuple-element.57), channel_id=1, source_target_pairs={{0,16},{1,17},{2,18},{3,19},{4,20},{5,21},{6,22},{7,23},{8,24},{9,... | collective-permute-start | bytes 73736 | tf_op jit(solution)/shard_map/ppermute | solution.py:666
  38.9 15.2 %all-to-all-start.1 = ((f32[128,4,128]{2,1,0:T(4,128)}), f32[128,4,128]{2,1,0:T(4,128)S(1)}, u32[]{:S(2)}, u32[]{:S(2)}) async-start(f32[128,4,128]{2,1,0:T(4,128)} %bitcast.6), calls=%async_computation.1 | async-start | bytes 524288 | tf_op jit(solution)/shard_map/all_to_all | solution.py:670
  42.5 5.0 %collective-permute-start.11 = (f32[24,256]{1,0:T(8,128)S(1)}, f32[24,256]{1,0:T(8,128)S(1)}, u32[]{:S(2)}, u32[]{:S(2)}) collective-permute-start(f32[24,256]{1,0:T(8,128)S(1)} %get-tuple-element.59), channel_id=1, source_target_pairs={{0,112},{1,113},{2,114},{3,115},{4,116},{5,117},{6,118},{7,119},{8... | collective-permute-start | bytes 73736 | tf_op jit(solution)/shard_map/ppermute | solution.py:661
  47.5 10.1 %collective-permute-start.12 = (f32[36,256]{1,0:T(8,128)S(1)}, f32[36,256]{1,0:T(8,128)S(1)}, u32[]{:S(2)}, u32[]{:S(2)}) collective-permute-start(f32[36,256]{1,0:T(8,128)S(1)} %get-tuple-element.60), channel_id=1, source_target_pairs={{0,1},{1,0},{2,3},{3,2},{4,5},{5,4},{6,7},{7,6},{8,9},{9,8},{10,11... | collective-permute-start | bytes 110600 | tf_op jit(solution)/shard_map/ppermute | solution.py:666
  49.1 8.6 %collective-permute-start.13 = (f32[36,256]{1,0:T(8,128)S(1)}, f32[36,256]{1,0:T(8,128)S(1)}, u32[]{:S(2)}, u32[]{:S(2)}) collective-permute-start(f32[36,256]{1,0:T(8,128)S(1)} %get-tuple-element.61), channel_id=1, source_target_pairs={{0,16},{1,2},{2,1},{3,4},{4,3},{5,6},{6,5},{7,8},{8,7},{9,10},{10,... | collective-permute-start | bytes 110600 | tf_op jit(solution)/shard_map/ppermute | solution.py:661
  56.8 1.6 %collective-permute-start.14 = (f32[8,256]{1,0:T(8,128)S(1)}, f32[8,256]{1,0:T(8,128)S(1)}, u32[]{:S(2)}, u32[]{:S(2)}) collective-permute-start(f32[8,256]{1,0:T(8,128)S(1)} %get-tuple-element.72), channel_id=1, source_target_pairs={{0,16},{1,17},{2,18},{3,19},{4,20},{5,21},{6,22},{7,23},{8,24},{9,... | collective-permute-start | bytes 24584 | tf_op jit(solution)/shard_map/ppermute | solution.py:666
  57.6 3.1 %collective-permute-start.15 = (f32[8,256]{1,0:T(8,128)S(1)}, f32[8,256]{1,0:T(8,128)S(1)}, u32[]{:S(2)}, u32[]{:S(2)}) collective-permute-start(f32[8,256]{1,0:T(8,128)S(1)} %get-tuple-element.73), channel_id=1, source_target_pairs={{0,112},{1,113},{2,114},{3,115},{4,116},{5,117},{6,118},{7,119},{8... | collective-permute-start | bytes 24584 | tf_op jit(solution)/shard_map/ppermute | solution.py:661
  57.6 3.0 %copy-start.7 = (f32[4,8,256]{2,1,0:T(8,128)S(1)}, f32[4,8,256]{2,1,0:T(8,128)}, u32[]{:S(2)}) copy-start(f32[4,8,256]{2,1,0:T(8,128)} %get-tuple-element.41.s) | copy-start | bytes 98308
  57.6 18.2 %copy-start = (f32[16,4,8,256]{3,2,1,0:T(8,128)S(1)}, f32[16,4,8,256]{3,2,1,0:T(8,128)}, u32[]{:S(2)}) copy-start(f32[16,4,8,256]{3,2,1,0:T(8,128)} %s_old.1) | copy-start | bytes 1572868
  57.6 18.1 %copy-start.1 = (f32[16,4,8,256]{3,2,1,0:T(8,128)S(1)}, f32[16,4,8,256]{3,2,1,0:T(8,128)}, u32[]{:S(2)}) copy-start(f32[16,4,8,256]{3,2,1,0:T(8,128)} %rate.1) | copy-start | bytes 1572868
